TPU v7x, 32 devices: a whole 2x2x4 slice. The times are simulated.
32 devices in a mesh: gx: 2 (over x), gy: 4 (over y, core), gz: 4 (over z).
Axes of the slice: x: 2, y: 2, z: 4, core: 2. Of those that a mesh axis runs over, the one named last changes fastest.
Arguments:
- initial: float32 [32, 64, 512], P('gx', 'gy', 'gz'), may hold values from -6 to 6
- right_side: float32 [32, 64, 512], P('gx', 'gy', 'gz'), may hold values from -8 to 8
- alpha: float32 [32, 64, 512], P('gx', 'gy', 'gz'), may hold values from 0.5 to 2
- beta_x: float32 [32, 64, 512], P('gx', 'gy', 'gz'), may hold values from 0.25 to 4
- beta_y: float32 [32, 64, 512], P('gx', 'gy', 'gz'), may hold values from 0.25 to 4
- beta_z: float32 [32, 64, 512], P('gx', 'gy', 'gz'), may hold values from 0.25 to 4
Outputs:
- solution: float32 [32, 64, 512], P('gx', 'gy', 'gz')
All inputs are finite; a program needn't handle non-finite values.
Results may differ from a plain program's by a relative error of at most 0.000098.
Values sent between devices are 32-bit elements; how exact they have to be, the bound alone decides.
No kernel may reach another device: no remote copies, remote signals or barrier semaphores. Data moves between devices by JAX's collectives and lax.ppermute only.
A program may use at most 128 MiB of HBM per device.

v0:
```python
import jax
import jax.numpy as jnp
from jax import lax
from jax.sharding import PartitionSpec as P

LEVELS = 6
SWEEPS = 2
BOTTOM = 8


relax = 2.0 / 3.0


def from_behind(block, axis, distance):
    devices = range(lax.axis_size(axis))
    route = [(i - distance, i) for i in devices if i - distance in devices]
    return lax.ppermute(block, axis, route)


def with_halo(cells, sides, width):
    for axis, dim in sides:
        count = lax.axis_size(axis)
        ends = count - 1
        head = lax.slice_in_dim(cells, 0, width, axis=dim)
        tail = lax.slice_in_dim(cells, cells.shape[dim] - width, cells.shape[dim], axis=dim)
        cells = jnp.concatenate(
            [
                lax.ppermute(tail, axis, [(i, (i + 1) % count) for i in range(ends)]),
                cells,
                lax.ppermute(head, axis, [((i + 1) % count, i) for i in range(ends)]),
            ],
            axis=dim,
        )
    return cells


def pair_table(count):
    rows = lax.broadcasted_iota(jnp.int32, (count, count // 2), 0)
    cols = lax.broadcasted_iota(jnp.int32, (count, count // 2), 1)
    return (rows // 2 == cols).astype(jnp.float32)


def odd_table(count):
    rows = lax.broadcasted_iota(jnp.int32, (count, count // 2), 0)
    cols = lax.broadcasted_iota(jnp.int32, (count, count // 2), 1)
    return (rows == 2 * cols + 1).astype(jnp.float32)


def along_second(values, table):
    return jnp.einsum(
        "ayc,yb->abc",
        values,
        table,
        precision=lax.Precision.HIGHEST,
        preferred_element_type=jnp.float32,
    )


def along_third(values, table):
    return jnp.einsum(
        "abz,zc->abc",
        values,
        table,
        precision=lax.Precision.HIGHEST,
        preferred_element_type=jnp.float32,
    )


def reduce_first(values, pick_odd):
    sx, sy, sz = values.shape
    blocks = values.reshape(sx // 2, 2, sy, sz)
    if pick_odd:
        return blocks[:, 1]
    return blocks[:, 0] + blocks[:, 1]


def reduce_dims(values, odd_axis):
    sx, sy, sz = values.shape
    values = reduce_first(values, odd_axis == 0)
    second = odd_table(sy) if odd_axis == 1 else pair_table(sy)
    values = along_second(values, second)
    third = odd_table(sz) if odd_axis == 2 else pair_table(sz)
    return along_third(values, third)


def coarsen_cells(values):
    return 0.125 * reduce_dims(values, -1)


def coarsen_faces(values, axis):
    return 0.25 * reduce_dims(values, axis)


def coarsen_all(base):
    alpha, beta_x, beta_y, beta_z = base
    return (
        coarsen_cells(alpha),
        coarsen_faces(beta_x, 0),
        coarsen_faces(beta_y, 1),
        coarsen_faces(beta_z, 2),
    )


def prolong(values):
    sx, sy, sz = values.shape
    spread = along_third(values, jnp.transpose(pair_table(2 * sz)))
    spread = along_second(spread, jnp.transpose(pair_table(2 * sy)))
    return jnp.repeat(spread, 2, 0)


def lower_faces(values, axis):
    widths = [(0, 0), (0, 0), (0, 0)]
    widths[axis] = (1, 0)
    padded = jnp.pad(values, widths)
    sizes = values.shape
    return padded[: sizes[0], : sizes[1], : sizes[2]]


def full_coeffs(base):
    alpha, beta_x, beta_y, beta_z = base
    weight = 0.25 ** (LEVELS - 1)
    return (
        weight * alpha,
        beta_x,
        beta_y,
        beta_z,
        lower_faces(beta_x, 0),
        lower_faces(beta_y, 1),
        lower_faces(beta_z, 2),
    )


def local_coeffs(base):
    alpha, beta_x, beta_y, beta_z = base
    weight = 0.25 ** (LEVELS - 1)
    edge_x = from_behind(beta_x[-1:, :, :], "gx", 1)
    edge_y = from_behind(beta_y[:, -1:, :], "gy", 1)
    edge_z = from_behind(beta_z[:, :, -1:], "gz", 1)
    low_x = jnp.concatenate([edge_x, beta_x[:-1, :, :]], axis=0)
    low_y = jnp.concatenate([edge_y, beta_y[:, :-1, :]], axis=1)
    low_z = jnp.concatenate([edge_z, beta_z[:, :, :-1]], axis=2)
    return (weight * alpha, beta_x, beta_y, beta_z, low_x, low_y, low_z)


def apply_op(padded, coeffs, scale):
    alpha, beta_x, beta_y, beta_z, low_x, low_y, low_z = coeffs
    centre = padded[1:-1, 1:-1, 1:-1]
    flux = beta_x * (centre - padded[2:, 1:-1, 1:-1]) + low_x * (centre - padded[:-2, 1:-1, 1:-1])
    flux = (
        flux
        + beta_y * (centre - padded[1:-1, 2:, 1:-1])
        + low_y * (centre - padded[1:-1, :-2, 1:-1])
    )
    flux = (
        flux
        + beta_z * (centre - padded[1:-1, 1:-1, 2:])
        + low_z * (centre - padded[1:-1, 1:-1, :-2])
    )
    return alpha * centre + scale * flux


def diagonal_of(coeffs, scale):
    alpha, beta_x, beta_y, beta_z, low_x, low_y, low_z = coeffs
    return alpha + scale * (beta_x + low_x + beta_y + low_y + beta_z + low_z)


def zero_pad(values):
    return jnp.pad(values, 1)


def halo_pad(values):
    return with_halo(values, (("gx", 0), ("gy", 1), ("gz", 2)), 1)


def smooth(field, rhs, coeffs, scale, count, pad_fn):
    diag = diagonal_of(coeffs, scale)
    for sweep in range(count):
        field = field + relax * (rhs - apply_op(pad_fn(field), coeffs, scale)) / diag
    return field


def full_cycle(level, rhs, base):
    coeffs = full_coeffs(base)
    scale = 0.25**level
    field = jnp.zeros(rhs.shape, jnp.float32)
    if level == LEVELS - 1:
        return smooth(field, rhs, coeffs, scale, BOTTOM, zero_pad)
    field = smooth(field, rhs, coeffs, scale, SWEEPS, zero_pad)
    remain = rhs - apply_op(zero_pad(field), coeffs, scale)
    correction = full_cycle(level + 1, coarsen_cells(remain), coarsen_all(base))
    field = field + prolong(correction)
    return smooth(field, rhs, coeffs, scale, SWEEPS, zero_pad)


def local(initial, right_side, alpha, beta_x, beta_y, beta_z):
    gather_level = 2
    base = (alpha, beta_x, beta_y, beta_z)
    field = initial
    rhs = right_side
    saved = []
    for level in range(gather_level):
        scale = 0.25**level
        coeffs = local_coeffs(base)
        if level > 0:
            field = jnp.zeros(rhs.shape, jnp.float32)
        field = smooth(field, rhs, coeffs, scale, SWEEPS, halo_pad)
        remain = rhs - apply_op(halo_pad(field), coeffs, scale)
        saved.append((field, rhs, coeffs, scale))
        rhs = coarsen_cells(remain)
        base = coarsen_all(base)
    block_x, block_y, block_z = rhs.shape
    packed = jnp.stack([rhs, base[0], base[1], base[2], base[3]])[None]
    gathered = lax.all_gather(packed, ("gx", "gy", "gz"), axis=0, tiled=True)
    count_x = lax.axis_size("gx")
    count_y = lax.axis_size("gy")
    count_z = lax.axis_size("gz")
    whole = gathered.reshape(count_x, count_y, count_z, 5, block_x, block_y, block_z)
    whole = whole.transpose(3, 0, 4, 1, 5, 2, 6).reshape(
        5, count_x * block_x, count_y * block_y, count_z * block_z
    )
    correction_full = full_cycle(gather_level, whole[0], (whole[1], whole[2], whole[3], whole[4]))
    start_x = lax.axis_index("gx") * block_x
    start_y = lax.axis_index("gy") * block_y
    start_z = lax.axis_index("gz") * block_z
    correction = lax.dynamic_slice(
        correction_full, (start_x, start_y, start_z), (block_x, block_y, block_z)
    )
    for level in reversed(range(gather_level)):
        field, rhs, coeffs, scale = saved[level]
        field = field + prolong(correction)
        correction = smooth(field, rhs, coeffs, scale, SWEEPS, halo_pad)
    return correction


def solution(mesh):
    in_specs = (
        P("gx", "gy", "gz"),
        P("gx", "gy", "gz"),
        P("gx", "gy", "gz"),
        P("gx", "gy", "gz"),
        P("gx", "gy", "gz"),
        P("gx", "gy", "gz"),
    )
    out_specs = P("gx", "gy", "gz")
    return jax.shard_map(local, mesh=mesh, in_specs=in_specs, out_specs=out_specs, check_vma=False)
```

profile of v0, /device:TPU:1, one launch (start us, length us, event | category | flops | bytes accessed | tf_op | source)
XLA Modules:
  0.0 338.7 jit_solution(3653560250888677563)
XLA Ops:
  0.8 3.9 %collective-permute-start.2 = (f32[1,16,128]{2,1,0:T(8,128)S(1)}, f32[1,16,128]{2,1,0:T(8,128)S(1)}, u32[]{:S(2)}, u32[]{:S(2)}) collective-permute-start(f32[1,16,128]{2,1,0:T(8,128)S(1)} %get-tuple-element.49), channel_id=1, source_target_pairs={{0,16},{1,17},{2,18},{3,19},{4,20},{5,21},{6,22},{7,23},{8,24},{9,... | collective-permute-start | bytes 24584 | tf_op jit(solution)/shard_map/ppermute | solution.py:28
  6.7 4.0 %collective-permute-start.1 = (f32[1,16,128]{2,1,0:T(8,128)S(1)}, f32[1,16,128]{2,1,0:T(8,128)S(1)}, u32[]{:S(2)}, u32[]{:S(2)}) collective-permute-start(f32[1,16,128]{2,1,0:T(8,128)S(1)} %slice.1046), channel_id=1, source_target_pairs={{0,16},{1,17},{2,18},{3,19},{4,20},{5,21},{6,22},{7,23},{8,24},{9,... | collective-permute-start | bytes 24584 | tf_op jit(solution)/shard_map/ppermute | solution.py:17
  11.5 4.5 %collective-permute-start.4 = (f32[16,1,128]{2,1,0:T(1,128)S(1)}, f32[16,1,128]{2,1,0:T(1,128)S(1)}, u32[]{:S(2)}, u32[]{:S(2)}) collective-permute-start(f32[16,1,128]{2,1,0:T(1,128)S(1)} %slice.1052), channel_id=1, source_target_pairs={{0,4},{4,8},{8,12},{1,5},{5,9},{9,13},{2,6},{6,10},{10,14},{3,7},{... | collective-permute-start | bytes 24584 | tf_op jit(solution)/shard_map/ppermute | solution.py:17
  28.2 3.6 %collective-permute-start.5 = (f32[18,1,128]{2,1,0:T(1,128)S(1)}, f32[18,1,128]{2,1,0:T(1,128)S(1)}, u32[]{:S(2)}, u32[]{:S(2)}) collective-permute-start(f32[18,1,128]{2,1,0:T(1,128)S(1)} %get-tuple-element.38), channel_id=1, source_target_pairs={{0,4},{4,8},{8,12},{1,5},{5,9},{9,13},{2,6},{6,10},{10,14},{3,7},{... | collective-permute-start | bytes 27656 | tf_op jit(solution)/shard_map/ppermute | solution.py:28
  34.1 4.0 %collective-permute-start.8 = (f32[18,18,1]{2,1,0:T(8,128)S(1)}, f32[18,18,1]{2,1,0:T(8,128)S(1)}, u32[]{:S(2)}, u32[]{:S(2)}) collective-permute-start(f32[18,18,1]{2,1,0:T(8,128)S(1)} %get-tuple-element.29), channel_id=1, source_target_pairs={{0,1},{1,2},{2,3},{4,5},{5,6},{6,7},{8,9},{9,10},{10,11},{12,13},{... | collective-permute-start | bytes 3896 | tf_op jit(solution)/shard_map/ppermute | solution.py:28
  39.5 4.0 %collective-permute-start.23 = (f32[1,8,64]{2,1,0:T(8,128)S(1)}, f32[1,8,64]{2,1,0:T(8,128)S(1)}, u32[]{:S(2)}, u32[]{:S(2)}) collective-permute-start(f32[1,8,64]{2,1,0:T(8,128)S(1)} %broadcast.384), channel_id=1, source_target_pairs={{0,16},{1,17},{2,18},{3,19},{4,20},{5,21},{6,22},{7,23},{8,24},{9,... | collective-permute-start | bytes 6152 | tf_op jit(solution)/shard_map/ppermute | solution.py:28
  53.9 5.4 %collective-permute-start.12 = (f32[18,1,128]{2,1,0:T(1,128)S(1)}, f32[18,1,128]{2,1,0:T(1,128)S(1)}, u32[]{:S(2)}, u32[]{:S(2)}) collective-permute-start(f32[18,1,128]{2,1,0:T(1,128)S(1)} %get-tuple-element.36), channel_id=1, source_target_pairs={{0,4},{4,8},{8,12},{1,5},{5,9},{9,13},{2,6},{6,10},{10,14},{3,7},{... | collective-permute-start | bytes 27656 | tf_op jit(solution)/shard_map/ppermute | solution.py:28
  61.6 4.0 %collective-permute-start.14 = (f32[18,18,1]{2,1,0:T(8,128)S(1)}, f32[18,18,1]{2,1,0:T(8,128)S(1)}, u32[]{:S(2)}, u32[]{:S(2)}) collective-permute-start(f32[18,18,1]{2,1,0:T(8,128)S(1)} %get-tuple-element.27), channel_id=1, source_target_pairs={{0,1},{1,2},{2,3},{4,5},{5,6},{6,7},{8,9},{9,10},{10,11},{12,13},{... | collective-permute-start | bytes 3896 | tf_op jit(solution)/shard_map/ppermute | solution.py:28
  67.0 5.3 %collective-permute-start.25 = (f32[8,1,64]{2,1,0:T(1,128)S(1)}, f32[8,1,64]{2,1,0:T(1,128)S(1)}, u32[]{:S(2)}, u32[]{:S(2)}) collective-permute-start(f32[8,1,64]{2,1,0:T(1,128)S(1)} %slice.1378), channel_id=1, source_target_pairs={{0,4},{4,8},{8,12},{1,5},{5,9},{9,13},{2,6},{6,10},{10,14},{3,7},{... | collective-permute-start | bytes 6152 | tf_op jit(solution)/shard_map/ppermute | solution.py:17
  77.1 4.0 %collective-permute-start.16 = (f32[1,16,128]{2,1,0:T(8,128)S(1)}, f32[1,16,128]{2,1,0:T(8,128)S(1)}, u32[]{:S(2)}, u32[]{:S(2)}) collective-permute-start(f32[1,16,128]{2,1,0:T(8,128)S(1)} %get-tuple-element.44), channel_id=1, source_target_pairs={{0,16},{1,17},{2,18},{3,19},{4,20},{5,21},{6,22},{7,23},{8,24},{9,... | collective-permute-start | bytes 24584 | tf_op jit(solution)/shard_map/ppermute | solution.py:28
  83.1 3.6 %collective-permute-start.26 = (f32[10,1,64]{2,1,0:T(1,128)S(1)}, f32[10,1,64]{2,1,0:T(1,128)S(1)}, u32[]{:S(2)}, u32[]{:S(2)}) collective-permute-start(f32[10,1,64]{2,1,0:T(1,128)S(1)} %get-tuple-element.68), channel_id=1, source_target_pairs={{0,4},{4,8},{8,12},{1,5},{5,9},{9,13},{2,6},{6,10},{10,14},{3,7},{... | collective-permute-start | bytes 7688 | tf_op jit(solution)/shard_map/ppermute | solution.py:28
  94.6 4.0 %collective-permute-start.20 = (f32[18,18,1]{2,1,0:T(8,128)S(1)}, f32[18,18,1]{2,1,0:T(8,128)S(1)}, u32[]{:S(2)}, u32[]{:S(2)}) collective-permute-start(f32[18,18,1]{2,1,0:T(8,128)S(1)} %get-tuple-element.25), channel_id=1, source_target_pairs={{0,1},{1,2},{2,3},{4,5},{5,6},{6,7},{8,9},{9,10},{10,11},{12,13},{... | collective-permute-start | bytes 3896 | tf_op jit(solution)/shard_map/ppermute | solution.py:28
  103.4 3.8 %collective-permute-start.29 = (f32[10,10,1]{2,1,0:T(8,128)S(1)}, f32[10,10,1]{2,1,0:T(8,128)S(1)}, u32[]{:S(2)}, u32[]{:S(2)}) collective-permute-start(f32[10,10,1]{2,1,0:T(8,128)S(1)} %get-tuple-element.59), channel_id=1, source_target_pairs={{0,1},{1,2},{2,3},{4,5},{5,6},{6,7},{8,9},{9,10},{10,11},{12,13},{... | collective-permute-start | bytes 1208 | tf_op jit(solution)/shard_map/ppermute | solution.py:28
  110.2 4.0 %collective-permute-start.31 = (f32[1,8,64]{2,1,0:T(8,128)S(1)}, f32[1,8,64]{2,1,0:T(8,128)S(1)}, u32[]{:S(2)}, u32[]{:S(2)}) collective-permute-start(f32[1,8,64]{2,1,0:T(8,128)S(1)} %get-tuple-element.76), channel_id=1, source_target_pairs={{0,16},{1,17},{2,18},{3,19},{4,20},{5,21},{6,22},{7,23},{8,24},{9,... | collective-permute-start | bytes 6152 | tf_op jit(solution)/shard_map/ppermute | solution.py:28
  114.9 4.2 %collective-permute-start.32 = (f32[10,1,64]{2,1,0:T(1,128)S(1)}, f32[10,1,64]{2,1,0:T(1,128)S(1)}, u32[]{:S(2)}, u32[]{:S(2)}) collective-permute-start(f32[10,1,64]{2,1,0:T(1,128)S(1)} %get-tuple-element.67), channel_id=1, source_target_pairs={{4,0},{8,4},{12,8},{5,1},{9,5},{13,9},{6,2},{10,6},{14,10},{7,3},{... | collective-permute-start | bytes 7688 | tf_op jit(solution)/shard_map/ppermute | solution.py:30
  124.7 4.6 %collective-permute-start.35 = (f32[10,10,1]{2,1,0:T(8,128)S(1)}, f32[10,10,1]{2,1,0:T(8,128)S(1)}, u32[]{:S(2)}, u32[]{:S(2)}) collective-permute-start(f32[10,10,1]{2,1,0:T(8,128)S(1)} %get-tuple-element.57), channel_id=1, source_target_pairs={{0,1},{1,2},{2,3},{4,5},{5,6},{6,7},{8,9},{9,10},{10,11},{12,13},{... | collective-permute-start | bytes 1208 | tf_op jit(solution)/shard_map/ppermute | solution.py:28
  132.7 4.0 %collective-permute-start.37 = (f32[1,8,64]{2,1,0:T(8,128)S(1)}, f32[1,8,64]{2,1,0:T(8,128)S(1)}, u32[]{:S(2)}, u32[]{:S(2)}) collective-permute-start(f32[1,8,64]{2,1,0:T(8,128)S(1)} %get-tuple-element.74), channel_id=1, source_target_pairs={{0,16},{1,17},{2,18},{3,19},{4,20},{5,21},{6,22},{7,23},{8,24},{9,... | collective-permute-start | bytes 6152 | tf_op jit(solution)/shard_map/ppermute | solution.py:28
  140.5 4.5 %collective-permute-start.39 = (f32[10,1,64]{2,1,0:T(1,128)S(1)}, f32[10,1,64]{2,1,0:T(1,128)S(1)}, u32[]{:S(2)}, u32[]{:S(2)}) collective-permute-start(f32[10,1,64]{2,1,0:T(1,128)S(1)} %get-tuple-element.64), channel_id=1, source_target_pairs={{0,4},{4,8},{8,12},{1,5},{5,9},{9,13},{2,6},{6,10},{10,14},{3,7},{... | collective-permute-start | bytes 7688 | tf_op jit(solution)/shard_map/ppermute | solution.py:28
  147.3 4.6 %collective-permute-start.41 = (f32[10,10,1]{2,1,0:T(8,128)S(1)}, f32[10,10,1]{2,1,0:T(8,128)S(1)}, u32[]{:S(2)}, u32[]{:S(2)}) collective-permute-start(f32[10,10,1]{2,1,0:T(8,128)S(1)} %get-tuple-element.55), channel_id=1, source_target_pairs={{0,1},{1,2},{2,3},{4,5},{5,6},{6,7},{8,9},{9,10},{10,11},{12,13},{... | collective-permute-start | bytes 1208 | tf_op jit(solution)/shard_map/ppermute | solution.py:28
  154.5 76.2 %all-gather = f32[160,4,4,32]{3,2,1,0:T(4,128)S(1)} all-gather(f32[5,4,4,32]{3,2,1,0:T(4,128)S(1)} %fusion.1), channel_id=2, replica_groups=mesh['gx'=2,'gy'=4,'gz'=4] {'gx','gy','gz'}, dimensions={0}, use_global_device_ids=true | all-gather | bytes 337920 | tf_op jit(solution)/shard_map/all_gather | solution.py:213
  243.2 4.0 %collective-permute-start.43 = (f32[1,8,64]{2,1,0:T(8,128)S(1)}, f32[1,8,64]{2,1,0:T(8,128)S(1)}, u32[]{:S(2)}, u32[]{:S(2)}) collective-permute-start(f32[1,8,64]{2,1,0:T(8,128)S(1)} %get-tuple-element.72), channel_id=1, source_target_pairs={{0,16},{1,17},{2,18},{3,19},{4,20},{5,21},{6,22},{7,23},{8,24},{9,... | collective-permute-start | bytes 6152 | tf_op jit(solution)/shard_map/ppermute | solution.py:28
  248.0 8.6 %collective-permute-start.44 = (f32[10,1,64]{2,1,0:T(1,128)S(1)}, f32[10,1,64]{2,1,0:T(1,128)S(1)}, u32[]{:S(2)}, u32[]{:S(2)}) collective-permute-start(f32[10,1,64]{2,1,0:T(1,128)S(1)} %get-tuple-element.63), channel_id=1, source_target_pairs={{4,0},{8,4},{12,8},{5,1},{9,5},{13,9},{6,2},{10,6},{14,10},{7,3},{... | collective-permute-start | bytes 7688 | tf_op jit(solution)/shard_map/ppermute | solution.py:30
  261.0 4.0 %collective-permute-start.47 = (f32[10,10,1]{2,1,0:T(8,128)S(1)}, f32[10,10,1]{2,1,0:T(8,128)S(1)}, u32[]{:S(2)}, u32[]{:S(2)}) collective-permute-start(f32[10,10,1]{2,1,0:T(8,128)S(1)} %get-tuple-element.53), channel_id=1, source_target_pairs={{0,1},{1,2},{2,3},{4,5},{5,6},{6,7},{8,9},{9,10},{10,11},{12,13},{... | collective-permute-start | bytes 1208 | tf_op jit(solution)/shard_map/ppermute | solution.py:28
  267.9 4.0 %collective-permute-start.49 = (f32[1,8,64]{2,1,0:T(8,128)S(1)}, f32[1,8,64]{2,1,0:T(8,128)S(1)}, u32[]{:S(2)}, u32[]{:S(2)}) collective-permute-start(f32[1,8,64]{2,1,0:T(8,128)S(1)} %get-tuple-element.70), channel_id=1, source_target_pairs={{0,16},{1,17},{2,18},{3,19},{4,20},{5,21},{6,22},{7,23},{8,24},{9,... | collective-permute-start | bytes 6152 | tf_op jit(solution)/shard_map/ppermute | solution.py:28
  272.7 4.3 %collective-permute-start.50 = (f32[10,1,64]{2,1,0:T(1,128)S(1)}, f32[10,1,64]{2,1,0:T(1,128)S(1)}, u32[]{:S(2)}, u32[]{:S(2)}) collective-permute-start(f32[10,1,64]{2,1,0:T(1,128)S(1)} %get-tuple-element.61), channel_id=1, source_target_pairs={{4,0},{8,4},{12,8},{5,1},{9,5},{13,9},{6,2},{10,6},{14,10},{7,3},{... | collective-permute-start | bytes 7688 | tf_op jit(solution)/shard_map/ppermute | solution.py:30
  282.8 4.6 %collective-permute-start.53 = (f32[10,10,1]{2,1,0:T(8,128)S(1)}, f32[10,10,1]{2,1,0:T(8,128)S(1)}, u32[]{:S(2)}, u32[]{:S(2)}) collective-permute-start(f32[10,10,1]{2,1,0:T(8,128)S(1)} %get-tuple-element.51), channel_id=1, source_target_pairs={{0,1},{1,2},{2,3},{4,5},{5,6},{6,7},{8,9},{9,10},{10,11},{12,13},{... | collective-permute-start | bytes 1208 | tf_op jit(solution)/shard_map/ppermute | solution.py:28
  290.9 4.0 %collective-permute-start.55 = (f32[1,16,128]{2,1,0:T(8,128)S(1)}, f32[1,16,128]{2,1,0:T(8,128)S(1)}, u32[]{:S(2)}, u32[]{:S(2)}) collective-permute-start(f32[1,16,128]{2,1,0:T(8,128)S(1)} %get-tuple-element.42), channel_id=1, source_target_pairs={{0,16},{1,17},{2,18},{3,19},{4,20},{5,21},{6,22},{7,23},{8,24},{9,... | collective-permute-start | bytes 24584 | tf_op jit(solution)/shard_map/ppermute | solution.py:28
  298.4 5.2 %collective-permute-start.57 = (f32[18,1,128]{2,1,0:T(1,128)S(1)}, f32[18,1,128]{2,1,0:T(1,128)S(1)}, u32[]{:S(2)}, u32[]{:S(2)}) collective-permute-start(f32[18,1,128]{2,1,0:T(1,128)S(1)} %get-tuple-element.32), channel_id=1, source_target_pairs={{0,4},{4,8},{8,12},{1,5},{5,9},{9,13},{2,6},{6,10},{10,14},{3,7},{... | collective-permute-start | bytes 27656 | tf_op jit(solution)/shard_map/ppermute | solution.py:28
  305.9 4.6 %collective-permute-start.59 = (f32[18,18,1]{2,1,0:T(8,128)S(1)}, f32[18,18,1]{2,1,0:T(8,128)S(1)}, u32[]{:S(2)}, u32[]{:S(2)}) collective-permute-start(f32[18,18,1]{2,1,0:T(8,128)S(1)} %get-tuple-element.23), channel_id=1, source_target_pairs={{0,1},{1,2},{2,3},{4,5},{5,6},{6,7},{8,9},{9,10},{10,11},{12,13},{... | collective-permute-start | bytes 3896 | tf_op jit(solution)/shard_map/ppermute | solution.py:28
  315.2 4.0 %collective-permute-start.61 = (f32[1,16,128]{2,1,0:T(8,128)S(1)}, f32[1,16,128]{2,1,0:T(8,128)S(1)}, u32[]{:S(2)}, u32[]{:S(2)}) collective-permute-start(f32[1,16,128]{2,1,0:T(8,128)S(1)} %get-tuple-element.40), channel_id=1, source_target_pairs={{0,16},{1,17},{2,18},{3,19},{4,20},{5,21},{6,22},{7,23},{8,24},{9,... | collective-permute-start | bytes 24584 | tf_op jit(solution)/shard_map/ppermute | solution.py:28
  321.9 6.1 %collective-permute-start.63 = (f32[18,1,128]{2,1,0:T(1,128)S(1)}, f32[18,1,128]{2,1,0:T(1,128)S(1)}, u32[]{:S(2)}, u32[]{:S(2)}) collective-permute-start(f32[18,1,128]{2,1,0:T(1,128)S(1)} %get-tuple-element.30), channel_id=1, source_target_pairs={{0,4},{4,8},{8,12},{1,5},{5,9},{9,13},{2,6},{6,10},{10,14},{3,7},{... | collective-permute-start | bytes 27656 | tf_op jit(solution)/shard_map/ppermute | solution.py:28
  330.2 4.7 %collective-permute-start.65 = (f32[18,18,1]{2,1,0:T(8,128)S(1)}, f32[18,18,1]{2,1,0:T(8,128)S(1)}, u32[]{:S(2)}, u32[]{:S(2)}) collective-permute-start(f32[18,18,1]{2,1,0:T(8,128)S(1)} %get-tuple-element.21), channel_id=1, source_target_pairs={{0,1},{1,2},{2,3},{4,5},{5,6},{6,7},{8,9},{9,10},{10,11},{12,13},{... | collective-permute-start | bytes 3896 | tf_op jit(solution)/shard_map/ppermute | solution.py:28
  (293 shorter events, 122.4 us)
Async XLA Ops:
  0.8 25.4 %collective-permute-start.2 = (f32[1,16,128]{2,1,0:T(8,128)S(1)}, f32[1,16,128]{2,1,0:T(8,128)S(1)}, u32[]{:S(2)}, u32[]{:S(2)}) collective-permute-start(f32[1,16,128]{2,1,0:T(8,128)S(1)} %get-tuple-element.49), channel_id=1, source_target_pairs={{0,16},{1,17},{2,18},{3,19},{4,20},{5,21},{6,22},{7,23},{8,24},{9,... | collective-permute-start | bytes 24584 | tf_op jit(solution)/shard_map/ppermute | solution.py:28
  4.7 21.5 %collective-permute-start = (f32[1,16,128]{2,1,0:T(8,128)S(1)}, f32[1,16,128]{2,1,0:T(8,128)S(1)}, u32[]{:S(2)}, u32[]{:S(2)}) collective-permute-start(f32[1,16,128]{2,1,0:T(8,128)S(1)} %get-tuple-element.48), channel_id=1, source_target_pairs={{16,0},{17,1},{18,2},{19,3},{20,4},{21,5},{22,6},{23,7},{24,8},{25... | collective-permute-start | bytes 24584 | tf_op jit(solution)/shard_map/ppermute | solution.py:30
  6.7 32.8 %collective-permute-start.1 = (f32[1,16,128]{2,1,0:T(8,128)S(1)}, f32[1,16,128]{2,1,0:T(8,128)S(1)}, u32[]{:S(2)}, u32[]{:S(2)}) collective-permute-start(f32[1,16,128]{2,1,0:T(8,128)S(1)} %slice.1046), channel_id=1, source_target_pairs={{0,16},{1,17},{2,18},{3,19},{4,20},{5,21},{6,22},{7,23},{8,24},{9,... | collective-permute-start | bytes 24584 | tf_op jit(solution)/shard_map/ppermute | solution.py:17
  11.5 31.9 %collective-permute-start.4 = (f32[16,1,128]{2,1,0:T(1,128)S(1)}, f32[16,1,128]{2,1,0:T(1,128)S(1)}, u32[]{:S(2)}, u32[]{:S(2)}) collective-permute-start(f32[16,1,128]{2,1,0:T(1,128)S(1)} %slice.1052), channel_id=1, source_target_pairs={{0,4},{4,8},{8,12},{1,5},{5,9},{9,13},{2,6},{6,10},{10,14},{3,7},{... | collective-permute-start | bytes 24584 | tf_op jit(solution)/shard_map/ppermute | solution.py:17
  17.1 21.1 %collective-permute-start.7 = (f32[16,16,1]{2,1,0:T(8,128)S(1)}, f32[16,16,1]{2,1,0:T(8,128)S(1)}, u32[]{:S(2)}, u32[]{:S(2)}) collective-permute-start(f32[16,16,1]{2,1,0:T(8,128)S(1)} %slice.1058), channel_id=1, source_target_pairs={{0,1},{1,2},{2,3},{4,5},{5,6},{6,7},{8,9},{9,10},{10,11},{12,13},{... | collective-permute-start | bytes 3080 | tf_op jit(solution)/shard_map/ppermute | solution.py:17
  32.8 12.0 %collective-permute-start.6 = (f32[18,18,1]{2,1,0:T(8,128)S(1)}, f32[18,18,1]{2,1,0:T(8,128)S(1)}, u32[]{:S(2)}, u32[]{:S(2)}) collective-permute-start(f32[18,18,1]{2,1,0:T(8,128)S(1)} %get-tuple-element.28), channel_id=1, source_target_pairs={{1,0},{2,1},{3,2},{5,4},{6,5},{7,6},{9,8},{10,9},{11,10},{13,12},{... | collective-permute-start | bytes 3896 | tf_op jit(solution)/shard_map/ppermute | solution.py:30
  34.1 10.7 %collective-permute-start.8 = (f32[18,18,1]{2,1,0:T(8,128)S(1)}, f32[18,18,1]{2,1,0:T(8,128)S(1)}, u32[]{:S(2)}, u32[]{:S(2)}) collective-permute-start(f32[18,18,1]{2,1,0:T(8,128)S(1)} %get-tuple-element.29), channel_id=1, source_target_pairs={{0,1},{1,2},{2,3},{4,5},{5,6},{6,7},{8,9},{9,10},{10,11},{12,13},{... | collective-permute-start | bytes 3896 | tf_op jit(solution)/shard_map/ppermute | solution.py:28
  38.2 37.6 %collective-permute-start.21 = (f32[1,8,64]{2,1,0:T(8,128)S(1)}, f32[1,8,64]{2,1,0:T(8,128)S(1)}, u32[]{:S(2)}, u32[]{:S(2)}) collective-permute-start(f32[1,8,64]{2,1,0:T(8,128)S(1)} %broadcast.384), channel_id=1, source_target_pairs={{16,0},{17,1},{18,2},{19,3},{20,4},{21,5},{22,6},{23,7},{24,8},{25... | collective-permute-start | bytes 6152 | tf_op jit(solution)/shard_map/ppermute | solution.py:30
  39.5 37.6 %collective-permute-start.23 = (f32[1,8,64]{2,1,0:T(8,128)S(1)}, f32[1,8,64]{2,1,0:T(8,128)S(1)}, u32[]{:S(2)}, u32[]{:S(2)}) collective-permute-start(f32[1,8,64]{2,1,0:T(8,128)S(1)} %broadcast.384), channel_id=1, source_target_pairs={{0,16},{1,17},{2,18},{3,19},{4,20},{5,21},{6,22},{7,23},{8,24},{9,... | collective-permute-start | bytes 6152 | tf_op jit(solution)/shard_map/ppermute | solution.py:28
  43.5 64.1 %collective-permute-start.22 = (f32[1,8,64]{2,1,0:T(8,128)S(1)}, f32[1,8,64]{2,1,0:T(8,128)S(1)}, u32[]{:S(2)}, u32[]{:S(2)}) collective-permute-start(f32[1,8,64]{2,1,0:T(8,128)S(1)} %slice.1374), channel_id=1, source_target_pairs={{0,16},{1,17},{2,18},{3,19},{4,20},{5,21},{6,22},{7,23},{8,24},{9,... | collective-permute-start | bytes 6152 | tf_op jit(solution)/shard_map/ppermute | solution.py:17
  50.9 8.4 %collective-permute-start.11 = (f32[18,1,128]{2,1,0:T(1,128)S(1)}, f32[18,1,128]{2,1,0:T(1,128)S(1)}, u32[]{:S(2)}, u32[]{:S(2)}) collective-permute-start(f32[18,1,128]{2,1,0:T(1,128)S(1)} %get-tuple-element.37), channel_id=1, source_target_pairs={{4,0},{8,4},{12,8},{5,1},{9,5},{13,9},{6,2},{10,6},{14,10},{7,3},{... | collective-permute-start | bytes 27656 | tf_op jit(solution)/shard_map/ppermute | solution.py:30
  53.9 6.2 %collective-permute-start.12 = (f32[18,1,128]{2,1,0:T(1,128)S(1)}, f32[18,1,128]{2,1,0:T(1,128)S(1)}, u32[]{:S(2)}, u32[]{:S(2)}) collective-permute-start(f32[18,1,128]{2,1,0:T(1,128)S(1)} %get-tuple-element.36), channel_id=1, source_target_pairs={{0,4},{4,8},{8,12},{1,5},{5,9},{9,13},{2,6},{6,10},{10,14},{3,7},{... | collective-permute-start | bytes 27656 | tf_op jit(solution)/shard_map/ppermute | solution.py:28
  60.3 6.7 %collective-permute-start.13 = (f32[18,18,1]{2,1,0:T(8,128)S(1)}, f32[18,18,1]{2,1,0:T(8,128)S(1)}, u32[]{:S(2)}, u32[]{:S(2)}) collective-permute-start(f32[18,18,1]{2,1,0:T(8,128)S(1)} %get-tuple-element.26), channel_id=1, source_target_pairs={{1,0},{2,1},{3,2},{5,4},{6,5},{7,6},{9,8},{10,9},{11,10},{13,12},{... | collective-permute-start | bytes 3896 | tf_op jit(solution)/shard_map/ppermute | solution.py:30
  61.6 10.7 %collective-permute-start.14 = (f32[18,18,1]{2,1,0:T(8,128)S(1)}, f32[18,18,1]{2,1,0:T(8,128)S(1)}, u32[]{:S(2)}, u32[]{:S(2)}) collective-permute-start(f32[18,18,1]{2,1,0:T(8,128)S(1)} %get-tuple-element.27), channel_id=1, source_target_pairs={{0,1},{1,2},{2,3},{4,5},{5,6},{6,7},{8,9},{9,10},{10,11},{12,13},{... | collective-permute-start | bytes 3896 | tf_op jit(solution)/shard_map/ppermute | solution.py:28
  67.0 40.7 %collective-permute-start.25 = (f32[8,1,64]{2,1,0:T(1,128)S(1)}, f32[8,1,64]{2,1,0:T(1,128)S(1)}, u32[]{:S(2)}, u32[]{:S(2)}) collective-permute-start(f32[8,1,64]{2,1,0:T(1,128)S(1)} %slice.1378), channel_id=1, source_target_pairs={{0,4},{4,8},{8,12},{1,5},{5,9},{9,13},{2,6},{6,10},{10,14},{3,7},{... | collective-permute-start | bytes 6152 | tf_op jit(solution)/shard_map/ppermute | solution.py:17
  72.3 35.3 %collective-permute-start.28 = (f32[8,8,1]{2,1,0:T(8,128)S(1)}, f32[8,8,1]{2,1,0:T(8,128)S(1)}, u32[]{:S(2)}, u32[]{:S(2)}) collective-permute-start(f32[8,8,1]{2,1,0:T(8,128)S(1)} %slice.1383), channel_id=1, source_target_pairs={{0,1},{1,2},{2,3},{4,5},{5,6},{6,7},{8,9},{9,10},{10,11},{12,13},{... | collective-permute-start | bytes 776 | tf_op jit(solution)/shard_map/ppermute | solution.py:17
  93.3 8.3 %collective-permute-start.19 = (f32[18,18,1]{2,1,0:T(8,128)S(1)}, f32[18,18,1]{2,1,0:T(8,128)S(1)}, u32[]{:S(2)}, u32[]{:S(2)}) collective-permute-start(f32[18,18,1]{2,1,0:T(8,128)S(1)} %get-tuple-element.24), channel_id=1, source_target_pairs={{1,0},{2,1},{3,2},{5,4},{6,5},{7,6},{9,8},{10,9},{11,10},{13,12},{... | collective-permute-start | bytes 3896 | tf_op jit(solution)/shard_map/ppermute | solution.py:30
  94.6 8.8 %collective-permute-start.20 = (f32[18,18,1]{2,1,0:T(8,128)S(1)}, f32[18,18,1]{2,1,0:T(8,128)S(1)}, u32[]{:S(2)}, u32[]{:S(2)}) collective-permute-start(f32[18,18,1]{2,1,0:T(8,128)S(1)} %get-tuple-element.25), channel_id=1, source_target_pairs={{0,1},{1,2},{2,3},{4,5},{5,6},{6,7},{8,9},{9,10},{10,11},{12,13},{... | collective-permute-start | bytes 3896 | tf_op jit(solution)/shard_map/ppermute | solution.py:28
  101.6 6.2 %collective-permute-start.27 = (f32[10,10,1]{2,1,0:T(8,128)S(1)}, f32[10,10,1]{2,1,0:T(8,128)S(1)}, u32[]{:S(2)}, u32[]{:S(2)}) collective-permute-start(f32[10,10,1]{2,1,0:T(8,128)S(1)} %get-tuple-element.58), channel_id=1, source_target_pairs={{1,0},{2,1},{3,2},{5,4},{6,5},{7,6},{9,8},{10,9},{11,10},{13,12},{... | collective-permute-start | bytes 1208 | tf_op jit(solution)/shard_map/ppermute | solution.py:30
  114.9 7.7 %collective-permute-start.32 = (f32[10,1,64]{2,1,0:T(1,128)S(1)}, f32[10,1,64]{2,1,0:T(1,128)S(1)}, u32[]{:S(2)}, u32[]{:S(2)}) collective-permute-start(f32[10,1,64]{2,1,0:T(1,128)S(1)} %get-tuple-element.67), channel_id=1, source_target_pairs={{4,0},{8,4},{12,8},{5,1},{9,5},{13,9},{6,2},{10,6},{14,10},{7,3},{... | collective-permute-start | bytes 7688 | tf_op jit(solution)/shard_map/ppermute | solution.py:30
  124.7 6.5 %collective-permute-start.35 = (f32[10,10,1]{2,1,0:T(8,128)S(1)}, f32[10,10,1]{2,1,0:T(8,128)S(1)}, u32[]{:S(2)}, u32[]{:S(2)}) collective-permute-start(f32[10,10,1]{2,1,0:T(8,128)S(1)} %get-tuple-element.57), channel_id=1, source_target_pairs={{0,1},{1,2},{2,3},{4,5},{5,6},{6,7},{8,9},{9,10},{10,11},{12,13},{... | collective-permute-start | bytes 1208 | tf_op jit(solution)/shard_map/ppermute | solution.py:28
  137.4 7.7 %collective-permute-start.38 = (f32[10,1,64]{2,1,0:T(1,128)S(1)}, f32[10,1,64]{2,1,0:T(1,128)S(1)}, u32[]{:S(2)}, u32[]{:S(2)}) collective-permute-start(f32[10,1,64]{2,1,0:T(1,128)S(1)} %get-tuple-element.65), channel_id=1, source_target_pairs={{4,0},{8,4},{12,8},{5,1},{9,5},{13,9},{6,2},{10,6},{14,10},{7,3},{... | collective-permute-start | bytes 7688 | tf_op jit(solution)/shard_map/ppermute | solution.py:30
  248.0 10.5 %collective-permute-start.44 = (f32[10,1,64]{2,1,0:T(1,128)S(1)}, f32[10,1,64]{2,1,0:T(1,128)S(1)}, u32[]{:S(2)}, u32[]{:S(2)}) collective-permute-start(f32[10,1,64]{2,1,0:T(1,128)S(1)} %get-tuple-element.63), channel_id=1, source_target_pairs={{4,0},{8,4},{12,8},{5,1},{9,5},{13,9},{6,2},{10,6},{14,10},{7,3},{... | collective-permute-start | bytes 7688 | tf_op jit(solution)/shard_map/ppermute | solution.py:30
  272.7 8.0 %collective-permute-start.50 = (f32[10,1,64]{2,1,0:T(1,128)S(1)}, f32[10,1,64]{2,1,0:T(1,128)S(1)}, u32[]{:S(2)}, u32[]{:S(2)}) collective-permute-start(f32[10,1,64]{2,1,0:T(1,128)S(1)} %get-tuple-element.61), channel_id=1, source_target_pairs={{4,0},{8,4},{12,8},{5,1},{9,5},{13,9},{6,2},{10,6},{14,10},{7,3},{... | collective-permute-start | bytes 7688 | tf_op jit(solution)/shard_map/ppermute | solution.py:30
  282.8 6.2 %collective-permute-start.53 = (f32[10,10,1]{2,1,0:T(8,128)S(1)}, f32[10,10,1]{2,1,0:T(8,128)S(1)}, u32[]{:S(2)}, u32[]{:S(2)}) collective-permute-start(f32[10,10,1]{2,1,0:T(8,128)S(1)} %get-tuple-element.51), channel_id=1, source_target_pairs={{0,1},{1,2},{2,3},{4,5},{5,6},{6,7},{8,9},{9,10},{10,11},{12,13},{... | collective-permute-start | bytes 1208 | tf_op jit(solution)/shard_map/ppermute | solution.py:28
  295.6 8.0 %collective-permute-start.56 = (f32[18,1,128]{2,1,0:T(1,128)S(1)}, f32[18,1,128]{2,1,0:T(1,128)S(1)}, u32[]{:S(2)}, u32[]{:S(2)}) collective-permute-start(f32[18,1,128]{2,1,0:T(1,128)S(1)} %get-tuple-element.33), channel_id=1, source_target_pairs={{4,0},{8,4},{12,8},{5,1},{9,5},{13,9},{6,2},{10,6},{14,10},{7,3},{... | collective-permute-start | bytes 27656 | tf_op jit(solution)/shard_map/ppermute | solution.py:30
  304.6 7.3 %collective-permute-start.58 = (f32[18,18,1]{2,1,0:T(8,128)S(1)}, f32[18,18,1]{2,1,0:T(8,128)S(1)}, u32[]{:S(2)}, u32[]{:S(2)}) collective-permute-start(f32[18,18,1]{2,1,0:T(8,128)S(1)} %get-tuple-element.22), channel_id=1, source_target_pairs={{1,0},{2,1},{3,2},{5,4},{6,5},{7,6},{9,8},{10,9},{11,10},{13,12},{... | collective-permute-start | bytes 3896 | tf_op jit(solution)/shard_map/ppermute | solution.py:30
  305.9 7.6 %collective-permute-start.59 = (f32[18,18,1]{2,1,0:T(8,128)S(1)}, f32[18,18,1]{2,1,0:T(8,128)S(1)}, u32[]{:S(2)}, u32[]{:S(2)}) collective-permute-start(f32[18,18,1]{2,1,0:T(8,128)S(1)} %get-tuple-element.23), channel_id=1, source_target_pairs={{0,1},{1,2},{2,3},{4,5},{5,6},{6,7},{8,9},{9,10},{10,11},{12,13},{... | collective-permute-start | bytes 3896 | tf_op jit(solution)/shard_map/ppermute | solution.py:28
  319.9 8.0 %collective-permute-start.62 = (f32[18,1,128]{2,1,0:T(1,128)S(1)}, f32[18,1,128]{2,1,0:T(1,128)S(1)}, u32[]{:S(2)}, u32[]{:S(2)}) collective-permute-start(f32[18,1,128]{2,1,0:T(1,128)S(1)} %get-tuple-element.31), channel_id=1, source_target_pairs={{4,0},{8,4},{12,8},{5,1},{9,5},{13,9},{6,2},{10,6},{14,10},{7,3},{... | collective-permute-start | bytes 27656 | tf_op jit(solution)/shard_map/ppermute | solution.py:30
  321.9 6.8 %collective-permute-start.63 = (f32[18,1,128]{2,1,0:T(1,128)S(1)}, f32[18,1,128]{2,1,0:T(1,128)S(1)}, u32[]{:S(2)}, u32[]{:S(2)}) collective-permute-start(f32[18,1,128]{2,1,0:T(1,128)S(1)} %get-tuple-element.30), channel_id=1, source_target_pairs={{0,4},{4,8},{8,12},{1,5},{5,9},{9,13},{2,6},{6,10},{10,14},{3,7},{... | collective-permute-start | bytes 27656 | tf_op jit(solution)/shard_map/ppermute | solution.py:28
  328.9 7.4 %collective-permute-start.64 = (f32[18,18,1]{2,1,0:T(8,128)S(1)}, f32[18,18,1]{2,1,0:T(8,128)S(1)}, u32[]{:S(2)}, u32[]{:S(2)}) collective-permute-start(f32[18,18,1]{2,1,0:T(8,128)S(1)} %get-tuple-element.20), channel_id=1, source_target_pairs={{1,0},{2,1},{3,2},{5,4},{6,5},{7,6},{9,8},{10,9},{11,10},{13,12},{... | collective-permute-start | bytes 3896 | tf_op jit(solution)/shard_map/ppermute | solution.py:30
  330.2 7.6 %collective-permute-start.65 = (f32[18,18,1]{2,1,0:T(8,128)S(1)}, f32[18,18,1]{2,1,0:T(8,128)S(1)}, u32[]{:S(2)}, u32[]{:S(2)}) collective-permute-start(f32[18,18,1]{2,1,0:T(8,128)S(1)} %get-tuple-element.21), channel_id=1, source_target_pairs={{0,1},{1,2},{2,3},{4,5},{5,6},{6,7},{8,9},{9,10},{10,11},{12,13},{... | collective-permute-start | bytes 3896 | tf_op jit(solution)/shard_map/ppermute | solution.py:28
  (40 other events, 313.7 us)
where the time goes:
time: 344 us; the launch traced here: 339 us
  starting transfers between devices  203 us (59%)
  blocking collectives  76.2 us (22%)
  waiting for transfers between devices  32.4 us (9%)
  matrix products  13.8 us (4%)
  local copies, waits for them, and re-layouts  6.72 us (2%)
  other arithmetic  5.41 us (2%)
    ppermute x30, starting transfers between devices, with_halo(): lax.ppermute(tail, axis, [(i, (i + 1) % count) for i in range(ends)])  121 us
    all_gather x1, blocking collectives, local(): gathered = lax.all_gather(packed, ('gx', 'gy', 'gz'), axis=0, tiled=True)  76.2 us
    ppermute x30, starting transfers between devices, with_halo(): lax.ppermute(head, axis, [((i + 1) % count, i) for i in range(ends)])  59.5 us
    ppermute x6, starting transfers between devices, from_behind(): return lax.ppermute(block, axis, route)  21.7 us
    ppermute x30, waiting for transfers between devices, with_halo(): lax.ppermute(tail, axis, [(i, (i + 1) % count) for i in range(ends)])  21.6 us
    ppermute x30, waiting for transfers between devices, with_halo(): lax.ppermute(head, axis, [((i + 1) % count, i) for i in range(ends)])  10.8 us
    dot_general x30, matrix products, along_second(): jnp.einsum('ayc,yb->abc', values, table, precision=lax.Precision.HIGHEST,...  8.42 us
  transfers between devices with their start and end apart: 66, of which 31 were waited for; matrix products, arithmetic and copies ran while one was open for 3% of the time, Pallas kernels for 0%

commit v1 on v0

--- a/solution.py
+++ b/solution.py
@@ -20,17 +20,19 @@
 def with_halo(cells, sides, width):
     for axis, dim in sides:
         count = lax.axis_size(axis)
-        ends = count - 1
+        odd = lax.axis_index(axis) % 2 == 1
         head = lax.slice_in_dim(cells, 0, width, axis=dim)
         tail = lax.slice_in_dim(cells, cells.shape[dim] - width, cells.shape[dim], axis=dim)
-        cells = jnp.concatenate(
-            [
-                lax.ppermute(tail, axis, [(i, (i + 1) % count) for i in range(ends)]),
-                cells,
-                lax.ppermute(head, axis, [((i + 1) % count, i) for i in range(ends)]),
-            ],
-            axis=dim,
-        )
+        first = [(i, i ^ 1) for i in range(count) if i ^ 1 < count]
+        second = [(i, ((i + 1) ^ 1) - 1) for i in range(1, count) if ((i + 1) ^ 1) - 1 < count]
+        one = lax.ppermute(jnp.where(odd, head, tail), axis, first)
+        if second:
+            two = lax.ppermute(jnp.where(odd, tail, head), axis, second)
+        else:
+            two = jnp.zeros_like(one)
+        below = jnp.where(odd, one, two)
+        above = jnp.where(odd, two, one)
+        cells = jnp.concatenate([below, cells, above], axis=dim)
     return cells
 
 
@@ -210,7 +212,9 @@
         base = coarsen_all(base)
     block_x, block_y, block_z = rhs.shape
     packed = jnp.stack([rhs, base[0], base[1], base[2], base[3]])[None]
-    gathered = lax.all_gather(packed, ("gx", "gy", "gz"), axis=0, tiled=True)
+    devices = lax.axis_size("gx") * lax.axis_size("gy") * lax.axis_size("gz")
+    copies = jnp.broadcast_to(packed, (devices,) + packed.shape[1:])
+    gathered = lax.all_to_all(copies, ("gx", "gy", "gz"), 0, 0, tiled=True)
     count_x = lax.axis_size("gx")
     count_y = lax.axis_size("gy")
     count_z = lax.axis_size("gz")

time: 344 us -> 226 us (0.66); the launches traced: 339 us -> 224 us
  starting transfers between devices: 203 us -> 111 us
  blocking collectives: 76.2 us -> 0 us
  waiting for transfers between devices: 32.4 us -> 80.7 us
  other arithmetic: 5.41 us -> 9.62 us
    ppermute x60 -> x50, starting transfers between devices: 181 us -> 88 us  [the longest x20 46 us: with_halo(): two = lax.ppermute(jnp.where(odd, tail, head), axis, second)]
    all_gather x1 -> x0, blocking collectives: 76.2 us -> none  [local(): gathered = lax.all_gather(packed, ('gx', 'gy', 'gz'), axis=0, tiled=True)]
    ppermute x60 -> x50, waiting for transfers between devices: 32.4 us -> 69.7 us  [the longest x30 55.5 us: with_halo(): one = lax.ppermute(jnp.where(odd, head, tail), axis, first)]
    all_to_all x0 -> x1, waiting for transfers between devices: none -> 11 us  [local(): gathered = lax.all_to_all(copies, ('gx', 'gy', 'gz'), 0, 0, tiled=True)]
    all_to_all x0 -> x1, starting transfers between devices: none -> 4.13 us  [local(): gathered = lax.all_to_all(copies, ('gx', 'gy', 'gz'), 0, 0, tiled=True)]
  transfers between devices with their start and end apart: 66 -> 57, of which waited for: 31 -> 29; matrix products, arithmetic and copies ran while one was open for 3% -> 5% of each run, Pallas kernels for 0% -> 0%
where the time goes in v1:
time: 226 us; the launch traced here: 224 us
  starting transfers between devices  111 us (49%)
  waiting for transfers between devices  80.7 us (36%)
  matrix products  13.7 us (6%)
  other arithmetic  9.62 us (4%)
  local copies, waits for them, and re-layouts  8.08 us (4%)
    ppermute x30, waiting for transfers between devices, with_halo(): one = lax.ppermute(jnp.where(odd, head, tail), axis, first)  55.5 us
    ppermute x20, starting transfers between devices, with_halo(): two = lax.ppermute(jnp.where(odd, tail, head), axis, second)  46 us
    ppermute x30, starting transfers between devices, with_halo(): one = lax.ppermute(jnp.where(odd, head, tail), axis, first)  41.9 us
    ppermute x6, starting transfers between devices, from_behind(): return lax.ppermute(block, axis, route)  18.7 us
    ppermute x20, waiting for transfers between devices, with_halo(): two = lax.ppermute(jnp.where(odd, tail, head), axis, second)  14.2 us
    all_to_all x1, waiting for transfers between devices, local(): gathered = lax.all_to_all(copies, ('gx', 'gy', 'gz'), 0, 0, tiled=True)  11 us
    dot_general x30, matrix products, along_second(): jnp.einsum('ayc,yb->abc', values, table, precision=lax.Precision.HIGHEST,...  8.35 us
    dot_general x30, matrix products, along_third(): jnp.einsum('abz,zc->abc', values, table, precision=lax.Precision.HIGHEST,...  5.39 us
  transfers between devices with their start and end apart: 57, of which 29 were waited for; matrix products, arithmetic and copies ran while one was open for 5% of the time, Pallas kernels for 0%

profile of v1, /device:TPU:1, one launch (start us, length us, event | category | flops | bytes accessed | tf_op | source)
XLA Modules:
  0.0 224.5 jit_solution(8519469986967464247)
XLA Ops:
  6.3 4.5 %collective-permute-start.4 = (f32[16,1,128]{2,1,0:T(1,128)S(1)}, f32[16,1,128]{2,1,0:T(1,128)S(1)}, u32[]{:S(2)}, u32[]{:S(2)}) collective-permute-start(f32[16,1,128]{2,1,0:T(1,128)S(1)} %slice.1053), channel_id=1, source_target_pairs={{0,4},{4,8},{8,12},{1,5},{5,9},{9,13},{2,6},{6,10},{10,14},{3,7},{... | collective-permute-start | bytes 24584 | tf_op jit(solution)/shard_map/ppermute | solution.py:17
  11.8 3.3 %collective-permute-start.7 = (f32[16,16,1]{2,1,0:T(8,128)S(1)}, f32[16,16,1]{2,1,0:T(8,128)S(1)}, u32[]{:S(2)}, u32[]{:S(2)}) collective-permute-start(f32[16,16,1]{2,1,0:T(8,128)S(1)} %slice.1059), channel_id=1, source_target_pairs={{0,1},{1,2},{2,3},{4,5},{5,6},{6,7},{8,9},{9,10},{10,11},{12,13},{... | collective-permute-start | bytes 3080 | tf_op jit(solution)/shard_map/ppermute | solution.py:17
  23.0 2.7 %collective-permute-done.2 = f32[18,1,128]{2,1,0:T(1,128)S(1)} collective-permute-done((f32[18,1,128]{2,1,0:T(1,128)S(1)}, f32[18,1,128]{2,1,0:T(1,128)S(1)}, u32[]{:S(2)}, u32[]{:S(2)}) %collective-permute-start.2) | collective-permute-done | bytes 9248 | tf_op jit(solution)/shard_map/ppermute | solution.py:30
  26.7 3.9 %collective-permute-start.6 = (f32[18,18,1]{2,1,0:T(8,128)S(1)}, f32[18,18,1]{2,1,0:T(8,128)S(1)}, u32[]{:S(2)}, u32[]{:S(2)}) collective-permute-start(f32[18,18,1]{2,1,0:T(8,128)S(1)} %get-tuple-element.66), channel_id=1, source_target_pairs={{0,1},{1,0},{2,3},{3,2},{4,5},{5,4},{6,7},{7,6},{8,9},{9,8},{10,11... | collective-permute-start | bytes 3896 | tf_op jit(solution)/shard_map/ppermute | solution.py:28
  31.0 4.4 %collective-permute-done.6 = f32[18,18,1]{2,1,0:T(8,128)S(1)} collective-permute-done((f32[18,18,1]{2,1,0:T(8,128)S(1)}, f32[18,18,1]{2,1,0:T(8,128)S(1)}, u32[]{:S(2)}, u32[]{:S(2)}) %collective-permute-start.6) | collective-permute-done | bytes 1328 | tf_op jit(solution)/shard_map/ppermute | solution.py:28
  36.7 3.1 %collective-permute-start.22 = (f32[8,1,64]{2,1,0:T(1,128)S(1)}, f32[8,1,64]{2,1,0:T(1,128)S(1)}, u32[]{:S(2)}, u32[]{:S(2)}) collective-permute-start(f32[8,1,64]{2,1,0:T(1,128)S(1)} %slice.1376), channel_id=1, source_target_pairs={{0,4},{4,8},{8,12},{1,5},{5,9},{9,13},{2,6},{6,10},{10,14},{3,7},{... | collective-permute-start | bytes 6152 | tf_op jit(solution)/shard_map/ppermute | solution.py:17
  39.8 4.6 %collective-permute-start.25 = (f32[8,8,1]{2,1,0:T(8,128)S(1)}, f32[8,8,1]{2,1,0:T(8,128)S(1)}, u32[]{:S(2)}, u32[]{:S(2)}) collective-permute-start(f32[8,8,1]{2,1,0:T(8,128)S(1)} %slice.1382), channel_id=1, source_target_pairs={{0,1},{1,2},{2,3},{4,5},{5,6},{6,7},{8,9},{9,10},{10,11},{12,13},{... | collective-permute-start | bytes 776 | tf_op jit(solution)/shard_map/ppermute | solution.py:17
  44.9 2.6 %collective-permute-done.8 = f32[1,16,128]{2,1,0:T(8,128)S(1)} collective-permute-done((f32[1,16,128]{2,1,0:T(8,128)S(1)}, f32[1,16,128]{2,1,0:T(8,128)S(1)}, u32[]{:S(2)}, u32[]{:S(2)}) %collective-permute-start.8) | collective-permute-done | bytes 8224 | tf_op jit(solution)/shard_map/ppermute | solution.py:28
  47.6 3.2 %collective-permute-start.9 = (f32[18,1,128]{2,1,0:T(1,128)S(1)}, f32[18,1,128]{2,1,0:T(1,128)S(1)}, u32[]{:S(2)}, u32[]{:S(2)}) collective-permute-start(f32[18,1,128]{2,1,0:T(1,128)S(1)} %broadcast_select_fusion.35), channel_id=1, source_target_pairs={{4,8},{8,4},{5,9},{9,5},{6,10},{10,6},{7,11},{11,7},{20,24},{24,20... | collective-permute-start | bytes 27656 | tf_op jit(solution)/shard_map/ppermute | solution.py:30
  52.5 3.2 %collective-permute-start.20 = (f32[10,1,64]{2,1,0:T(1,128)S(1)}, f32[10,1,64]{2,1,0:T(1,128)S(1)}, u32[]{:S(2)}, u32[]{:S(2)}) collective-permute-start(f32[10,1,64]{2,1,0:T(1,128)S(1)} %get-tuple-element.88), channel_id=1, source_target_pairs={{4,8},{8,4},{5,9},{9,5},{6,10},{10,6},{7,11},{11,7},{20,24},{24,20... | collective-permute-start | bytes 7688 | tf_op jit(solution)/shard_map/ppermute | solution.py:30
  58.1 2.6 %collective-permute-start.12 = (f32[18,18,1]{2,1,0:T(8,128)S(1)}, f32[18,18,1]{2,1,0:T(8,128)S(1)}, u32[]{:S(2)}, u32[]{:S(2)}) collective-permute-start(f32[18,18,1]{2,1,0:T(8,128)S(1)} %get-tuple-element.64), channel_id=1, source_target_pairs={{0,1},{1,0},{2,3},{3,2},{4,5},{5,4},{6,7},{7,6},{8,9},{9,8},{10,11... | collective-permute-start | bytes 3896 | tf_op jit(solution)/shard_map/ppermute | solution.py:28
  60.7 5.0 %collective-permute-done.12 = f32[18,18,1]{2,1,0:T(8,128)S(1)} collective-permute-done((f32[18,18,1]{2,1,0:T(8,128)S(1)}, f32[18,18,1]{2,1,0:T(8,128)S(1)}, u32[]{:S(2)}, u32[]{:S(2)}) %collective-permute-start.12) | collective-permute-done | bytes 1328 | tf_op jit(solution)/shard_map/ppermute | solution.py:28
  68.7 3.6 %collective-permute-start.14 = (f32[18,1,128]{2,1,0:T(1,128)S(1)}, f32[18,1,128]{2,1,0:T(1,128)S(1)}, u32[]{:S(2)}, u32[]{:S(2)}) collective-permute-start(f32[18,1,128]{2,1,0:T(1,128)S(1)} %broadcast_select_fusion.31), channel_id=1, source_target_pairs={{4,8},{8,4},{5,9},{9,5},{6,10},{10,6},{7,11},{11,7},{20,24},{24,20... | collective-permute-start | bytes 27656 | tf_op jit(solution)/shard_map/ppermute | solution.py:30
  74.4 5.0 %collective-permute-start.24 = (f32[10,10,1]{2,1,0:T(8,128)S(1)}, f32[10,10,1]{2,1,0:T(8,128)S(1)}, u32[]{:S(2)}, u32[]{:S(2)}) collective-permute-start(f32[10,10,1]{2,1,0:T(8,128)S(1)} %get-tuple-element.86), channel_id=1, source_target_pairs={{0,1},{1,0},{2,3},{3,2},{4,5},{5,4},{6,7},{7,6},{8,9},{9,8},{10,11... | collective-permute-start | bytes 1208 | tf_op jit(solution)/shard_map/ppermute | solution.py:28
  81.6 3.4 %collective-permute-start.17 = (f32[18,18,1]{2,1,0:T(8,128)S(1)}, f32[18,18,1]{2,1,0:T(8,128)S(1)}, u32[]{:S(2)}, u32[]{:S(2)}) collective-permute-start(f32[18,18,1]{2,1,0:T(8,128)S(1)} %get-tuple-element.62), channel_id=1, source_target_pairs={{0,1},{1,0},{2,3},{3,2},{4,5},{5,4},{6,7},{7,6},{8,9},{9,8},{10,11... | collective-permute-start | bytes 3896 | tf_op jit(solution)/shard_map/ppermute | solution.py:28
  85.1 5.3 %collective-permute-done.17 = f32[18,18,1]{2,1,0:T(8,128)S(1)} collective-permute-done((f32[18,18,1]{2,1,0:T(8,128)S(1)}, f32[18,18,1]{2,1,0:T(8,128)S(1)}, u32[]{:S(2)}, u32[]{:S(2)}) %collective-permute-start.17) | collective-permute-done | bytes 1328 | tf_op jit(solution)/shard_map/ppermute | solution.py:28
  93.6 4.4 %collective-permute-start.27 = (f32[10,1,64]{2,1,0:T(1,128)S(1)}, f32[10,1,64]{2,1,0:T(1,128)S(1)}, u32[]{:S(2)}, u32[]{:S(2)}) collective-permute-start(f32[10,1,64]{2,1,0:T(1,128)S(1)} %broadcast_select_fusion.55), channel_id=1, source_target_pairs={{4,8},{8,4},{5,9},{9,5},{6,10},{10,6},{7,11},{11,7},{20,24},{24,20... | collective-permute-start | bytes 7688 | tf_op jit(solution)/shard_map/ppermute | solution.py:30
  100.0 3.1 %collective-permute-start.30 = (f32[10,10,1]{2,1,0:T(8,128)S(1)}, f32[10,10,1]{2,1,0:T(8,128)S(1)}, u32[]{:S(2)}, u32[]{:S(2)}) collective-permute-start(f32[10,10,1]{2,1,0:T(8,128)S(1)} %get-tuple-element.84), channel_id=1, source_target_pairs={{0,1},{1,0},{2,3},{3,2},{4,5},{5,4},{6,7},{7,6},{8,9},{9,8},{10,11... | collective-permute-start | bytes 1208 | tf_op jit(solution)/shard_map/ppermute | solution.py:28
  103.1 2.7 %collective-permute-done.30 = f32[10,10,1]{2,1,0:T(8,128)S(1)} collective-permute-done((f32[10,10,1]{2,1,0:T(8,128)S(1)}, f32[10,10,1]{2,1,0:T(8,128)S(1)}, u32[]{:S(2)}, u32[]{:S(2)}) %collective-permute-start.30) | collective-permute-done | bytes 432 | tf_op jit(solution)/shard_map/ppermute | solution.py:28
  108.5 4.8 %collective-permute-start.32 = (f32[10,1,64]{2,1,0:T(1,128)S(1)}, f32[10,1,64]{2,1,0:T(1,128)S(1)}, u32[]{:S(2)}, u32[]{:S(2)}) collective-permute-start(f32[10,1,64]{2,1,0:T(1,128)S(1)} %broadcast_select_fusion.51), channel_id=1, source_target_pairs={{4,8},{8,4},{5,9},{9,5},{6,10},{10,6},{7,11},{11,7},{20,24},{24,20... | collective-permute-start | bytes 7688 | tf_op jit(solution)/shard_map/ppermute | solution.py:30
  115.4 4.8 %collective-permute-start.35 = (f32[10,10,1]{2,1,0:T(8,128)S(1)}, f32[10,10,1]{2,1,0:T(8,128)S(1)}, u32[]{:S(2)}, u32[]{:S(2)}) collective-permute-start(f32[10,10,1]{2,1,0:T(8,128)S(1)} %get-tuple-element.82), channel_id=1, source_target_pairs={{0,1},{1,0},{2,3},{3,2},{4,5},{5,4},{6,7},{7,6},{8,9},{9,8},{10,11... | collective-permute-start | bytes 1208 | tf_op jit(solution)/shard_map/ppermute | solution.py:28
  125.7 4.1 %all-to-all-start = ((f32[32,1,2560]{2,1,0:T(1,128)}), f32[32,1,2560]{2,1,0:T(1,128)S(1)}, u32[]{:S(2)}, u32[]{:S(2)}) async-start(f32[32,1,2560]{2,1,0:T(1,128)} %reshape.241), calls=%async_computation | async-start | bytes 655360 | tf_op jit(solution)/shard_map/all_to_all | solution.py:217
  130.4 11.0 %all-to-all-done = f32[32,1,2560]{2,1,0:T(1,128)S(1)} async-done(((f32[32,1,2560]{2,1,0:T(1,128)}), f32[32,1,2560]{2,1,0:T(1,128)S(1)}, u32[]{:S(2)}, u32[]{:S(2)}) %all-to-all-start) | async-done | bytes 327712 | tf_op jit(solution)/shard_map/all_to_all | solution.py:217
  157.9 3.6 %collective-permute-start.37 = (f32[10,1,64]{2,1,0:T(1,128)S(1)}, f32[10,1,64]{2,1,0:T(1,128)S(1)}, u32[]{:S(2)}, u32[]{:S(2)}) collective-permute-start(f32[10,1,64]{2,1,0:T(1,128)S(1)} %broadcast_select_fusion.47), channel_id=1, source_target_pairs={{4,8},{8,4},{5,9},{9,5},{6,10},{10,6},{7,11},{11,7},{20,24},{24,20... | collective-permute-start | bytes 7688 | tf_op jit(solution)/shard_map/ppermute | solution.py:30
  171.5 5.2 %collective-permute-start.42 = (f32[10,1,64]{2,1,0:T(1,128)S(1)}, f32[10,1,64]{2,1,0:T(1,128)S(1)}, u32[]{:S(2)}, u32[]{:S(2)}) collective-permute-start(f32[10,1,64]{2,1,0:T(1,128)S(1)} %broadcast_select_fusion.43), channel_id=1, source_target_pairs={{4,8},{8,4},{5,9},{9,5},{6,10},{10,6},{7,11},{11,7},{20,24},{24,20... | collective-permute-start | bytes 7688 | tf_op jit(solution)/shard_map/ppermute | solution.py:30
  178.8 4.0 %collective-permute-start.45 = (f32[10,10,1]{2,1,0:T(8,128)S(1)}, f32[10,10,1]{2,1,0:T(8,128)S(1)}, u32[]{:S(2)}, u32[]{:S(2)}) collective-permute-start(f32[10,10,1]{2,1,0:T(8,128)S(1)} %get-tuple-element.78), channel_id=1, source_target_pairs={{0,1},{1,0},{2,3},{3,2},{4,5},{5,4},{6,7},{7,6},{8,9},{9,8},{10,11... | collective-permute-start | bytes 1208 | tf_op jit(solution)/shard_map/ppermute | solution.py:28
  188.5 5.2 %collective-permute-start.47 = (f32[18,1,128]{2,1,0:T(1,128)S(1)}, f32[18,1,128]{2,1,0:T(1,128)S(1)}, u32[]{:S(2)}, u32[]{:S(2)}) collective-permute-start(f32[18,1,128]{2,1,0:T(1,128)S(1)} %broadcast_select_fusion.27), channel_id=1, source_target_pairs={{4,8},{8,4},{5,9},{9,5},{6,10},{10,6},{7,11},{11,7},{20,24},{24,20... | collective-permute-start | bytes 27656 | tf_op jit(solution)/shard_map/ppermute | solution.py:30
  196.0 3.5 %collective-permute-start.50 = (f32[18,18,1]{2,1,0:T(8,128)S(1)}, f32[18,18,1]{2,1,0:T(8,128)S(1)}, u32[]{:S(2)}, u32[]{:S(2)}) collective-permute-start(f32[18,18,1]{2,1,0:T(8,128)S(1)} %get-tuple-element.60), channel_id=1, source_target_pairs={{0,1},{1,0},{2,3},{3,2},{4,5},{5,4},{6,7},{7,6},{8,9},{9,8},{10,11... | collective-permute-start | bytes 3896 | tf_op jit(solution)/shard_map/ppermute | solution.py:28
  199.5 5.5 %collective-permute-done.50 = f32[18,18,1]{2,1,0:T(8,128)S(1)} collective-permute-done((f32[18,18,1]{2,1,0:T(8,128)S(1)}, f32[18,18,1]{2,1,0:T(8,128)S(1)}, u32[]{:S(2)}, u32[]{:S(2)}) %collective-permute-start.50) | collective-permute-done | bytes 1328 | tf_op jit(solution)/shard_map/ppermute | solution.py:28
  208.0 3.7 %collective-permute-start.52 = (f32[18,1,128]{2,1,0:T(1,128)S(1)}, f32[18,1,128]{2,1,0:T(1,128)S(1)}, u32[]{:S(2)}, u32[]{:S(2)}) collective-permute-start(f32[18,1,128]{2,1,0:T(1,128)S(1)} %broadcast_select_fusion.23), channel_id=1, source_target_pairs={{4,8},{8,4},{5,9},{9,5},{6,10},{10,6},{7,11},{11,7},{20,24},{24,20... | collective-permute-start | bytes 27656 | tf_op jit(solution)/shard_map/ppermute | solution.py:30
  214.0 4.0 %collective-permute-start.55 = (f32[18,18,1]{2,1,0:T(8,128)S(1)}, f32[18,18,1]{2,1,0:T(8,128)S(1)}, u32[]{:S(2)}, u32[]{:S(2)}) collective-permute-start(f32[18,18,1]{2,1,0:T(8,128)S(1)} %get-tuple-element.58), channel_id=1, source_target_pairs={{0,1},{1,0},{2,3},{3,2},{4,5},{5,4},{6,7},{7,6},{8,9},{9,8},{10,11... | collective-permute-start | bytes 3896 | tf_op jit(solution)/shard_map/ppermute | solution.py:28
  218.0 5.5 %collective-permute-done.55 = f32[18,18,1]{2,1,0:T(8,128)S(1)} collective-permute-done((f32[18,18,1]{2,1,0:T(8,128)S(1)}, f32[18,18,1]{2,1,0:T(8,128)S(1)}, u32[]{:S(2)}, u32[]{:S(2)}) %collective-permute-start.55) | collective-permute-done | bytes 1328 | tf_op jit(solution)/shard_map/ppermute | solution.py:28
  (324 shorter events, 87.4 us)
Async XLA Ops:
  0.8 19.8 %collective-permute-start = (f32[1,16,128]{2,1,0:T(8,128)S(1)}, f32[1,16,128]{2,1,0:T(8,128)S(1)}, u32[]{:S(2)}, u32[]{:S(2)}) collective-permute-start(f32[1,16,128]{2,1,0:T(8,128)S(1)} %slice_select_fusion.24), channel_id=1, source_target_pairs={{0,16},{16,0},{1,17},{17,1},{2,18},{18,2},{3,19},{19,3},{4,20},{20... | collective-permute-start | bytes 24584 | tf_op jit(solution)/shard_map/ppermute | solution.py:28
  3.5 36.3 %collective-permute-start.1 = (f32[1,16,128]{2,1,0:T(8,128)S(1)}, f32[1,16,128]{2,1,0:T(8,128)S(1)}, u32[]{:S(2)}, u32[]{:S(2)}) collective-permute-start(f32[1,16,128]{2,1,0:T(8,128)S(1)} %slice.1047), channel_id=1, source_target_pairs={{0,16},{1,17},{2,18},{3,19},{4,20},{5,21},{6,22},{7,23},{8,24},{9,... | collective-permute-start | bytes 24584 | tf_op jit(solution)/shard_map/ppermute | solution.py:17
  6.3 38.2 %collective-permute-start.4 = (f32[16,1,128]{2,1,0:T(1,128)S(1)}, f32[16,1,128]{2,1,0:T(1,128)S(1)}, u32[]{:S(2)}, u32[]{:S(2)}) collective-permute-start(f32[16,1,128]{2,1,0:T(1,128)S(1)} %slice.1053), channel_id=1, source_target_pairs={{0,4},{4,8},{8,12},{1,5},{5,9},{9,13},{2,6},{6,10},{10,14},{3,7},{... | collective-permute-start | bytes 24584 | tf_op jit(solution)/shard_map/ppermute | solution.py:17
  11.8 24.9 %collective-permute-start.7 = (f32[16,16,1]{2,1,0:T(8,128)S(1)}, f32[16,16,1]{2,1,0:T(8,128)S(1)}, u32[]{:S(2)}, u32[]{:S(2)}) collective-permute-start(f32[16,16,1]{2,1,0:T(8,128)S(1)} %slice.1059), channel_id=1, source_target_pairs={{0,1},{1,2},{2,3},{4,5},{5,6},{6,7},{8,9},{9,10},{10,11},{12,13},{... | collective-permute-start | bytes 3080 | tf_op jit(solution)/shard_map/ppermute | solution.py:17
  20.6 5.0 %collective-permute-start.2 = (f32[18,1,128]{2,1,0:T(1,128)S(1)}, f32[18,1,128]{2,1,0:T(1,128)S(1)}, u32[]{:S(2)}, u32[]{:S(2)}) collective-permute-start(f32[18,1,128]{2,1,0:T(1,128)S(1)} %broadcast_select_fusion.39), channel_id=1, source_target_pairs={{4,8},{8,4},{5,9},{9,5},{6,10},{10,6},{7,11},{11,7},{20,24},{24,20... | collective-permute-start | bytes 27656 | tf_op jit(solution)/shard_map/ppermute | solution.py:30
  25.9 5.0 %collective-permute-start.5 = (f32[18,18,1]{2,1,0:T(8,128)S(1)}, f32[18,18,1]{2,1,0:T(8,128)S(1)}, u32[]{:S(2)}, u32[]{:S(2)}) collective-permute-start(f32[18,18,1]{2,1,0:T(8,128)S(1)} %get-tuple-element.65), channel_id=1, source_target_pairs={{1,2},{2,1},{5,6},{6,5},{9,10},{10,9},{13,14},{14,13},{17,18},{18,... | collective-permute-start | bytes 3896 | tf_op jit(solution)/shard_map/ppermute | solution.py:30
  26.7 8.7 %collective-permute-start.6 = (f32[18,18,1]{2,1,0:T(8,128)S(1)}, f32[18,18,1]{2,1,0:T(8,128)S(1)}, u32[]{:S(2)}, u32[]{:S(2)}) collective-permute-start(f32[18,18,1]{2,1,0:T(8,128)S(1)} %get-tuple-element.66), channel_id=1, source_target_pairs={{0,1},{1,0},{2,3},{3,2},{4,5},{5,4},{6,7},{7,6},{8,9},{9,8},{10,11... | collective-permute-start | bytes 3896 | tf_op jit(solution)/shard_map/ppermute | solution.py:28
  30.9 14.0 %collective-permute-start.18 = (f32[1,8,64]{2,1,0:T(8,128)S(1)}, f32[1,8,64]{2,1,0:T(8,128)S(1)}, u32[]{:S(2)}, u32[]{:S(2)}) collective-permute-start(f32[1,8,64]{2,1,0:T(8,128)S(1)} %broadcast.396), channel_id=1, source_target_pairs={{0,16},{16,0},{1,17},{17,1},{2,18},{18,2},{3,19},{19,3},{4,20},{20... | collective-permute-start | bytes 6152 | tf_op jit(solution)/shard_map/ppermute | solution.py:28
  35.4 55.4 %collective-permute-start.19 = (f32[1,8,64]{2,1,0:T(8,128)S(1)}, f32[1,8,64]{2,1,0:T(8,128)S(1)}, u32[]{:S(2)}, u32[]{:S(2)}) collective-permute-start(f32[1,8,64]{2,1,0:T(8,128)S(1)} %slice.1372), channel_id=1, source_target_pairs={{0,16},{1,17},{2,18},{3,19},{4,20},{5,21},{6,22},{7,23},{8,24},{9,... | collective-permute-start | bytes 6152 | tf_op jit(solution)/shard_map/ppermute | solution.py:17
  36.7 54.1 %collective-permute-start.22 = (f32[8,1,64]{2,1,0:T(1,128)S(1)}, f32[8,1,64]{2,1,0:T(1,128)S(1)}, u32[]{:S(2)}, u32[]{:S(2)}) collective-permute-start(f32[8,1,64]{2,1,0:T(1,128)S(1)} %slice.1376), channel_id=1, source_target_pairs={{0,4},{4,8},{8,12},{1,5},{5,9},{9,13},{2,6},{6,10},{10,14},{3,7},{... | collective-permute-start | bytes 6152 | tf_op jit(solution)/shard_map/ppermute | solution.py:17
  39.8 51.0 %collective-permute-start.25 = (f32[8,8,1]{2,1,0:T(8,128)S(1)}, f32[8,8,1]{2,1,0:T(8,128)S(1)}, u32[]{:S(2)}, u32[]{:S(2)}) collective-permute-start(f32[8,8,1]{2,1,0:T(8,128)S(1)} %slice.1382), channel_id=1, source_target_pairs={{0,1},{1,2},{2,3},{4,5},{5,6},{6,7},{8,9},{9,10},{10,11},{12,13},{... | collective-permute-start | bytes 776 | tf_op jit(solution)/shard_map/ppermute | solution.py:17
  47.6 5.0 %collective-permute-start.9 = (f32[18,1,128]{2,1,0:T(1,128)S(1)}, f32[18,1,128]{2,1,0:T(1,128)S(1)}, u32[]{:S(2)}, u32[]{:S(2)}) collective-permute-start(f32[18,1,128]{2,1,0:T(1,128)S(1)} %broadcast_select_fusion.35), channel_id=1, source_target_pairs={{4,8},{8,4},{5,9},{9,5},{6,10},{10,6},{7,11},{11,7},{20,24},{24,20... | collective-permute-start | bytes 27656 | tf_op jit(solution)/shard_map/ppermute | solution.py:30
  50.8 5.0 %collective-permute-start.10 = (f32[18,1,128]{2,1,0:T(1,128)S(1)}, f32[18,1,128]{2,1,0:T(1,128)S(1)}, u32[]{:S(2)}, u32[]{:S(2)}) collective-permute-start(f32[18,1,128]{2,1,0:T(1,128)S(1)} %get-tuple-element.30), channel_id=1, source_target_pairs={{0,4},{4,0},{8,12},{12,8},{1,5},{5,1},{9,13},{13,9},{2,6},{6,2},{1... | collective-permute-start | bytes 27656 | tf_op jit(solution)/shard_map/ppermute | solution.py:28
  58.1 7.6 %collective-permute-start.12 = (f32[18,18,1]{2,1,0:T(8,128)S(1)}, f32[18,18,1]{2,1,0:T(8,128)S(1)}, u32[]{:S(2)}, u32[]{:S(2)}) collective-permute-start(f32[18,18,1]{2,1,0:T(8,128)S(1)} %get-tuple-element.64), channel_id=1, source_target_pairs={{0,1},{1,0},{2,3},{3,2},{4,5},{5,4},{6,7},{7,6},{8,9},{9,8},{10,11... | collective-permute-start | bytes 3896 | tf_op jit(solution)/shard_map/ppermute | solution.py:28
  68.7 5.0 %collective-permute-start.14 = (f32[18,1,128]{2,1,0:T(1,128)S(1)}, f32[18,1,128]{2,1,0:T(1,128)S(1)}, u32[]{:S(2)}, u32[]{:S(2)}) collective-permute-start(f32[18,1,128]{2,1,0:T(1,128)S(1)} %broadcast_select_fusion.31), channel_id=1, source_target_pairs={{4,8},{8,4},{5,9},{9,5},{6,10},{10,6},{7,11},{11,7},{20,24},{24,20... | collective-permute-start | bytes 27656 | tf_op jit(solution)/shard_map/ppermute | solution.py:30
  73.7 5.8 %collective-permute-start.23 = (f32[10,10,1]{2,1,0:T(8,128)S(1)}, f32[10,10,1]{2,1,0:T(8,128)S(1)}, u32[]{:S(2)}, u32[]{:S(2)}) collective-permute-start(f32[10,10,1]{2,1,0:T(8,128)S(1)} %get-tuple-element.85), channel_id=1, source_target_pairs={{1,2},{2,1},{5,6},{6,5},{9,10},{10,9},{13,14},{14,13},{17,18},{18,... | collective-permute-start | bytes 1208 | tf_op jit(solution)/shard_map/ppermute | solution.py:30
  74.4 7.3 %collective-permute-start.24 = (f32[10,10,1]{2,1,0:T(8,128)S(1)}, f32[10,10,1]{2,1,0:T(8,128)S(1)}, u32[]{:S(2)}, u32[]{:S(2)}) collective-permute-start(f32[10,10,1]{2,1,0:T(8,128)S(1)} %get-tuple-element.86), channel_id=1, source_target_pairs={{0,1},{1,0},{2,3},{3,2},{4,5},{5,4},{6,7},{7,6},{8,9},{9,8},{10,11... | collective-permute-start | bytes 1208 | tf_op jit(solution)/shard_map/ppermute | solution.py:28
  79.5 5.5 %collective-permute-start.16 = (f32[18,18,1]{2,1,0:T(8,128)S(1)}, f32[18,18,1]{2,1,0:T(8,128)S(1)}, u32[]{:S(2)}, u32[]{:S(2)}) collective-permute-start(f32[18,18,1]{2,1,0:T(8,128)S(1)} %get-tuple-element.61), channel_id=1, source_target_pairs={{1,2},{2,1},{5,6},{6,5},{9,10},{10,9},{13,14},{14,13},{17,18},{18,... | collective-permute-start | bytes 3896 | tf_op jit(solution)/shard_map/ppermute | solution.py:30
  81.6 8.7 %collective-permute-start.17 = (f32[18,18,1]{2,1,0:T(8,128)S(1)}, f32[18,18,1]{2,1,0:T(8,128)S(1)}, u32[]{:S(2)}, u32[]{:S(2)}) collective-permute-start(f32[18,18,1]{2,1,0:T(8,128)S(1)} %get-tuple-element.62), channel_id=1, source_target_pairs={{0,1},{1,0},{2,3},{3,2},{4,5},{5,4},{6,7},{7,6},{8,9},{9,8},{10,11... | collective-permute-start | bytes 3896 | tf_op jit(solution)/shard_map/ppermute | solution.py:28
  93.6 5.7 %collective-permute-start.27 = (f32[10,1,64]{2,1,0:T(1,128)S(1)}, f32[10,1,64]{2,1,0:T(1,128)S(1)}, u32[]{:S(2)}, u32[]{:S(2)}) collective-permute-start(f32[10,1,64]{2,1,0:T(1,128)S(1)} %broadcast_select_fusion.55), channel_id=1, source_target_pairs={{4,8},{8,4},{5,9},{9,5},{6,10},{10,6},{7,11},{11,7},{20,24},{24,20... | collective-permute-start | bytes 7688 | tf_op jit(solution)/shard_map/ppermute | solution.py:30
  100.0 5.8 %collective-permute-start.30 = (f32[10,10,1]{2,1,0:T(8,128)S(1)}, f32[10,10,1]{2,1,0:T(8,128)S(1)}, u32[]{:S(2)}, u32[]{:S(2)}) collective-permute-start(f32[10,10,1]{2,1,0:T(8,128)S(1)} %get-tuple-element.84), channel_id=1, source_target_pairs={{0,1},{1,0},{2,3},{3,2},{4,5},{5,4},{6,7},{7,6},{8,9},{9,8},{10,11... | collective-permute-start | bytes 1208 | tf_op jit(solution)/shard_map/ppermute | solution.py:28
  108.5 6.1 %collective-permute-start.32 = (f32[10,1,64]{2,1,0:T(1,128)S(1)}, f32[10,1,64]{2,1,0:T(1,128)S(1)}, u32[]{:S(2)}, u32[]{:S(2)}) collective-permute-start(f32[10,1,64]{2,1,0:T(1,128)S(1)} %broadcast_select_fusion.51), channel_id=1, source_target_pairs={{4,8},{8,4},{5,9},{9,5},{6,10},{10,6},{7,11},{11,7},{20,24},{24,20... | collective-permute-start | bytes 7688 | tf_op jit(solution)/shard_map/ppermute | solution.py:30
  114.8 5.5 %collective-permute-start.34 = (f32[10,10,1]{2,1,0:T(8,128)S(1)}, f32[10,10,1]{2,1,0:T(8,128)S(1)}, u32[]{:S(2)}, u32[]{:S(2)}) collective-permute-start(f32[10,10,1]{2,1,0:T(8,128)S(1)} %get-tuple-element.81), channel_id=1, source_target_pairs={{1,2},{2,1},{5,6},{6,5},{9,10},{10,9},{13,14},{14,13},{17,18},{18,... | collective-permute-start | bytes 1208 | tf_op jit(solution)/shard_map/ppermute | solution.py:30
  115.4 7.3 %collective-permute-start.35 = (f32[10,10,1]{2,1,0:T(8,128)S(1)}, f32[10,10,1]{2,1,0:T(8,128)S(1)}, u32[]{:S(2)}, u32[]{:S(2)}) collective-permute-start(f32[10,10,1]{2,1,0:T(8,128)S(1)} %get-tuple-element.82), channel_id=1, source_target_pairs={{0,1},{1,0},{2,3},{3,2},{4,5},{5,4},{6,7},{7,6},{8,9},{9,8},{10,11... | collective-permute-start | bytes 1208 | tf_op jit(solution)/shard_map/ppermute | solution.py:28
  125.7 15.7 %all-to-all-start = ((f32[32,1,2560]{2,1,0:T(1,128)}), f32[32,1,2560]{2,1,0:T(1,128)S(1)}, u32[]{:S(2)}, u32[]{:S(2)}) async-start(f32[32,1,2560]{2,1,0:T(1,128)} %reshape.241), calls=%async_computation | async-start | bytes 655360 | tf_op jit(solution)/shard_map/all_to_all | solution.py:217
  163.7 5.1 %collective-permute-start.40 = (f32[10,10,1]{2,1,0:T(8,128)S(1)}, f32[10,10,1]{2,1,0:T(8,128)S(1)}, u32[]{:S(2)}, u32[]{:S(2)}) collective-permute-start(f32[10,10,1]{2,1,0:T(8,128)S(1)} %get-tuple-element.80), channel_id=1, source_target_pairs={{0,1},{1,0},{2,3},{3,2},{4,5},{5,4},{6,7},{7,6},{8,9},{9,8},{10,11... | collective-permute-start | bytes 1208 | tf_op jit(solution)/shard_map/ppermute | solution.py:28
  171.5 6.5 %collective-permute-start.42 = (f32[10,1,64]{2,1,0:T(1,128)S(1)}, f32[10,1,64]{2,1,0:T(1,128)S(1)}, u32[]{:S(2)}, u32[]{:S(2)}) collective-permute-start(f32[10,1,64]{2,1,0:T(1,128)S(1)} %broadcast_select_fusion.43), channel_id=1, source_target_pairs={{4,8},{8,4},{5,9},{9,5},{6,10},{10,6},{7,11},{11,7},{20,24},{24,20... | collective-permute-start | bytes 7688 | tf_op jit(solution)/shard_map/ppermute | solution.py:30
  178.8 6.6 %collective-permute-start.45 = (f32[10,10,1]{2,1,0:T(8,128)S(1)}, f32[10,10,1]{2,1,0:T(8,128)S(1)}, u32[]{:S(2)}, u32[]{:S(2)}) collective-permute-start(f32[10,10,1]{2,1,0:T(8,128)S(1)} %get-tuple-element.78), channel_id=1, source_target_pairs={{0,1},{1,0},{2,3},{3,2},{4,5},{5,4},{6,7},{7,6},{8,9},{9,8},{10,11... | collective-permute-start | bytes 1208 | tf_op jit(solution)/shard_map/ppermute | solution.py:28
  188.5 6.6 %collective-permute-start.47 = (f32[18,1,128]{2,1,0:T(1,128)S(1)}, f32[18,1,128]{2,1,0:T(1,128)S(1)}, u32[]{:S(2)}, u32[]{:S(2)}) collective-permute-start(f32[18,1,128]{2,1,0:T(1,128)S(1)} %broadcast_select_fusion.27), channel_id=1, source_target_pairs={{4,8},{8,4},{5,9},{9,5},{6,10},{10,6},{7,11},{11,7},{20,24},{24,20... | collective-permute-start | bytes 27656 | tf_op jit(solution)/shard_map/ppermute | solution.py:30
  196.0 9.1 %collective-permute-start.50 = (f32[18,18,1]{2,1,0:T(8,128)S(1)}, f32[18,18,1]{2,1,0:T(8,128)S(1)}, u32[]{:S(2)}, u32[]{:S(2)}) collective-permute-start(f32[18,18,1]{2,1,0:T(8,128)S(1)} %get-tuple-element.60), channel_id=1, source_target_pairs={{0,1},{1,0},{2,3},{3,2},{4,5},{5,4},{6,7},{7,6},{8,9},{9,8},{10,11... | collective-permute-start | bytes 3896 | tf_op jit(solution)/shard_map/ppermute | solution.py:28
  208.0 5.1 %collective-permute-start.52 = (f32[18,1,128]{2,1,0:T(1,128)S(1)}, f32[18,1,128]{2,1,0:T(1,128)S(1)}, u32[]{:S(2)}, u32[]{:S(2)}) collective-permute-start(f32[18,1,128]{2,1,0:T(1,128)S(1)} %broadcast_select_fusion.23), channel_id=1, source_target_pairs={{4,8},{8,4},{5,9},{9,5},{6,10},{10,6},{7,11},{11,7},{20,24},{24,20... | collective-permute-start | bytes 27656 | tf_op jit(solution)/shard_map/ppermute | solution.py:30
  214.0 9.5 %collective-permute-start.55 = (f32[18,18,1]{2,1,0:T(8,128)S(1)}, f32[18,18,1]{2,1,0:T(8,128)S(1)}, u32[]{:S(2)}, u32[]{:S(2)}) collective-permute-start(f32[18,18,1]{2,1,0:T(8,128)S(1)} %get-tuple-element.58), channel_id=1, source_target_pairs={{0,1},{1,0},{2,3},{3,2},{4,5},{5,4},{6,7},{7,6},{8,9},{9,8},{10,11... | collective-permute-start | bytes 3896 | tf_op jit(solution)/shard_map/ppermute | solution.py:28
  (32 other events, 188.9 us)

commit v2 on v0

v2 whole, which is shorter than its diff:
```python
import functools

import jax
import jax.numpy as jnp
from jax import lax
from jax.experimental import pallas as pl
from jax.experimental.pallas import tpu as pltpu
from jax.sharding import PartitionSpec as P

LEVELS = 6
SWEEPS = 2
BOTTOM = 8
WEIGHT = 0.25 ** (LEVELS - 1)
RELAX = 2.0 / 3.0
KEEP = 1.0 / 3.0

WIDE = 7
SIDE = 8
NEAR = 4
LANES = 128

VM = pl.BlockSpec(memory_space=pltpu.VMEM)
SM = pl.BlockSpec(memory_space=pltpu.SMEM)
F32 = jnp.float32


def lane_of(shape):
    return lax.broadcasted_iota(jnp.int32, shape, len(shape) - 1)


def pick(flag, yes, no):
    return jnp.where(jnp.full(yes.shape, flag, jnp.int32) == 1, yes, no)


def neighbours(axis_size, odd, one, two):
    if axis_size == 2:
        two = jnp.zeros_like(one)
    return pick(odd, one, two), pick(odd, two, one)


def turn(values, shift, axis):
    return pltpu.roll(values, shift % values.shape[axis], axis)


def parts_of(values):
    high = values.astype(jnp.bfloat16)
    rest = values - high.astype(F32)
    middle = rest.astype(jnp.bfloat16)
    low = (rest - middle.astype(F32)).astype(jnp.bfloat16)
    return high, middle, low


def times_table(values, table):
    table = table.astype(jnp.bfloat16)
    total = None
    for part in reversed(parts_of(values)):
        term = jnp.dot(part, table, preferred_element_type=F32)
        total = term if total is None else total + term
    return total


def table_times(table, values):
    table = table.astype(jnp.bfloat16)
    total = None
    for part in reversed(parts_of(values)):
        term = jnp.dot(table, part, preferred_element_type=F32)
        total = term if total is None else total + term
    return total


def iota2(shape, axis):
    return lax.broadcasted_iota(jnp.int32, shape, axis)


def pair_table(rows, cols, odd):
    row = iota2((rows, cols), 0)
    col = iota2((rows, cols), 1)
    hit = (row == 2 * col + 1) if odd else (row // 2 == col)
    return hit.astype(F32)


def below_x(values):
    if values.shape[0] == 1:
        return jnp.zeros_like(values)
    return jnp.concatenate([jnp.zeros_like(values[:1]), values[:-1]], axis=0)


def above_x(values):
    if values.shape[0] == 1:
        return jnp.zeros_like(values)
    return jnp.concatenate([values[1:], jnp.zeros_like(values[:1])], axis=0)


def pull(values, faces):
    bx, by, bz = faces
    total = bx * above_x(values) + below_x(bx * values)
    total = total + (by * turn(values, -1, 1) + turn(by * values, 1, 1))
    return total + (bz * turn(values, -1, 2) + turn(bz * values, 1, 2))


def diagonal(mass, faces, coupled):
    bx, by, bz = faces
    _, cy, cz = coupled
    return mass + bx + below_x(bx) + by + turn(cy, 1, 1) + bz + turn(cz, 1, 2)


def relaxer(mass, diag):
    inside = mass > 0.0
    return jnp.where(inside, RELAX / jnp.where(inside, diag, 1.0), 0.0)


def sweep(values, rhs, weight, faces):
    return KEEP * values + weight * (rhs + pull(values, faces))


def pack_z_kernel(where_ref, *refs):
    ins, (first, second) = refs[:6], refs[6:]
    odd = where_ref[2] % 2
    sx, sy, sz = ins[0].shape
    half = sx // 2
    lane = lane_of((half, sy, LANES))
    head = jnp.zeros((half, sy, LANES), F32)
    tail = head
    for a, ref in enumerate(ins):
        for g in range(2):
            block = ref[g * half:(g + 1) * half]
            at = 64 * g + SIDE * a
            mask = (lane >= at) & (lane < at + SIDE)
            head = jnp.where(mask, turn(block, at, 2), head)
            tail = jnp.where(mask, turn(block, at + SIDE, 2), tail)
    first[...] = pick(odd, head, tail)
    second[...] = pick(odd, tail, head)


def face_x_kernel(counts, where_ref, *refs):
    ins, one_ref, two_ref = refs[:6], refs[6], refs[7]
    zpack, sends = refs[8], refs[9:]
    sx, sy, sz = ins[0].shape
    half = sx // 2
    below, above = neighbours(counts[2], where_ref[2] % 2, one_ref[...], two_ref[...])
    lane = lane_of(below.shape)
    zpack[:half] = jnp.where(lane < 64, above, turn(below, 64, 2))
    zpack[half:] = jnp.where(lane < 64, turn(above, 64, 2), below)
    odd = where_ref[0] % 2
    for k, send in enumerate(sends):
        start = (1 - odd if k == 0 else odd) * (sx - WIDE)
        for a, ref in enumerate(tuple(ins) + (zpack,)):
            send[a] = ref[pl.ds(start, WIDE)]


def face_y_kernel(counts, where_ref, *refs):
    ins, halos, sends = refs[:7], refs[7:-2], refs[-2:]
    sx, sy, sz = ins[0].shape
    odd_x = where_ref[0] % 2
    odd = where_ref[1] % 2
    for k, send in enumerate(sends):
        start = pl.multiple_of((1 - odd if k == 0 else odd) * (sy - SIDE), SIDE)
        rows = pl.ds(start, SIDE)
        for a, ref in enumerate(ins):
            one = halos[0][a, :, rows, :]
            two = halos[-1][a, :, rows, :]
            below, above = neighbours(counts[0], odd_x, one, two)
            send[a, :WIDE] = below
            send[a, WIDE:WIDE + sx] = ref[:, rows, :]
            send[a, WIDE + sx:] = above


def ring_up(main, halo, lane):
    main_up, halo_up = turn(main, -1, 1), turn(halo, -1, 1)
    last = lane == LANES - 1
    return jnp.where(last, halo_up, main_up), jnp.where(last, main_up, halo_up)


def ring_down(main, halo, lane):
    main_down, halo_down = turn(main, 1, 1), turn(halo, 1, 1)
    zero = lane == 0
    return jnp.where(zero, halo_down, main_down), jnp.where(zero, main_down, halo_down)


def pull_slab(field, bx, by, bz, x, lane):
    centre = [half[x] for half in field]
    out = []
    for k in range(2):
        c, face = centre[k], by[k][x]
        t = bx[k][x] * field[k][x + 1] + bx[k][x - 1] * field[k][x - 1]
        out.append(t + (face * turn(c, -1, 0) + turn(face * c, 1, 0)))
    faces = [half[x] for half in bz]
    ups = ring_up(centre[0], centre[1], lane)
    downs = ring_down(faces[0] * centre[0], faces[1] * centre[1], lane)
    return centre, [out[k] + (faces[k] * ups[k] + downs[k]) for k in range(2)]


def down_kernel(counts, devices, where_ref, *refs):
    ins = refs[:7]
    n_x = 1 if counts[0] == 2 else 2
    halos_x = refs[7:7 + n_x]
    one_y, two_y = refs[7 + n_x:9 + n_x]
    outs = refs[9 + n_x:16 + n_x]
    copies, own1, first1, second1, kept, weight_out, faces_out = outs
    grid, other, scales, summed, left = refs[16 + n_x:]
    sx, sy, sz = ins[0].shape
    ex, ey = sx + 2 * WIDE, sy + 2 * SIDE
    odd_x, odd_y, odd_z = where_ref[0] % 2, where_ref[1] % 2, where_ref[2] % 2

    mid_x = slice(WIDE, WIDE + sx)
    mid_y = slice(SIDE, SIDE + sy)
    for a in range(7):
        to = grid.at[a, 0]
        below, above = neighbours(counts[0], odd_x, halos_x[0][a], halos_x[-1][a])
        to[:WIDE, mid_y, :] = below
        to[mid_x, mid_y, :] = ins[a][...]
        to[WIDE + sx:, mid_y, :] = above
        below, above = neighbours(counts[1], odd_y, one_y[a], two_y[a])
        to[:, :SIDE, :] = below
        to[:, SIDE + sy:, :] = above
    lane = lane_of((ey, LANES))

    def unpack(x, carry):
        packed = grid[6, 0, x]
        for a in range(6):
            right = turn(packed, -SIDE * a, 1)
            other_side = turn(packed, 56 - SIDE * a, 1)
            grid[a, 1, x] = jnp.where(
                lane < SIDE, right, jnp.where(lane >= LANES - SIDE, other_side, 0.0)
            )
        return carry

    lax.fori_loop(0, ex, unpack, 0)

    field = [grid.at[0, k] for k in range(2)]
    rhs = [grid.at[1, k] for k in range(2)]
    alpha = [grid.at[2, k] for k in range(2)]
    bx = [grid.at[3, k] for k in range(2)]
    by = [grid.at[4, k] for k in range(2)]
    bz = [grid.at[5, k] for k in range(2)]
    diag = [scales.at[0, k] for k in range(2)]
    weight = [scales.at[1, k] for k in range(2)]
    halfway = [other.at[k] for k in range(2)]

    def first_sweep(x, carry):
        faces = [half[x] for half in bz]
        downs = ring_down(faces[0], faces[1], lane)
        centre, near = pull_slab(field, bx, by, bz, x, lane)
        for k in range(2):
            face = by[k][x]
            mass = WEIGHT * alpha[k][x]
            d = mass + bx[k][x] + bx[k][x - 1] + face + turn(face, 1, 0) + faces[k] + downs[k]
            w = relaxer(mass, d)
            diag[k][x] = d
            weight[k][x] = w
            halfway[k][x] = KEEP * centre[k] + w * (rhs[k][x] + near[k])
        return carry

    lax.fori_loop(1, ex - 1, first_sweep, 0)

    def second_sweep(x, carry):
        centre, near = pull_slab(halfway, bx, by, bz, x, lane)
        for k in range(2):
            field[k][x] = KEEP * centre[k] + weight[k][x] * (rhs[k][x] + near[k])
        return carry

    lax.fori_loop(2, ex - 2, second_sweep, 0)

    def residual(x, carry):
        centre, near = pull_slab(field, bx, by, bz, x, lane)
        for k in range(2):
            halfway[k][x] = rhs[k][x] - diag[k][x] * centre[k] + near[k]
        return carry

    lax.fori_loop(3, ex - 3, residual, 0)

    for k in range(2):
        kept[k] = grid[0, k, WIDE - 2:WIDE + sx + 2]
        weight_out[k] = scales[1, k, WIDE - 2:WIDE + sx + 2]
        for n, a in enumerate((1, 3, 4, 5)):
            faces_out[n, k] = grid[a, k, WIDE - 2:WIDE + sx + 2]

    x1, y1 = sx // 2 + 6, ey // 2
    blocks = ((alpha, False, False), (bx, True, False), (by, False, True), (bz, False, False))
    for n, (source, odd_first, odd_second) in enumerate(blocks):
        for k in range(2):

            def add_up(i, carry, n=n, source=source, k=k, odd_first=odd_first, odd_second=odd_second):
                total = None
                for p in (1,) if odd_first else (0, 1):
                    for q in (1,) if odd_second else (0, 1):
                        term = source[k][2 * i + 1 + p, pl.ds(q, y1, stride=2), :]
                        total = term if total is None else total + term
                summed[n, i, :, k * LANES:(k + 1) * LANES] = total
                return carry

            lax.fori_loop(0, x1, add_up, 0)
    for k in range(2):

        def add_rhs(i, carry, k=k):
            total = None
            for p in range(2):
                for q in range(2):
                    term = halfway[k][2 * i + 1 + p, pl.ds(q, y1, stride=2), :]
                    total = term if total is None else total + term
            summed[4, i, :, k * LANES:(k + 1) * LANES] = total
            return carry

        lax.fori_loop(1, x1 - 1, add_rhs, 0)
    summed[4, 0] = jnp.zeros((y1, 2 * LANES), F32)
    summed[4, x1 - 1] = jnp.zeros((y1, 2 * LANES), F32)

    pairs = pair_table(2 * LANES, LANES, False)
    odds = pair_table(2 * LANES, LANES, True)

    def coarse(n, table, factor):
        flat = summed[n].reshape(x1 * y1, 2 * LANES)
        return factor * times_table(flat, table).reshape(x1, y1, LANES)

    mass1 = coarse(0, pairs, 0.125 * WEIGHT)
    faces1 = (coarse(1, pairs, 0.0625), coarse(2, pairs, 0.0625), coarse(3, odds, 0.0625))
    rhs1 = coarse(4, pairs, 0.125)
    diag1 = diagonal(mass1, faces1, faces1)
    weight1 = relaxer(mass1, diag1)
    field1 = weight1 * rhs1
    field1 = sweep(field1, rhs1, weight1, faces1)
    remain1 = rhs1 - diag1 * field1 + pull(field1, faces1)

    bx1, by1, bz1 = sx // 2, sy // 2, sz // 2
    mine = slice(3, 3 + bx1)
    rows = slice(NEAR, NEAR + by1)
    lane1 = lane_of((bx1, by1, LANES))
    head = jnp.zeros((bx1, by1, LANES), F32)
    tail = head
    for n, values in enumerate((rhs1, weight1) + faces1):
        block = jnp.where(lane1 < bz1, values[mine, rows, :], 0.0)
        own1[n] = block
        at = NEAR * n
        mask = (lane1 >= at) & (lane1 < at + NEAR)
        head = jnp.where(mask, turn(block, at, 2), head)
        tail = jnp.where(mask, turn(block, at + NEAR - bz1, 2), tail)
    first1[...] = pick(odd_z, head, tail)
    second1[...] = pick(odd_z, tail, head)

    x2, y2, z2 = bx1 // 2, by1 // 2, bz1 // 2
    parts = (
        (remain1, False, False, False, 0.125),
        (mass1, False, False, False, 0.125),
        (faces1[0], True, False, False, 0.0625),
        (faces1[1], False, True, False, 0.0625),
        (faces1[2], False, False, True, 0.0625),
    )
    pairs2 = pair_table(LANES, LANES, False)
    odds2 = pair_table(LANES, LANES, True)
    lane2 = lane_of((y2, LANES))
    for n, (values, odd_first, odd_second, odd_third, factor) in enumerate(parts):
        left[n] = values[mine]
        rows2 = []
        for i in range(x2):
            total = None
            for p in (1,) if odd_first else (0, 1):
                for q in (1,) if odd_second else (0, 1):
                    term = left[n, 2 * i + p, pl.ds(NEAR + q, y2, stride=2), :]
                    total = term if total is None else total + term
            rows2.append(total)
        flat = jnp.concatenate(rows2, axis=0)
        flat = factor * times_table(flat, odds2 if odd_third else pairs2)
        packed = jnp.zeros((y2, LANES), F32)
        for i in range(x2):
            block = flat[i * y2:(i + 1) * y2]
            mask = (lane2 >= i * z2) & (lane2 < (i + 1) * z2)
            packed = jnp.where(mask, turn(block, i * z2, 1), packed)
        for d in range(devices):
            copies[d, n] = packed


def near_x_kernel(counts, where_ref, own_ref, one_ref, two_ref, ring, *sends):
    n, bx, by, _ = own_ref.shape
    below, above = neighbours(counts[2], where_ref[2] % 2, one_ref[...], two_ref[...])
    lane = lane_of(below.shape)
    for a in range(n):
        right = turn(above, LANES // 2 - NEAR * a, 2)
        left = turn(below, LANES - NEAR - NEAR * a, 2)
        block = jnp.where(lane < LANES // 2, own_ref[a], 0.0)
        block = jnp.where((lane >= LANES // 2) & (lane < LANES // 2 + NEAR), right, block)
        ring[a] = jnp.where(lane >= LANES - NEAR, left, block)
    odd = where_ref[0] % 2
    for k, send in enumerate(sends):
        start = (1 - odd if k == 0 else odd) * (bx - NEAR)
        for a in range(n):
            send[a] = ring[a, pl.ds(start, NEAR)]


def near_y_kernel(counts, where_ref, ring, *refs):
    halos, sends = refs[:-2], refs[-2:]
    n, bx, by, _ = ring.shape
    odd_x, odd = where_ref[0] % 2, where_ref[1] % 2
    for a in range(n):
        below, above = neighbours(counts[0], odd_x, halos[0][a], halos[-1][a])
        block = jnp.concatenate([below, ring[a], above], axis=0)
        head, tail = block[:, :NEAR], block[:, by - NEAR:]
        sends[0][a] = pick(odd, head, tail)
        sends[1][a] = pick(odd, tail, head)


def halve(values, factor, odd_axis):
    x, y, z = values.shape
    if odd_axis == 0:
        values = jnp.concatenate([values[2 * i + 1:2 * i + 2] for i in range(x // 2)], axis=0)
    else:
        values = jnp.concatenate(
            [values[2 * i:2 * i + 1] + values[2 * i + 1:2 * i + 2] for i in range(x // 2)], axis=0
        )
    to_y = max(8, y // 2)
    to_z = max(LANES, z // 2)
    flat = values.reshape(x // 2 * y, z)
    flat = times_table(flat, pair_table(z, to_z, odd_axis == 2))
    row = iota2((to_y, y), 0)
    col = iota2((to_y, y), 1)
    table = (col == 2 * row + 1) if odd_axis == 1 else (col // 2 == row)
    table = table.astype(F32)
    blocks = [table_times(table, flat[i * y:(i + 1) * y])[None] for i in range(x // 2)]
    return factor * jnp.concatenate(blocks, axis=0)


def double(values, shape):
    x, y, z = values.shape
    to_x, to_y, to_z = shape
    row = iota2((to_y, y), 0)
    col = iota2((to_y, y), 1)
    table_y = (row // 2 == col).astype(F32)
    row = iota2((z, to_z), 0)
    col = iota2((z, to_z), 1)
    table_z = (col // 2 == row).astype(F32)
    blocks = [table_times(table_y, values[i])[None] for i in range(x)]
    flat = jnp.concatenate(blocks, axis=0).reshape(x * to_y, z)
    flat = times_table(flat, table_z).reshape(x, to_y, to_z)
    return jnp.concatenate([flat[i // 2:i // 2 + 1] for i in range(to_x)], axis=0)


def coupled_faces(faces, y, z):
    bx, by, bz = faces
    row = lax.broadcasted_iota(jnp.int32, by.shape, 1)
    return bx, jnp.where(row == y - 1, 0.0, by), jnp.where(lane_of(bz.shape) == z - 1, 0.0, bz)


def coarse_cycle(level, rhs, mass, faces, y, z):
    coupled = coupled_faces(faces, y, z)
    diag = diagonal(mass, faces, coupled)
    weight = relaxer(mass, diag)
    field = weight * rhs
    if level == LEVELS - 1:
        for _ in range(BOTTOM - 1):
            field = sweep(field, rhs, weight, coupled)
        return field
    for _ in range(SWEEPS - 1):
        field = sweep(field, rhs, weight, coupled)
    remain = rhs - diag * field + pull(field, coupled)
    correction = coarse_cycle(
        level + 1,
        halve(remain, 0.125, -1),
        halve(mass, 0.125, -1),
        tuple(halve(face, 0.0625, axis) for axis, face in enumerate(faces)),
        y // 2,
        z // 2,
    )
    field = field + double(correction, field.shape)
    for _ in range(SWEEPS):
        field = sweep(field, rhs, weight, coupled)
    return field


def up_kernel(counts, where_ref, gathered, ring, *refs):
    n_x = 1 if counts[0] == 2 else 2
    halos_x = refs[:n_x]
    one_y, two_y, kept, weight_ref, faces_ref = refs[n_x:n_x + 5]
    out = refs[n_x + 5]
    whole, second, field, halfway, spread = refs[n_x + 6:]
    odd_x, odd_y = where_ref[0] % 2, where_ref[1] % 2
    gx, gy, gz = counts
    n, bx1, by1, _ = ring.shape
    x2, y2, z2 = bx1 // 2, by1 // 2, LANES // 4
    columns = max(LANES, gz * z2)
    lane = lane_of((y2, LANES))

    for a in range(n):
        for i in range(gx):
            for j in range(gy):
                for x in range(x2):
                    for part in range(columns // LANES):
                        total = jnp.zeros((y2, LANES), F32)
                        for k in range(LANES // z2):
                            column = part * (LANES // z2) + k
                            if column < gz:
                                block = gathered[(i * gy + j) * gz + column, a]
                                mask = (lane >= k * z2) & (lane < (k + 1) * z2)
                                total = jnp.where(mask, turn(block, (k - x) * z2, 1), total)
                        whole[
                            a, i * x2 + x, j * y2:(j + 1) * y2, part * LANES:(part + 1) * LANES
                        ] = total
    correction = coarse_cycle(
        2, whole[0], whole[1], (whole[2], whole[3], whole[4]), gy * y2, gz * z2
    )

    wide = gx * x2
    half = NEAR // 2
    ex1, ey1 = bx1 + 2 * NEAR, by1 + 2 * NEAR
    second[:half] = jnp.zeros((half,) + correction.shape[1:], F32)
    second[half:half + wide] = correction
    second[half + wide:] = jnp.zeros((half,) + correction.shape[1:], F32)
    window = second[pl.ds(where_ref[0] * x2, x2 + NEAR)]
    rows = correction.shape[1]
    row = iota2((ey1, rows), 0)
    col = iota2((ey1, rows), 1)
    table_y = (col == where_ref[1] * y2 + (row // 2 - half)).astype(F32)
    row = iota2((columns, LANES), 0)
    col = iota2((columns, LANES), 1)
    place = jnp.where(col < LANES * 3 // 4, col, col - LANES)
    table_z = (row == where_ref[2] * z2 + lax.shift_right_arithmetic(place, 1)).astype(F32)
    flat = times_table(window.reshape((x2 + NEAR) * rows, columns), table_z)
    blocks = [table_times(table_y, flat[i * rows:(i + 1) * rows])[None] for i in range(x2 + NEAR)]
    lifted = jnp.concatenate([blocks[i // 2] for i in range(ex1)], axis=0)

    level1 = []
    for a in range(n):
        below, above = neighbours(gx, odd_x, halos_x[0][a], halos_x[-1][a])
        block = jnp.concatenate([below, ring[a], above], axis=0)
        below, above = neighbours(gy, odd_y, one_y[a], two_y[a])
        level1.append(jnp.concatenate([below, block, above], axis=1))
    rhs1, weight1 = level1[:2]
    faces1 = tuple(level1[2:])
    field1 = weight1 * rhs1
    field1 = sweep(field1, rhs1, weight1, faces1)
    field1 = field1 + jnp.where(weight1 > 0.0, lifted, 0.0)
    for _ in range(SWEEPS):
        field1 = sweep(field1, rhs1, weight1, faces1)

    sx, sy, sz = out.shape
    ex, ey = sx + 4, sy + 2 * SIDE
    near = field1[NEAR - 1:NEAR + bx1 + 1].reshape((bx1 + 2) * ey1, LANES)
    row = iota2((LANES, 2 * LANES), 0)
    col = iota2((LANES, 2 * LANES), 1)
    lifted = times_table(near, (col // 2 == row).astype(F32))
    for k in range(2):
        block = lifted[:, k * LANES:(k + 1) * LANES].reshape(bx1 + 2, ey1, LANES)
        for i in range(bx1 + 2):
            for q in range(2):
                spread[k, i, pl.ds(q, ey1, stride=2), :] = block[i]
    for x in range(ex):
        for k in range(2):
            field[k, x] = kept[k, x] + spread[k, x // 2]

    lane = lane_of((ey, LANES))
    rhs, bx, by, bz = ([faces_ref.at[a, k] for k in range(2)] for a in range(4))
    before = [field.at[k] for k in range(2)]
    after = [halfway.at[k] for k in range(2)]

    def sweep_out(x, carry):
        centre, around = pull_slab(before, bx, by, bz, x, lane)
        for k in range(2):
            after[k][x] = KEEP * centre[k] + weight_ref[k, x] * (rhs[k][x] + around[k])
        return carry

    lax.fori_loop(1, ex - 1, sweep_out, 0)

    def sweep_own(x, carry):
        centre, around = pull_slab(after, bx, by, bz, x, lane)
        value = KEEP * centre[0] + weight_ref[0, x] * (rhs[0][x] + around[0])
        out[x - 2] = value[SIDE:SIDE + sy]
        return carry

    lax.fori_loop(2, ex - 2, sweep_own, 0)


def run(kernel, outs, where, arrays, scratch=()):
    return pl.pallas_call(
        kernel,
        out_shape=tuple(jax.ShapeDtypeStruct(shape, F32) for shape in outs),
        in_specs=[SM] + [VM] * len(arrays),
        out_specs=tuple(VM for _ in outs),
        scratch_shapes=[pltpu.VMEM(shape, F32) for shape in scratch],
        compiler_params=pltpu.CompilerParams(vmem_limit_bytes=56 * 1024 * 1024),
    )(where, *arrays)


def swaps(axis, sends):
    count = lax.axis_size(axis)
    got = []
    for k, block in enumerate(sends):
        pairs = [(i, i + 1) for i in range(k, count - 1, 2)]
        pairs = [pair for low, high in pairs for pair in ((low, high), (high, low))]
        got.append(lax.ppermute(block, axis, pairs))
    return got


def local(initial, right_side, alpha, beta_x, beta_y, beta_z):
    axes = ("gx", "gy", "gz")
    counts = tuple(lax.axis_size(axis) for axis in axes)
    devices = counts[0] * counts[1] * counts[2]
    where = jnp.stack([lax.axis_index(axis) for axis in axes]).astype(jnp.int32)
    ins = (initial, right_side, alpha, beta_x, beta_y, beta_z)
    sx, sy, sz = initial.shape
    n_x = 1 if counts[0] == 2 else 2
    ex, ey = sx + 2 * WIDE, sy + 2 * SIDE
    sends = run(pack_z_kernel, [(sx // 2, sy, LANES)] * 2, where, ins)
    got = swaps("gz", sends)
    zpack, *sends = run(
        functools.partial(face_x_kernel, counts),
        [(sx, sy, LANES)] + [(7, WIDE, sy, LANES)] * n_x,
        where,
        ins + tuple(got),
    )
    ins = ins + (zpack,)
    got_x = swaps("gx", sends)
    sends = run(
        functools.partial(face_y_kernel, counts),
        [(7, ex, SIDE, LANES)] * 2,
        where,
        ins + tuple(got_x),
    )
    got_y = swaps("gy", sends)
    x1, y1 = sx // 2, sy // 2
    copies, own1, first1, second1, kept, weight, faces = run(
        functools.partial(down_kernel, counts, devices),
        [
            (devices, 5, y1 // 2, LANES),
            (5, x1, y1, LANES),
            (x1, y1, LANES),
            (x1, y1, LANES),
            (2, sx + 4, ey, LANES),
            (2, sx + 4, ey, LANES),
            (4, 2, sx + 4, ey, LANES),
        ],
        where,
        ins + tuple(got_x) + tuple(got_y),
        [
            (7, 2, ex, ey, LANES),
            (2, ex, ey, LANES),
            (2, 2, ex, ey, LANES),
            (5, x1 + 6, ey // 2, 2 * LANES),
            (5, x1, ey // 2, LANES),
        ],
    )
    gathered = lax.all_to_all(copies, axes, 0, 0, tiled=True)
    got = swaps("gz", (first1, second1))
    ring, *sends = run(
        functools.partial(near_x_kernel, counts),
        [(5, x1, y1, LANES)] + [(5, NEAR, y1, LANES)] * n_x,
        where,
        (own1,) + tuple(got),
    )
    near_x = swaps("gx", sends)
    sends = run(
        functools.partial(near_y_kernel, counts),
        [(5, x1 + 2 * NEAR, NEAR, LANES)] * 2,
        where,
        (ring,) + tuple(near_x),
    )
    near_y = swaps("gy", sends)
    wide, rows = counts[0] * x1 // 2, counts[1] * y1 // 2
    columns = max(LANES, counts[2] * sz // 4)
    (result,) = run(
        functools.partial(up_kernel, counts),
        [(sx, sy, sz)],
        where,
        (gathered, ring) + tuple(near_x) + tuple(near_y) + (kept, weight, faces),
        [
            (5, wide, rows, columns),
            (wide + NEAR, rows, columns),
            (2, sx + 4, ey, LANES),
            (2, sx + 4, ey, LANES),
            (2, x1 + 2, ey, LANES),
        ],
    )
    return result


def solution(mesh):
    spec = P("gx", "gy", "gz")
    return jax.shard_map(
        local, mesh=mesh, in_specs=(spec,) * 6, out_specs=spec, check_vma=False
    )
```

time: 344 us -> 106 us (0.31)
  the two profiles are of different devices: /device:TPU:1 before, /device:TPU:9 now
where the time goes in v2:
time: 106 us; the launch traced here: 105 us
  Pallas kernels  40.7 us (38%)
  waiting for transfers between devices  32.6 us (31%)
  starting transfers between devices  26.8 us (25%)
  local copies, waits for them, and re-layouts  4.38 us (4%)
    pallas_call x7, Pallas kernels, run(): pl.pallas_call(kernel, out_shape=tuple((jax.ShapeDtypeStruct(shape, F32)...  40.7 us
    ppermute x10, waiting for transfers between devices, swaps(): got.append(lax.ppermute(block, axis, pairs))  32.6 us
    ppermute x10, starting transfers between devices, swaps(): got.append(lax.ppermute(block, axis, pairs))  22 us
    all_to_all x1, starting transfers between devices, local(): gathered = lax.all_to_all(copies, axes, 0, 0, tiled=True)  4.82 us
    unnamed x22, local copies, waits for them, and re-layouts  4.38 us
  transfers between devices with their start and end apart: 11, of which 7 were waited for; matrix products, arithmetic and copies ran while one was open for 0% of the time, Pallas kernels for 3%

profile of v2, /device:TPU:9, one launch (start us, length us, event | category | flops | bytes accessed | tf_op | source)
XLA Modules:
  0.0 105.2 jit_solution(7962252404422058966)
XLA Ops:
  0.0 0.6 pad_add_fusion.where_ref
  0.6 2.3 %shard_map.64 = (f32[8,16,128]{2,1,0:T(8,128)}, f32[8,16,128]{2,1,0:T(8,128)}) custom-call(s32[3]{0:T(128)} %pad_add_fusion.where_ref, f32[16,16,128]{2,1,0:T(8,128)} %refs_0_.7, f32[16,16,128]{2,1,0:T(8,128)} %refs_1_.7, f32[16,16,128]{2,1,0:T(8,128)} %refs_2_.7, f32[16,16,128]{2,1,0:T(8,128)} %refs_3_.7, f32[16,16,128]{2,1,0:T(8,128)} %refs_4_.7, ...), custom_call_target="tpu_custom_call" | custom-call | tf_op jit(solution)/shard_map/pallas_call | solution.py:571
  2.9 4.5 %collective-permute-start.1 = (f32[8,16,128]{2,1,0:T(8,128)}, f32[8,16,128]{2,1,0:T(8,128)S(1)}, u32[]{:S(2)}, u32[]{:S(2)}) collective-permute-start(f32[8,16,128]{2,1,0:T(8,128)} %get-tuple-element.23), channel_id=1, source_target_pairs={{1,2},{2,1},{5,6},{6,5},{9,10},{10,9},{13,14},{14,13},{17,18},{18,... | collective-permute-start | bytes 196616 | tf_op jit(solution)/shard_map/ppermute | solution.py:587
  7.4 1.8 %collective-permute-done.1.refs_7_ = f32[8,16,128]{2,1,0:T(8,128)S(1)} collective-permute-done((f32[8,16,128]{2,1,0:T(8,128)}, f32[8,16,128]{2,1,0:T(8,128)S(1)}, u32[]{:S(2)}, u32[]{:S(2)}) %collective-permute-start.1) | collective-permute-done | bytes 65568 | tf_op jit(solution)/shard_map/ppermute | solution.py:587
  9.3 0.6 copy-done.8
  9.9 2.1 %shard_map.65 = (f32[16,16,128]{2,1,0:T(8,128)}, f32[7,7,16,128]{3,2,1,0:T(8,128)}) custom-call(s32[3]{0:T(128)} %pad_add_fusion.where_ref, f32[16,16,128]{2,1,0:T(8,128)} %refs_0_.7, f32[16,16,128]{2,1,0:T(8,128)} %refs_1_.7, f32[16,16,128]{2,1,0:T(8,128)} %refs_2_.7, f32[16,16,128]{2,1,0:T(8,128)} %refs_3_.7, f32[16,16,128]{2,1,0:T(8,128)} %refs_4_.7, ...), custom_call_target="tpu_custom_call" | custom-call | tf_op jit(solution)/shard_map/pallas_call | solution.py:571
  12.0 1.2 %collective-permute-start.2 = (f32[7,7,16,128]{3,2,1,0:T(8,128)}, f32[7,7,16,128]{3,2,1,0:T(8,128)S(1)}, u32[]{:S(2)}, u32[]{:S(2)}) collective-permute-start(f32[7,7,16,128]{3,2,1,0:T(8,128)} %get-tuple-element.25), channel_id=1, source_target_pairs={{0,16},{16,0},{1,17},{17,1},{2,18},{18,2},{3,19},{19,3},{4,20},{20... | collective-permute-start | bytes 1204232 | tf_op jit(solution)/shard_map/ppermute | solution.py:587
  13.2 8.0 %collective-permute-done.2.refs_7_ = f32[7,7,16,128]{3,2,1,0:T(8,128)S(1)} collective-permute-done((f32[7,7,16,128]{3,2,1,0:T(8,128)}, f32[7,7,16,128]{3,2,1,0:T(8,128)S(1)}, u32[]{:S(2)}, u32[]{:S(2)}) %collective-permute-start.2) | collective-permute-done | bytes 401440 | tf_op jit(solution)/shard_map/ppermute | solution.py:587
  21.2 0.8 copy-done
  21.9 2.7 %shard_map.66 = (f32[7,30,8,128]{3,2,1,0:T(8,128)}, f32[7,30,8,128]{3,2,1,0:T(8,128)}) custom-call(s32[3]{0:T(128)} %pad_add_fusion.where_ref, f32[16,16,128]{2,1,0:T(8,128)} %refs_0_.7, f32[16,16,128]{2,1,0:T(8,128)} %refs_1_.7, f32[16,16,128]{2,1,0:T(8,128)} %refs_2_.7, f32[16,16,128]{2,1,0:T(8,128)} %refs_3_.7, f32[16,16,128]{2,1,0:T(8,128)} %refs_4_.7, ...), custom_call_target="tpu_custom_call" | custom-call | tf_op jit(solution)/shard_map/pallas_call | solution.py:571
  24.6 2.7 %collective-permute-start.3 = (f32[7,30,8,128]{3,2,1,0:T(8,128)}, f32[7,30,8,128]{3,2,1,0:T(8,128)S(1)}, u32[]{:S(2)}, u32[]{:S(2)}) collective-permute-start(f32[7,30,8,128]{3,2,1,0:T(8,128)} %get-tuple-element.26), channel_id=1, source_target_pairs={{0,4},{4,0},{8,12},{12,8},{1,5},{5,1},{9,13},{13,9},{2,6},{6,2},{1... | collective-permute-start | bytes 2580488 | tf_op jit(solution)/shard_map/ppermute | solution.py:587
  27.4 3.0 %collective-permute-start.4 = (f32[7,30,8,128]{3,2,1,0:T(8,128)}, f32[7,30,8,128]{3,2,1,0:T(8,128)S(1)}, u32[]{:S(2)}, u32[]{:S(2)}) collective-permute-start(f32[7,30,8,128]{3,2,1,0:T(8,128)} %get-tuple-element.27), channel_id=1, source_target_pairs={{4,8},{8,4},{5,9},{9,5},{6,10},{10,6},{7,11},{11,7},{20,24},{24,20... | collective-permute-start | bytes 2580488 | tf_op jit(solution)/shard_map/ppermute | solution.py:587
  30.4 11.2 %collective-permute-done.4.refs_9_ = f32[7,30,8,128]{3,2,1,0:T(8,128)S(1)} collective-permute-done((f32[7,30,8,128]{3,2,1,0:T(8,128)}, f32[7,30,8,128]{3,2,1,0:T(8,128)S(1)}, u32[]{:S(2)}, u32[]{:S(2)}) %collective-permute-start.4) | collective-permute-done | bytes 860192 | tf_op jit(solution)/shard_map/ppermute | solution.py:587
  41.7 0.9 copy-done.3
  42.6 16.9 %shard_map.67 = (f32[32,5,4,128]{3,2,1,0:T(4,128)}, f32[5,8,8,128]{3,2,1,0:T(8,128)}, f32[8,8,128]{2,1,0:T(8,128)}, f32[8,8,128]{2,1,0:T(8,128)}, f32[2,20,32,12...) custom-call(s32[3]{0:T(128)} %pad_add_fusion.where_ref, f32[16,16,128]{2,1,0:T(8,128)} %refs_0_.7, ...), custom_call_target="tpu_custom_call" | custom-call | tf_op jit(solution)/shard_map/pallas_call | solution.py:571
  59.5 4.8 %all-to-all-start = ((f32[32,5,4,128]{3,2,1,0:T(4,128)}), f32[32,5,4,128]{3,2,1,0:T(4,128)S(1)}, u32[]{:S(2)}, u32[]{:S(2)}) async-start(f32[32,5,4,128]{3,2,1,0:T(4,128)} %get-tuple-element.28), calls=%async_computation | async-start | bytes 655360 | tf_op jit(solution)/shard_map/all_to_all | solution.py:639
  64.3 0.1 collective-permute-start.5
  64.5 4.2 %collective-permute-start.6 = (f32[8,8,128]{2,1,0:T(8,128)}, f32[8,8,128]{2,1,0:T(8,128)S(1)}, u32[]{:S(2)}, u32[]{:S(2)}) collective-permute-start(f32[8,8,128]{2,1,0:T(8,128)} %get-tuple-element.31), channel_id=1, source_target_pairs={{1,2},{2,1},{5,6},{6,5},{9,10},{10,9},{13,14},{14,13},{17,18},{18,... | collective-permute-start | bytes 98312 | tf_op jit(solution)/shard_map/ppermute | solution.py:587
  68.7 2.7 %collective-permute-done.5.one_ref = f32[8,8,128]{2,1,0:T(8,128)S(1)} collective-permute-done((f32[8,8,128]{2,1,0:T(8,128)}, f32[8,8,128]{2,1,0:T(8,128)S(1)}, u32[]{:S(2)}, u32[]{:S(2)}) %collective-permute-start.5) | collective-permute-done | bytes 32800 | tf_op jit(solution)/shard_map/ppermute | solution.py:587
  71.4 2.7 %collective-permute-done.6.two_ref = f32[8,8,128]{2,1,0:T(8,128)S(1)} collective-permute-done((f32[8,8,128]{2,1,0:T(8,128)}, f32[8,8,128]{2,1,0:T(8,128)S(1)}, u32[]{:S(2)}, u32[]{:S(2)}) %collective-permute-start.6) | collective-permute-done | bytes 32800 | tf_op jit(solution)/shard_map/ppermute | solution.py:587
  74.1 0.6 copy-done.10
  74.7 1.8 %shard_map.68 = (f32[5,8,8,128]{3,2,1,0:T(8,128)}, f32[5,4,8,128]{3,2,1,0:T(8,128)}) custom-call(s32[3]{0:T(128)} %pad_add_fusion.where_ref, f32[5,8,8,128]{3,2,1,0:T(8,128)} %get-tuple-element.29.own_ref, f32[8,8,128]{2,1,0:T(8,128)} %copy-done.9, f32[8,8,128]{2,1,0:T(8,128)} %copy-done.10), custom_call_target="tpu_custom_call" | custom-call | tf_op jit(solution)/shard_map/pallas_call | solution.py:571
  76.5 1.2 %collective-permute-start.7 = (f32[5,4,8,128]{3,2,1,0:T(8,128)}, f32[5,4,8,128]{3,2,1,0:T(8,128)S(1)}, u32[]{:S(2)}, u32[]{:S(2)}) collective-permute-start(f32[5,4,8,128]{3,2,1,0:T(8,128)} %get-tuple-element.33), channel_id=1, source_target_pairs={{0,16},{16,0},{1,17},{17,1},{2,18},{18,2},{3,19},{19,3},{4,20},{20... | collective-permute-start | bytes 245768 | tf_op jit(solution)/shard_map/ppermute | solution.py:587
  77.7 2.3 %collective-permute-done.7.refs_0_ = f32[5,4,8,128]{3,2,1,0:T(8,128)S(1)} collective-permute-done((f32[5,4,8,128]{3,2,1,0:T(8,128)}, f32[5,4,8,128]{3,2,1,0:T(8,128)S(1)}, u32[]{:S(2)}, u32[]{:S(2)}) %collective-permute-start.7) | collective-permute-done | bytes 81952 | tf_op jit(solution)/shard_map/ppermute | solution.py:587
  80.0 0.6 copy-done.4
  80.7 1.8 %shard_map.69 = (f32[5,16,4,128]{3,2,1,0:T(4,128)}, f32[5,16,4,128]{3,2,1,0:T(4,128)}) custom-call(s32[3]{0:T(128)} %pad_add_fusion.where_ref, f32[5,8,8,128]{3,2,1,0:T(8,128)} %get-tuple-element.32.ring, f32[5,4,8,128]{3,2,1,0:T(8,128)} %copy-done.4), custom_call_target="tpu_custom_call" | custom-call | tf_op jit(solution)/shard_map/pallas_call | solution.py:571
  82.4 2.0 %collective-permute-start.8 = (f32[5,16,4,128]{3,2,1,0:T(4,128)}, f32[5,16,4,128]{3,2,1,0:T(4,128)S(1)}, u32[]{:S(2)}, u32[]{:S(2)}) collective-permute-start(f32[5,16,4,128]{3,2,1,0:T(4,128)} %get-tuple-element.34), channel_id=1, source_target_pairs={{0,4},{4,0},{8,12},{12,8},{1,5},{5,1},{9,13},{13,9},{2,6},{6,2},{1... | collective-permute-start | bytes 491528 | tf_op jit(solution)/shard_map/ppermute | solution.py:587
  84.5 3.0 %collective-permute-start.9 = (f32[5,16,4,128]{3,2,1,0:T(4,128)}, f32[5,16,4,128]{3,2,1,0:T(4,128)S(1)}, u32[]{:S(2)}, u32[]{:S(2)}) collective-permute-start(f32[5,16,4,128]{3,2,1,0:T(4,128)} %get-tuple-element.35), channel_id=1, source_target_pairs={{4,8},{8,4},{5,9},{9,5},{6,10},{10,6},{7,11},{11,7},{20,24},{24,20... | collective-permute-start | bytes 491528 | tf_op jit(solution)/shard_map/ppermute | solution.py:587
  87.5 3.8 %collective-permute-done.9.refs_2_ = f32[5,16,4,128]{3,2,1,0:T(4,128)S(1)} collective-permute-done((f32[5,16,4,128]{3,2,1,0:T(4,128)}, f32[5,16,4,128]{3,2,1,0:T(4,128)S(1)}, u32[]{:S(2)}, u32[]{:S(2)}) %collective-permute-start.9) | collective-permute-done | bytes 163872 | tf_op jit(solution)/shard_map/ppermute | solution.py:587
  91.3 0.7 copy-done.6
  92.0 0.2 copy-done.1
  92.1 13.1 %shard_map.70 = f32[16,16,128]{2,1,0:T(8,128)} custom-call(s32[3]{0:T(128)} %pad_add_fusion.where_ref, f32[32,5,4,128]{3,2,1,0:T(4,128)} %copy-done.1, f32[5,8,8,128]{3,2,1,0:T(8,128)} %get-tuple-element.32.ring, f32[5,4,8,128]{3,2,1,0:T(8,128)} %copy-done.4, f32[5,16,4,128]{3,2,1,0:T(4,128)} %copy-done.5, f32[5,16,4,128]{3,2,1,0:T(4,128)} %copy-done.6, ...), custom_call_target="tpu_custom_call" | custom-call | tf_op jit(solution)/shard_map/pallas_call | solution.py:571
  (20 shorter events, 0.0 us)
Async XLA Ops:
  2.9 4.5 %collective-permute-start = (f32[8,16,128]{2,1,0:T(8,128)}, f32[8,16,128]{2,1,0:T(8,128)S(1)}, u32[]{:S(2)}, u32[]{:S(2)}) collective-permute-start(f32[8,16,128]{2,1,0:T(8,128)} %get-tuple-element.22), channel_id=1, source_target_pairs={{0,1},{1,0},{2,3},{3,2},{4,5},{5,4},{6,7},{7,6},{8,9},{9,8},{10,11... | collective-permute-start | bytes 196616 | tf_op jit(solution)/shard_map/ppermute | solution.py:587
  2.9 6.3 %collective-permute-start.1 = (f32[8,16,128]{2,1,0:T(8,128)}, f32[8,16,128]{2,1,0:T(8,128)S(1)}, u32[]{:S(2)}, u32[]{:S(2)}) collective-permute-start(f32[8,16,128]{2,1,0:T(8,128)} %get-tuple-element.23), channel_id=1, source_target_pairs={{1,2},{2,1},{5,6},{6,5},{9,10},{10,9},{13,14},{14,13},{17,18},{18,... | collective-permute-start | bytes 196616 | tf_op jit(solution)/shard_map/ppermute | solution.py:587
  7.4 1.8 %copy-start.7 = (f32[8,16,128]{2,1,0:T(8,128)}, f32[8,16,128]{2,1,0:T(8,128)S(1)}, u32[]{:S(2)}) copy-start(f32[8,16,128]{2,1,0:T(8,128)S(1)} %collective-permute-done.refs_6_) | copy-start | bytes 196612
  9.3 0.6 copy-start.8
  12.0 9.2 %collective-permute-start.2 = (f32[7,7,16,128]{3,2,1,0:T(8,128)}, f32[7,7,16,128]{3,2,1,0:T(8,128)S(1)}, u32[]{:S(2)}, u32[]{:S(2)}) collective-permute-start(f32[7,7,16,128]{3,2,1,0:T(8,128)} %get-tuple-element.25), channel_id=1, source_target_pairs={{0,16},{16,0},{1,17},{17,1},{2,18},{18,2},{3,19},{19,3},{4,20},{20... | collective-permute-start | bytes 1204232 | tf_op jit(solution)/shard_map/ppermute | solution.py:587
  21.2 0.8 copy-start
  24.6 5.8 %collective-permute-start.3 = (f32[7,30,8,128]{3,2,1,0:T(8,128)}, f32[7,30,8,128]{3,2,1,0:T(8,128)S(1)}, u32[]{:S(2)}, u32[]{:S(2)}) collective-permute-start(f32[7,30,8,128]{3,2,1,0:T(8,128)} %get-tuple-element.26), channel_id=1, source_target_pairs={{0,4},{4,0},{8,12},{12,8},{1,5},{5,1},{9,13},{13,9},{2,6},{6,2},{1... | collective-permute-start | bytes 2580488 | tf_op jit(solution)/shard_map/ppermute | solution.py:587
  27.4 14.3 %collective-permute-start.4 = (f32[7,30,8,128]{3,2,1,0:T(8,128)}, f32[7,30,8,128]{3,2,1,0:T(8,128)S(1)}, u32[]{:S(2)}, u32[]{:S(2)}) collective-permute-start(f32[7,30,8,128]{3,2,1,0:T(8,128)} %get-tuple-element.27), channel_id=1, source_target_pairs={{4,8},{8,4},{5,9},{9,5},{6,10},{10,6},{7,11},{11,7},{20,24},{24,20... | collective-permute-start | bytes 2580488 | tf_op jit(solution)/shard_map/ppermute | solution.py:587
  30.4 11.3 %copy-start.2 = (f32[7,30,8,128]{3,2,1,0:T(8,128)}, f32[7,30,8,128]{3,2,1,0:T(8,128)S(1)}, u32[]{:S(2)}) copy-start(f32[7,30,8,128]{3,2,1,0:T(8,128)S(1)} %collective-permute-done.3.refs_8_) | copy-start | bytes 2580484
  41.7 0.9 copy-start.3
  59.5 31.8 %all-to-all-start = ((f32[32,5,4,128]{3,2,1,0:T(4,128)}), f32[32,5,4,128]{3,2,1,0:T(4,128)S(1)}, u32[]{:S(2)}, u32[]{:S(2)}) async-start(f32[32,5,4,128]{3,2,1,0:T(4,128)} %get-tuple-element.28), calls=%async_computation | async-start | bytes 655360 | tf_op jit(solution)/shard_map/all_to_all | solution.py:639
  64.3 7.1 %collective-permute-start.5 = (f32[8,8,128]{2,1,0:T(8,128)}, f32[8,8,128]{2,1,0:T(8,128)S(1)}, u32[]{:S(2)}, u32[]{:S(2)}) collective-permute-start(f32[8,8,128]{2,1,0:T(8,128)} %get-tuple-element.30), channel_id=1, source_target_pairs={{0,1},{1,0},{2,3},{3,2},{4,5},{5,4},{6,7},{7,6},{8,9},{9,8},{10,11... | collective-permute-start | bytes 98312 | tf_op jit(solution)/shard_map/ppermute | solution.py:587
  64.5 9.6 %collective-permute-start.6 = (f32[8,8,128]{2,1,0:T(8,128)}, f32[8,8,128]{2,1,0:T(8,128)S(1)}, u32[]{:S(2)}, u32[]{:S(2)}) collective-permute-start(f32[8,8,128]{2,1,0:T(8,128)} %get-tuple-element.31), channel_id=1, source_target_pairs={{1,2},{2,1},{5,6},{6,5},{9,10},{10,9},{13,14},{14,13},{17,18},{18,... | collective-permute-start | bytes 98312 | tf_op jit(solution)/shard_map/ppermute | solution.py:587
  71.4 2.7 %copy-start.9 = (f32[8,8,128]{2,1,0:T(8,128)}, f32[8,8,128]{2,1,0:T(8,128)S(1)}, u32[]{:S(2)}) copy-start(f32[8,8,128]{2,1,0:T(8,128)S(1)} %collective-permute-done.5.one_ref) | copy-start | bytes 98308
  74.1 0.6 copy-start.10
  76.5 3.5 %collective-permute-start.7 = (f32[5,4,8,128]{3,2,1,0:T(8,128)}, f32[5,4,8,128]{3,2,1,0:T(8,128)S(1)}, u32[]{:S(2)}, u32[]{:S(2)}) collective-permute-start(f32[5,4,8,128]{3,2,1,0:T(8,128)} %get-tuple-element.33), channel_id=1, source_target_pairs={{0,16},{16,0},{1,17},{17,1},{2,18},{18,2},{3,19},{19,3},{4,20},{20... | collective-permute-start | bytes 245768 | tf_op jit(solution)/shard_map/ppermute | solution.py:587
  80.0 0.6 copy-start.4
  82.4 5.0 %collective-permute-start.8 = (f32[5,16,4,128]{3,2,1,0:T(4,128)}, f32[5,16,4,128]{3,2,1,0:T(4,128)S(1)}, u32[]{:S(2)}, u32[]{:S(2)}) collective-permute-start(f32[5,16,4,128]{3,2,1,0:T(4,128)} %get-tuple-element.34), channel_id=1, source_target_pairs={{0,4},{4,0},{8,12},{12,8},{1,5},{5,1},{9,13},{13,9},{2,6},{6,2},{1... | collective-permute-start | bytes 491528 | tf_op jit(solution)/shard_map/ppermute | solution.py:587
  84.5 6.8 %collective-permute-start.9 = (f32[5,16,4,128]{3,2,1,0:T(4,128)}, f32[5,16,4,128]{3,2,1,0:T(4,128)S(1)}, u32[]{:S(2)}, u32[]{:S(2)}) collective-permute-start(f32[5,16,4,128]{3,2,1,0:T(4,128)} %get-tuple-element.35), channel_id=1, source_target_pairs={{4,8},{8,4},{5,9},{9,5},{6,10},{10,6},{7,11},{11,7},{20,24},{24,20... | collective-permute-start | bytes 491528 | tf_op jit(solution)/shard_map/ppermute | solution.py:587
  87.5 3.8 %copy-start.5 = (f32[5,16,4,128]{3,2,1,0:T(4,128)}, f32[5,16,4,128]{3,2,1,0:T(4,128)S(1)}, u32[]{:S(2)}) copy-start(f32[5,16,4,128]{3,2,1,0:T(4,128)S(1)} %collective-permute-done.8.refs_1_) | copy-start | bytes 491524
  91.3 0.7 copy-start.6
  91.3 0.8 copy-start.1

commit v3 on v2

v3 whole, which is shorter than its diff:
```python
import functools

import jax
import jax.numpy as jnp
from jax import lax
from jax.experimental import pallas as pl
from jax.experimental.pallas import tpu as pltpu
from jax.sharding import PartitionSpec as P

LEVELS = 6
SWEEPS = 2
BOTTOM = 8
WEIGHT = 0.25 ** (LEVELS - 1)
RELAX = 2.0 / 3.0
KEEP = 1.0 / 3.0

HALO = 4
NEAR = 4
LANES = 128

VM = pl.BlockSpec(memory_space=pltpu.VMEM)
SM = pl.BlockSpec(memory_space=pltpu.SMEM)
F32 = jnp.float32


def lane_of(shape):
    return lax.broadcasted_iota(jnp.int32, shape, len(shape) - 1)


def pick(flag, yes, no):
    return jnp.where(jnp.full(yes.shape, flag, jnp.int32) == 1, yes, no)


def neighbours(axis_size, odd, one, two):
    if axis_size == 2:
        two = jnp.zeros_like(one)
    return pick(odd, one, two), pick(odd, two, one)


def turn(values, shift, axis):
    return pltpu.roll(values, shift % values.shape[axis], axis)


def parts_of(values):
    high = values.astype(jnp.bfloat16)
    rest = values - high.astype(F32)
    middle = rest.astype(jnp.bfloat16)
    low = (rest - middle.astype(F32)).astype(jnp.bfloat16)
    return high, middle, low


def times_table(values, table):
    table = table.astype(jnp.bfloat16)
    total = None
    for part in reversed(parts_of(values)):
        term = jnp.dot(part, table, preferred_element_type=F32)
        total = term if total is None else total + term
    return total


def table_times(table, values):
    table = table.astype(jnp.bfloat16)
    total = None
    for part in reversed(parts_of(values)):
        term = jnp.dot(table, part, preferred_element_type=F32)
        total = term if total is None else total + term
    return total


def iota2(shape, axis):
    return lax.broadcasted_iota(jnp.int32, shape, axis)


def pair_table(rows, cols, odd):
    row = iota2((rows, cols), 0)
    col = iota2((rows, cols), 1)
    hit = (row == 2 * col + 1) if odd else (row // 2 == col)
    return hit.astype(F32)


def below_x(values):
    if values.shape[0] == 1:
        return jnp.zeros_like(values)
    return jnp.concatenate([jnp.zeros_like(values[:1]), values[:-1]], axis=0)


def above_x(values):
    if values.shape[0] == 1:
        return jnp.zeros_like(values)
    return jnp.concatenate([values[1:], jnp.zeros_like(values[:1])], axis=0)


def pull(values, faces):
    bx, by, bz = faces
    total = bx * above_x(values) + below_x(bx * values)
    total = total + (by * turn(values, -1, 1) + turn(by * values, 1, 1))
    return total + (bz * turn(values, -1, 2) + turn(bz * values, 1, 2))


def diagonal(mass, faces, coupled):
    bx, by, bz = faces
    _, cy, cz = coupled
    return mass + bx + below_x(bx) + by + turn(cy, 1, 1) + bz + turn(cz, 1, 2)


def relaxer(mass, diag):
    inside = mass > 0.0
    return jnp.where(inside, RELAX / jnp.where(inside, diag, 1.0), 0.0)


def sweep(values, rhs, weight, faces):
    return KEEP * values + weight * (rhs + pull(values, faces))


def pack_z_kernel(where_ref, *refs):
    ins, (first, second) = refs[:6], refs[6:]
    odd = where_ref[2] % 2
    sx, sy, sz = ins[0].shape
    half = sx // 2
    lane = lane_of((half, sy, LANES))
    head = jnp.zeros((half, sy, LANES), F32)
    tail = head
    for a, ref in enumerate(ins):
        for g in range(2):
            block = ref[g * half:(g + 1) * half]
            at = 64 * g + HALO * a
            mask = (lane >= at) & (lane < at + HALO)
            head = jnp.where(mask, turn(block, at, 2), head)
            tail = jnp.where(mask, turn(block, at + HALO, 2), tail)
    first[...] = pick(odd, head, tail)
    second[...] = pick(odd, tail, head)


def face_x_kernel(counts, where_ref, *refs):
    ins, one_ref, two_ref = refs[:6], refs[6], refs[7]
    zpack, sends = refs[8], refs[9:]
    sx, sy, sz = ins[0].shape
    half = sx // 2
    below, above = neighbours(counts[2], where_ref[2] % 2, one_ref[...], two_ref[...])
    lane = lane_of(below.shape)
    zpack[:half] = jnp.where(lane < 64, above, turn(below, 64, 2))
    zpack[half:] = jnp.where(lane < 64, turn(above, 64, 2), below)
    odd = where_ref[0] % 2
    for k, send in enumerate(sends):
        start = (1 - odd if k == 0 else odd) * (sx - HALO)
        for a, ref in enumerate(tuple(ins) + (zpack,)):
            send[a] = ref[pl.ds(start, HALO)]


def face_y_kernel(counts, where_ref, *refs):
    ins, halos, sends = refs[:7], refs[7:-2], refs[-2:]
    sx, sy, sz = ins[0].shape
    odd_x = where_ref[0] % 2
    odd = where_ref[1] % 2
    for a, ref in enumerate(ins):
        below, above = neighbours(counts[0], odd_x, halos[0][a], halos[-1][a])
        for at, block in ((0, below), (HALO, ref[...]), (HALO + sx, above)):
            head, tail = block[:, :HALO], block[:, sy - HALO:]
            span = slice(at, at + block.shape[0])
            sends[0][a, span] = pick(odd, head, tail)
            sends[1][a, span] = pick(odd, tail, head)


def each(first, last, step, body):
    rounds = (last - first) // step

    def go(i, carry):
        for j in range(step):
            body(first + i * step + j)
        return carry

    if rounds:
        lax.fori_loop(0, rounds, go, 0)
    for x in range(first + rounds * step, last):
        body(x)


def ring_up(main, halo, lane):
    main_up, halo_up = turn(main, -1, 1), turn(halo, -1, 1)
    last = lane == LANES - 1
    return jnp.where(last, halo_up, main_up), jnp.where(last, main_up, halo_up)


def ring_down(main, halo, lane):
    main_down, halo_down = turn(main, 1, 1), turn(halo, 1, 1)
    zero = lane == 0
    return jnp.where(zero, halo_down, main_down), jnp.where(zero, main_down, halo_down)


def pull_slab(field, bx, by, bz, x, lane):
    centre = [half[x] for half in field]
    out = []
    for k in range(2):
        c, face = centre[k], by[k][x]
        t = bx[k][x] * field[k][x + 1] + bx[k][x - 1] * field[k][x - 1]
        out.append(t + (face * turn(c, -1, 0) + turn(face * c, 1, 0)))
    faces = [half[x] for half in bz]
    ups = ring_up(centre[0], centre[1], lane)
    downs = ring_down(faces[0] * centre[0], faces[1] * centre[1], lane)
    return centre, [out[k] + (faces[k] * ups[k] + downs[k]) for k in range(2)]


def down_kernel(counts, where_ref, *refs):
    ins = refs[:7]
    n_x = 1 if counts[0] == 2 else 2
    halos_x = refs[7:7 + n_x]
    one_y, two_y = refs[7 + n_x:9 + n_x]
    own1, first1, second1, coarse2, kept_m, kept_h, weight_m, weight_h = refs[9 + n_x:17 + n_x]
    faces_out, scratch = refs[17 + n_x:25 + n_x], refs[25 + n_x:]
    mains, halves = scratch[:7], scratch[7:13]
    half_m, half_h, diag, sums, left = scratch[13:]
    sx, sy, sz = ins[0].shape
    ex, ey = sx + 2 * HALO, sy + 2 * HALO
    odd_x, odd_y, odd_z = where_ref[0] % 2, where_ref[1] % 2, where_ref[2] % 2

    for a in range(7):
        to = mains[a]
        below, above = neighbours(counts[0], odd_x, halos_x[0][a], halos_x[-1][a])
        to[:HALO, :sy] = below
        to[HALO:HALO + sx, :sy] = ins[a][...]
        to[HALO + sx:, :sy] = above
        below, above = neighbours(counts[1], odd_y, one_y[a], two_y[a])
        to[:, sy:] = jnp.concatenate([above, below], axis=1)
    lane = lane_of((ey, LANES))

    def unpack(x):
        packed = mains[6][x]
        for a in range(6):
            right = turn(packed, -HALO * a, 1)
            other_side = turn(packed, 64 - HALO - HALO * a, 1)
            halves[a][x] = jnp.where(
                lane < HALO, right, jnp.where(lane >= LANES - HALO, other_side, 0.0)
            )

    each(0, ex, 4, unpack)
    field, rhs, alpha, bx, by, bz = zip(mains[:6], halves)
    halfway, weight, kept = (half_m, half_h), (weight_m, weight_h), (kept_m, kept_h)

    def first_sweep(x):
        faces = [half[x] for half in bz]
        downs = ring_down(faces[0], faces[1], lane)
        centre, near = pull_slab(field, bx, by, bz, x, lane)
        for k in range(2):
            face = by[k][x]
            mass = WEIGHT * alpha[k][x]
            d = mass + bx[k][x] + bx[k][x - 1] + face + turn(face, 1, 0) + faces[k] + downs[k]
            w = relaxer(mass, d)
            if k == 0:
                diag[x] = d
            weight[k][x] = w
            halfway[k][x] = KEEP * centre[k] + w * (rhs[k][x] + near[k])

    each(1, ex - 1, 4, first_sweep)

    def second_sweep(x):
        centre, near = pull_slab(halfway, bx, by, bz, x, lane)
        for k in range(2):
            kept[k][x] = KEEP * centre[k] + weight[k][x] * (rhs[k][x] + near[k])

    each(2, ex - 2, 4, second_sweep)

    def residual(x):
        centre, near = pull_slab(kept, bx, by, bz, x, lane)
        half_m[x] = rhs[0][x] - diag[x] * centre[0] + near[0]

    each(HALO, ex - HALO, 4, residual)
    for n, source in enumerate((rhs, bx, by, bz)):
        for k in range(2):
            faces_out[2 * n + k][...] = source[k][...]

    x1, y1, z1 = sx // 2, sy // 2, sz // 2

    def rows_of(source, x, firsts, seconds):
        total = None
        for p in firsts:
            for q in seconds:
                term = source[x + p, pl.ds(q, y1, stride=2), :]
                total = term if total is None else total + term
        return total

    both, last = (0, 1), (1,)
    for i in range(x1):
        x = HALO + 2 * i
        sums[0, i] = rows_of(half_m, x, both, both)
        sums[1, i] = rows_of(alpha[0], x, both, both)
        sums[2, i] = rows_of(bx[0], x, last, both)
        sums[3, i] = rows_of(by[0], x, both, last)
        left[...] = turn(by[0][x] + by[0][x + 1], 1, 0)
        sums[4, i] = left[pl.ds(0, y1, stride=2), :]
        sums[5, i] = rows_of(bz[0], x, both, both)
    sums[6, 0] = rows_of(bx[0], HALO - 2, last, both)
    edge_z = [rows_of(bz[1], HALO + 2 * i, both, both)[None] for i in range(x1)]
    edge_z = 0.0625 * jnp.concatenate(edge_z, axis=0)
    pairs = pair_table(LANES, LANES, False)
    odds = pair_table(LANES, LANES, True)

    def to_level1(first, count, table, factor):
        flat = sums[first:first + count].reshape(count * x1 * y1, LANES)
        return factor * times_table(flat, table).reshape(count, x1, y1, LANES)

    paired = to_level1(0, 5, pairs, 0.0625)
    rhs1, mass1 = 2.0 * paired[0], (2.0 * WEIGHT) * paired[1]
    faces1 = (paired[2], paired[3], to_level1(5, 1, odds, 0.0625)[0])
    edge_x = 0.0625 * times_table(sums[6, 0], pairs)[None]
    lane1 = lane_of((x1, y1, LANES))
    diag1 = mass1 + faces1[0] + jnp.concatenate([edge_x, faces1[0][:-1]], axis=0)
    diag1 = diag1 + faces1[1] + paired[4]
    diag1 = diag1 + faces1[2] + jnp.where(lane1 == 0, turn(edge_z, 1, 2), turn(faces1[2], 1, 2))
    inside = lane1 < z1
    weight1 = jnp.where(inside, RELAX / jnp.where(inside, diag1, 1.0), 0.0)

    head = jnp.zeros((x1, y1, LANES), F32)
    tail = head
    for n, values in enumerate((rhs1, weight1) + faces1):
        block = jnp.where(inside, values, 0.0)
        own1[n] = block
        at = NEAR * n
        mask = (lane1 >= at) & (lane1 < at + NEAR)
        head = jnp.where(mask, turn(block, at, 2), head)
        tail = jnp.where(mask, turn(block, at + NEAR - z1, 2), tail)
    first1[...] = pick(odd_z, head, tail)
    second1[...] = pick(odd_z, tail, head)

    parts = (
        (mass1, False, False, False, 0.125),
        (faces1[0], True, False, False, 0.0625),
        (faces1[1], False, True, False, 0.0625),
        (faces1[2], False, False, True, 0.0625),
    )
    for n, (values, *odd_axes, factor) in enumerate(parts):
        sums[n] = values
        coarse2[n] = level2_rows(sums.at[n], odd_axes, factor, x1 // 2, y1 // 2, z1 // 2)


def level2_rows(source, odd_axes, factor, x2, y2, z2):
    rows = []
    for i in range(x2):
        total = None
        for p in (1,) if odd_axes[0] else (0, 1):
            for q in (1,) if odd_axes[1] else (0, 1):
                term = source[2 * i + p, pl.ds(q, y2, stride=2), :]
                total = term if total is None else total + term
        rows.append(total)
    flat = jnp.concatenate(rows, axis=0)
    flat = factor * times_table(flat, pair_table(LANES, LANES, odd_axes[2]))
    lane = lane_of((y2, LANES))
    packed = jnp.zeros((y2, LANES), F32)
    for i in range(x2):
        mask = (lane >= i * z2) & (lane < (i + 1) * z2)
        packed = jnp.where(mask, turn(flat[i * y2:(i + 1) * y2], i * z2, 1), packed)
    return packed


def near_x_kernel(counts, where_ref, own_ref, one_ref, two_ref, ring, *sends):
    n, bx, by, _ = own_ref.shape
    below, above = neighbours(counts[2], where_ref[2] % 2, one_ref[...], two_ref[...])
    lane = lane_of(below.shape)
    for a in range(n):
        right = turn(above, LANES // 2 - NEAR * a, 2)
        left = turn(below, LANES - NEAR - NEAR * a, 2)
        block = jnp.where(lane < LANES // 2, own_ref[a], 0.0)
        block = jnp.where((lane >= LANES // 2) & (lane < LANES // 2 + NEAR), right, block)
        ring[a] = jnp.where(lane >= LANES - NEAR, left, block)
    odd = where_ref[0] % 2
    for k, send in enumerate(sends):
        start = (1 - odd if k == 0 else odd) * (bx - NEAR)
        for a in range(n):
            send[a] = ring[a, pl.ds(start, NEAR)]


def near_y_kernel(counts, where_ref, ring, *refs):
    halos, sends = refs[:-2], refs[-2:]
    n, bx, by, _ = ring.shape
    odd_x, odd = where_ref[0] % 2, where_ref[1] % 2
    for a in range(n):
        below, above = neighbours(counts[0], odd_x, halos[0][a], halos[-1][a])
        block = jnp.concatenate([below, ring[a], above], axis=0)
        head, tail = block[:, :NEAR], block[:, by - NEAR:]
        sends[0][a] = pick(odd, head, tail)
        sends[1][a] = pick(odd, tail, head)


def near_kernel(counts, devices, where_ref, ring, *refs):
    n_x = 1 if counts[0] == 2 else 2
    halos_x = refs[:n_x]
    one_y, two_y, coarse2, copies, level1, left = refs[n_x:]
    n, bx1, by1, _ = ring.shape
    odd_x, odd_y = where_ref[0] % 2, where_ref[1] % 2
    whole = []
    for a in range(n):
        below, above = neighbours(counts[0], odd_x, halos_x[0][a], halos_x[-1][a])
        block = jnp.concatenate([below, ring[a], above], axis=0)
        below, above = neighbours(counts[1], odd_y, one_y[a], two_y[a])
        whole.append(jnp.concatenate([block, above, below], axis=1))
    rhs1, weight1 = whole[:2]
    faces1 = tuple(whole[2:])
    field1 = weight1 * rhs1
    field1 = sweep(field1, rhs1, weight1, faces1)
    for a, values in enumerate([field1] + whole):
        level1[a] = values
    mine = slice(NEAR, NEAR + bx1)
    inner = weight1[mine]
    diag1 = RELAX / jnp.where(inner > 0.0, inner, 1.0)
    remain = rhs1[mine] - diag1 * field1[mine] + pull(field1, faces1)[mine]
    left[...] = remain
    packed = level2_rows(left, (False,) * 3, 0.125, bx1 // 2, by1 // 2, LANES // 4)
    for d in range(devices):
        copies[d, 0] = packed
        for a in range(n - 1):
            copies[d, a + 1] = coarse2[a]


def halve(values, factor, odd_axis):
    x, y, z = values.shape
    if odd_axis == 0:
        values = jnp.concatenate([values[2 * i + 1:2 * i + 2] for i in range(x // 2)], axis=0)
    else:
        values = jnp.concatenate(
            [values[2 * i:2 * i + 1] + values[2 * i + 1:2 * i + 2] for i in range(x // 2)], axis=0
        )
    to_y = max(8, y // 2)
    to_z = max(LANES, z // 2)
    flat = values.reshape(x // 2 * y, z)
    flat = times_table(flat, pair_table(z, to_z, odd_axis == 2))
    row = iota2((to_y, y), 0)
    col = iota2((to_y, y), 1)
    table = (col == 2 * row + 1) if odd_axis == 1 else (col // 2 == row)
    table = table.astype(F32)
    blocks = [table_times(table, flat[i * y:(i + 1) * y])[None] for i in range(x // 2)]
    return factor * jnp.concatenate(blocks, axis=0)


def double(values, shape):
    x, y, z = values.shape
    to_x, to_y, to_z = shape
    row = iota2((to_y, y), 0)
    col = iota2((to_y, y), 1)
    table_y = (row // 2 == col).astype(F32)
    row = iota2((z, to_z), 0)
    col = iota2((z, to_z), 1)
    table_z = (col // 2 == row).astype(F32)
    blocks = [table_times(table_y, values[i])[None] for i in range(x)]
    flat = jnp.concatenate(blocks, axis=0).reshape(x * to_y, z)
    flat = times_table(flat, table_z).reshape(x, to_y, to_z)
    return jnp.concatenate([flat[i // 2:i // 2 + 1] for i in range(to_x)], axis=0)


def coupled_faces(faces, y, z):
    bx, by, bz = faces
    row = lax.broadcasted_iota(jnp.int32, by.shape, 1)
    return bx, jnp.where(row == y - 1, 0.0, by), jnp.where(lane_of(bz.shape) == z - 1, 0.0, bz)


def coarse_cycle(level, rhs, mass, faces, y, z):
    coupled = coupled_faces(faces, y, z)
    diag = diagonal(mass, faces, coupled)
    weight = relaxer(mass, diag)
    field = weight * rhs
    if level == LEVELS - 1:
        for _ in range(BOTTOM - 1):
            field = sweep(field, rhs, weight, coupled)
        return field
    for _ in range(SWEEPS - 1):
        field = sweep(field, rhs, weight, coupled)
    remain = rhs - diag * field + pull(field, coupled)
    correction = coarse_cycle(
        level + 1,
        halve(remain, 0.125, -1),
        halve(mass, 0.125, -1),
        tuple(halve(face, 0.0625, axis) for axis, face in enumerate(faces)),
        y // 2,
        z // 2,
    )
    field = field + double(correction, field.shape)
    for _ in range(SWEEPS):
        field = sweep(field, rhs, weight, coupled)
    return field


def up_kernel(counts, where_ref, gathered, level1, *refs):
    kept, weight, rhs, bx, by, bz = zip(refs[0:12:2], refs[1:12:2])
    out, whole, second, spread_m, spread_h, field_m, field_h, half_m, half_h = refs[12:]
    gx, gy, gz = counts
    sx, sy, sz = out.shape
    x1, y1 = sx // 2, sy // 2
    x2, y2, z2 = x1 // 2, y1 // 2, sz // 4
    columns = max(LANES, gz * z2)
    lane = lane_of((y2, LANES))

    for a in range(5):
        for i in range(gx):
            for j in range(gy):
                for x in range(x2):
                    for part in range(columns // LANES):
                        total = jnp.zeros((y2, LANES), F32)
                        for k in range(LANES // z2):
                            column = part * (LANES // z2) + k
                            if column < gz:
                                block = gathered[(i * gy + j) * gz + column, a]
                                mask = (lane >= k * z2) & (lane < (k + 1) * z2)
                                total = jnp.where(mask, turn(block, (k - x) * z2, 1), total)
                        whole[
                            a, i * x2 + x, j * y2:(j + 1) * y2, part * LANES:(part + 1) * LANES
                        ] = total
    correction = coarse_cycle(
        2, whole[0], whole[1], (whole[2], whole[3], whole[4]), gy * y2, gz * z2
    )

    wide = gx * x2
    half = NEAR // 2
    ex1, ey1 = x1 + 2 * NEAR, y1 + 2 * NEAR
    second[:half] = jnp.zeros((half,) + correction.shape[1:], F32)
    second[half:half + wide] = correction
    second[half + wide:] = jnp.zeros((half,) + correction.shape[1:], F32)
    window = second[pl.ds(where_ref[0] * x2, x2 + NEAR)]
    rows = correction.shape[1]
    row = iota2((ey1, rows), 0)
    col = iota2((ey1, rows), 1)
    place = jnp.where(row < y1 + NEAR, row, row - ey1)
    table_y = (col == where_ref[1] * y2 + lax.shift_right_arithmetic(place, 1)).astype(F32)
    row = iota2((columns, LANES), 0)
    col = iota2((columns, LANES), 1)
    place = jnp.where(col < LANES * 3 // 4, col, col - LANES)
    table_z = (row == where_ref[2] * z2 + lax.shift_right_arithmetic(place, 1)).astype(F32)
    flat = times_table(window.reshape((x2 + NEAR) * rows, columns), table_z)
    blocks = [table_times(table_y, flat[i * rows:(i + 1) * rows])[None] for i in range(x2 + NEAR)]
    lifted = jnp.concatenate([blocks[i // 2] for i in range(ex1)], axis=0)
    field1, rhs1, weight1 = level1[0], level1[1], level1[2]
    faces1 = (level1[3], level1[4], level1[5])
    field1 = field1 + jnp.where(weight1 > 0.0, lifted, 0.0)
    for _ in range(SWEEPS):
        field1 = sweep(field1, rhs1, weight1, faces1)

    ex, ey = sx + 2 * HALO, sy + 2 * HALO
    near = field1[NEAR - 1:NEAR + x1 + 1].reshape((x1 + 2) * ey1, LANES)
    row = iota2((LANES, 2 * LANES), 0)
    col = iota2((LANES, 2 * LANES), 1)
    lifted = times_table(near, (col // 2 == row).astype(F32))
    quarter = NEAR // 2
    for k, spread in enumerate((spread_m, spread_h)):
        block = lifted[:, k * LANES:(k + 1) * LANES].reshape(x1 + 2, ey1, LANES)
        for i in range(x1 + 2):
            for q in range(2):
                spread[i, pl.ds(q, y1, stride=2), :] = block[i, :y1]
                spread[i, pl.ds(sy + q, quarter, stride=2), :] = block[i, y1:y1 + quarter]
                spread[i, pl.ds(sy + HALO + q, quarter, stride=2), :] = block[i, ey1 - quarter:]
    before, after = (field_m, field_h), (half_m, half_h)
    first = HALO - 2
    for x in range(first, ex - first):
        for k, spread in enumerate((spread_m, spread_h)):
            before[k][x] = kept[k][x] + spread[(x - first) // 2]

    lane = lane_of((ey, LANES))

    def sweep_out(x):
        centre, around = pull_slab(before, bx, by, bz, x, lane)
        for k in range(2):
            after[k][x] = KEEP * centre[k] + weight[k][x] * (rhs[k][x] + around[k])

    each(first + 1, ex - first - 1, 4, sweep_out)

    def sweep_own(x):
        centre, around = pull_slab(after, bx, by, bz, x, lane)
        value = KEEP * centre[0] + weight[0][x] * (rhs[0][x] + around[0])
        out[x - HALO] = value[:sy]

    each(HALO, ex - HALO, 4, sweep_own)


def run(kernel, outs, where, arrays, scratch=(), grant=16):
    return pl.pallas_call(
        kernel,
        out_shape=tuple(jax.ShapeDtypeStruct(shape, F32) for shape in outs),
        in_specs=[SM] + [VM] * len(arrays),
        out_specs=tuple(VM for _ in outs),
        scratch_shapes=[pltpu.VMEM(shape, F32) for shape in scratch],
        compiler_params=pltpu.CompilerParams(vmem_limit_bytes=grant * 1024 * 1024),
    )(where, *arrays)


def swaps(axis, sends):
    count = lax.axis_size(axis)
    got = []
    for k, block in enumerate(sends):
        pairs = [(i, i + 1) for i in range(k, count - 1, 2)]
        pairs = [pair for low, high in pairs for pair in ((low, high), (high, low))]
        got.append(lax.ppermute(block, axis, pairs))
    return got


def local(initial, right_side, alpha, beta_x, beta_y, beta_z):
    axes = ("gx", "gy", "gz")
    counts = tuple(lax.axis_size(axis) for axis in axes)
    devices = counts[0] * counts[1] * counts[2]
    where = jnp.stack([lax.axis_index(axis) for axis in axes]).astype(jnp.int32)
    ins = (initial, right_side, alpha, beta_x, beta_y, beta_z)
    sx, sy, sz = initial.shape
    n_x = 1 if counts[0] == 2 else 2
    ex, ey = sx + 2 * HALO, sy + 2 * HALO
    fine = (ex, ey, LANES)

    sends = run(pack_z_kernel, [(sx // 2, sy, LANES)] * 2, where, ins)
    got = swaps("gz", sends)
    zpack, *sends = run(
        functools.partial(face_x_kernel, counts),
        [(sx, sy, LANES)] + [(7, HALO, sy, LANES)] * n_x,
        where,
        ins + tuple(got),
    )
    ins = ins + (zpack,)
    got_x = swaps("gx", sends)
    sends = run(
        functools.partial(face_y_kernel, counts),
        [(7, ex, HALO, LANES)] * 2,
        where,
        ins + tuple(got_x),
    )
    got_y = swaps("gy", sends)
    x1, y1 = sx // 2, sy // 2
    own1, first1, second1, coarse2, *fine_arrays = run(
        functools.partial(down_kernel, counts),
        [(5, x1, y1, LANES), (x1, y1, LANES), (x1, y1, LANES), (4, y1 // 2, LANES)] + [fine] * 12,
        where,
        ins + tuple(got_x) + tuple(got_y),
        [fine] * 16 + [(7, x1, y1, LANES), (ey, LANES)],
        24,
    )

    got = swaps("gz", (first1, second1))
    ring, *sends = run(
        functools.partial(near_x_kernel, counts),
        [(5, x1, y1, LANES)] + [(5, NEAR, y1, LANES)] * n_x,
        where,
        (own1,) + tuple(got),
    )
    near_x = swaps("gx", sends)
    sends = run(
        functools.partial(near_y_kernel, counts),
        [(5, x1 + 2 * NEAR, NEAR, LANES)] * 2,
        where,
        (ring,) + tuple(near_x),
    )
    near_y = swaps("gy", sends)
    copies, level1 = run(
        functools.partial(near_kernel, counts, devices),
        [(devices, 5, y1 // 2, LANES), (6, x1 + 2 * NEAR, y1 + 2 * NEAR, LANES)],
        where,
        (ring,) + tuple(near_x) + tuple(near_y) + (coarse2,),
        [(x1, y1 + 2 * NEAR, LANES)],
    )

    gathered = lax.all_to_all(copies, axes, 0, 0, tiled=True)
    wide, rows = counts[0] * x1 // 2, counts[1] * y1 // 2
    columns = max(LANES, counts[2] * sz // 4)
    (result,) = run(
        functools.partial(up_kernel, counts),
        [(sx, sy, sz)],
        where,
        (gathered, level1) + tuple(fine_arrays),
        [(5, wide, rows, columns), (wide + NEAR, rows, columns)]
        + [(x1 + 2, ey, LANES)] * 2
        + [fine] * 4,
        24,
    )
    return result


def solution(mesh):
    spec = P("gx", "gy", "gz")
    return jax.shard_map(
        local, mesh=mesh, in_specs=(spec,) * 6, out_specs=spec, check_vma=False
    )
```

time: 106 us -> 81.5 us (0.77)
  the two profiles are of different devices: /device:TPU:9 before, /device:TPU:1 now
where the time goes in v3:
time: 81.5 us; the launch traced here: 81.2 us
  starting transfers between devices  21.6 us (27%)
  blocking collectives  19.2 us (24%)
  Pallas kernels  18.5 us (23%)
  waiting for transfers between devices  16.2 us (20%)
  local copies, waits for them, and re-layouts  5.45 us (7%)
    ppermute x10, starting transfers between devices, swaps(): got.append(lax.ppermute(block, axis, pairs))  21.6 us
    all_to_all x1, blocking collectives, local(): gathered = lax.all_to_all(copies, axes, 0, 0, tiled=True)  19.2 us
    pallas_call x8, Pallas kernels, run(): pl.pallas_call(kernel, out_shape=tuple((jax.ShapeDtypeStruct(shape, F32)...  18.5 us
    ppermute x10, waiting for transfers between devices, swaps(): got.append(lax.ppermute(block, axis, pairs))  16.2 us
    unnamed x24, local copies, waits for them, and re-layouts  5.45 us
  transfers between devices with their start and end apart: 10, of which 6 were waited for; matrix products, arithmetic and copies ran while one was open for 0% of the time, Pallas kernels for 0%

profile of v3, /device:TPU:1, one launch (start us, length us, event | category | flops | bytes accessed | tf_op | source)
XLA Modules:
  0.0 81.2 jit_solution(4228599492736551104)
XLA Ops:
  0.0 0.1 pad_add_fusion.where_ref
  0.1 0.9 %copy-done = f32[16,16,128]{2,1,0:T(8,128)S(1)} copy-done((f32[16,16,128]{2,1,0:T(8,128)S(1)}, f32[16,16,128]{2,1,0:T(8,128)}, u32[]{:S(2)}) %copy-start) | copy-done | bytes 131096
  1.0 0.9 %copy-done.2 = f32[16,16,128]{2,1,0:T(8,128)S(1)} copy-done((f32[16,16,128]{2,1,0:T(8,128)S(1)}, f32[16,16,128]{2,1,0:T(8,128)}, u32[]{:S(2)}) %copy-start.2) | copy-done | bytes 131096
  1.9 0.9 %copy-done.4 = f32[16,16,128]{2,1,0:T(8,128)S(1)} copy-done((f32[16,16,128]{2,1,0:T(8,128)S(1)}, f32[16,16,128]{2,1,0:T(8,128)}, u32[]{:S(2)}) %copy-start.4) | copy-done | bytes 131096
  2.8 0.9 %copy-done.6 = f32[16,16,128]{2,1,0:T(8,128)S(1)} copy-done((f32[16,16,128]{2,1,0:T(8,128)S(1)}, f32[16,16,128]{2,1,0:T(8,128)}, u32[]{:S(2)}) %copy-start.6) | copy-done | bytes 131096
  3.7 0.9 %copy-done.8 = f32[16,16,128]{2,1,0:T(8,128)S(1)} copy-done((f32[16,16,128]{2,1,0:T(8,128)S(1)}, f32[16,16,128]{2,1,0:T(8,128)}, u32[]{:S(2)}) %copy-start.8) | copy-done | bytes 131096
  4.6 0.9 %copy-done.10 = f32[16,16,128]{2,1,0:T(8,128)S(1)} copy-done((f32[16,16,128]{2,1,0:T(8,128)S(1)}, f32[16,16,128]{2,1,0:T(8,128)}, u32[]{:S(2)}) %copy-start.10) | copy-done | bytes 131096
  5.5 1.0 %shard_map.64 = (f32[8,16,128]{2,1,0:T(8,128)S(1)}, f32[8,16,128]{2,1,0:T(8,128)S(1)}) custom-call(s32[3]{0:T(128)S(1)} %pad_add_fusion.where_ref, f32[16,16,128]{2,1,0:T(8,128)S(1)} %copy-done, f32[16,16,128]{2,1,0:T(8,128)S(1)} %copy-done.2, f32[16,16,128]{2,1,0:T(8,128)S(1)} %copy-done.4, f32[16,16,128]{2,1,0:T(8,128)S(1)} %copy-done.6, ...), custom_call_target="tpu_custom_call" | custom-call | tf_op jit(solution)/shard_map/pallas_call | solution.py:571
  6.5 2.2 %collective-permute-start = (f32[8,16,128]{2,1,0:T(8,128)S(1)}, f32[8,16,128]{2,1,0:T(8,128)S(1)}, u32[]{:S(2)}, u32[]{:S(2)}) collective-permute-start(f32[8,16,128]{2,1,0:T(8,128)S(1)} %get-tuple-element.33), channel_id=1, source_target_pairs={{0,1},{1,0},{2,3},{3,2},{4,5},{5,4},{6,7},{7,6},{8,9},{9,8},{10,11... | collective-permute-start | bytes 196616 | tf_op jit(solution)/shard_map/ppermute | solution.py:587
  8.7 0.7 collective-permute-start.1
  9.4 1.0 %collective-permute-done.refs_6_ = f32[8,16,128]{2,1,0:T(8,128)S(1)} collective-permute-done((f32[8,16,128]{2,1,0:T(8,128)S(1)}, f32[8,16,128]{2,1,0:T(8,128)S(1)}, u32[]{:S(2)}, u32[]{:S(2)}) %collective-permute-start) | collective-permute-done | bytes 65568 | tf_op jit(solution)/shard_map/ppermute | solution.py:587
  10.4 0.6 shard_map.65
  11.0 1.4 %collective-permute-start.2 = (f32[7,4,16,128]{3,2,1,0:T(8,128)S(1)}, f32[7,4,16,128]{3,2,1,0:T(8,128)S(1)}, u32[]{:S(2)}, u32[]{:S(2)}) collective-permute-start(f32[7,4,16,128]{3,2,1,0:T(8,128)S(1)} %get-tuple-element.36), channel_id=1, source_target_pairs={{0,16},{16,0},{1,17},{17,1},{2,18},{18,2},{3,19},{19,3},{4,20},{20... | collective-permute-start | bytes 688136 | tf_op jit(solution)/shard_map/ppermute | solution.py:587
  12.5 4.2 %collective-permute-done.2.refs_7_ = f32[7,4,16,128]{3,2,1,0:T(8,128)S(1)} collective-permute-done((f32[7,4,16,128]{3,2,1,0:T(8,128)S(1)}, f32[7,4,16,128]{3,2,1,0:T(8,128)S(1)}, u32[]{:S(2)}, u32[]{:S(2)}) %collective-permute-start.2) | collective-permute-done | bytes 229408 | tf_op jit(solution)/shard_map/ppermute | solution.py:587
  16.7 0.7 shard_map.66
  17.3 2.5 %collective-permute-start.3 = (f32[7,24,4,128]{3,2,1,0:T(4,128)S(1)}, f32[7,24,4,128]{3,2,1,0:T(4,128)S(1)}, u32[]{:S(2)}, u32[]{:S(2)}) collective-permute-start(f32[7,24,4,128]{3,2,1,0:T(4,128)S(1)} %get-tuple-element.37), channel_id=1, source_target_pairs={{0,4},{4,0},{8,12},{12,8},{1,5},{5,1},{9,13},{13,9},{2,6},{6,2},{1... | collective-permute-start | bytes 1032200 | tf_op jit(solution)/shard_map/ppermute | solution.py:587
  19.9 3.2 %collective-permute-start.4 = (f32[7,24,4,128]{3,2,1,0:T(4,128)S(1)}, f32[7,24,4,128]{3,2,1,0:T(4,128)S(1)}, u32[]{:S(2)}, u32[]{:S(2)}) collective-permute-start(f32[7,24,4,128]{3,2,1,0:T(4,128)S(1)} %get-tuple-element.38), channel_id=1, source_target_pairs={{4,8},{8,4},{5,9},{9,5},{6,10},{10,6},{7,11},{11,7},{20,24},{24,20... | collective-permute-start | bytes 1032200 | tf_op jit(solution)/shard_map/ppermute | solution.py:587
  23.1 5.3 %collective-permute-done.4.refs_9_ = f32[7,24,4,128]{3,2,1,0:T(4,128)S(1)} collective-permute-done((f32[7,24,4,128]{3,2,1,0:T(4,128)S(1)}, f32[7,24,4,128]{3,2,1,0:T(4,128)S(1)}, u32[]{:S(2)}, u32[]{:S(2)}) %collective-permute-start.4) | collective-permute-done | bytes 344096 | tf_op jit(solution)/shard_map/ppermute | solution.py:587
  28.5 4.7 %shard_map.67 = (f32[5,8,8,128]{3,2,1,0:T(8,128)S(1)}, f32[8,8,128]{2,1,0:T(8,128)S(1)}, f32[8,8,128]{2,1,0:T(8,128)S(1)}, f32[4,4,128]{2,1,0:T(4,128)S(1)}, f32...) custom-call(s32[3]{0:T(128)S(1)} %pad_add_fusion.where_ref, ...), custom_call_target="tpu_custom_call" | custom-call | tf_op jit(solution)/shard_map/pallas_call | solution.py:571
  33.2 4.5 %collective-permute-start.5 = (f32[8,8,128]{2,1,0:T(8,128)S(1)}, f32[8,8,128]{2,1,0:T(8,128)S(1)}, u32[]{:S(2)}, u32[]{:S(2)}) collective-permute-start(f32[8,8,128]{2,1,0:T(8,128)S(1)} %get-tuple-element.40), channel_id=1, source_target_pairs={{0,1},{1,0},{2,3},{3,2},{4,5},{5,4},{6,7},{7,6},{8,9},{9,8},{10,11... | collective-permute-start | bytes 98312 | tf_op jit(solution)/shard_map/ppermute | solution.py:587
  37.7 0.7 collective-permute-start.6
  38.4 0.6 collective-permute-done.5.one_ref
  39.1 0.7 shard_map.68
  39.8 1.3 %collective-permute-start.7 = (f32[5,4,8,128]{3,2,1,0:T(8,128)S(1)}, f32[5,4,8,128]{3,2,1,0:T(8,128)S(1)}, u32[]{:S(2)}, u32[]{:S(2)}) collective-permute-start(f32[5,4,8,128]{3,2,1,0:T(8,128)S(1)} %get-tuple-element.43), channel_id=1, source_target_pairs={{0,16},{16,0},{1,17},{17,1},{2,18},{18,2},{3,19},{19,3},{4,20},{20... | collective-permute-start | bytes 245768 | tf_op jit(solution)/shard_map/ppermute | solution.py:587
  41.0 2.1 %collective-permute-done.7.refs_0_ = f32[5,4,8,128]{3,2,1,0:T(8,128)S(1)} collective-permute-done((f32[5,4,8,128]{3,2,1,0:T(8,128)S(1)}, f32[5,4,8,128]{3,2,1,0:T(8,128)S(1)}, u32[]{:S(2)}, u32[]{:S(2)}) %collective-permute-start.7) | collective-permute-done | bytes 81952 | tf_op jit(solution)/shard_map/ppermute | solution.py:587
  43.1 0.6 shard_map.69
  43.7 0.1 collective-permute-start.8
  43.8 5.1 %collective-permute-start.9 = (f32[5,16,4,128]{3,2,1,0:T(4,128)S(1)}, f32[5,16,4,128]{3,2,1,0:T(4,128)S(1)}, u32[]{:S(2)}, u32[]{:S(2)}) collective-permute-start(f32[5,16,4,128]{3,2,1,0:T(4,128)S(1)} %get-tuple-element.45), channel_id=1, source_target_pairs={{4,8},{8,4},{5,9},{9,5},{6,10},{10,6},{7,11},{11,7},{20,24},{24,20... | collective-permute-start | bytes 491528 | tf_op jit(solution)/shard_map/ppermute | solution.py:587
  48.9 3.0 %collective-permute-done.9.refs_2_ = f32[5,16,4,128]{3,2,1,0:T(4,128)S(1)} collective-permute-done((f32[5,16,4,128]{3,2,1,0:T(4,128)S(1)}, f32[5,16,4,128]{3,2,1,0:T(4,128)S(1)}, u32[]{:S(2)}, u32[]{:S(2)}) %collective-permute-start.9) | collective-permute-done | bytes 163872 | tf_op jit(solution)/shard_map/ppermute | solution.py:587
  51.9 1.0 %shard_map.70 = (f32[32,5,4,128]{3,2,1,0:T(4,128)S(1)}, f32[6,16,16,128]{3,2,1,0:T(8,128)S(1)}) custom-call(s32[3]{0:T(128)S(1)} %pad_add_fusion.where_ref, f32[5,8,8,128]{3,2,1,0:T(8,128)S(1)} %get-tuple-element.42.ring, f32[5,4,8,128]{3,2,1,0:T(8,128)S(1)} %collective-permute-done.7.refs_0_, f32[5,16,4,128]{3,2,1,0:T(4,128)S(1)} %collective-permute-done.8.refs_1_, ...), custom_call_target="tpu_custom_call" | custom-call | tf_op jit(solution)/shard_map/pallas_call | solution.py:571
  52.8 19.2 %all_to_all.5.gathered = f32[32,5,4,128]{3,2,1,0:T(4,128)S(1)} all-to-all(f32[32,5,4,128]{3,2,1,0:T(4,128)S(1)} %get-tuple-element.47), channel_id=1, replica_groups=mesh['gx'=2,'gy'=4,'gz'=4] {'gx','gy','gz'}, dimensions={0} | all-to-all | bytes 655360 | tf_op jit(solution)/shard_map/all_to_all | solution.py:652
  72.0 9.2 %shard_map.71 = f32[16,16,128]{2,1,0:T(8,128)} custom-call(s32[3]{0:T(128)S(1)} %pad_add_fusion.where_ref, f32[32,5,4,128]{3,2,1,0:T(4,128)S(1)} %all_to_all.5.gathered, f32[6,16,16,128]{3,2,1,0:T(8,128)S(1)} %get-tuple-element.48.level1, f32[24,24,128]{2,1,0:T(8,128)S(1)} %get-tuple-element.49.refs_0_, f32[24,24,128]{2,1,0:T(8,128)S(1)} %get-tuple-element.50.refs_1_, ...), custom_call_target="tpu_custom_call" | custom-call | tf_op jit(solution)/shard_map/pallas_call | solution.py:571
  (22 shorter events, 0.0 us)
Async XLA Ops:
  0.1 0.9 %copy-start = (f32[16,16,128]{2,1,0:T(8,128)S(1)}, f32[16,16,128]{2,1,0:T(8,128)}, u32[]{:S(2)}) copy-start(f32[16,16,128]{2,1,0:T(8,128)} %refs_0_.7) | copy-start | bytes 393220
  1.0 0.9 %copy-start.2 = (f32[16,16,128]{2,1,0:T(8,128)S(1)}, f32[16,16,128]{2,1,0:T(8,128)}, u32[]{:S(2)}) copy-start(f32[16,16,128]{2,1,0:T(8,128)} %refs_1_.7) | copy-start | bytes 393220
  1.9 0.9 %copy-start.4 = (f32[16,16,128]{2,1,0:T(8,128)S(1)}, f32[16,16,128]{2,1,0:T(8,128)}, u32[]{:S(2)}) copy-start(f32[16,16,128]{2,1,0:T(8,128)} %refs_2_.7) | copy-start | bytes 393220
  2.8 0.9 %copy-start.6 = (f32[16,16,128]{2,1,0:T(8,128)S(1)}, f32[16,16,128]{2,1,0:T(8,128)}, u32[]{:S(2)}) copy-start(f32[16,16,128]{2,1,0:T(8,128)} %refs_3_.7) | copy-start | bytes 393220
  3.7 0.9 %copy-start.8 = (f32[16,16,128]{2,1,0:T(8,128)S(1)}, f32[16,16,128]{2,1,0:T(8,128)}, u32[]{:S(2)}) copy-start(f32[16,16,128]{2,1,0:T(8,128)} %refs_4_.7) | copy-start | bytes 393220
  4.6 0.9 %copy-start.10 = (f32[16,16,128]{2,1,0:T(8,128)S(1)}, f32[16,16,128]{2,1,0:T(8,128)}, u32[]{:S(2)}) copy-start(f32[16,16,128]{2,1,0:T(8,128)} %refs_5_.7) | copy-start | bytes 393220
  6.5 3.8 %collective-permute-start = (f32[8,16,128]{2,1,0:T(8,128)S(1)}, f32[8,16,128]{2,1,0:T(8,128)S(1)}, u32[]{:S(2)}, u32[]{:S(2)}) collective-permute-start(f32[8,16,128]{2,1,0:T(8,128)S(1)} %get-tuple-element.33), channel_id=1, source_target_pairs={{0,1},{1,0},{2,3},{3,2},{4,5},{5,4},{6,7},{7,6},{8,9},{9,8},{10,11... | collective-permute-start | bytes 196616 | tf_op jit(solution)/shard_map/ppermute | solution.py:587
  8.7 1.7 %collective-permute-start.1 = (f32[8,16,128]{2,1,0:T(8,128)S(1)}, f32[8,16,128]{2,1,0:T(8,128)S(1)}, u32[]{:S(2)}, u32[]{:S(2)}) collective-permute-start(f32[8,16,128]{2,1,0:T(8,128)S(1)} %get-tuple-element.34), channel_id=1, source_target_pairs={{1,2},{2,1},{5,6},{6,5},{9,10},{10,9},{13,14},{14,13},{17,18},{18,... | collective-permute-start | bytes 196616 | tf_op jit(solution)/shard_map/ppermute | solution.py:587
  11.0 5.6 %collective-permute-start.2 = (f32[7,4,16,128]{3,2,1,0:T(8,128)S(1)}, f32[7,4,16,128]{3,2,1,0:T(8,128)S(1)}, u32[]{:S(2)}, u32[]{:S(2)}) collective-permute-start(f32[7,4,16,128]{3,2,1,0:T(8,128)S(1)} %get-tuple-element.36), channel_id=1, source_target_pairs={{0,16},{16,0},{1,17},{17,1},{2,18},{18,2},{3,19},{19,3},{4,20},{20... | collective-permute-start | bytes 688136 | tf_op jit(solution)/shard_map/ppermute | solution.py:587
  16.6 11.8 %copy-start.1 = (f32[16,16,128]{2,1,0:T(8,128)S(1)}, f32[16,16,128]{2,1,0:T(8,128)}, u32[]{:S(2)}) copy-start(f32[16,16,128]{2,1,0:T(8,128)} %refs_0_.7) | copy-start | bytes 393220
  16.6 11.8 %copy-start.3 = (f32[16,16,128]{2,1,0:T(8,128)S(1)}, f32[16,16,128]{2,1,0:T(8,128)}, u32[]{:S(2)}) copy-start(f32[16,16,128]{2,1,0:T(8,128)} %refs_1_.7) | copy-start | bytes 393220
  16.6 11.8 %copy-start.5 = (f32[16,16,128]{2,1,0:T(8,128)S(1)}, f32[16,16,128]{2,1,0:T(8,128)}, u32[]{:S(2)}) copy-start(f32[16,16,128]{2,1,0:T(8,128)} %refs_2_.7) | copy-start | bytes 393220
  16.6 11.8 %copy-start.7 = (f32[16,16,128]{2,1,0:T(8,128)S(1)}, f32[16,16,128]{2,1,0:T(8,128)}, u32[]{:S(2)}) copy-start(f32[16,16,128]{2,1,0:T(8,128)} %refs_3_.7) | copy-start | bytes 393220
  16.6 11.8 %copy-start.9 = (f32[16,16,128]{2,1,0:T(8,128)S(1)}, f32[16,16,128]{2,1,0:T(8,128)}, u32[]{:S(2)}) copy-start(f32[16,16,128]{2,1,0:T(8,128)} %refs_4_.7) | copy-start | bytes 393220
  16.6 11.8 %copy-start.11 = (f32[16,16,128]{2,1,0:T(8,128)S(1)}, f32[16,16,128]{2,1,0:T(8,128)}, u32[]{:S(2)}) copy-start(f32[16,16,128]{2,1,0:T(8,128)} %refs_5_.7) | copy-start | bytes 393220
  17.3 5.8 %collective-permute-start.3 = (f32[7,24,4,128]{3,2,1,0:T(4,128)S(1)}, f32[7,24,4,128]{3,2,1,0:T(4,128)S(1)}, u32[]{:S(2)}, u32[]{:S(2)}) collective-permute-start(f32[7,24,4,128]{3,2,1,0:T(4,128)S(1)} %get-tuple-element.37), channel_id=1, source_target_pairs={{0,4},{4,0},{8,12},{12,8},{1,5},{5,1},{9,13},{13,9},{2,6},{6,2},{1... | collective-permute-start | bytes 1032200 | tf_op jit(solution)/shard_map/ppermute | solution.py:587
  19.9 8.6 %collective-permute-start.4 = (f32[7,24,4,128]{3,2,1,0:T(4,128)S(1)}, f32[7,24,4,128]{3,2,1,0:T(4,128)S(1)}, u32[]{:S(2)}, u32[]{:S(2)}) collective-permute-start(f32[7,24,4,128]{3,2,1,0:T(4,128)S(1)} %get-tuple-element.38), channel_id=1, source_target_pairs={{4,8},{8,4},{5,9},{9,5},{6,10},{10,6},{7,11},{11,7},{20,24},{24,20... | collective-permute-start | bytes 1032200 | tf_op jit(solution)/shard_map/ppermute | solution.py:587
  33.2 5.8 %collective-permute-start.5 = (f32[8,8,128]{2,1,0:T(8,128)S(1)}, f32[8,8,128]{2,1,0:T(8,128)S(1)}, u32[]{:S(2)}, u32[]{:S(2)}) collective-permute-start(f32[8,8,128]{2,1,0:T(8,128)S(1)} %get-tuple-element.40), channel_id=1, source_target_pairs={{0,1},{1,0},{2,3},{3,2},{4,5},{5,4},{6,7},{7,6},{8,9},{9,8},{10,11... | collective-permute-start | bytes 98312 | tf_op jit(solution)/shard_map/ppermute | solution.py:587
  37.7 1.3 %collective-permute-start.6 = (f32[8,8,128]{2,1,0:T(8,128)S(1)}, f32[8,8,128]{2,1,0:T(8,128)S(1)}, u32[]{:S(2)}, u32[]{:S(2)}) collective-permute-start(f32[8,8,128]{2,1,0:T(8,128)S(1)} %get-tuple-element.41), channel_id=1, source_target_pairs={{1,2},{2,1},{5,6},{6,5},{9,10},{10,9},{13,14},{14,13},{17,18},{18,... | collective-permute-start | bytes 98312 | tf_op jit(solution)/shard_map/ppermute | solution.py:587
  39.8 3.4 %collective-permute-start.7 = (f32[5,4,8,128]{3,2,1,0:T(8,128)S(1)}, f32[5,4,8,128]{3,2,1,0:T(8,128)S(1)}, u32[]{:S(2)}, u32[]{:S(2)}) collective-permute-start(f32[5,4,8,128]{3,2,1,0:T(8,128)S(1)} %get-tuple-element.43), channel_id=1, source_target_pairs={{0,16},{16,0},{1,17},{17,1},{2,18},{18,2},{3,19},{19,3},{4,20},{20... | collective-permute-start | bytes 245768 | tf_op jit(solution)/shard_map/ppermute | solution.py:587
  43.7 5.2 %collective-permute-start.8 = (f32[5,16,4,128]{3,2,1,0:T(4,128)S(1)}, f32[5,16,4,128]{3,2,1,0:T(4,128)S(1)}, u32[]{:S(2)}, u32[]{:S(2)}) collective-permute-start(f32[5,16,4,128]{3,2,1,0:T(4,128)S(1)} %get-tuple-element.44), channel_id=1, source_target_pairs={{0,4},{4,0},{8,12},{12,8},{1,5},{5,1},{9,13},{13,9},{2,6},{6,2},{1... | collective-permute-start | bytes 491528 | tf_op jit(solution)/shard_map/ppermute | solution.py:587
  43.8 8.1 %collective-permute-start.9 = (f32[5,16,4,128]{3,2,1,0:T(4,128)S(1)}, f32[5,16,4,128]{3,2,1,0:T(4,128)S(1)}, u32[]{:S(2)}, u32[]{:S(2)}) collective-permute-start(f32[5,16,4,128]{3,2,1,0:T(4,128)S(1)} %get-tuple-element.45), channel_id=1, source_target_pairs={{4,8},{8,4},{5,9},{9,5},{6,10},{10,6},{7,11},{11,7},{20,24},{24,20... | collective-permute-start | bytes 491528 | tf_op jit(solution)/shard_map/ppermute | solution.py:587

commit v4 on v3

--- a/solution.py
+++ b/solution.py
@@ -17,6 +17,9 @@
 HALO = 4
 NEAR = 4
 LANES = 128
+PLACE = (0, 11, 21, 31, 41, 51)
+DEPTH = (11, 10, 10, 10, 10, 11)
+SIDE = LANES // 2
 
 VM = pl.BlockSpec(memory_space=pltpu.VMEM)
 SM = pl.BlockSpec(memory_space=pltpu.SMEM)
@@ -122,11 +125,11 @@
     tail = head
     for a, ref in enumerate(ins):
         for g in range(2):
-            block = ref[g * half:(g + 1) * half]
-            at = 64 * g + HALO * a
-            mask = (lane >= at) & (lane < at + HALO)
-            head = jnp.where(mask, turn(block, at, 2), head)
-            tail = jnp.where(mask, turn(block, at + HALO, 2), tail)
+            values = ref[g * half:(g + 1) * half]
+            at = SIDE * g + PLACE[a]
+            mask = (lane >= at) & (lane < at + DEPTH[a])
+            head = jnp.where(mask, turn(values, at, 2), head)
+            tail = jnp.where(mask, turn(values, at + DEPTH[a], 2), tail)
     first[...] = pick(odd, head, tail)
     second[...] = pick(odd, tail, head)
 
@@ -138,8 +141,8 @@
     half = sx // 2
     below, above = neighbours(counts[2], where_ref[2] % 2, one_ref[...], two_ref[...])
     lane = lane_of(below.shape)
-    zpack[:half] = jnp.where(lane < 64, above, turn(below, 64, 2))
-    zpack[half:] = jnp.where(lane < 64, turn(above, 64, 2), below)
+    zpack[:half] = jnp.where(lane < SIDE, above, turn(below, SIDE, 2))
+    zpack[half:] = jnp.where(lane < SIDE, turn(above, SIDE, 2), below)
     odd = where_ref[0] % 2
     for k, send in enumerate(sends):
         start = (1 - odd if k == 0 else odd) * (sx - HALO)
@@ -201,17 +204,18 @@
 
 
 def down_kernel(counts, where_ref, *refs):
-    ins = refs[:7]
+    ins, refs = refs[:7], refs[7:]
     n_x = 1 if counts[0] == 2 else 2
-    halos_x = refs[7:7 + n_x]
-    one_y, two_y = refs[7 + n_x:9 + n_x]
-    own1, first1, second1, coarse2, kept_m, kept_h, weight_m, weight_h = refs[9 + n_x:17 + n_x]
-    faces_out, scratch = refs[17 + n_x:25 + n_x], refs[25 + n_x:]
+    halos_x = refs[:n_x]
+    one_y, two_y, own1, coarse2 = refs[n_x:4 + n_x]
+    sends, refs = refs[4 + n_x:4 + 2 * n_x], refs[4 + 2 * n_x:]
+    kept_m, kept_h, weight_m, weight_h = refs[:4]
+    faces_out, scratch = refs[4:12], refs[12:]
     mains, halves = scratch[:7], scratch[7:13]
-    half_m, half_h, diag, sums, left = scratch[13:]
+    half_m, half_h, diag_m, diag_h, sums, left, pairing = scratch[13:]
     sx, sy, sz = ins[0].shape
     ex, ey = sx + 2 * HALO, sy + 2 * HALO
-    odd_x, odd_y, odd_z = where_ref[0] % 2, where_ref[1] % 2, where_ref[2] % 2
+    odd_x, odd_y = where_ref[0] % 2, where_ref[1] % 2
 
     for a in range(7):
         to = mains[a]
@@ -226,15 +230,17 @@
     def unpack(x):
         packed = mains[6][x]
         for a in range(6):
-            right = turn(packed, -HALO * a, 1)
-            other_side = turn(packed, 64 - HALO - HALO * a, 1)
+            at, depth = PLACE[a], DEPTH[a]
+            right = turn(packed, -at, 1)
+            other_side = turn(packed, SIDE - depth - at, 1)
             halves[a][x] = jnp.where(
-                lane < HALO, right, jnp.where(lane >= LANES - HALO, other_side, 0.0)
+                lane < depth, right, jnp.where(lane >= LANES - depth, other_side, 0.0)
             )
 
     each(0, ex, 4, unpack)
     field, rhs, alpha, bx, by, bz = zip(mains[:6], halves)
     halfway, weight, kept = (half_m, half_h), (weight_m, weight_h), (kept_m, kept_h)
+    diag = (diag_m, diag_h)
 
     def first_sweep(x):
         faces = [half[x] for half in bz]
@@ -245,8 +251,7 @@
             mass = WEIGHT * alpha[k][x]
             d = mass + bx[k][x] + bx[k][x - 1] + face + turn(face, 1, 0) + faces[k] + downs[k]
             w = relaxer(mass, d)
-            if k == 0:
-                diag[x] = d
+            diag[k][x] = d
             weight[k][x] = w
             halfway[k][x] = KEEP * centre[k] + w * (rhs[k][x] + near[k])
 
@@ -261,14 +266,15 @@
 
     def residual(x):
         centre, near = pull_slab(kept, bx, by, bz, x, lane)
-        half_m[x] = rhs[0][x] - diag[x] * centre[0] + near[0]
+        for k in range(2):
+            halfway[k][x] = rhs[k][x] - diag[k][x] * centre[k] + near[k]
 
     each(HALO, ex - HALO, 4, residual)
     for n, source in enumerate((rhs, bx, by, bz)):
         for k in range(2):
             faces_out[2 * n + k][...] = source[k][...]
 
-    x1, y1, z1 = sx // 2, sy // 2, sz // 2
+    x1, y1 = sx // 2, sy // 2
 
     def rows_of(source, x, firsts, seconds):
         total = None
@@ -279,47 +285,37 @@
         return total
 
     both, last = (0, 1), (1,)
-    for i in range(x1):
-        x = HALO + 2 * i
-        sums[0, i] = rows_of(half_m, x, both, both)
-        sums[1, i] = rows_of(alpha[0], x, both, both)
-        sums[2, i] = rows_of(bx[0], x, last, both)
-        sums[3, i] = rows_of(by[0], x, both, last)
-        left[...] = turn(by[0][x] + by[0][x + 1], 1, 0)
-        sums[4, i] = left[pl.ds(0, y1, stride=2), :]
-        sums[5, i] = rows_of(bz[0], x, both, both)
-    sums[6, 0] = rows_of(bx[0], HALO - 2, last, both)
-    edge_z = [rows_of(bz[1], HALO + 2 * i, both, both)[None] for i in range(x1)]
-    edge_z = 0.0625 * jnp.concatenate(edge_z, axis=0)
-    pairs = pair_table(LANES, LANES, False)
-    odds = pair_table(LANES, LANES, True)
+    for k in range(2):
+        lanes = slice(k * LANES, (k + 1) * LANES)
+        for i in range(x1):
+            x = HALO + 2 * i
+            sums[0, i, :, lanes] = rows_of(halfway[k], x, both, both)
+            sums[1, i, :, lanes] = rows_of(alpha[k], x, both, both)
+            sums[2, i, :, lanes] = rows_of(bx[k], x, last, both)
+            sums[3, i, :, lanes] = rows_of(by[k], x, both, last)
+            left[...] = turn(by[k][x] + by[k][x + 1], 1, 0)
+            sums[4, i, :, lanes] = left[pl.ds(0, y1, stride=2), :]
+            sums[5, i, :, lanes] = rows_of(bz[k], x, both, both)
+        sums[6, 0, :, lanes] = rows_of(bx[k], HALO - 2, last, both)
+    pairs = pair_table(2 * LANES, LANES, False)
+    odds = pair_table(2 * LANES, LANES, True)
 
     def to_level1(first, count, table, factor):
-        flat = sums[first:first + count].reshape(count * x1 * y1, LANES)
+        flat = sums[first:first + count].reshape(count * x1 * y1, 2 * LANES)
         return factor * times_table(flat, table).reshape(count, x1, y1, LANES)
 
     paired = to_level1(0, 5, pairs, 0.0625)
     rhs1, mass1 = 2.0 * paired[0], (2.0 * WEIGHT) * paired[1]
     faces1 = (paired[2], paired[3], to_level1(5, 1, odds, 0.0625)[0])
     edge_x = 0.0625 * times_table(sums[6, 0], pairs)[None]
-    lane1 = lane_of((x1, y1, LANES))
     diag1 = mass1 + faces1[0] + jnp.concatenate([edge_x, faces1[0][:-1]], axis=0)
-    diag1 = diag1 + faces1[1] + paired[4]
-    diag1 = diag1 + faces1[2] + jnp.where(lane1 == 0, turn(edge_z, 1, 2), turn(faces1[2], 1, 2))
-    inside = lane1 < z1
-    weight1 = jnp.where(inside, RELAX / jnp.where(inside, diag1, 1.0), 0.0)
-
-    head = jnp.zeros((x1, y1, LANES), F32)
-    tail = head
+    diag1 = diag1 + faces1[1] + paired[4] + faces1[2] + turn(faces1[2], 1, 2)
+    weight1 = relaxer(mass1, diag1)
     for n, values in enumerate((rhs1, weight1) + faces1):
-        block = jnp.where(inside, values, 0.0)
-        own1[n] = block
-        at = NEAR * n
-        mask = (lane1 >= at) & (lane1 < at + NEAR)
-        head = jnp.where(mask, turn(block, at, 2), head)
-        tail = jnp.where(mask, turn(block, at + NEAR - z1, 2), tail)
-    first1[...] = pick(odd_z, head, tail)
-    second1[...] = pick(odd_z, tail, head)
+        own1[n] = values
+        head, tail = values[:NEAR], values[x1 - NEAR:]
+        for k, send in enumerate(sends):
+            send[n] = pick(odd_x, head, tail) if k == 0 else pick(odd_x, tail, head)
 
     parts = (
         (mass1, False, False, False, 0.125),
@@ -328,8 +324,8 @@
         (faces1[2], False, False, True, 0.0625),
     )
     for n, (values, *odd_axes, factor) in enumerate(parts):
-        sums[n] = values
-        coarse2[n] = level2_rows(sums.at[n], odd_axes, factor, x1 // 2, y1 // 2, z1 // 2)
+        pairing[n] = values
+        coarse2[n] = level2_rows(pairing.at[n], odd_axes, factor, x1 // 2, y1 // 2, sz // 4)
 
 
 def level2_rows(source, odd_axes, factor, x2, y2, z2):
@@ -349,23 +345,6 @@
         mask = (lane >= i * z2) & (lane < (i + 1) * z2)
         packed = jnp.where(mask, turn(flat[i * y2:(i + 1) * y2], i * z2, 1), packed)
     return packed
-
-
-def near_x_kernel(counts, where_ref, own_ref, one_ref, two_ref, ring, *sends):
-    n, bx, by, _ = own_ref.shape
-    below, above = neighbours(counts[2], where_ref[2] % 2, one_ref[...], two_ref[...])
-    lane = lane_of(below.shape)
-    for a in range(n):
-        right = turn(above, LANES // 2 - NEAR * a, 2)
-        left = turn(below, LANES - NEAR - NEAR * a, 2)
-        block = jnp.where(lane < LANES // 2, own_ref[a], 0.0)
-        block = jnp.where((lane >= LANES // 2) & (lane < LANES // 2 + NEAR), right, block)
-        ring[a] = jnp.where(lane >= LANES - NEAR, left, block)
-    odd = where_ref[0] % 2
-    for k, send in enumerate(sends):
-        start = (1 - odd if k == 0 else odd) * (bx - NEAR)
-        for a in range(n):
-            send[a] = ring[a, pl.ds(start, NEAR)]
 
 
 def near_y_kernel(counts, where_ref, ring, *refs):
@@ -581,11 +560,11 @@
 def swaps(axis, sends):
     count = lax.axis_size(axis)
     got = []
-    for k, block in enumerate(sends):
+    for k, block in reversed(list(enumerate(sends))):
         pairs = [(i, i + 1) for i in range(k, count - 1, 2)]
         pairs = [pair for low, high in pairs for pair in ((low, high), (high, low))]
         got.append(lax.ppermute(block, axis, pairs))
-    return got
+    return got[::-1]
 
 
 def local(initial, right_side, alpha, beta_x, beta_y, beta_z):
@@ -599,7 +578,7 @@
     ex, ey = sx + 2 * HALO, sy + 2 * HALO
     fine = (ex, ey, LANES)
 
-    sends = run(pack_z_kernel, [(sx // 2, sy, LANES)] * 2, where, ins)
+    sends = run(pack_z_kernel, [(sx // 2, sy, LANES)] * 2, where, ins, grant=60)
     got = swaps("gz", sends)
     zpack, *sends = run(
         functools.partial(face_x_kernel, counts),
@@ -617,22 +596,16 @@
     )
     got_y = swaps("gy", sends)
     x1, y1 = sx // 2, sy // 2
-    own1, first1, second1, coarse2, *fine_arrays = run(
+    ring, coarse2, *outs = run(
         functools.partial(down_kernel, counts),
-        [(5, x1, y1, LANES), (x1, y1, LANES), (x1, y1, LANES), (4, y1 // 2, LANES)] + [fine] * 12,
+        [(5, x1, y1, LANES), (4, y1 // 2, LANES)] + [(5, NEAR, y1, LANES)] * n_x + [fine] * 12,
         where,
         ins + tuple(got_x) + tuple(got_y),
-        [fine] * 16 + [(7, x1, y1, LANES), (ey, LANES)],
+        [fine] * 17 + [(7, x1, y1, 2 * LANES), (ey, LANES), (4, x1, y1, LANES)],
         24,
     )
-
-    got = swaps("gz", (first1, second1))
-    ring, *sends = run(
-        functools.partial(near_x_kernel, counts),
-        [(5, x1, y1, LANES)] + [(5, NEAR, y1, LANES)] * n_x,
-        where,
-        (own1,) + tuple(got),
-    )
+    sends, fine_arrays = outs[:n_x], outs[n_x:]
+
     near_x = swaps("gx", sends)
     sends = run(
         functools.partial(near_y_kernel, counts),

time: 81.5 us -> 71.6 us (0.88)
  starting transfers between devices: 21.6 us -> 15.8 us
  local copies, waits for them, and re-layouts: 5.45 us -> 0.03 us
  Pallas kernels: 18.5 us -> 19.4 us
    ppermute x10 -> x8, starting transfers between devices: 21.6 us -> 15.8 us  [swaps(): got.append(lax.ppermute(block, axis, pairs))]
    unnamed x24 -> x14, local copies, waits for them, and re-layouts: 5.45 us -> 0.03 us
    pallas_call x8 -> x7, Pallas kernels: 18.5 us -> 19.4 us  [run(): pl.pallas_call(kernel, out_shape=tuple((jax.ShapeDtypeStruct(shape, F32)...]
    ppermute x10 -> x8, waiting for transfers between devices: 16.2 us -> 15.6 us  [swaps(): got.append(lax.ppermute(block, axis, pairs))]
  transfers between devices with their start and end apart: 10 -> 8, of which waited for: 6 -> 5; matrix products, arithmetic and copies ran while one was open for 0% -> 0% of each run, Pallas kernels for 0% -> 0%
where the time goes in v4:
time: 71.6 us; the launch traced here: 71.4 us
  blocking collectives  19.8 us (28%)
  Pallas kernels  19.4 us (27%)
  starting transfers between devices  15.8 us (22%)
  waiting for transfers between devices  15.6 us (22%)
    all_to_all x1, blocking collectives, local(): gathered = lax.all_to_all(copies, axes, 0, 0, tiled=True)  19.8 us
    pallas_call x7, Pallas kernels, run(): pl.pallas_call(kernel, out_shape=tuple((jax.ShapeDtypeStruct(shape, F32)...  19.4 us
    ppermute x8, starting transfers between devices, swaps(): got.append(lax.ppermute(block, axis, pairs))  15.8 us
    ppermute x8, waiting for transfers between devices, swaps(): got.append(lax.ppermute(block, axis, pairs))  15.6 us
  transfers between devices with their start and end apart: 8, of which 5 were waited for; matrix products, arithmetic and copies ran while one was open for 0% of the time, Pallas kernels for 0%

profile of v4, /device:TPU:1, one launch (start us, length us, event | category | flops | bytes accessed | tf_op | source)
XLA Modules:
  0.0 71.4 jit_solution(2030396300343356323)
XLA Ops:
  0.0 0.6 pad_add_fusion.where_ref
  0.6 0.0 copy-start.4
  0.6 0.0 copy-start.5
  0.6 2.4 %shard_map.64 = (f32[8,16,128]{2,1,0:T(8,128)}, f32[8,16,128]{2,1,0:T(8,128)}) custom-call(s32[3]{0:T(128)} %pad_add_fusion.where_ref, f32[16,16,128]{2,1,0:T(8,128)} %refs_0_.7, f32[16,16,128]{2,1,0:T(8,128)} %refs_1_.7, f32[16,16,128]{2,1,0:T(8,128)} %refs_2_.7, f32[16,16,128]{2,1,0:T(8,128)} %refs_3_.7, f32[16,16,128]{2,1,0:T(8,128)} %refs_4_.7, ...), custom_call_target="tpu_custom_call" | custom-call | tf_op jit(solution)/shard_map/pallas_call | solution.py:550
  3.0 2.1 %collective-permute-start = (f32[8,16,128]{2,1,0:T(8,128)}, f32[8,16,128]{2,1,0:T(8,128)S(1)}, u32[]{:S(2)}, u32[]{:S(2)}) collective-permute-start(f32[8,16,128]{2,1,0:T(8,128)} %get-tuple-element.30), channel_id=1, source_target_pairs={{0,1},{1,0},{2,3},{3,2},{4,5},{5,4},{6,7},{7,6},{8,9},{9,8},{10,11... | collective-permute-start | bytes 196616 | tf_op jit(solution)/shard_map/ppermute | solution.py:566
  5.1 0.7 collective-permute-start.1
  5.8 1.2 %collective-permute-done.refs_6_ = f32[8,16,128]{2,1,0:T(8,128)S(1)} collective-permute-done((f32[8,16,128]{2,1,0:T(8,128)}, f32[8,16,128]{2,1,0:T(8,128)S(1)}, u32[]{:S(2)}, u32[]{:S(2)}) %collective-permute-start) | collective-permute-done | bytes 65568 | tf_op jit(solution)/shard_map/ppermute | solution.py:566
  7.0 0.0 collective-permute-done.1.refs_7_
  7.0 0.0 copy-done
  7.0 0.0 copy-done.1
  7.0 0.0 copy-done.2
  7.0 0.0 copy-done.3
  7.0 0.0 copy-done.4
  7.1 0.6 shard_map.65
  7.7 1.4 %collective-permute-start.2 = (f32[7,4,16,128]{3,2,1,0:T(8,128)S(1)}, f32[7,4,16,128]{3,2,1,0:T(8,128)S(1)}, u32[]{:S(2)}, u32[]{:S(2)}) collective-permute-start(f32[7,4,16,128]{3,2,1,0:T(8,128)S(1)} %get-tuple-element.33), channel_id=1, source_target_pairs={{0,16},{16,0},{1,17},{17,1},{2,18},{18,2},{3,19},{19,3},{4,20},{20... | collective-permute-start | bytes 688136 | tf_op jit(solution)/shard_map/ppermute | solution.py:566
  9.2 4.2 %collective-permute-done.2.refs_7_ = f32[7,4,16,128]{3,2,1,0:T(8,128)S(1)} collective-permute-done((f32[7,4,16,128]{3,2,1,0:T(8,128)S(1)}, f32[7,4,16,128]{3,2,1,0:T(8,128)S(1)}, u32[]{:S(2)}, u32[]{:S(2)}) %collective-permute-start.2) | collective-permute-done | bytes 229408 | tf_op jit(solution)/shard_map/ppermute | solution.py:566
  13.3 0.7 shard_map.66
  14.0 2.5 %collective-permute-start.3 = (f32[7,24,4,128]{3,2,1,0:T(4,128)S(1)}, f32[7,24,4,128]{3,2,1,0:T(4,128)S(1)}, u32[]{:S(2)}, u32[]{:S(2)}) collective-permute-start(f32[7,24,4,128]{3,2,1,0:T(4,128)S(1)} %get-tuple-element.34), channel_id=1, source_target_pairs={{0,4},{4,0},{8,12},{12,8},{1,5},{5,1},{9,13},{13,9},{2,6},{6,2},{1... | collective-permute-start | bytes 1032200 | tf_op jit(solution)/shard_map/ppermute | solution.py:566
  16.5 3.2 %collective-permute-start.4 = (f32[7,24,4,128]{3,2,1,0:T(4,128)S(1)}, f32[7,24,4,128]{3,2,1,0:T(4,128)S(1)}, u32[]{:S(2)}, u32[]{:S(2)}) collective-permute-start(f32[7,24,4,128]{3,2,1,0:T(4,128)S(1)} %get-tuple-element.35), channel_id=1, source_target_pairs={{4,8},{8,4},{5,9},{9,5},{6,10},{10,6},{7,11},{11,7},{20,24},{24,20... | collective-permute-start | bytes 1032200 | tf_op jit(solution)/shard_map/ppermute | solution.py:566
  19.8 0.0 collective-permute-done.3.refs_8_
  19.8 5.3 %collective-permute-done.4.refs_9_ = f32[7,24,4,128]{3,2,1,0:T(4,128)S(1)} collective-permute-done((f32[7,24,4,128]{3,2,1,0:T(4,128)S(1)}, f32[7,24,4,128]{3,2,1,0:T(4,128)S(1)}, u32[]{:S(2)}, u32[]{:S(2)}) %collective-permute-start.4) | collective-permute-done | bytes 344096 | tf_op jit(solution)/shard_map/ppermute | solution.py:566
  25.1 5.0 %shard_map.67 = (f32[5,8,8,128]{3,2,1,0:T(8,128)S(1)}, f32[4,4,128]{2,1,0:T(4,128)S(1)}, f32[5,4,8,128]{3,2,1,0:T(8,128)S(1)}, f32[24,24,128]{2,1,0:T(8,128)S(1)...) custom-call(s32[3]{0:T(128)S(1)} %copy-done.6, ...), custom_call_target="tpu_custom_call" | custom-call | tf_op jit(solution)/shard_map/pallas_call | solution.py:550
  30.1 1.4 %collective-permute-start.5 = (f32[5,4,8,128]{3,2,1,0:T(8,128)S(1)}, f32[5,4,8,128]{3,2,1,0:T(8,128)S(1)}, u32[]{:S(2)}, u32[]{:S(2)}) collective-permute-start(f32[5,4,8,128]{3,2,1,0:T(8,128)S(1)} %get-tuple-element.37), channel_id=1, source_target_pairs={{0,16},{16,0},{1,17},{17,1},{2,18},{18,2},{3,19},{19,3},{4,20},{20... | collective-permute-start | bytes 245768 | tf_op jit(solution)/shard_map/ppermute | solution.py:566
  31.5 1.9 %collective-permute-done.5.refs_0_ = f32[5,4,8,128]{3,2,1,0:T(8,128)S(1)} collective-permute-done((f32[5,4,8,128]{3,2,1,0:T(8,128)S(1)}, f32[5,4,8,128]{3,2,1,0:T(8,128)S(1)}, u32[]{:S(2)}, u32[]{:S(2)}) %collective-permute-start.5) | collective-permute-done | bytes 81952 | tf_op jit(solution)/shard_map/ppermute | solution.py:566
  33.4 0.6 shard_map.68
  34.0 0.1 collective-permute-start.6
  34.1 4.4 %collective-permute-start.7 = (f32[5,16,4,128]{3,2,1,0:T(4,128)S(1)}, f32[5,16,4,128]{3,2,1,0:T(4,128)S(1)}, u32[]{:S(2)}, u32[]{:S(2)}) collective-permute-start(f32[5,16,4,128]{3,2,1,0:T(4,128)S(1)} %get-tuple-element.39), channel_id=1, source_target_pairs={{4,8},{8,4},{5,9},{9,5},{6,10},{10,6},{7,11},{11,7},{20,24},{24,20... | collective-permute-start | bytes 491528 | tf_op jit(solution)/shard_map/ppermute | solution.py:566
  38.4 0.0 collective-permute-done.6.refs_1_
  38.5 3.0 %collective-permute-done.7.refs_2_ = f32[5,16,4,128]{3,2,1,0:T(4,128)S(1)} collective-permute-done((f32[5,16,4,128]{3,2,1,0:T(4,128)S(1)}, f32[5,16,4,128]{3,2,1,0:T(4,128)S(1)}, u32[]{:S(2)}, u32[]{:S(2)}) %collective-permute-start.7) | collective-permute-done | bytes 163872 | tf_op jit(solution)/shard_map/ppermute | solution.py:566
  41.4 1.0 %shard_map.69 = (f32[32,5,4,128]{3,2,1,0:T(4,128)S(1)}, f32[6,16,16,128]{3,2,1,0:T(8,128)S(1)}) custom-call(s32[3]{0:T(128)S(1)} %copy-done.6, f32[5,8,8,128]{3,2,1,0:T(8,128)S(1)} %get-tuple-element.36.ring, f32[5,4,8,128]{3,2,1,0:T(8,128)S(1)} %collective-permute-done.5.refs_0_, f32[5,16,4,128]{3,2,1,0:T(4,128)S(1)} %collective-permute-done.6.refs_1_, ...), custom_call_target="tpu_custom_call" | custom-call | tf_op jit(solution)/shard_map/pallas_call | solution.py:550
  42.4 19.8 %all_to_all.5.gathered = f32[32,5,4,128]{3,2,1,0:T(4,128)S(1)} all-to-all(f32[32,5,4,128]{3,2,1,0:T(4,128)S(1)} %get-tuple-element.41), channel_id=1, replica_groups=mesh['gx'=2,'gy'=4,'gz'=4] {'gx','gy','gz'}, dimensions={0} | all-to-all | bytes 655360 | tf_op jit(solution)/shard_map/all_to_all | solution.py:625
  62.2 9.2 %shard_map.70 = f32[16,16,128]{2,1,0:T(8,128)} custom-call(s32[3]{0:T(128)S(1)} %copy-done.6, f32[32,5,4,128]{3,2,1,0:T(4,128)S(1)} %all_to_all.5.gathered, f32[6,16,16,128]{3,2,1,0:T(8,128)S(1)} %get-tuple-element.42.level1, f32[24,24,128]{2,1,0:T(8,128)S(1)} %get-tuple-element.43.refs_0_, f32[24,24,128]{2,1,0:T(8,128)S(1)} %get-tuple-element.44.refs_1_, ...), custom_call_target="tpu_custom_call" | custom-call | tf_op jit(solution)/shard_map/pallas_call | solution.py:550
  (7 shorter events, 0.0 us)
Async XLA Ops:
  0.6 6.4 %copy-start = (f32[16,16,128]{2,1,0:T(8,128)S(1)}, f32[16,16,128]{2,1,0:T(8,128)}, u32[]{:S(2)}) copy-start(f32[16,16,128]{2,1,0:T(8,128)} %refs_0_.7) | copy-start | bytes 393220
  0.6 6.4 %copy-start.1 = (f32[16,16,128]{2,1,0:T(8,128)S(1)}, f32[16,16,128]{2,1,0:T(8,128)}, u32[]{:S(2)}) copy-start(f32[16,16,128]{2,1,0:T(8,128)} %refs_1_.7) | copy-start | bytes 393220
  0.6 6.4 %copy-start.2 = (f32[16,16,128]{2,1,0:T(8,128)S(1)}, f32[16,16,128]{2,1,0:T(8,128)}, u32[]{:S(2)}) copy-start(f32[16,16,128]{2,1,0:T(8,128)} %refs_2_.7) | copy-start | bytes 393220
  0.6 6.4 %copy-start.3 = (f32[16,16,128]{2,1,0:T(8,128)S(1)}, f32[16,16,128]{2,1,0:T(8,128)}, u32[]{:S(2)}) copy-start(f32[16,16,128]{2,1,0:T(8,128)} %refs_3_.7) | copy-start | bytes 393220
  0.6 6.4 %copy-start.4 = (f32[16,16,128]{2,1,0:T(8,128)S(1)}, f32[16,16,128]{2,1,0:T(8,128)}, u32[]{:S(2)}) copy-start(f32[16,16,128]{2,1,0:T(8,128)} %refs_4_.7) | copy-start | bytes 393220
  0.6 6.4 %copy-start.5 = (f32[16,16,128]{2,1,0:T(8,128)S(1)}, f32[16,16,128]{2,1,0:T(8,128)}, u32[]{:S(2)}) copy-start(f32[16,16,128]{2,1,0:T(8,128)} %refs_5_.7) | copy-start | bytes 393220
  3.0 4.0 %copy-start.6 = (s32[3]{0:T(128)S(1)}, s32[3]{0:T(128)}, u32[]{:S(2)}) copy-start(s32[3]{0:T(128)} %pad_add_fusion.where_ref) | copy-start | bytes 40
  3.0 4.0 %collective-permute-start = (f32[8,16,128]{2,1,0:T(8,128)}, f32[8,16,128]{2,1,0:T(8,128)S(1)}, u32[]{:S(2)}, u32[]{:S(2)}) collective-permute-start(f32[8,16,128]{2,1,0:T(8,128)} %get-tuple-element.30), channel_id=1, source_target_pairs={{0,1},{1,0},{2,3},{3,2},{4,5},{5,4},{6,7},{7,6},{8,9},{9,8},{10,11... | collective-permute-start | bytes 196616 | tf_op jit(solution)/shard_map/ppermute | solution.py:566
  5.1 1.9 %collective-permute-start.1 = (f32[8,16,128]{2,1,0:T(8,128)}, f32[8,16,128]{2,1,0:T(8,128)S(1)}, u32[]{:S(2)}, u32[]{:S(2)}) collective-permute-start(f32[8,16,128]{2,1,0:T(8,128)} %get-tuple-element.31), channel_id=1, source_target_pairs={{1,2},{2,1},{5,6},{6,5},{9,10},{10,9},{13,14},{14,13},{17,18},{18,... | collective-permute-start | bytes 196616 | tf_op jit(solution)/shard_map/ppermute | solution.py:566
  7.7 5.6 %collective-permute-start.2 = (f32[7,4,16,128]{3,2,1,0:T(8,128)S(1)}, f32[7,4,16,128]{3,2,1,0:T(8,128)S(1)}, u32[]{:S(2)}, u32[]{:S(2)}) collective-permute-start(f32[7,4,16,128]{3,2,1,0:T(8,128)S(1)} %get-tuple-element.33), channel_id=1, source_target_pairs={{0,16},{16,0},{1,17},{17,1},{2,18},{18,2},{3,19},{19,3},{4,20},{20... | collective-permute-start | bytes 688136 | tf_op jit(solution)/shard_map/ppermute | solution.py:566
  14.0 5.8 %collective-permute-start.3 = (f32[7,24,4,128]{3,2,1,0:T(4,128)S(1)}, f32[7,24,4,128]{3,2,1,0:T(4,128)S(1)}, u32[]{:S(2)}, u32[]{:S(2)}) collective-permute-start(f32[7,24,4,128]{3,2,1,0:T(4,128)S(1)} %get-tuple-element.34), channel_id=1, source_target_pairs={{0,4},{4,0},{8,12},{12,8},{1,5},{5,1},{9,13},{13,9},{2,6},{6,2},{1... | collective-permute-start | bytes 1032200 | tf_op jit(solution)/shard_map/ppermute | solution.py:566
  16.5 8.6 %collective-permute-start.4 = (f32[7,24,4,128]{3,2,1,0:T(4,128)S(1)}, f32[7,24,4,128]{3,2,1,0:T(4,128)S(1)}, u32[]{:S(2)}, u32[]{:S(2)}) collective-permute-start(f32[7,24,4,128]{3,2,1,0:T(4,128)S(1)} %get-tuple-element.35), channel_id=1, source_target_pairs={{4,8},{8,4},{5,9},{9,5},{6,10},{10,6},{7,11},{11,7},{20,24},{24,20... | collective-permute-start | bytes 1032200 | tf_op jit(solution)/shard_map/ppermute | solution.py:566
  30.1 3.3 %collective-permute-start.5 = (f32[5,4,8,128]{3,2,1,0:T(8,128)S(1)}, f32[5,4,8,128]{3,2,1,0:T(8,128)S(1)}, u32[]{:S(2)}, u32[]{:S(2)}) collective-permute-start(f32[5,4,8,128]{3,2,1,0:T(8,128)S(1)} %get-tuple-element.37), channel_id=1, source_target_pairs={{0,16},{16,0},{1,17},{17,1},{2,18},{18,2},{3,19},{19,3},{4,20},{20... | collective-permute-start | bytes 245768 | tf_op jit(solution)/shard_map/ppermute | solution.py:566
  34.0 4.5 %collective-permute-start.6 = (f32[5,16,4,128]{3,2,1,0:T(4,128)S(1)}, f32[5,16,4,128]{3,2,1,0:T(4,128)S(1)}, u32[]{:S(2)}, u32[]{:S(2)}) collective-permute-start(f32[5,16,4,128]{3,2,1,0:T(4,128)S(1)} %get-tuple-element.38), channel_id=1, source_target_pairs={{0,4},{4,0},{8,12},{12,8},{1,5},{5,1},{9,13},{13,9},{2,6},{6,2},{1... | collective-permute-start | bytes 491528 | tf_op jit(solution)/shard_map/ppermute | solution.py:566
  34.1 7.4 %collective-permute-start.7 = (f32[5,16,4,128]{3,2,1,0:T(4,128)S(1)}, f32[5,16,4,128]{3,2,1,0:T(4,128)S(1)}, u32[]{:S(2)}, u32[]{:S(2)}) collective-permute-start(f32[5,16,4,128]{3,2,1,0:T(4,128)S(1)} %get-tuple-element.39), channel_id=1, source_target_pairs={{4,8},{8,4},{5,9},{9,5},{6,10},{10,6},{7,11},{11,7},{20,24},{24,20... | collective-permute-start | bytes 491528 | tf_op jit(solution)/shard_map/ppermute | solution.py:566

commit v5 on v4

--- a/solution.py
+++ b/solution.py
@@ -20,10 +20,16 @@
 PLACE = (0, 11, 21, 31, 41, 51)
 DEPTH = (11, 10, 10, 10, 10, 11)
 SIDE = LANES // 2
+STRIDE = 256
 
 VM = pl.BlockSpec(memory_space=pltpu.VMEM)
 SM = pl.BlockSpec(memory_space=pltpu.SMEM)
 F32 = jnp.float32
+
+
+def position(where_ref):
+    code = where_ref[0]
+    return code // (STRIDE * STRIDE), code // STRIDE % STRIDE, code % STRIDE
 
 
 def lane_of(shape):
@@ -93,17 +99,17 @@
     return jnp.concatenate([values[1:], jnp.zeros_like(values[:1])], axis=0)
 
 
-def pull(values, faces):
+def pull(values, faces, step=1):
     bx, by, bz = faces
     total = bx * above_x(values) + below_x(bx * values)
-    total = total + (by * turn(values, -1, 1) + turn(by * values, 1, 1))
-    return total + (bz * turn(values, -1, 2) + turn(bz * values, 1, 2))
-
-
-def diagonal(mass, faces, coupled):
+    total = total + (by * turn(values, -step, 1) + turn(by * values, step, 1))
+    return total + (bz * turn(values, -step, 2) + turn(bz * values, step, 2))
+
+
+def diagonal(mass, faces, coupled, step=1):
     bx, by, bz = faces
     _, cy, cz = coupled
-    return mass + bx + below_x(bx) + by + turn(cy, 1, 1) + bz + turn(cz, 1, 2)
+    return mass + bx + below_x(bx) + by + turn(cy, step, 1) + bz + turn(cz, step, 2)
 
 
 def relaxer(mass, diag):
@@ -111,13 +117,13 @@
     return jnp.where(inside, RELAX / jnp.where(inside, diag, 1.0), 0.0)
 
 
-def sweep(values, rhs, weight, faces):
-    return KEEP * values + weight * (rhs + pull(values, faces))
+def sweep(values, rhs, weight, faces, step=1):
+    return KEEP * values + weight * (rhs + pull(values, faces, step))
 
 
 def pack_z_kernel(where_ref, *refs):
     ins, (first, second) = refs[:6], refs[6:]
-    odd = where_ref[2] % 2
+    odd = position(where_ref)[2] % 2
     sx, sy, sz = ins[0].shape
     half = sx // 2
     lane = lane_of((half, sy, LANES))
@@ -139,11 +145,11 @@
     zpack, sends = refs[8], refs[9:]
     sx, sy, sz = ins[0].shape
     half = sx // 2
-    below, above = neighbours(counts[2], where_ref[2] % 2, one_ref[...], two_ref[...])
+    below, above = neighbours(counts[2], position(where_ref)[2] % 2, one_ref[...], two_ref[...])
     lane = lane_of(below.shape)
     zpack[:half] = jnp.where(lane < SIDE, above, turn(below, SIDE, 2))
     zpack[half:] = jnp.where(lane < SIDE, turn(above, SIDE, 2), below)
-    odd = where_ref[0] % 2
+    odd = position(where_ref)[0] % 2
     for k, send in enumerate(sends):
         start = (1 - odd if k == 0 else odd) * (sx - HALO)
         for a, ref in enumerate(tuple(ins) + (zpack,)):
@@ -151,10 +157,9 @@
 
 
 def face_y_kernel(counts, where_ref, *refs):
-    ins, halos, sends = refs[:7], refs[7:-2], refs[-2:]
+    ins, halos, sends = refs[:7], refs[7:-2], refs[:-3:-1]
     sx, sy, sz = ins[0].shape
-    odd_x = where_ref[0] % 2
-    odd = where_ref[1] % 2
+    odd_x, odd = (place % 2 for place in position(where_ref)[:2])
     for a, ref in enumerate(ins):
         below, above = neighbours(counts[0], odd_x, halos[0][a], halos[-1][a])
         for at, block in ((0, below), (HALO, ref[...]), (HALO + sx, above)):
@@ -207,18 +212,20 @@
     ins, refs = refs[:7], refs[7:]
     n_x = 1 if counts[0] == 2 else 2
     halos_x = refs[:n_x]
-    one_y, two_y, own1, coarse2 = refs[n_x:4 + n_x]
+    two_y, one_y, own1, coarse2 = refs[n_x:4 + n_x]
     sends, refs = refs[4 + n_x:4 + 2 * n_x], refs[4 + 2 * n_x:]
     kept_m, kept_h, weight_m, weight_h = refs[:4]
     faces_out, scratch = refs[4:12], refs[12:]
-    mains, halves = scratch[:7], scratch[7:13]
-    half_m, half_h, diag_m, diag_h, sums, left, pairing = scratch[13:]
+    rhs, bx, by, bz = zip(faces_out[::2], faces_out[1::2])
+    field, alpha = scratch[:2], scratch[2:4]
+    packs, half_m, half_h, diag_m, diag_h, sums, left, pairing = scratch[4:]
+    arrays = (field, rhs, alpha, bx, by, bz)
     sx, sy, sz = ins[0].shape
     ex, ey = sx + 2 * HALO, sy + 2 * HALO
-    odd_x, odd_y = where_ref[0] % 2, where_ref[1] % 2
+    odd_x, odd_y = (place % 2 for place in position(where_ref)[:2])
 
     for a in range(7):
-        to = mains[a]
+        to = packs if a == 6 else arrays[a][0]
         below, above = neighbours(counts[0], odd_x, halos_x[0][a], halos_x[-1][a])
         to[:HALO, :sy] = below
         to[HALO:HALO + sx, :sy] = ins[a][...]
@@ -228,17 +235,16 @@
     lane = lane_of((ey, LANES))
 
     def unpack(x):
-        packed = mains[6][x]
+        packed = packs[x]
         for a in range(6):
             at, depth = PLACE[a], DEPTH[a]
             right = turn(packed, -at, 1)
             other_side = turn(packed, SIDE - depth - at, 1)
-            halves[a][x] = jnp.where(
+            arrays[a][1][x] = jnp.where(
                 lane < depth, right, jnp.where(lane >= LANES - depth, other_side, 0.0)
             )
 
     each(0, ex, 4, unpack)
-    field, rhs, alpha, bx, by, bz = zip(mains[:6], halves)
     halfway, weight, kept = (half_m, half_h), (weight_m, weight_h), (kept_m, kept_h)
     diag = (diag_m, diag_h)
 
@@ -270,9 +276,6 @@
             halfway[k][x] = rhs[k][x] - diag[k][x] * centre[k] + near[k]
 
     each(HALO, ex - HALO, 4, residual)
-    for n, source in enumerate((rhs, bx, by, bz)):
-        for k in range(2):
-            faces_out[2 * n + k][...] = source[k][...]
 
     x1, y1 = sx // 2, sy // 2
 
@@ -348,9 +351,9 @@
 
 
 def near_y_kernel(counts, where_ref, ring, *refs):
-    halos, sends = refs[:-2], refs[-2:]
+    halos, sends = refs[:-2], refs[:-3:-1]
     n, bx, by, _ = ring.shape
-    odd_x, odd = where_ref[0] % 2, where_ref[1] % 2
+    odd_x, odd = (place % 2 for place in position(where_ref)[:2])
     for a in range(n):
         below, above = neighbours(counts[0], odd_x, halos[0][a], halos[-1][a])
         block = jnp.concatenate([below, ring[a], above], axis=0)
@@ -362,9 +365,9 @@
 def near_kernel(counts, devices, where_ref, ring, *refs):
     n_x = 1 if counts[0] == 2 else 2
     halos_x = refs[:n_x]
-    one_y, two_y, coarse2, copies, level1, left = refs[n_x:]
+    two_y, one_y, coarse2, copies, level1, left = refs[n_x:]
     n, bx1, by1, _ = ring.shape
-    odd_x, odd_y = where_ref[0] % 2, where_ref[1] % 2
+    odd_x, odd_y = (place % 2 for place in position(where_ref)[:2])
     whole = []
     for a in range(n):
         below, above = neighbours(counts[0], odd_x, halos_x[0][a], halos_x[-1][a])
@@ -389,70 +392,62 @@
             copies[d, a + 1] = coarse2[a]
 
 
-def halve(values, factor, odd_axis):
-    x, y, z = values.shape
-    if odd_axis == 0:
-        values = jnp.concatenate([values[2 * i + 1:2 * i + 2] for i in range(x // 2)], axis=0)
-    else:
-        values = jnp.concatenate(
-            [values[2 * i:2 * i + 1] + values[2 * i + 1:2 * i + 2] for i in range(x // 2)], axis=0
+def halve(values, odd_axis, step):
+    half = values.shape[0] // 2
+    even = [values[2 * i:2 * i + 1] for i in range(half)]
+    odd = [values[2 * i + 1:2 * i + 2] for i in range(half)]
+    if odd_axis != 0:
+        odd = [a + b for a, b in zip(even, odd)]
+    values = jnp.concatenate(odd, axis=0)
+    for axis in (1, 2):
+        next_one = turn(values, -step, axis)
+        values = next_one if odd_axis == axis else values + next_one
+    return values
+
+
+def double(values, step):
+    values = values + turn(values, step, 1)
+    values = values + turn(values, step, 2)
+    return jnp.concatenate([values[i // 2:i // 2 + 1] for i in range(2 * values.shape[0])], axis=0)
+
+
+def coarse_levels(mass, faces, y, z):
+    levels = []
+    for level in range(2, LEVELS):
+        step = 2 ** (level - 2)
+        bx, by, bz = faces
+        row = lax.broadcasted_iota(jnp.int32, by.shape, 1)
+        lane = lane_of(bz.shape)
+        coupled = (
+            bx,
+            jnp.where(row == (y - 1) * step, 0.0, by),
+            jnp.where(lane == (z - 1) * step, 0.0, bz),
         )
-    to_y = max(8, y // 2)
-    to_z = max(LANES, z // 2)
-    flat = values.reshape(x // 2 * y, z)
-    flat = times_table(flat, pair_table(z, to_z, odd_axis == 2))
-    row = iota2((to_y, y), 0)
-    col = iota2((to_y, y), 1)
-    table = (col == 2 * row + 1) if odd_axis == 1 else (col // 2 == row)
-    table = table.astype(F32)
-    blocks = [table_times(table, flat[i * y:(i + 1) * y])[None] for i in range(x // 2)]
-    return factor * jnp.concatenate(blocks, axis=0)
-
-
-def double(values, shape):
-    x, y, z = values.shape
-    to_x, to_y, to_z = shape
-    row = iota2((to_y, y), 0)
-    col = iota2((to_y, y), 1)
-    table_y = (row // 2 == col).astype(F32)
-    row = iota2((z, to_z), 0)
-    col = iota2((z, to_z), 1)
-    table_z = (col // 2 == row).astype(F32)
-    blocks = [table_times(table_y, values[i])[None] for i in range(x)]
-    flat = jnp.concatenate(blocks, axis=0).reshape(x * to_y, z)
-    flat = times_table(flat, table_z).reshape(x, to_y, to_z)
-    return jnp.concatenate([flat[i // 2:i // 2 + 1] for i in range(to_x)], axis=0)
-
-
-def coupled_faces(faces, y, z):
-    bx, by, bz = faces
-    row = lax.broadcasted_iota(jnp.int32, by.shape, 1)
-    return bx, jnp.where(row == y - 1, 0.0, by), jnp.where(lane_of(bz.shape) == z - 1, 0.0, bz)
-
-
-def coarse_cycle(level, rhs, mass, faces, y, z):
-    coupled = coupled_faces(faces, y, z)
-    diag = diagonal(mass, faces, coupled)
-    weight = relaxer(mass, diag)
+        mass = jnp.where((row % step == 0) & (lane % step == 0), mass, 0.0)
+        diag = diagonal(mass, faces, coupled, step)
+        levels.append((diag, relaxer(mass, diag), coupled))
+        if level < LEVELS - 1:
+            faces = tuple(0.0625 * halve(face, axis, step) for axis, face in enumerate(faces))
+            mass = 0.125 * halve(mass, -1, step)
+            y, z = y // 2, z // 2
+    return levels
+
+
+def coarse_cycle(level, rhs, levels):
+    step = 2 ** (level - 2)
+    diag, weight, faces = levels[level - 2]
     field = weight * rhs
     if level == LEVELS - 1:
         for _ in range(BOTTOM - 1):
-            field = sweep(field, rhs, weight, coupled)
+            field = sweep(field, rhs, weight, faces, step)
         return field
     for _ in range(SWEEPS - 1):
-        field = sweep(field, rhs, weight, coupled)
-    remain = rhs - diag * field + pull(field, coupled)
-    correction = coarse_cycle(
-        level + 1,
-        halve(remain, 0.125, -1),
-        halve(mass, 0.125, -1),
-        tuple(halve(face, 0.0625, axis) for axis, face in enumerate(faces)),
-        y // 2,
-        z // 2,
-    )
-    field = field + double(correction, field.shape)
+        field = sweep(field, rhs, weight, faces, step)
+    remain = rhs - diag * field + pull(field, faces, step)
+    correction = coarse_cycle(level + 1, 0.125 * halve(remain, -1, step), levels)
+    field = field + double(correction, step)
     for _ in range(SWEEPS):
-        field = sweep(field, rhs, weight, coupled)
+        field = sweep(field, rhs, weight, faces, step)
     return field
 
 
@@ -460,6 +455,7 @@
     kept, weight, rhs, bx, by, bz = zip(refs[0:12:2], refs[1:12:2])
     out, whole, second, spread_m, spread_h, field_m, field_h, half_m, half_h = refs[12:]
     gx, gy, gz = counts
+    at_x, at_y, at_z = position(where_ref)
     sx, sy, sz = out.shape
     x1, y1 = sx // 2, sy // 2
     x2, y2, z2 = x1 // 2, y1 // 2, sz // 4
@@ -481,9 +477,8 @@
                         whole[
                             a, i * x2 + x, j * y2:(j + 1) * y2, part * LANES:(part + 1) * LANES
                         ] = total
-    correction = coarse_cycle(
-        2, whole[0], whole[1], (whole[2], whole[3], whole[4]), gy * y2, gz * z2
-    )
+    levels = coarse_levels(whole[1], (whole[2], whole[3], whole[4]), gy * y2, gz * z2)
+    correction = coarse_cycle(2, whole[0], levels)
 
     wide = gx * x2
     half = NEAR // 2
@@ -491,16 +486,16 @@
     second[:half] = jnp.zeros((half,) + correction.shape[1:], F32)
     second[half:half + wide] = correction
     second[half + wide:] = jnp.zeros((half,) + correction.shape[1:], F32)
-    window = second[pl.ds(where_ref[0] * x2, x2 + NEAR)]
+    window = second[pl.ds(at_x * x2, x2 + NEAR)]
     rows = correction.shape[1]
     row = iota2((ey1, rows), 0)
     col = iota2((ey1, rows), 1)
     place = jnp.where(row < y1 + NEAR, row, row - ey1)
-    table_y = (col == where_ref[1] * y2 + lax.shift_right_arithmetic(place, 1)).astype(F32)
+    table_y = (col == at_y * y2 + lax.shift_right_arithmetic(place, 1)).astype(F32)
     row = iota2((columns, LANES), 0)
     col = iota2((columns, LANES), 1)
     place = jnp.where(col < LANES * 3 // 4, col, col - LANES)
-    table_z = (row == where_ref[2] * z2 + lax.shift_right_arithmetic(place, 1)).astype(F32)
+    table_z = (row == at_z * z2 + lax.shift_right_arithmetic(place, 1)).astype(F32)
     flat = times_table(window.reshape((x2 + NEAR) * rows, columns), table_z)
     blocks = [table_times(table_y, flat[i * rows:(i + 1) * rows])[None] for i in range(x2 + NEAR)]
     lifted = jnp.concatenate([blocks[i // 2] for i in range(ex1)], axis=0)
@@ -571,7 +566,8 @@
     axes = ("gx", "gy", "gz")
     counts = tuple(lax.axis_size(axis) for axis in axes)
     devices = counts[0] * counts[1] * counts[2]
-    where = jnp.stack([lax.axis_index(axis) for axis in axes]).astype(jnp.int32)
+    where = (lax.axis_index("gx") * STRIDE + lax.axis_index("gy")) * STRIDE + lax.axis_index("gz")
+    where = where.astype(jnp.int32).reshape(1)
     ins = (initial, right_side, alpha, beta_x, beta_y, beta_z)
     sx, sy, sz = initial.shape
     n_x = 1 if counts[0] == 2 else 2
@@ -594,14 +590,14 @@
         where,
         ins + tuple(got_x),
     )
-    got_y = swaps("gy", sends)
+    two_y, one_y = swaps("gy", sends[::-1])[::-1]
     x1, y1 = sx // 2, sy // 2
     ring, coarse2, *outs = run(
         functools.partial(down_kernel, counts),
         [(5, x1, y1, LANES), (4, y1 // 2, LANES)] + [(5, NEAR, y1, LANES)] * n_x + [fine] * 12,
         where,
-        ins + tuple(got_x) + tuple(got_y),
-        [fine] * 17 + [(7, x1, y1, 2 * LANES), (ey, LANES), (4, x1, y1, LANES)],
+        ins + tuple(got_x) + (two_y, one_y),
+        [fine] * 9 + [(7, x1, y1, 2 * LANES), (ey, LANES), (4, x1, y1, LANES)],
         24,
     )
     sends, fine_arrays = outs[:n_x], outs[n_x:]
@@ -613,7 +609,7 @@
         where,
         (ring,) + tuple(near_x),
     )
-    near_y = swaps("gy", sends)
+    near_y = swaps("gy", sends[::-1])[::-1]
     copies, level1 = run(
         functools.partial(near_kernel, counts, devices),
         [(devices, 5, y1 // 2, LANES), (6, x1 + 2 * NEAR, y1 + 2 * NEAR, LANES)],

time: 71.6 us -> 64.1 us (0.90)
  Pallas kernels: 19.4 us -> 12.7 us
    pallas_call x7, Pallas kernels: 19.4 us -> 12.7 us  [run(): pl.pallas_call(kernel, out_shape=tuple((jax.ShapeDtypeStruct(shape, F32)...]
where the time goes in v5:
time: 64.1 us; the launch traced here: 63.9 us
  blocking collectives  19.8 us (31%)
  starting transfers between devices  16.1 us (25%)
  waiting for transfers between devices  15.2 us (24%)
  Pallas kernels  12.7 us (20%)
    all_to_all x1, blocking collectives, local(): gathered = lax.all_to_all(copies, axes, 0, 0, tiled=True)  19.8 us
    ppermute x8, starting transfers between devices, swaps(): got.append(lax.ppermute(block, axis, pairs))  16.1 us
    ppermute x8, waiting for transfers between devices, swaps(): got.append(lax.ppermute(block, axis, pairs))  15.2 us
    pallas_call x7, Pallas kernels, run(): pl.pallas_call(kernel, out_shape=tuple((jax.ShapeDtypeStruct(shape, F32)...  12.7 us
  transfers between devices with their start and end apart: 8, of which 5 were waited for; matrix products, arithmetic and copies ran while one was open for 0% of the time, Pallas kernels for 0%

profile of v5, /device:TPU:1, one launch (start us, length us, event | category | flops | bytes accessed | tf_op | source)
XLA Modules:
  0.0 63.9 jit_solution(8130749891298242047)
XLA Ops:
  0.0 0.0 copy-start.3
  0.0 0.0 copy-start.4
  0.0 0.0 copy-start.5
  0.0 2.4 %shard_map.64 = (f32[8,16,128]{2,1,0:T(8,128)}, f32[8,16,128]{2,1,0:T(8,128)}) custom-call(s32[1]{0:T(128)} %bitcast.where_ref, f32[16,16,128]{2,1,0:T(8,128)} %refs_0_.7, f32[16,16,128]{2,1,0:T(8,128)} %refs_1_.7, f32[16,16,128]{2,1,0:T(8,128)} %refs_2_.7, f32[16,16,128]{2,1,0:T(8,128)} %refs_3_.7, f32[16,16,128]{2,1,0:T(8,128)} %refs_4_.7, ...), custom_call_target="tpu_custom_call" | custom-call | tf_op jit(solution)/shard_map/pallas_call | solution.py:545
  2.4 2.1 %collective-permute-start = (f32[8,16,128]{2,1,0:T(8,128)}, f32[8,16,128]{2,1,0:T(8,128)S(1)}, u32[]{:S(2)}, u32[]{:S(2)}) collective-permute-start(f32[8,16,128]{2,1,0:T(8,128)} %get-tuple-element.30), channel_id=1, source_target_pairs={{0,1},{1,0},{2,3},{3,2},{4,5},{5,4},{6,7},{7,6},{8,9},{9,8},{10,11... | collective-permute-start | bytes 196616 | tf_op jit(solution)/shard_map/ppermute | solution.py:561
  4.5 0.7 %collective-permute-start.1 = (f32[8,16,128]{2,1,0:T(8,128)}, f32[8,16,128]{2,1,0:T(8,128)S(1)}, u32[]{:S(2)}, u32[]{:S(2)}) collective-permute-start(f32[8,16,128]{2,1,0:T(8,128)} %get-tuple-element.31), channel_id=1, source_target_pairs={{1,2},{2,1},{5,6},{6,5},{9,10},{10,9},{13,14},{14,13},{17,18},{18,... | collective-permute-start | bytes 196616 | tf_op jit(solution)/shard_map/ppermute | solution.py:561
  5.2 1.2 %collective-permute-done.refs_6_ = f32[8,16,128]{2,1,0:T(8,128)S(1)} collective-permute-done((f32[8,16,128]{2,1,0:T(8,128)}, f32[8,16,128]{2,1,0:T(8,128)S(1)}, u32[]{:S(2)}, u32[]{:S(2)}) %collective-permute-start) | collective-permute-done | bytes 65568 | tf_op jit(solution)/shard_map/ppermute | solution.py:561
  6.4 0.0 collective-permute-done.1.refs_7_
  6.4 0.0 copy-done
  6.4 0.0 copy-done.2
  6.4 0.0 copy-done.3
  6.4 0.0 copy-done.4
  6.4 0.0 copy-done.5
  6.5 0.1 shard_map.65
  6.6 1.4 %collective-permute-start.2 = (f32[7,4,16,128]{3,2,1,0:T(8,128)S(1)}, f32[7,4,16,128]{3,2,1,0:T(8,128)S(1)}, u32[]{:S(2)}, u32[]{:S(2)}) collective-permute-start(f32[7,4,16,128]{3,2,1,0:T(8,128)S(1)} %get-tuple-element.33), channel_id=1, source_target_pairs={{0,16},{16,0},{1,17},{17,1},{2,18},{18,2},{3,19},{19,3},{4,20},{20... | collective-permute-start | bytes 688136 | tf_op jit(solution)/shard_map/ppermute | solution.py:561
  8.0 4.2 %collective-permute-done.2.refs_7_ = f32[7,4,16,128]{3,2,1,0:T(8,128)S(1)} collective-permute-done((f32[7,4,16,128]{3,2,1,0:T(8,128)S(1)}, f32[7,4,16,128]{3,2,1,0:T(8,128)S(1)}, u32[]{:S(2)}, u32[]{:S(2)}) %collective-permute-start.2) | collective-permute-done | bytes 229408 | tf_op jit(solution)/shard_map/ppermute | solution.py:561
  12.2 0.1 shard_map.66
  12.3 5.7 %collective-permute-start.3 = (f32[7,24,4,128]{3,2,1,0:T(4,128)S(1)}, f32[7,24,4,128]{3,2,1,0:T(4,128)S(1)}, u32[]{:S(2)}, u32[]{:S(2)}) collective-permute-start(f32[7,24,4,128]{3,2,1,0:T(4,128)S(1)} %get-tuple-element.34), channel_id=1, source_target_pairs={{4,8},{8,4},{5,9},{9,5},{6,10},{10,6},{7,11},{11,7},{20,24},{24,20... | collective-permute-start | bytes 1032200 | tf_op jit(solution)/shard_map/ppermute | solution.py:561
  18.0 0.1 collective-permute-start.4
  18.1 4.8 %collective-permute-done.3.refs_8_ = f32[7,24,4,128]{3,2,1,0:T(4,128)S(1)} collective-permute-done((f32[7,24,4,128]{3,2,1,0:T(4,128)S(1)}, f32[7,24,4,128]{3,2,1,0:T(4,128)S(1)}, u32[]{:S(2)}, u32[]{:S(2)}) %collective-permute-start.3) | collective-permute-done | bytes 344096 | tf_op jit(solution)/shard_map/ppermute | solution.py:561
  22.9 0.0 collective-permute-done.4.refs_9_
  22.9 4.5 %shard_map.67 = (f32[5,8,8,128]{3,2,1,0:T(8,128)S(1)}, f32[4,4,128]{2,1,0:T(4,128)S(1)}, f32[5,4,8,128]{3,2,1,0:T(8,128)S(1)}, f32[24,24,128]{2,1,0:T(8,128)S(1)...) custom-call(s32[1]{0:T(128)} %bitcast.where_ref, ...), custom_call_target="tpu_custom_call" | custom-call | tf_op jit(solution)/shard_map/pallas_call | solution.py:545
  27.4 1.2 %collective-permute-start.5 = (f32[5,4,8,128]{3,2,1,0:T(8,128)S(1)}, f32[5,4,8,128]{3,2,1,0:T(8,128)S(1)}, u32[]{:S(2)}, u32[]{:S(2)}) collective-permute-start(f32[5,4,8,128]{3,2,1,0:T(8,128)S(1)} %get-tuple-element.37), channel_id=1, source_target_pairs={{0,16},{16,0},{1,17},{17,1},{2,18},{18,2},{3,19},{19,3},{4,20},{20... | collective-permute-start | bytes 245768 | tf_op jit(solution)/shard_map/ppermute | solution.py:561
  28.6 2.1 %collective-permute-done.5.refs_0_ = f32[5,4,8,128]{3,2,1,0:T(8,128)S(1)} collective-permute-done((f32[5,4,8,128]{3,2,1,0:T(8,128)S(1)}, f32[5,4,8,128]{3,2,1,0:T(8,128)S(1)}, u32[]{:S(2)}, u32[]{:S(2)}) %collective-permute-start.5) | collective-permute-done | bytes 81952 | tf_op jit(solution)/shard_map/ppermute | solution.py:561
  30.7 0.1 shard_map.68
  30.8 4.8 %collective-permute-start.6 = (f32[5,16,4,128]{3,2,1,0:T(4,128)S(1)}, f32[5,16,4,128]{3,2,1,0:T(4,128)S(1)}, u32[]{:S(2)}, u32[]{:S(2)}) collective-permute-start(f32[5,16,4,128]{3,2,1,0:T(4,128)S(1)} %get-tuple-element.38), channel_id=1, source_target_pairs={{4,8},{8,4},{5,9},{9,5},{6,10},{10,6},{7,11},{11,7},{20,24},{24,20... | collective-permute-start | bytes 491528 | tf_op jit(solution)/shard_map/ppermute | solution.py:561
  35.6 0.1 collective-permute-start.7
  35.6 2.9 %collective-permute-done.6.refs_1_ = f32[5,16,4,128]{3,2,1,0:T(4,128)S(1)} collective-permute-done((f32[5,16,4,128]{3,2,1,0:T(4,128)S(1)}, f32[5,16,4,128]{3,2,1,0:T(4,128)S(1)}, u32[]{:S(2)}, u32[]{:S(2)}) %collective-permute-start.6) | collective-permute-done | bytes 163872 | tf_op jit(solution)/shard_map/ppermute | solution.py:561
  38.6 0.0 collective-permute-done.7.refs_2_
  38.6 0.4 shard_map.69
  39.0 19.8 %all_to_all.5.gathered = f32[32,5,4,128]{3,2,1,0:T(4,128)S(1)} all-to-all(f32[32,5,4,128]{3,2,1,0:T(4,128)S(1)} %get-tuple-element.41), channel_id=1, replica_groups=mesh['gx'=2,'gy'=4,'gz'=4] {'gx','gy','gz'}, dimensions={0} | all-to-all | bytes 655360 | tf_op jit(solution)/shard_map/all_to_all | solution.py:621
  58.8 5.1 %shard_map.70 = f32[16,16,128]{2,1,0:T(8,128)} custom-call(s32[1]{0:T(128)} %bitcast.where_ref, f32[32,5,4,128]{3,2,1,0:T(4,128)S(1)} %all_to_all.5.gathered, f32[6,16,16,128]{3,2,1,0:T(8,128)S(1)} %get-tuple-element.42.level1, f32[24,24,128]{2,1,0:T(8,128)S(1)} %get-tuple-element.43.refs_0_, f32[24,24,128]{2,1,0:T(8,128)S(1)} %get-tuple-element.44.refs_1_, ...), custom_call_target="tpu_custom_call" | custom-call | tf_op jit(solution)/shard_map/pallas_call | solution.py:545
  (4 shorter events, 0.0 us)
Async XLA Ops:
  0.0 6.4 %copy-start = (f32[16,16,128]{2,1,0:T(8,128)S(1)}, f32[16,16,128]{2,1,0:T(8,128)}, u32[]{:S(2)}) copy-start(f32[16,16,128]{2,1,0:T(8,128)} %refs_0_.7) | copy-start | bytes 393220
  0.0 6.4 %copy-start.1 = (f32[16,16,128]{2,1,0:T(8,128)S(1)}, f32[16,16,128]{2,1,0:T(8,128)}, u32[]{:S(2)}) copy-start(f32[16,16,128]{2,1,0:T(8,128)} %refs_1_.7) | copy-start | bytes 393220
  0.0 6.4 %copy-start.2 = (f32[16,16,128]{2,1,0:T(8,128)S(1)}, f32[16,16,128]{2,1,0:T(8,128)}, u32[]{:S(2)}) copy-start(f32[16,16,128]{2,1,0:T(8,128)} %refs_2_.7) | copy-start | bytes 393220
  0.0 6.4 %copy-start.3 = (f32[16,16,128]{2,1,0:T(8,128)S(1)}, f32[16,16,128]{2,1,0:T(8,128)}, u32[]{:S(2)}) copy-start(f32[16,16,128]{2,1,0:T(8,128)} %refs_3_.7) | copy-start | bytes 393220
  0.0 6.4 %copy-start.4 = (f32[16,16,128]{2,1,0:T(8,128)S(1)}, f32[16,16,128]{2,1,0:T(8,128)}, u32[]{:S(2)}) copy-start(f32[16,16,128]{2,1,0:T(8,128)} %refs_4_.7) | copy-start | bytes 393220
  0.0 6.4 %copy-start.5 = (f32[16,16,128]{2,1,0:T(8,128)S(1)}, f32[16,16,128]{2,1,0:T(8,128)}, u32[]{:S(2)}) copy-start(f32[16,16,128]{2,1,0:T(8,128)} %refs_5_.7) | copy-start | bytes 393220
  2.4 4.0 %collective-permute-start = (f32[8,16,128]{2,1,0:T(8,128)}, f32[8,16,128]{2,1,0:T(8,128)S(1)}, u32[]{:S(2)}, u32[]{:S(2)}) collective-permute-start(f32[8,16,128]{2,1,0:T(8,128)} %get-tuple-element.30), channel_id=1, source_target_pairs={{0,1},{1,0},{2,3},{3,2},{4,5},{5,4},{6,7},{7,6},{8,9},{9,8},{10,11... | collective-permute-start | bytes 196616 | tf_op jit(solution)/shard_map/ppermute | solution.py:561
  4.5 1.9 %collective-permute-start.1 = (f32[8,16,128]{2,1,0:T(8,128)}, f32[8,16,128]{2,1,0:T(8,128)S(1)}, u32[]{:S(2)}, u32[]{:S(2)}) collective-permute-start(f32[8,16,128]{2,1,0:T(8,128)} %get-tuple-element.31), channel_id=1, source_target_pairs={{1,2},{2,1},{5,6},{6,5},{9,10},{10,9},{13,14},{14,13},{17,18},{18,... | collective-permute-start | bytes 196616 | tf_op jit(solution)/shard_map/ppermute | solution.py:561
  6.6 5.6 %collective-permute-start.2 = (f32[7,4,16,128]{3,2,1,0:T(8,128)S(1)}, f32[7,4,16,128]{3,2,1,0:T(8,128)S(1)}, u32[]{:S(2)}, u32[]{:S(2)}) collective-permute-start(f32[7,4,16,128]{3,2,1,0:T(8,128)S(1)} %get-tuple-element.33), channel_id=1, source_target_pairs={{0,16},{16,0},{1,17},{17,1},{2,18},{18,2},{3,19},{19,3},{4,20},{20... | collective-permute-start | bytes 688136 | tf_op jit(solution)/shard_map/ppermute | solution.py:561
  12.3 10.6 %collective-permute-start.3 = (f32[7,24,4,128]{3,2,1,0:T(4,128)S(1)}, f32[7,24,4,128]{3,2,1,0:T(4,128)S(1)}, u32[]{:S(2)}, u32[]{:S(2)}) collective-permute-start(f32[7,24,4,128]{3,2,1,0:T(4,128)S(1)} %get-tuple-element.34), channel_id=1, source_target_pairs={{4,8},{8,4},{5,9},{9,5},{6,10},{10,6},{7,11},{11,7},{20,24},{24,20... | collective-permute-start | bytes 1032200 | tf_op jit(solution)/shard_map/ppermute | solution.py:561
  18.0 4.9 %collective-permute-start.4 = (f32[7,24,4,128]{3,2,1,0:T(4,128)S(1)}, f32[7,24,4,128]{3,2,1,0:T(4,128)S(1)}, u32[]{:S(2)}, u32[]{:S(2)}) collective-permute-start(f32[7,24,4,128]{3,2,1,0:T(4,128)S(1)} %get-tuple-element.35), channel_id=1, source_target_pairs={{0,4},{4,0},{8,12},{12,8},{1,5},{5,1},{9,13},{13,9},{2,6},{6,2},{1... | collective-permute-start | bytes 1032200 | tf_op jit(solution)/shard_map/ppermute | solution.py:561
  27.4 3.3 %collective-permute-start.5 = (f32[5,4,8,128]{3,2,1,0:T(8,128)S(1)}, f32[5,4,8,128]{3,2,1,0:T(8,128)S(1)}, u32[]{:S(2)}, u32[]{:S(2)}) collective-permute-start(f32[5,4,8,128]{3,2,1,0:T(8,128)S(1)} %get-tuple-element.37), channel_id=1, source_target_pairs={{0,16},{16,0},{1,17},{17,1},{2,18},{18,2},{3,19},{19,3},{4,20},{20... | collective-permute-start | bytes 245768 | tf_op jit(solution)/shard_map/ppermute | solution.py:561
  30.8 7.8 %collective-permute-start.6 = (f32[5,16,4,128]{3,2,1,0:T(4,128)S(1)}, f32[5,16,4,128]{3,2,1,0:T(4,128)S(1)}, u32[]{:S(2)}, u32[]{:S(2)}) collective-permute-start(f32[5,16,4,128]{3,2,1,0:T(4,128)S(1)} %get-tuple-element.38), channel_id=1, source_target_pairs={{4,8},{8,4},{5,9},{9,5},{6,10},{10,6},{7,11},{11,7},{20,24},{24,20... | collective-permute-start | bytes 491528 | tf_op jit(solution)/shard_map/ppermute | solution.py:561
  35.6 3.0 %collective-permute-start.7 = (f32[5,16,4,128]{3,2,1,0:T(4,128)S(1)}, f32[5,16,4,128]{3,2,1,0:T(4,128)S(1)}, u32[]{:S(2)}, u32[]{:S(2)}) collective-permute-start(f32[5,16,4,128]{3,2,1,0:T(4,128)S(1)} %get-tuple-element.39), channel_id=1, source_target_pairs={{0,4},{4,0},{8,12},{12,8},{1,5},{5,1},{9,13},{13,9},{2,6},{6,2},{1... | collective-permute-start | bytes 491528 | tf_op jit(solution)/shard_map/ppermute | solution.py:561

commit v6 on v5

--- a/solution.py
+++ b/solution.py
@@ -208,17 +208,85 @@
     return centre, [out[k] + (faces[k] * ups[k] + downs[k]) for k in range(2)]
 
 
+def unpacked(packed, a, lane):
+    at, depth = PLACE[a], DEPTH[a]
+    axis = packed.ndim - 1
+    right, left = turn(packed, -at, axis), turn(packed, SIDE - depth - at, axis)
+    return jnp.where(lane < depth, right, jnp.where(lane >= LANES - depth, left, 0.0))
+
+
+def rows_of(source, x, firsts, seconds):
+    total = None
+    for p in firsts:
+        for q in seconds:
+            term = source[x + p, pl.ds(q, source.shape[1] // 2, stride=2), :]
+            total = term if total is None else total + term
+    return total
+
+
+BOTH, ODD = (0, 1), (1,)
+
+
+def to_level1(sums, first, count, table, factor):
+    _, x1, y1, _ = sums.shape
+    flat = sums[first:first + count].reshape(count * x1 * y1, 2 * LANES)
+    return factor * times_table(flat, table).reshape(count, x1, y1, LANES)
+
+
+def coefficient_kernel(counts, devices, where_ref, *refs):
+    ins, refs = refs[2:7], refs[7:]
+    n_x = 1 if counts[0] == 2 else 2
+    halos_x, (copies, coeffs1, halo, sums, pairing) = refs[:n_x], refs[n_x:]
+    sx, sy, sz = ins[0].shape
+    odd_x = position(where_ref)[0] % 2
+    x1, y1 = sx // 2, sy // 2
+    lane = lane_of((sx, sy, LANES))
+    lanes = [slice(k * LANES, (k + 1) * LANES) for k in range(2)]
+    edge_lane = lane_of((1, sy, LANES))
+    below, _ = neighbours(counts[0], odd_x, halos_x[0][3, HALO - 1:], halos_x[-1][3, HALO - 1:])
+    packed, _ = neighbours(counts[0], odd_x, halos_x[0][6, HALO - 1:], halos_x[-1][6, HALO - 1:])
+    for k, edge in enumerate((below, unpacked(packed, 3, edge_lane))):
+        halo[k, 0:1] = edge
+        sums[4, 0, :, lanes[k]] = rows_of(halo.at[k], 0, (0,), BOTH)
+    for n, (firsts, seconds) in enumerate(((BOTH, BOTH), (ODD, BOTH), (BOTH, ODD), (BOTH, BOTH))):
+        halo[0] = unpacked(ins[4][...], n + 2, lane)
+        for i in range(x1):
+            sums[n, i, :, lanes[0]] = rows_of(ins[n], 2 * i, firsts, seconds)
+            sums[n, i, :, lanes[1]] = rows_of(halo.at[0], 2 * i, firsts, seconds)
+    pairs = pair_table(2 * LANES, LANES, False)
+    odds = pair_table(2 * LANES, LANES, True)
+    paired = to_level1(sums, 0, 3, pairs, 0.0625)
+    mass1 = (2.0 * WEIGHT) * paired[0]
+    faces1 = (paired[1], paired[2], to_level1(sums, 3, 1, odds, 0.0625)[0])
+    edge = 0.0625 * times_table(sums[4, 0], pairs)[None]
+    diag1 = mass1 + faces1[0] + jnp.concatenate([edge, faces1[0][:-1]], axis=0)
+    diag1 = diag1 + faces1[1] + faces1[2] + turn(faces1[2], 1, 2)
+    for n, values in enumerate((mass1, diag1) + faces1):
+        coeffs1[n] = values
+    parts = (
+        (mass1, False, False, False, 0.125),
+        (faces1[0], True, False, False, 0.0625),
+        (faces1[1], False, True, False, 0.0625),
+        (faces1[2], False, False, True, 0.0625),
+    )
+    for n, (values, *odd_axes, factor) in enumerate(parts):
+        pairing[n] = values
+        packed = level2_rows(pairing.at[n], odd_axes, factor, x1 // 2, y1 // 2, sz // 4)
+        for d in range(devices):
+            copies[d, n] = packed
+
+
 def down_kernel(counts, where_ref, *refs):
     ins, refs = refs[:7], refs[7:]
     n_x = 1 if counts[0] == 2 else 2
     halos_x = refs[:n_x]
-    two_y, one_y, own1, coarse2 = refs[n_x:4 + n_x]
+    two_y, one_y, coeffs1, own1 = refs[n_x:4 + n_x]
     sends, refs = refs[4 + n_x:4 + 2 * n_x], refs[4 + 2 * n_x:]
     kept_m, kept_h, weight_m, weight_h = refs[:4]
     faces_out, scratch = refs[4:12], refs[12:]
     rhs, bx, by, bz = zip(faces_out[::2], faces_out[1::2])
     field, alpha = scratch[:2], scratch[2:4]
-    packs, half_m, half_h, diag_m, diag_h, sums, left, pairing = scratch[4:]
+    packs, half_m, half_h, diag_m, diag_h, sums, left = scratch[4:]
     arrays = (field, rhs, alpha, bx, by, bz)
     sx, sy, sz = ins[0].shape
     ex, ey = sx + 2 * HALO, sy + 2 * HALO
@@ -237,12 +305,7 @@
     def unpack(x):
         packed = packs[x]
         for a in range(6):
-            at, depth = PLACE[a], DEPTH[a]
-            right = turn(packed, -at, 1)
-            other_side = turn(packed, SIDE - depth - at, 1)
-            arrays[a][1][x] = jnp.where(
-                lane < depth, right, jnp.where(lane >= LANES - depth, other_side, 0.0)
-            )
+            arrays[a][1][x] = unpacked(packed, a, lane)
 
     each(0, ex, 4, unpack)
     halfway, weight, kept = (half_m, half_h), (weight_m, weight_h), (kept_m, kept_h)
@@ -278,57 +341,25 @@
     each(HALO, ex - HALO, 4, residual)
 
     x1, y1 = sx // 2, sy // 2
-
-    def rows_of(source, x, firsts, seconds):
-        total = None
-        for p in firsts:
-            for q in seconds:
-                term = source[x + p, pl.ds(q, y1, stride=2), :]
-                total = term if total is None else total + term
-        return total
-
-    both, last = (0, 1), (1,)
     for k in range(2):
         lanes = slice(k * LANES, (k + 1) * LANES)
         for i in range(x1):
             x = HALO + 2 * i
-            sums[0, i, :, lanes] = rows_of(halfway[k], x, both, both)
-            sums[1, i, :, lanes] = rows_of(alpha[k], x, both, both)
-            sums[2, i, :, lanes] = rows_of(bx[k], x, last, both)
-            sums[3, i, :, lanes] = rows_of(by[k], x, both, last)
+            total = None
+            for p in BOTH:
+                for q in BOTH:
+                    term = halfway[k][x + p, pl.ds(q, y1, stride=2), :]
+                    total = term if total is None else total + term
+            sums[0, i, :, lanes] = total
             left[...] = turn(by[k][x] + by[k][x + 1], 1, 0)
-            sums[4, i, :, lanes] = left[pl.ds(0, y1, stride=2), :]
-            sums[5, i, :, lanes] = rows_of(bz[k], x, both, both)
-        sums[6, 0, :, lanes] = rows_of(bx[k], HALO - 2, last, both)
-    pairs = pair_table(2 * LANES, LANES, False)
-    odds = pair_table(2 * LANES, LANES, True)
-
-    def to_level1(first, count, table, factor):
-        flat = sums[first:first + count].reshape(count * x1 * y1, 2 * LANES)
-        return factor * times_table(flat, table).reshape(count, x1, y1, LANES)
-
-    paired = to_level1(0, 5, pairs, 0.0625)
-    rhs1, mass1 = 2.0 * paired[0], (2.0 * WEIGHT) * paired[1]
-    faces1 = (paired[2], paired[3], to_level1(5, 1, odds, 0.0625)[0])
-    edge_x = 0.0625 * times_table(sums[6, 0], pairs)[None]
-    diag1 = mass1 + faces1[0] + jnp.concatenate([edge_x, faces1[0][:-1]], axis=0)
-    diag1 = diag1 + faces1[1] + paired[4] + faces1[2] + turn(faces1[2], 1, 2)
-    weight1 = relaxer(mass1, diag1)
-    for n, values in enumerate((rhs1, weight1) + faces1):
+            sums[1, i, :, lanes] = left[pl.ds(0, y1, stride=2), :]
+    rhs1, low_y = to_level1(sums, 0, 2, pair_table(2 * LANES, LANES, False), 0.0625)
+    weight1 = relaxer(coeffs1[0], coeffs1[1] + low_y)
+    for n, values in enumerate((2.0 * rhs1, weight1, coeffs1[2], coeffs1[3], coeffs1[4])):
         own1[n] = values
         head, tail = values[:NEAR], values[x1 - NEAR:]
         for k, send in enumerate(sends):
             send[n] = pick(odd_x, head, tail) if k == 0 else pick(odd_x, tail, head)
-
-    parts = (
-        (mass1, False, False, False, 0.125),
-        (faces1[0], True, False, False, 0.0625),
-        (faces1[1], False, True, False, 0.0625),
-        (faces1[2], False, False, True, 0.0625),
-    )
-    for n, (values, *odd_axes, factor) in enumerate(parts):
-        pairing[n] = values
-        coarse2[n] = level2_rows(pairing.at[n], odd_axes, factor, x1 // 2, y1 // 2, sz // 4)
 
 
 def level2_rows(source, odd_axes, factor, x2, y2, z2):
@@ -351,6 +382,7 @@
 
 
 def near_y_kernel(counts, where_ref, ring, *refs):
+    refs = refs[:-3] + refs[-2:]
     halos, sends = refs[:-2], refs[:-3:-1]
     n, bx, by, _ = ring.shape
     odd_x, odd = (place % 2 for place in position(where_ref)[:2])
@@ -365,7 +397,7 @@
 def near_kernel(counts, devices, where_ref, ring, *refs):
     n_x = 1 if counts[0] == 2 else 2
     halos_x = refs[:n_x]
-    two_y, one_y, coarse2, copies, level1, left = refs[n_x:]
+    two_y, one_y, copies, level1, left = refs[n_x:]
     n, bx1, by1, _ = ring.shape
     odd_x, odd_y = (place % 2 for place in position(where_ref)[:2])
     whole = []
@@ -387,9 +419,7 @@
     left[...] = remain
     packed = level2_rows(left, (False,) * 3, 0.125, bx1 // 2, by1 // 2, LANES // 4)
     for d in range(devices):
-        copies[d, 0] = packed
-        for a in range(n - 1):
-            copies[d, a + 1] = coarse2[a]
+        copies[d] = packed
 
 
 def halve(values, odd_axis, step):
@@ -451,34 +481,54 @@
     return field
 
 
+def spread_out(counts, slots, whole):
+    gx, gy, gz = counts
+    y2 = slots.shape[-2]
+    x2 = whole.shape[0] // gx
+    z2 = LANES // x2
+    lane = lane_of((y2, LANES))
+    for i in range(gx):
+        for j in range(gy):
+            for x in range(x2):
+                for part in range(whole.shape[2] // LANES):
+                    total = jnp.zeros((y2, LANES), F32)
+                    for k in range(LANES // z2):
+                        column = part * (LANES // z2) + k
+                        if column < gz:
+                            block = slots[(i * gy + j) * gz + column]
+                            mask = (lane >= k * z2) & (lane < (k + 1) * z2)
+                            total = jnp.where(mask, turn(block, (k - x) * z2, 1), total)
+                    lanes = slice(part * LANES, (part + 1) * LANES)
+                    whole[i * x2 + x, j * y2:(j + 1) * y2, lanes] = total
+
+
+def coarse_kernel(counts, gathered, *refs):
+    outs, whole = refs[:-1], refs[-1]
+    y2 = gathered.shape[2]
+    z2 = LANES * counts[0] // whole.shape[1]
+    for a in range(4):
+        spread_out(counts, gathered.at[:, a], whole.at[a])
+    faces = (whole[1], whole[2], whole[3])
+    levels = coarse_levels(whole[0], faces, counts[1] * y2, counts[2] * z2)
+    for out, (diag, weight, coupled) in zip(outs, levels):
+        for n, values in enumerate((diag, weight) + coupled):
+            out[n] = values
+
+
 def up_kernel(counts, where_ref, gathered, level1, *refs):
     kept, weight, rhs, bx, by, bz = zip(refs[0:12:2], refs[1:12:2])
-    out, whole, second, spread_m, spread_h, field_m, field_h, half_m, half_h = refs[12:]
+    depth = LEVELS - 2
+    coarse, refs = refs[12:12 + depth], refs[12 + depth:]
+    out, whole, second, spread_m, spread_h, field_m, field_h, half_m, half_h = refs
     gx, gy, gz = counts
     at_x, at_y, at_z = position(where_ref)
     sx, sy, sz = out.shape
     x1, y1 = sx // 2, sy // 2
     x2, y2, z2 = x1 // 2, y1 // 2, sz // 4
     columns = max(LANES, gz * z2)
-    lane = lane_of((y2, LANES))
-
-    for a in range(5):
-        for i in range(gx):
-            for j in range(gy):
-                for x in range(x2):
-                    for part in range(columns // LANES):
-                        total = jnp.zeros((y2, LANES), F32)
-                        for k in range(LANES // z2):
-                            column = part * (LANES // z2) + k
-                            if column < gz:
-                                block = gathered[(i * gy + j) * gz + column, a]
-                                mask = (lane >= k * z2) & (lane < (k + 1) * z2)
-                                total = jnp.where(mask, turn(block, (k - x) * z2, 1), total)
-                        whole[
-                            a, i * x2 + x, j * y2:(j + 1) * y2, part * LANES:(part + 1) * LANES
-                        ] = total
-    levels = coarse_levels(whole[1], (whole[2], whole[3], whole[4]), gy * y2, gz * z2)
-    correction = coarse_cycle(2, whole[0], levels)
+    spread_out(counts, gathered, whole)
+    levels = [(ref[0], ref[1], (ref[2], ref[3], ref[4])) for ref in coarse]
+    correction = coarse_cycle(2, whole[...], levels)
 
     wide = gx * x2
     half = NEAR // 2
@@ -541,15 +591,18 @@
     each(HALO, ex - HALO, 4, sweep_own)
 
 
-def run(kernel, outs, where, arrays, scratch=(), grant=16):
+def run(kernel, outs, where, arrays, scratch=(), grant=16, micros=1):
     return pl.pallas_call(
         kernel,
         out_shape=tuple(jax.ShapeDtypeStruct(shape, F32) for shape in outs),
-        in_specs=[SM] + [VM] * len(arrays),
+        in_specs=[SM] * len(where) + [VM] * len(arrays),
         out_specs=tuple(VM for _ in outs),
         scratch_shapes=[pltpu.VMEM(shape, F32) for shape in scratch],
         compiler_params=pltpu.CompilerParams(vmem_limit_bytes=grant * 1024 * 1024),
-    )(where, *arrays)
+        cost_estimate=pl.CostEstimate(
+            flops=0, bytes_accessed=int(micros * 3.6e6), transcendentals=0
+        ),
+    )(*where, *arrays)
 
 
 def swaps(axis, sends):
@@ -567,7 +620,7 @@
     counts = tuple(lax.axis_size(axis) for axis in axes)
     devices = counts[0] * counts[1] * counts[2]
     where = (lax.axis_index("gx") * STRIDE + lax.axis_index("gy")) * STRIDE + lax.axis_index("gz")
-    where = where.astype(jnp.int32).reshape(1)
+    where = (where.astype(jnp.int32).reshape(1),)
     ins = (initial, right_side, alpha, beta_x, beta_y, beta_z)
     sx, sy, sz = initial.shape
     n_x = 1 if counts[0] == 2 else 2
@@ -592,13 +645,23 @@
     )
     two_y, one_y = swaps("gy", sends[::-1])[::-1]
     x1, y1 = sx // 2, sy // 2
-    ring, coarse2, *outs = run(
+    copies, coeffs1 = run(
+        functools.partial(coefficient_kernel, counts, devices),
+        [(devices, 4, y1 // 2, LANES), (5, x1, y1, LANES)],
+        where,
+        ins + tuple(got_x),
+        [(2, sx, sy, LANES), (5, x1, y1, 2 * LANES), (4, x1, y1, LANES)],
+        micros=2,
+    )
+    gathered = lax.all_to_all(copies, axes, 0, 0, tiled=True)
+    ring, *outs = run(
         functools.partial(down_kernel, counts),
-        [(5, x1, y1, LANES), (4, y1 // 2, LANES)] + [(5, NEAR, y1, LANES)] * n_x + [fine] * 12,
+        [(5, x1, y1, LANES)] + [(5, NEAR, y1, LANES)] * n_x + [fine] * 12,
         where,
-        ins + tuple(got_x) + (two_y, one_y),
-        [fine] * 9 + [(7, x1, y1, 2 * LANES), (ey, LANES), (4, x1, y1, LANES)],
+        ins + tuple(got_x) + (two_y, one_y, coeffs1),
+        [fine] * 9 + [(2, x1, y1, 2 * LANES), (ey, LANES)],
         24,
+        micros=4,
     )
     sends, fine_arrays = outs[:n_x], outs[n_x:]
 
@@ -607,29 +670,38 @@
         functools.partial(near_y_kernel, counts),
         [(5, x1 + 2 * NEAR, NEAR, LANES)] * 2,
         where,
-        (ring,) + tuple(near_x),
+        (ring,) + tuple(near_x) + (gathered,),
     )
     near_y = swaps("gy", sends[::-1])[::-1]
     copies, level1 = run(
         functools.partial(near_kernel, counts, devices),
-        [(devices, 5, y1 // 2, LANES), (6, x1 + 2 * NEAR, y1 + 2 * NEAR, LANES)],
+        [(devices, y1 // 2, LANES), (6, x1 + 2 * NEAR, y1 + 2 * NEAR, LANES)],
         where,
-        (ring,) + tuple(near_x) + tuple(near_y) + (coarse2,),
+        (ring,) + tuple(near_x) + tuple(near_y),
         [(x1, y1 + 2 * NEAR, LANES)],
     )
 
-    gathered = lax.all_to_all(copies, axes, 0, 0, tiled=True)
     wide, rows = counts[0] * x1 // 2, counts[1] * y1 // 2
     columns = max(LANES, counts[2] * sz // 4)
+    levels = run(
+        functools.partial(coarse_kernel, counts),
+        [(5, wide >> n, rows, columns) for n in range(LEVELS - 2)],
+        (),
+        (gathered,),
+        [(4, wide, rows, columns)],
+        micros=2,
+    )
+    gathered = lax.all_to_all(copies, axes, 0, 0, tiled=True)
     (result,) = run(
         functools.partial(up_kernel, counts),
         [(sx, sy, sz)],
         where,
-        (gathered, level1) + tuple(fine_arrays),
-        [(5, wide, rows, columns), (wide + NEAR, rows, columns)]
+        (gathered, level1) + tuple(fine_arrays) + tuple(levels),
+        [(wide, rows, columns), (wide + NEAR, rows, columns)]
         + [(x1 + 2, ey, LANES)] * 2
         + [fine] * 4,
         24,
+        micros=4,
     )
     return result
 

time: 64.1 us -> 78.3 us (1.22); the launches traced: 63.9 us -> 77 us
  blocking collectives: 19.8 us -> 0 us
  starting transfers between devices: 16.1 us -> 29.2 us
  local copies, waits for them, and re-layouts: 0.02 us -> 10.1 us
  waiting for transfers between devices: 15.2 us -> 22.9 us
  Pallas kernels: 12.7 us -> 14.6 us
    all_to_all x1 -> x0, blocking collectives: 19.8 us -> none  [local(): gathered = lax.all_to_all(copies, axes, 0, 0, tiled=True)]
    all_to_all x0 -> x2, starting transfers between devices: none -> 16 us  [local(): gathered = lax.all_to_all(copies, axes, 0, 0, tiled=True)]
    unnamed x12 -> x36, local copies, waits for them, and re-layouts: 0.02 us -> 10.1 us
    all_to_all x0 -> x2, waiting for transfers between devices: none -> 6.05 us  [local(): gathered = lax.all_to_all(copies, axes, 0, 0, tiled=True)]
    ppermute x8, starting transfers between devices: 16.1 us -> 13.2 us  [swaps(): got.append(lax.ppermute(block, axis, pairs))]
    pallas_call x7 -> x9, Pallas kernels: 12.7 us -> 14.6 us  [run(): pl.pallas_call(kernel, out_shape=tuple((jax.ShapeDtypeStruct(shape, F32)...]
    ppermute x8, waiting for transfers between devices: 15.2 us -> 16.8 us  [swaps(): got.append(lax.ppermute(block, axis, pairs))]
  transfers between devices with their start and end apart: 8 -> 10, of which waited for: 5 -> 6; matrix products, arithmetic and copies ran while one was open for 0% -> 0% of each run, Pallas kernels for 0% -> 6%
where the time goes in v6:
time: 78.3 us; the launch traced here: 77 us
  starting transfers between devices  29.2 us (37%)
  waiting for transfers between devices  22.9 us (29%)
  Pallas kernels  14.6 us (19%)
  local copies, waits for them, and re-layouts  10.1 us (13%)
    ppermute x8, waiting for transfers between devices, swaps(): got.append(lax.ppermute(block, axis, pairs))  16.8 us
    all_to_all x2, starting transfers between devices, local(): gathered = lax.all_to_all(copies, axes, 0, 0, tiled=True)  16 us
    pallas_call x9, Pallas kernels, run(): pl.pallas_call(kernel, out_shape=tuple((jax.ShapeDtypeStruct(shape, F32)...  14.6 us
    ppermute x8, starting transfers between devices, swaps(): got.append(lax.ppermute(block, axis, pairs))  13.2 us
    unnamed x36, local copies, waits for them, and re-layouts  10.1 us
    all_to_all x2, waiting for transfers between devices, local(): gathered = lax.all_to_all(copies, axes, 0, 0, tiled=True)  6.05 us
  transfers between devices with their start and end apart: 10, of which 6 were waited for; matrix products, arithmetic and copies ran while one was open for 0% of the time, Pallas kernels for 6%

profile of v6, /device:TPU:1, one launch (start us, length us, event | category | flops | bytes accessed | tf_op | source)
XLA Modules:
  0.0 77.0 jit_solution(18239127880782055886)
XLA Ops:
  0.0 2.4 %shard_map.64 = (f32[8,16,128]{2,1,0:T(8,128)}, f32[8,16,128]{2,1,0:T(8,128)}) custom-call(s32[1]{0:T(128)} %bitcast.where_ref, f32[16,16,128]{2,1,0:T(8,128)} %refs_0_.9, f32[16,16,128]{2,1,0:T(8,128)} %refs_1_.9, f32[16,16,128]{2,1,0:T(8,128)} %refs_2_.9, f32[16,16,128]{2,1,0:T(8,128)} %refs_3_.9, f32[16,16,128]{2,1,0:T(8,128)} %refs_4_.9, ...), custom_call_target="tpu_custom_call" | custom-call | bytes 3600000 | tf_op jit(solution)/shard_map/pallas_call | solution.py:595
  2.4 2.1 %collective-permute-start = (f32[8,16,128]{2,1,0:T(8,128)}, f32[8,16,128]{2,1,0:T(8,128)S(1)}, u32[]{:S(2)}, u32[]{:S(2)}) collective-permute-start(f32[8,16,128]{2,1,0:T(8,128)} %get-tuple-element.35), channel_id=1, source_target_pairs={{0,1},{1,0},{2,3},{3,2},{4,5},{5,4},{6,7},{7,6},{8,9},{9,8},{10,11... | collective-permute-start | bytes 196616 | tf_op jit(solution)/shard_map/ppermute | solution.py:614
  4.5 0.7 collective-permute-start.1
  5.2 1.2 %collective-permute-done.refs_6_ = f32[8,16,128]{2,1,0:T(8,128)S(1)} collective-permute-done((f32[8,16,128]{2,1,0:T(8,128)}, f32[8,16,128]{2,1,0:T(8,128)S(1)}, u32[]{:S(2)}, u32[]{:S(2)}) %collective-permute-start) | collective-permute-done | bytes 65568 | tf_op jit(solution)/shard_map/ppermute | solution.py:614
  6.6 1.4 %collective-permute-start.2 = (f32[7,4,16,128]{3,2,1,0:T(8,128)S(1)}, f32[7,4,16,128]{3,2,1,0:T(8,128)S(1)}, u32[]{:S(2)}, u32[]{:S(2)}) collective-permute-start(f32[7,4,16,128]{3,2,1,0:T(8,128)S(1)} %get-tuple-element.38), channel_id=1, source_target_pairs={{0,16},{16,0},{1,17},{17,1},{2,18},{18,2},{3,19},{19,3},{4,20},{20... | collective-permute-start | bytes 688136 | tf_op jit(solution)/shard_map/ppermute | solution.py:614
  8.0 4.2 %collective-permute-done.2.refs_7_ = f32[7,4,16,128]{3,2,1,0:T(8,128)S(1)} collective-permute-done((f32[7,4,16,128]{3,2,1,0:T(8,128)S(1)}, f32[7,4,16,128]{3,2,1,0:T(8,128)S(1)}, u32[]{:S(2)}, u32[]{:S(2)}) %collective-permute-start.2) | collective-permute-done | bytes 229408 | tf_op jit(solution)/shard_map/ppermute | solution.py:614
  12.2 1.5 %shard_map.67 = (f32[32,4,4,128]{3,2,1,0:T(4,128)}, f32[5,8,8,128]{3,2,1,0:T(8,128)S(1)}) custom-call(s32[1]{0:T(128)} %bitcast.where_ref, f32[16,16,128]{2,1,0:T(8,128)S(1)} %copy-done, f32[16,16,128]{2,1,0:T(8,128)S(1)} %copy-done.1, f32[16,16,128]{2,1,0:T(8,128)S(1)} %copy-done.2, f32[16,16,128]{2,1,0:T(8,128)S(1)} %copy-done.3, ...), custom_call_target="tpu_custom_call" | custom-call | bytes 7200000 | tf_op jit(solution)/shard_map/pallas_call | solution.py:595
  13.7 10.5 %all-to-all-start = ((f32[32,4,4,128]{3,2,1,0:T(4,128)}), f32[32,4,4,128]{3,2,1,0:T(4,128)S(1)}, u32[]{:S(2)}, u32[]{:S(2)}) async-start(f32[32,4,4,128]{3,2,1,0:T(4,128)} %get-tuple-element.44), calls=%async_computation | async-start | bytes 524288 | tf_op jit(solution)/shard_map/all_to_all | solution.py:656
  24.4 3.5 %collective-permute-start.3 = (f32[7,24,4,128]{3,2,1,0:T(4,128)S(1)}, f32[7,24,4,128]{3,2,1,0:T(4,128)S(1)}, u32[]{:S(2)}, u32[]{:S(2)}) collective-permute-start(f32[7,24,4,128]{3,2,1,0:T(4,128)S(1)} %get-tuple-element.39), channel_id=1, source_target_pairs={{4,8},{8,4},{5,9},{9,5},{6,10},{10,6},{7,11},{11,7},{20,24},{24,20... | collective-permute-start | bytes 1032200 | tf_op jit(solution)/shard_map/ppermute | solution.py:614
  28.0 6.4 %collective-permute-done.3.refs_8_ = f32[7,24,4,128]{3,2,1,0:T(4,128)S(1)} collective-permute-done((f32[7,24,4,128]{3,2,1,0:T(4,128)S(1)}, f32[7,24,4,128]{3,2,1,0:T(4,128)S(1)}, u32[]{:S(2)}, u32[]{:S(2)}) %collective-permute-start.3) | collective-permute-done | bytes 344096 | tf_op jit(solution)/shard_map/ppermute | solution.py:614
  34.3 3.9 %shard_map.68 = (f32[5,8,8,128]{3,2,1,0:T(8,128)S(1)}, f32[5,4,8,128]{3,2,1,0:T(8,128)S(1)}, f32[24,24,128]{2,1,0:T(8,128)S(1)}, f32[24,24,128]{2,1,0:T(8,128)S(...) custom-call(s32[1]{0:T(128)} %bitcast.where_ref, ...), custom_call_target="tpu_custom_call" | custom-call | bytes 14400000 | tf_op jit(solution)/shard_map/pallas_call | solution.py:595
  38.2 0.7 copy-done.6
  38.9 0.7 copy-done.8
  39.6 0.7 copy-done.10
  40.4 0.7 copy-done.12
  41.1 0.7 copy-done.14
  41.8 0.7 copy-done.16
  42.5 1.1 %collective-permute-start.5 = (f32[5,4,8,128]{3,2,1,0:T(8,128)S(1)}, f32[5,4,8,128]{3,2,1,0:T(8,128)S(1)}, u32[]{:S(2)}, u32[]{:S(2)}) collective-permute-start(f32[5,4,8,128]{3,2,1,0:T(8,128)S(1)} %get-tuple-element.43), channel_id=1, source_target_pairs={{0,16},{16,0},{1,17},{17,1},{2,18},{18,2},{3,19},{19,3},{4,20},{20... | collective-permute-start | bytes 245768 | tf_op jit(solution)/shard_map/ppermute | solution.py:614
  43.6 2.2 %collective-permute-done.5.refs_0_ = f32[5,4,8,128]{3,2,1,0:T(8,128)S(1)} collective-permute-done((f32[5,4,8,128]{3,2,1,0:T(8,128)S(1)}, f32[5,4,8,128]{3,2,1,0:T(8,128)S(1)}, u32[]{:S(2)}, u32[]{:S(2)}) %collective-permute-start.5) | collective-permute-done | bytes 81952 | tf_op jit(solution)/shard_map/ppermute | solution.py:614
  45.9 4.2 %collective-permute-start.6 = (f32[5,16,4,128]{3,2,1,0:T(4,128)S(1)}, f32[5,16,4,128]{3,2,1,0:T(4,128)S(1)}, u32[]{:S(2)}, u32[]{:S(2)}) collective-permute-start(f32[5,16,4,128]{3,2,1,0:T(4,128)S(1)} %get-tuple-element.45), channel_id=1, source_target_pairs={{4,8},{8,4},{5,9},{9,5},{6,10},{10,6},{7,11},{11,7},{20,24},{24,20... | collective-permute-start | bytes 491528 | tf_op jit(solution)/shard_map/ppermute | solution.py:614
  50.1 2.9 %collective-permute-done.6.refs_1_ = f32[5,16,4,128]{3,2,1,0:T(4,128)S(1)} collective-permute-done((f32[5,16,4,128]{3,2,1,0:T(4,128)S(1)}, f32[5,16,4,128]{3,2,1,0:T(4,128)S(1)}, u32[]{:S(2)}, u32[]{:S(2)}) %collective-permute-start.6) | collective-permute-done | bytes 163872 | tf_op jit(solution)/shard_map/ppermute | solution.py:614
  53.1 1.0 %shard_map.70 = (f32[32,4,128]{2,1,0:T(4,128)}, f32[6,16,16,128]{3,2,1,0:T(8,128)S(1)}) custom-call(s32[1]{0:T(128)} %bitcast.where_ref, f32[5,8,8,128]{3,2,1,0:T(8,128)S(1)} %get-tuple-element.42.ring, f32[5,4,8,128]{3,2,1,0:T(8,128)S(1)} %collective-permute-done.5.refs_0_, f32[5,16,4,128]{3,2,1,0:T(4,128)S(1)} %collective-permute-done.6.refs_1_, ...), custom_call_target="tpu_custom_call" | custom-call | bytes 3600000 | tf_op jit(solution)/shard_map/pallas_call | solution.py:595
  54.1 5.6 %all-to-all-start.1 = ((f32[32,4,128]{2,1,0:T(4,128)}), f32[32,4,128]{2,1,0:T(4,128)S(1)}, u32[]{:S(2)}, u32[]{:S(2)}) async-start(f32[32,4,128]{2,1,0:T(4,128)} %get-tuple-element.47), calls=%async_computation.1 | async-start | bytes 131072 | tf_op jit(solution)/shard_map/all_to_all | solution.py:694
  59.7 0.8 %shard_map.71 = (f32[5,8,16,128]{3,2,1,0:T(8,128)S(1)}, f32[5,4,16,128]{3,2,1,0:T(8,128)S(1)}, f32[5,2,16,128]{3,2,1,0:T(8,128)S(1)}, f32[5,1,16,128]{3,2,1,0:T(8,128)S(1)}) custom-call(f32[32,4,4,128]{3,2,1,0:T(4,128)S(1)} %all-to-all-done.refs_1_.gathered), custom_call_target="tpu_custom_call" | custom-call | bytes 7200000 | tf_op jit(solution)/shard_map/pallas_call | solution.py:595
  60.5 6.0 %all-to-all-done.1.gathered = f32[32,4,128]{2,1,0:T(4,128)S(1)} async-done(((f32[32,4,128]{2,1,0:T(4,128)}), f32[32,4,128]{2,1,0:T(4,128)S(1)}, u32[]{:S(2)}, u32[]{:S(2)}) %all-to-all-start.1) | async-done | bytes 65568 | tf_op jit(solution)/shard_map/all_to_all | solution.py:694
  66.5 1.0 %copy-done.7 = f32[24,24,128]{2,1,0:T(8,128)S(1)} copy-done((f32[24,24,128]{2,1,0:T(8,128)S(1)}, f32[24,24,128]{2,1,0:T(8,128)}, u32[]{:S(2)}) %copy-start.7) | copy-done | bytes 294936
  67.5 1.0 %copy-done.9 = f32[24,24,128]{2,1,0:T(8,128)S(1)} copy-done((f32[24,24,128]{2,1,0:T(8,128)S(1)}, f32[24,24,128]{2,1,0:T(8,128)}, u32[]{:S(2)}) %copy-start.9) | copy-done | bytes 294936
  68.4 1.0 %copy-done.11 = f32[24,24,128]{2,1,0:T(8,128)S(1)} copy-done((f32[24,24,128]{2,1,0:T(8,128)S(1)}, f32[24,24,128]{2,1,0:T(8,128)}, u32[]{:S(2)}) %copy-start.11) | copy-done | bytes 294936
  69.4 1.0 %copy-done.13 = f32[24,24,128]{2,1,0:T(8,128)S(1)} copy-done((f32[24,24,128]{2,1,0:T(8,128)S(1)}, f32[24,24,128]{2,1,0:T(8,128)}, u32[]{:S(2)}) %copy-start.13) | copy-done | bytes 294936
  70.4 1.0 %copy-done.15 = f32[24,24,128]{2,1,0:T(8,128)S(1)} copy-done((f32[24,24,128]{2,1,0:T(8,128)S(1)}, f32[24,24,128]{2,1,0:T(8,128)}, u32[]{:S(2)}) %copy-start.15) | copy-done | bytes 294936
  71.3 1.0 %copy-done.17 = f32[24,24,128]{2,1,0:T(8,128)S(1)} copy-done((f32[24,24,128]{2,1,0:T(8,128)S(1)}, f32[24,24,128]{2,1,0:T(8,128)}, u32[]{:S(2)}) %copy-start.17) | copy-done | bytes 294936
  72.3 4.7 %shard_map.72 = f32[16,16,128]{2,1,0:T(8,128)} custom-call(s32[1]{0:T(128)} %bitcast.where_ref, f32[32,4,128]{2,1,0:T(4,128)S(1)} %all-to-all-done.1.gathered, f32[6,16,16,128]{3,2,1,0:T(8,128)S(1)} %get-tuple-element.48.level1, f32[24,24,128]{2,1,0:T(8,128)S(1)} %get-tuple-element.49.refs_0_, f32[24,24,128]{2,1,0:T(8,128)S(1)} %get-tuple-element.50.refs_1_, ...), custom_call_target="tpu_custom_call" | custom-call | bytes 14400000 | tf_op jit(solution)/shard_map/pallas_call | solution.py:595
  (33 shorter events, 0.5 us)
Async XLA Ops:
  0.0 6.4 %copy-start = (f32[16,16,128]{2,1,0:T(8,128)S(1)}, f32[16,16,128]{2,1,0:T(8,128)}, u32[]{:S(2)}) copy-start(f32[16,16,128]{2,1,0:T(8,128)} %refs_0_.9) | copy-start | bytes 393220
  0.0 6.4 %copy-start.1 = (f32[16,16,128]{2,1,0:T(8,128)S(1)}, f32[16,16,128]{2,1,0:T(8,128)}, u32[]{:S(2)}) copy-start(f32[16,16,128]{2,1,0:T(8,128)} %refs_1_.9) | copy-start | bytes 393220
  0.0 6.4 %copy-start.2 = (f32[16,16,128]{2,1,0:T(8,128)S(1)}, f32[16,16,128]{2,1,0:T(8,128)}, u32[]{:S(2)}) copy-start(f32[16,16,128]{2,1,0:T(8,128)} %refs_2_.9) | copy-start | bytes 393220
  0.0 6.4 %copy-start.3 = (f32[16,16,128]{2,1,0:T(8,128)S(1)}, f32[16,16,128]{2,1,0:T(8,128)}, u32[]{:S(2)}) copy-start(f32[16,16,128]{2,1,0:T(8,128)} %refs_3_.9) | copy-start | bytes 393220
  0.0 6.4 %copy-start.4 = (f32[16,16,128]{2,1,0:T(8,128)S(1)}, f32[16,16,128]{2,1,0:T(8,128)}, u32[]{:S(2)}) copy-start(f32[16,16,128]{2,1,0:T(8,128)} %refs_4_.9) | copy-start | bytes 393220
  0.0 6.4 %copy-start.5 = (f32[16,16,128]{2,1,0:T(8,128)S(1)}, f32[16,16,128]{2,1,0:T(8,128)}, u32[]{:S(2)}) copy-start(f32[16,16,128]{2,1,0:T(8,128)} %refs_5_.9) | copy-start | bytes 393220
  2.4 4.0 %collective-permute-start = (f32[8,16,128]{2,1,0:T(8,128)}, f32[8,16,128]{2,1,0:T(8,128)S(1)}, u32[]{:S(2)}, u32[]{:S(2)}) collective-permute-start(f32[8,16,128]{2,1,0:T(8,128)} %get-tuple-element.35), channel_id=1, source_target_pairs={{0,1},{1,0},{2,3},{3,2},{4,5},{5,4},{6,7},{7,6},{8,9},{9,8},{10,11... | collective-permute-start | bytes 196616 | tf_op jit(solution)/shard_map/ppermute | solution.py:614
  4.5 1.9 %collective-permute-start.1 = (f32[8,16,128]{2,1,0:T(8,128)}, f32[8,16,128]{2,1,0:T(8,128)S(1)}, u32[]{:S(2)}, u32[]{:S(2)}) collective-permute-start(f32[8,16,128]{2,1,0:T(8,128)} %get-tuple-element.36), channel_id=1, source_target_pairs={{1,2},{2,1},{5,6},{6,5},{9,10},{10,9},{13,14},{14,13},{17,18},{18,... | collective-permute-start | bytes 196616 | tf_op jit(solution)/shard_map/ppermute | solution.py:614
  6.6 5.6 %collective-permute-start.2 = (f32[7,4,16,128]{3,2,1,0:T(8,128)S(1)}, f32[7,4,16,128]{3,2,1,0:T(8,128)S(1)}, u32[]{:S(2)}, u32[]{:S(2)}) collective-permute-start(f32[7,4,16,128]{3,2,1,0:T(8,128)S(1)} %get-tuple-element.38), channel_id=1, source_target_pairs={{0,16},{16,0},{1,17},{17,1},{2,18},{18,2},{3,19},{19,3},{4,20},{20... | collective-permute-start | bytes 688136 | tf_op jit(solution)/shard_map/ppermute | solution.py:614
  13.7 32.1 %all-to-all-start = ((f32[32,4,4,128]{3,2,1,0:T(4,128)}), f32[32,4,4,128]{3,2,1,0:T(4,128)S(1)}, u32[]{:S(2)}, u32[]{:S(2)}) async-start(f32[32,4,4,128]{3,2,1,0:T(4,128)} %get-tuple-element.44), calls=%async_computation | async-start | bytes 524288 | tf_op jit(solution)/shard_map/all_to_all | solution.py:656
  24.4 10.0 %collective-permute-start.3 = (f32[7,24,4,128]{3,2,1,0:T(4,128)S(1)}, f32[7,24,4,128]{3,2,1,0:T(4,128)S(1)}, u32[]{:S(2)}, u32[]{:S(2)}) collective-permute-start(f32[7,24,4,128]{3,2,1,0:T(4,128)S(1)} %get-tuple-element.39), channel_id=1, source_target_pairs={{4,8},{8,4},{5,9},{9,5},{6,10},{10,6},{7,11},{11,7},{20,24},{24,20... | collective-permute-start | bytes 1032200 | tf_op jit(solution)/shard_map/ppermute | solution.py:614
  27.9 6.4 %collective-permute-start.4 = (f32[7,24,4,128]{3,2,1,0:T(4,128)S(1)}, f32[7,24,4,128]{3,2,1,0:T(4,128)S(1)}, u32[]{:S(2)}, u32[]{:S(2)}) collective-permute-start(f32[7,24,4,128]{3,2,1,0:T(4,128)S(1)} %get-tuple-element.40), channel_id=1, source_target_pairs={{0,4},{4,0},{8,12},{12,8},{1,5},{5,1},{9,13},{13,9},{2,6},{6,2},{1... | collective-permute-start | bytes 1032200 | tf_op jit(solution)/shard_map/ppermute | solution.py:614
  38.2 0.7 copy-start.6
  38.9 0.7 copy-start.8
  39.6 0.7 copy-start.10
  40.4 0.7 copy-start.12
  41.1 0.7 copy-start.14
  41.8 0.7 copy-start.16
  42.5 3.3 %collective-permute-start.5 = (f32[5,4,8,128]{3,2,1,0:T(8,128)S(1)}, f32[5,4,8,128]{3,2,1,0:T(8,128)S(1)}, u32[]{:S(2)}, u32[]{:S(2)}) collective-permute-start(f32[5,4,8,128]{3,2,1,0:T(8,128)S(1)} %get-tuple-element.43), channel_id=1, source_target_pairs={{0,16},{16,0},{1,17},{17,1},{2,18},{18,2},{3,19},{19,3},{4,20},{20... | collective-permute-start | bytes 245768 | tf_op jit(solution)/shard_map/ppermute | solution.py:614
  45.9 7.2 %collective-permute-start.6 = (f32[5,16,4,128]{3,2,1,0:T(4,128)S(1)}, f32[5,16,4,128]{3,2,1,0:T(4,128)S(1)}, u32[]{:S(2)}, u32[]{:S(2)}) collective-permute-start(f32[5,16,4,128]{3,2,1,0:T(4,128)S(1)} %get-tuple-element.45), channel_id=1, source_target_pairs={{4,8},{8,4},{5,9},{9,5},{6,10},{10,6},{7,11},{11,7},{20,24},{24,20... | collective-permute-start | bytes 491528 | tf_op jit(solution)/shard_map/ppermute | solution.py:614
  50.1 3.0 %collective-permute-start.7 = (f32[5,16,4,128]{3,2,1,0:T(4,128)S(1)}, f32[5,16,4,128]{3,2,1,0:T(4,128)S(1)}, u32[]{:S(2)}, u32[]{:S(2)}) collective-permute-start(f32[5,16,4,128]{3,2,1,0:T(4,128)S(1)} %get-tuple-element.46), channel_id=1, source_target_pairs={{0,4},{4,0},{8,12},{12,8},{1,5},{5,1},{9,13},{13,9},{2,6},{6,2},{1... | collective-permute-start | bytes 491528 | tf_op jit(solution)/shard_map/ppermute | solution.py:614
  54.1 12.4 %all-to-all-start.1 = ((f32[32,4,128]{2,1,0:T(4,128)}), f32[32,4,128]{2,1,0:T(4,128)S(1)}, u32[]{:S(2)}, u32[]{:S(2)}) async-start(f32[32,4,128]{2,1,0:T(4,128)} %get-tuple-element.47), calls=%async_computation.1 | async-start | bytes 131072 | tf_op jit(solution)/shard_map/all_to_all | solution.py:694
  66.5 1.0 %copy-start.7 = (f32[24,24,128]{2,1,0:T(8,128)S(1)}, f32[24,24,128]{2,1,0:T(8,128)}, u32[]{:S(2)}) copy-start(f32[24,24,128]{2,1,0:T(8,128)} %copy-done.6) | copy-start | bytes 884740
  67.5 1.0 %copy-start.9 = (f32[24,24,128]{2,1,0:T(8,128)S(1)}, f32[24,24,128]{2,1,0:T(8,128)}, u32[]{:S(2)}) copy-start(f32[24,24,128]{2,1,0:T(8,128)} %copy-done.8) | copy-start | bytes 884740
  68.4 1.0 %copy-start.11 = (f32[24,24,128]{2,1,0:T(8,128)S(1)}, f32[24,24,128]{2,1,0:T(8,128)}, u32[]{:S(2)}) copy-start(f32[24,24,128]{2,1,0:T(8,128)} %copy-done.10) | copy-start | bytes 884740
  69.4 1.0 %copy-start.13 = (f32[24,24,128]{2,1,0:T(8,128)S(1)}, f32[24,24,128]{2,1,0:T(8,128)}, u32[]{:S(2)}) copy-start(f32[24,24,128]{2,1,0:T(8,128)} %copy-done.12) | copy-start | bytes 884740
  70.4 1.0 %copy-start.15 = (f32[24,24,128]{2,1,0:T(8,128)S(1)}, f32[24,24,128]{2,1,0:T(8,128)}, u32[]{:S(2)}) copy-start(f32[24,24,128]{2,1,0:T(8,128)} %copy-done.14) | copy-start | bytes 884740
  71.3 1.0 %copy-start.17 = (f32[24,24,128]{2,1,0:T(8,128)S(1)}, f32[24,24,128]{2,1,0:T(8,128)}, u32[]{:S(2)}) copy-start(f32[24,24,128]{2,1,0:T(8,128)} %copy-done.16) | copy-start | bytes 884740

commit v7 on v6

--- a/solution.py
+++ b/solution.py
@@ -121,15 +121,67 @@
     return KEEP * values + weight * (rhs + pull(values, faces, step))
 
 
-def pack_z_kernel(where_ref, *refs):
-    ins, (first, second) = refs[:6], refs[6:]
-    odd = position(where_ref)[2] % 2
+def faces_x(values, odd, n_x, width):
+    head, tail = values[:, :width], values[:, values.shape[1] - width:]
+    return [pick(odd, head, tail), pick(odd, tail, head)][:n_x]
+
+
+def faces_y(values, odd, width):
+    head, tail = values[:, :width], values[:, values.shape[1] - width:]
+    return pick(odd, head, tail), pick(odd, tail, head)
+
+
+def corner_sends(below, above, odd, corners):
+    packs = []
+    for rows, sign in ((slice(0, 8), 1), (slice(below.shape[1] - 8, below.shape[1]), -1)):
+        low = [below[3 - i, rows] for i in range(4)]
+        high = [above[i, rows] for i in range(4)]
+        pack = []
+        if corners:
+            pack = [low[0], high[0]]
+            low, high = low[1:], high[1:]
+        row = iota2(low[0].shape, 0)
+        row = row if sign == 1 else 7 - row
+        pack += [
+            jnp.where(row < 3, low[0], turn(low[2], 3 * sign, 0)),
+            jnp.where(row < 2, low[1], turn(high[1], 2 * sign, 0)),
+            jnp.where(row < 3, high[0], turn(high[2], 3 * sign, 0)),
+        ]
+        packs.append([p[:4] if sign == 1 else p[4:] for p in pack])
+    return [(pick(odd, h, t), pick(odd, t, h)) for h, t in zip(*packs)]
+
+
+def corner_tiles(tiles):
+    first, second, third = tiles[-3:]
+    upper = iota2(first.shape, 0) < 4
+
+    def inner(tile, by):
+        return jnp.where(upper, turn(tile, -by, 0), turn(tile, by, 0))
+
+    low = [first, second, inner(first, 3)]
+    high = [third, inner(second, 2), inner(third, 3)]
+    if len(tiles) == 5:
+        low, high = tiles[:1] + low, tiles[1:2] + high
+    else:
+        zero = jnp.zeros_like(first)
+        low, high = low + [zero], high + [zero]
+    return low[::-1], high
+
+
+def faces_kernel(counts, where_ref, *refs):
+    ins, refs = refs[:6], refs[6:]
+    n_x = 1 if counts[0] == 2 else 2
+    sends_x, (two_y, one_y, first, second) = refs[:n_x], refs[n_x:]
+    odd_x, odd_y, odd = (place % 2 for place in position(where_ref))
     sx, sy, sz = ins[0].shape
     half = sx // 2
     lane = lane_of((half, sy, LANES))
     head = jnp.zeros((half, sy, LANES), F32)
     tail = head
     for a, ref in enumerate(ins):
+        for send, face in zip(sends_x, faces_x(ref[...][None], odd_x, n_x, HALO)):
+            send[a] = face[0]
+        one_y[a], two_y[a] = faces_y(ref[...], odd_y, HALO)
         for g in range(2):
             values = ref[g * half:(g + 1) * half]
             at = SIDE * g + PLACE[a]
@@ -140,33 +192,29 @@
     second[...] = pick(odd, tail, head)
 
 
-def face_x_kernel(counts, where_ref, *refs):
-    ins, one_ref, two_ref = refs[:6], refs[6], refs[7]
-    zpack, sends = refs[8], refs[9:]
-    sx, sy, sz = ins[0].shape
-    half = sx // 2
-    below, above = neighbours(counts[2], position(where_ref)[2] % 2, one_ref[...], two_ref[...])
+def halo_z_kernel(counts, where_ref, one_ref, two_ref, zpack, *sends):
+    odd_x, _, odd = (place % 2 for place in position(where_ref))
+    half = one_ref.shape[0]
+    below, above = neighbours(counts[2], odd, one_ref[...], two_ref[...])
     lane = lane_of(below.shape)
     zpack[:half] = jnp.where(lane < SIDE, above, turn(below, SIDE, 2))
     zpack[half:] = jnp.where(lane < SIDE, turn(above, SIDE, 2), below)
-    odd = position(where_ref)[0] % 2
-    for k, send in enumerate(sends):
-        start = (1 - odd if k == 0 else odd) * (sx - HALO)
-        for a, ref in enumerate(tuple(ins) + (zpack,)):
-            send[a] = ref[pl.ds(start, HALO)]
-
-
-def face_y_kernel(counts, where_ref, *refs):
-    ins, halos, sends = refs[:7], refs[7:-2], refs[:-3:-1]
-    sx, sy, sz = ins[0].shape
+    for send, face in zip(sends, faces_x(zpack[...][None], odd_x, len(sends), HALO)):
+        send[...] = face[0]
+
+
+def corners_kernel(counts, where_ref, zpack, *refs):
+    n_x = 1 if counts[0] == 2 else 2
+    main_x, halos_x, (two_y, one_y) = refs[:n_x], refs[n_x:2 * n_x], refs[2 * n_x:]
     odd_x, odd = (place % 2 for place in position(where_ref)[:2])
-    for a, ref in enumerate(ins):
-        below, above = neighbours(counts[0], odd_x, halos[0][a], halos[-1][a])
-        for at, block in ((0, below), (HALO, ref[...]), (HALO + sx, above)):
-            head, tail = block[:, :HALO], block[:, sy - HALO:]
-            span = slice(at, at + block.shape[0])
-            sends[0][a, span] = pick(odd, head, tail)
-            sends[1][a, span] = pick(odd, tail, head)
+    for a in range(7):
+        if a < 6:
+            below, above = neighbours(counts[0], odd_x, main_x[0][a], main_x[-1][a])
+        else:
+            below, above = neighbours(counts[0], odd_x, halos_x[0][...], halos_x[-1][...])
+        for n, pair in enumerate(corner_sends(below, above, odd, False)):
+            one_y[3 * a + n], two_y[3 * a + n] = pair
+    one_y[21:], two_y[21:] = faces_y(zpack[...], odd, HALO)
 
 
 def each(first, last, step, body):
@@ -233,18 +281,20 @@
     return factor * times_table(flat, table).reshape(count, x1, y1, LANES)
 
 
-def coefficient_kernel(counts, devices, where_ref, *refs):
+def coefficient_kernel(counts, where_ref, *refs):
     ins, refs = refs[2:7], refs[7:]
     n_x = 1 if counts[0] == 2 else 2
-    halos_x, (copies, coeffs1, halo, sums, pairing) = refs[:n_x], refs[n_x:]
+    main_x, halos_x = refs[:n_x], refs[n_x:2 * n_x]
+    coarse2, coeffs1, halo, sums, pairing = refs[2 * n_x:]
     sx, sy, sz = ins[0].shape
     odd_x = position(where_ref)[0] % 2
     x1, y1 = sx // 2, sy // 2
     lane = lane_of((sx, sy, LANES))
     lanes = [slice(k * LANES, (k + 1) * LANES) for k in range(2)]
     edge_lane = lane_of((1, sy, LANES))
-    below, _ = neighbours(counts[0], odd_x, halos_x[0][3, HALO - 1:], halos_x[-1][3, HALO - 1:])
-    packed, _ = neighbours(counts[0], odd_x, halos_x[0][6, HALO - 1:], halos_x[-1][6, HALO - 1:])
+    last = slice(HALO - 1, HALO)
+    below, _ = neighbours(counts[0], odd_x, main_x[0][3, last], main_x[-1][3, last])
+    packed, _ = neighbours(counts[0], odd_x, halos_x[0][last], halos_x[-1][last])
     for k, edge in enumerate((below, unpacked(packed, 3, edge_lane))):
         halo[k, 0:1] = edge
         sums[4, 0, :, lanes[k]] = rows_of(halo.at[k], 0, (0,), BOTH)
@@ -271,17 +321,16 @@
     )
     for n, (values, *odd_axes, factor) in enumerate(parts):
         pairing[n] = values
-        packed = level2_rows(pairing.at[n], odd_axes, factor, x1 // 2, y1 // 2, sz // 4)
-        for d in range(devices):
-            copies[d, n] = packed
+        coarse2[n] = level2_rows(pairing.at[n], odd_axes, factor, x1 // 2, y1 // 2, sz // 4)
 
 
 def down_kernel(counts, where_ref, *refs):
     ins, refs = refs[:7], refs[7:]
     n_x = 1 if counts[0] == 2 else 2
-    halos_x = refs[:n_x]
-    two_y, one_y, coeffs1, own1 = refs[n_x:4 + n_x]
-    sends, refs = refs[4 + n_x:4 + 2 * n_x], refs[4 + 2 * n_x:]
+    main_x, halos_x = refs[:n_x], refs[n_x:2 * n_x]
+    main_two, main_one, rest_two, rest_one, coeffs1, own1 = refs[2 * n_x:6 + 2 * n_x]
+    refs = refs[6 + 2 * n_x:]
+    sends, near_two, near_one, refs = refs[:n_x], refs[n_x], refs[n_x + 1], refs[n_x + 2:]
     kept_m, kept_h, weight_m, weight_h = refs[:4]
     faces_out, scratch = refs[4:12], refs[12:]
     rhs, bx, by, bz = zip(faces_out[::2], faces_out[1::2])
@@ -292,14 +341,26 @@
     ex, ey = sx + 2 * HALO, sy + 2 * HALO
     odd_x, odd_y = (place % 2 for place in position(where_ref)[:2])
 
+    rest = neighbours(counts[1], odd_y, rest_one[...], rest_two[...])
+    rest = jnp.concatenate(rest[::-1], axis=1)
     for a in range(7):
-        to = packs if a == 6 else arrays[a][0]
-        below, above = neighbours(counts[0], odd_x, halos_x[0][a], halos_x[-1][a])
+        if a < 6:
+            to = arrays[a][0]
+            below, above = neighbours(counts[0], odd_x, main_x[0][a], main_x[-1][a])
+            rows = neighbours(counts[1], odd_y, main_one[a], main_two[a])
+            rows = jnp.concatenate(rows[::-1], axis=1)
+        else:
+            to = packs
+            below, above = neighbours(counts[0], odd_x, halos_x[0][...], halos_x[-1][...])
+            rows = rest[21:]
         to[:HALO, :sy] = below
         to[HALO:HALO + sx, :sy] = ins[a][...]
         to[HALO + sx:, :sy] = above
-        below, above = neighbours(counts[1], odd_y, one_y[a], two_y[a])
-        to[:, sy:] = jnp.concatenate([above, below], axis=1)
+        to[HALO:HALO + sx, sy:] = rows
+        low, high = corner_tiles([rest[3 * a + n] for n in range(3)])
+        for n in range(HALO):
+            to[n, sy:] = low[n]
+            to[HALO + sx + n, sy:] = high[n]
     lane = lane_of((ey, LANES))
 
     def unpack(x):
@@ -357,9 +418,9 @@
     weight1 = relaxer(coeffs1[0], coeffs1[1] + low_y)
     for n, values in enumerate((2.0 * rhs1, weight1, coeffs1[2], coeffs1[3], coeffs1[4])):
         own1[n] = values
-        head, tail = values[:NEAR], values[x1 - NEAR:]
-        for k, send in enumerate(sends):
-            send[n] = pick(odd_x, head, tail) if k == 0 else pick(odd_x, tail, head)
+        for send, face in zip(sends, faces_x(values[None], odd_x, n_x, NEAR)):
+            send[n] = face[0]
+        near_one[n], near_two[n] = faces_y(values, odd_y, NEAR)
 
 
 def level2_rows(source, odd_axes, factor, x2, y2, z2):
@@ -381,31 +442,34 @@
     return packed
 
 
-def near_y_kernel(counts, where_ref, ring, *refs):
-    refs = refs[:-3] + refs[-2:]
-    halos, sends = refs[:-2], refs[:-3:-1]
-    n, bx, by, _ = ring.shape
+def near_corners_kernel(counts, where_ref, *refs):
+    halos_x, (two_y, one_y) = refs[:-2], refs[-2:]
     odd_x, odd = (place % 2 for place in position(where_ref)[:2])
-    for a in range(n):
-        below, above = neighbours(counts[0], odd_x, halos[0][a], halos[-1][a])
-        block = jnp.concatenate([below, ring[a], above], axis=0)
-        head, tail = block[:, :NEAR], block[:, by - NEAR:]
-        sends[0][a] = pick(odd, head, tail)
-        sends[1][a] = pick(odd, tail, head)
+    for a in range(halos_x[0].shape[0]):
+        below, above = neighbours(counts[0], odd_x, halos_x[0][a], halos_x[-1][a])
+        for n, pair in enumerate(corner_sends(below, above, odd, True)):
+            one_y[5 * a + n], two_y[5 * a + n] = pair
 
 
 def near_kernel(counts, devices, where_ref, ring, *refs):
     n_x = 1 if counts[0] == 2 else 2
     halos_x = refs[:n_x]
-    two_y, one_y, copies, level1, left = refs[n_x:]
+    main_two, main_one, rest_two, rest_one, coarse2, copies, level1, left = refs[n_x:]
     n, bx1, by1, _ = ring.shape
     odd_x, odd_y = (place % 2 for place in position(where_ref)[:2])
+    rest = neighbours(counts[1], odd_y, rest_one[...], rest_two[...])
+    rest = jnp.concatenate(rest[::-1], axis=1)
     whole = []
     for a in range(n):
         below, above = neighbours(counts[0], odd_x, halos_x[0][a], halos_x[-1][a])
+        rows = neighbours(counts[1], odd_y, main_one[a], main_two[a])
+        rows = jnp.concatenate(rows[::-1], axis=1)
+        low, high = corner_tiles([rest[5 * a + k] for k in range(5)])
+        rows = jnp.concatenate(
+            [tile[None] for tile in low] + [rows] + [tile[None] for tile in high], axis=0
+        )
         block = jnp.concatenate([below, ring[a], above], axis=0)
-        below, above = neighbours(counts[1], odd_y, one_y[a], two_y[a])
-        whole.append(jnp.concatenate([block, above, below], axis=1))
+        whole.append(jnp.concatenate([block, rows], axis=1))
     rhs1, weight1 = whole[:2]
     faces1 = tuple(whole[2:])
     field1 = weight1 * rhs1
@@ -419,7 +483,9 @@
     left[...] = remain
     packed = level2_rows(left, (False,) * 3, 0.125, bx1 // 2, by1 // 2, LANES // 4)
     for d in range(devices):
-        copies[d] = packed
+        copies[d, 0] = packed
+        for a in range(n - 1):
+            copies[d, a + 1] = coarse2[a]
 
 
 def halve(values, odd_axis, step):
@@ -502,33 +568,19 @@
                     whole[i * x2 + x, j * y2:(j + 1) * y2, lanes] = total
 
 
-def coarse_kernel(counts, gathered, *refs):
-    outs, whole = refs[:-1], refs[-1]
-    y2 = gathered.shape[2]
-    z2 = LANES * counts[0] // whole.shape[1]
-    for a in range(4):
-        spread_out(counts, gathered.at[:, a], whole.at[a])
-    faces = (whole[1], whole[2], whole[3])
-    levels = coarse_levels(whole[0], faces, counts[1] * y2, counts[2] * z2)
-    for out, (diag, weight, coupled) in zip(outs, levels):
-        for n, values in enumerate((diag, weight) + coupled):
-            out[n] = values
-
-
 def up_kernel(counts, where_ref, gathered, level1, *refs):
     kept, weight, rhs, bx, by, bz = zip(refs[0:12:2], refs[1:12:2])
-    depth = LEVELS - 2
-    coarse, refs = refs[12:12 + depth], refs[12 + depth:]
-    out, whole, second, spread_m, spread_h, field_m, field_h, half_m, half_h = refs
+    out, whole, second, spread_m, spread_h, field_m, field_h, half_m, half_h = refs[12:]
     gx, gy, gz = counts
     at_x, at_y, at_z = position(where_ref)
     sx, sy, sz = out.shape
     x1, y1 = sx // 2, sy // 2
     x2, y2, z2 = x1 // 2, y1 // 2, sz // 4
     columns = max(LANES, gz * z2)
-    spread_out(counts, gathered, whole)
-    levels = [(ref[0], ref[1], (ref[2], ref[3], ref[4])) for ref in coarse]
-    correction = coarse_cycle(2, whole[...], levels)
+    for a in range(5):
+        spread_out(counts, gathered.at[:, a], whole.at[a])
+    levels = coarse_levels(whole[1], (whole[2], whole[3], whole[4]), gy * y2, gz * z2)
+    correction = coarse_cycle(2, whole[0], levels)
 
     wide = gx * x2
     half = NEAR // 2
@@ -627,77 +679,79 @@
     ex, ey = sx + 2 * HALO, sy + 2 * HALO
     fine = (ex, ey, LANES)
 
-    sends = run(pack_z_kernel, [(sx // 2, sy, LANES)] * 2, where, ins, grant=60)
-    got = swaps("gz", sends)
+    *sends_x, two_y, one_y, first, second = run(
+        functools.partial(faces_kernel, counts),
+        [(6, HALO, sy, LANES)] * n_x
+        + [(6, sx, HALO, LANES)] * 2
+        + [(sx // 2, sy, LANES)] * 2,
+        where,
+        ins,
+        grant=60,
+    )
+    main_x = tuple(swaps("gx", sends_x))
+    main_y = tuple(swaps("gy", (one_y, two_y))[::-1])
+    got = swaps("gz", (first, second))
     zpack, *sends = run(
-        functools.partial(face_x_kernel, counts),
-        [(sx, sy, LANES)] + [(7, HALO, sy, LANES)] * n_x,
+        functools.partial(halo_z_kernel, counts),
+        [(sx, sy, LANES)] + [(HALO, sy, LANES)] * n_x,
         where,
-        ins + tuple(got),
-    )
+        tuple(got),
+    )
+    halos_x = tuple(swaps("gx", sends))
+    two_y, one_y = run(
+        functools.partial(corners_kernel, counts),
+        [(21 + sx, HALO, LANES)] * 2,
+        where,
+        (zpack,) + main_x + halos_x,
+    )
+    rest_y = tuple(swaps("gy", (one_y, two_y))[::-1])
+    x1, y1 = sx // 2, sy // 2
     ins = ins + (zpack,)
-    got_x = swaps("gx", sends)
-    sends = run(
-        functools.partial(face_y_kernel, counts),
-        [(7, ex, HALO, LANES)] * 2,
+    coarse2, coeffs1 = run(
+        functools.partial(coefficient_kernel, counts),
+        [(4, y1 // 2, LANES), (5, x1, y1, LANES)],
         where,
-        ins + tuple(got_x),
-    )
-    two_y, one_y = swaps("gy", sends[::-1])[::-1]
-    x1, y1 = sx // 2, sy // 2
-    copies, coeffs1 = run(
-        functools.partial(coefficient_kernel, counts, devices),
-        [(devices, 4, y1 // 2, LANES), (5, x1, y1, LANES)],
-        where,
-        ins + tuple(got_x),
+        ins + main_x + halos_x,
         [(2, sx, sy, LANES), (5, x1, y1, 2 * LANES), (4, x1, y1, LANES)],
         micros=2,
     )
-    gathered = lax.all_to_all(copies, axes, 0, 0, tiled=True)
-    ring, *outs = run(
+    own1, *outs = run(
         functools.partial(down_kernel, counts),
-        [(5, x1, y1, LANES)] + [(5, NEAR, y1, LANES)] * n_x + [fine] * 12,
+        [(5, x1, y1, LANES)]
+        + [(5, NEAR, y1, LANES)] * n_x
+        + [(5, x1, NEAR, LANES)] * 2
+        + [fine] * 12,
         where,
-        ins + tuple(got_x) + (two_y, one_y, coeffs1),
+        ins + main_x + halos_x + main_y + rest_y + (coeffs1,),
         [fine] * 9 + [(2, x1, y1, 2 * LANES), (ey, LANES)],
         24,
         micros=4,
     )
-    sends, fine_arrays = outs[:n_x], outs[n_x:]
-
-    near_x = swaps("gx", sends)
-    sends = run(
-        functools.partial(near_y_kernel, counts),
-        [(5, x1 + 2 * NEAR, NEAR, LANES)] * 2,
-        where,
-        (ring,) + tuple(near_x) + (gathered,),
-    )
-    near_y = swaps("gy", sends[::-1])[::-1]
+    sends_x, (two_y, one_y), fine_arrays = outs[:n_x], outs[n_x:n_x + 2], outs[n_x + 2:]
+
+    near_x = tuple(swaps("gx", sends_x))
+    near_y = tuple(swaps("gy", (one_y, two_y))[::-1])
+    two_y, one_y = run(
+        functools.partial(near_corners_kernel, counts), [(25, NEAR, LANES)] * 2, where, near_x
+    )
+    rest_y = tuple(swaps("gy", (one_y, two_y))[::-1])
     copies, level1 = run(
         functools.partial(near_kernel, counts, devices),
-        [(devices, y1 // 2, LANES), (6, x1 + 2 * NEAR, y1 + 2 * NEAR, LANES)],
+        [(devices, 5, y1 // 2, LANES), (6, x1 + 2 * NEAR, y1 + 2 * NEAR, LANES)],
         where,
-        (ring,) + tuple(near_x) + tuple(near_y),
+        (own1,) + near_x + near_y + rest_y + (coarse2,),
         [(x1, y1 + 2 * NEAR, LANES)],
     )
 
+    gathered = lax.all_to_all(copies, axes, 0, 0, tiled=True)
     wide, rows = counts[0] * x1 // 2, counts[1] * y1 // 2
     columns = max(LANES, counts[2] * sz // 4)
-    levels = run(
-        functools.partial(coarse_kernel, counts),
-        [(5, wide >> n, rows, columns) for n in range(LEVELS - 2)],
-        (),
-        (gathered,),
-        [(4, wide, rows, columns)],
-        micros=2,
-    )
-    gathered = lax.all_to_all(copies, axes, 0, 0, tiled=True)
     (result,) = run(
         functools.partial(up_kernel, counts),
         [(sx, sy, sz)],
         where,
-        (gathered, level1) + tuple(fine_arrays) + tuple(levels),
-        [(wide, rows, columns), (wide + NEAR, rows, columns)]
+        (gathered, level1) + tuple(fine_arrays),
+        [(5, wide, rows, columns), (wide + NEAR, rows, columns)]
         + [(x1 + 2, ey, LANES)] * 2
         + [fine] * 4,
         24,

time: 78.3 us -> 60.3 us (0.77); the launches traced: 77 us -> 60.1 us
  blocking collectives: 0 us -> 18.9 us
  waiting for transfers between devices: 22.9 us -> 6.69 us
  local copies, waits for them, and re-layouts: 10.1 us -> 0.02 us
  starting transfers between devices: 29.2 us -> 21.2 us
  Pallas kernels: 14.6 us -> 13 us
    all_to_all x0 -> x1, blocking collectives: none -> 18.9 us  [local(): gathered = lax.all_to_all(copies, axes, 0, 0, tiled=True)]
    all_to_all x2 -> x0, starting transfers between devices: 16 us -> none  [local(): gathered = lax.all_to_all(copies, axes, 0, 0, tiled=True)]
    ppermute x8 -> x13, waiting for transfers between devices: 16.8 us -> 6.69 us  [swaps(): got.append(lax.ppermute(block, axis, pairs))]
    unnamed x36 -> x12, local copies, waits for them, and re-layouts: 10.1 us -> 0.02 us
    ppermute x8 -> x13, starting transfers between devices: 13.2 us -> 21.2 us  [swaps(): got.append(lax.ppermute(block, axis, pairs))]
    all_to_all x2 -> x0, waiting for transfers between devices: 6.05 us -> none  [local(): gathered = lax.all_to_all(copies, axes, 0, 0, tiled=True)]
    pallas_call x9 -> x8, Pallas kernels: 14.6 us -> 13 us  [run(): pl.pallas_call(kernel, out_shape=tuple((jax.ShapeDtypeStruct(shape, F32)...]
  transfers between devices with their start and end apart: 10 -> 13, of which waited for: 6 -> 4; matrix products, arithmetic and copies ran while one was open for 0% -> 0% of each run, Pallas kernels for 6% -> 2%
where the time goes in v7:
time: 60.3 us; the launch traced here: 60.1 us
  starting transfers between devices  21.2 us (35%)
  blocking collectives  18.9 us (31%)
  Pallas kernels  13 us (22%)
  waiting for transfers between devices  6.69 us (11%)
    ppermute x13, starting transfers between devices, swaps(): got.append(lax.ppermute(block, axis, pairs))  21.2 us
    all_to_all x1, blocking collectives, local(): gathered = lax.all_to_all(copies, axes, 0, 0, tiled=True)  18.9 us
    pallas_call x8, Pallas kernels, run(): pl.pallas_call(kernel, out_shape=tuple((jax.ShapeDtypeStruct(shape, F32)...  13 us
    ppermute x13, waiting for transfers between devices, swaps(): got.append(lax.ppermute(block, axis, pairs))  6.69 us
  transfers between devices with their start and end apart: 13, of which 4 were waited for; matrix products, arithmetic and copies ran while one was open for 0% of the time, Pallas kernels for 2%

profile of v7, /device:TPU:1, one launch (start us, length us, event | category | flops | bytes accessed | tf_op | source)
XLA Modules:
  0.0 60.1 jit_solution(7801852429672852691)
XLA Ops:
  0.0 2.6 %shard_map.64 = (f32[6,4,16,128]{3,2,1,0:T(8,128)}, f32[6,16,4,128]{3,2,1,0:T(4,128)}, f32[6,16,4,128]{3,2,1,0:T(4,128)}, f32[8,16,128]{2,1,0:T(8,128)}, f32[8,16,128]{2,1,0:T(8,128)}) custom-call(s32[1]{0:T(128)} %bitcast.where_ref, f32[16,16,128]{2,1,0:T(8,128)} %refs_0_.5, f32[16,16,128]{2,1,0:T(8,128)} %refs_1_.5, f32[16,16,128]{2,1,0:T(8,128)} %refs_2_.5, ...), custom_call_target="tpu_custom_call" | custom-call | bytes 3600000 | tf_op jit(solution)/shard_map/pallas_call | solution.py:647
  2.6 2.0 %collective-permute-start.2 = (f32[6,4,16,128]{3,2,1,0:T(8,128)}, f32[6,4,16,128]{3,2,1,0:T(8,128)S(1)}, u32[]{:S(2)}, u32[]{:S(2)}) collective-permute-start(f32[6,4,16,128]{3,2,1,0:T(8,128)} %get-tuple-element.39), channel_id=1, source_target_pairs={{0,16},{16,0},{1,17},{17,1},{2,18},{18,2},{3,19},{19,3},{4,20},{20... | collective-permute-start | bytes 589832 | tf_op jit(solution)/shard_map/ppermute | solution.py:666
  4.6 4.0 %collective-permute-start.4 = (f32[6,16,4,128]{3,2,1,0:T(4,128)}, f32[6,16,4,128]{3,2,1,0:T(4,128)S(1)}, u32[]{:S(2)}, u32[]{:S(2)}) collective-permute-start(f32[6,16,4,128]{3,2,1,0:T(4,128)} %get-tuple-element.41), channel_id=1, source_target_pairs={{4,8},{8,4},{5,9},{9,5},{6,10},{10,6},{7,11},{11,7},{20,24},{24,20... | collective-permute-start | bytes 589832 | tf_op jit(solution)/shard_map/ppermute | solution.py:666
  8.6 0.1 collective-permute-start.5
  8.7 1.4 %collective-permute-start = (f32[8,16,128]{2,1,0:T(8,128)}, f32[8,16,128]{2,1,0:T(8,128)S(1)}, u32[]{:S(2)}, u32[]{:S(2)}) collective-permute-start(f32[8,16,128]{2,1,0:T(8,128)} %get-tuple-element.36), channel_id=1, source_target_pairs={{0,1},{1,0},{2,3},{3,2},{4,5},{5,4},{6,7},{7,6},{8,9},{9,8},{10,11... | collective-permute-start | bytes 196616 | tf_op jit(solution)/shard_map/ppermute | solution.py:666
  10.1 0.7 %collective-permute-start.1 = (f32[8,16,128]{2,1,0:T(8,128)}, f32[8,16,128]{2,1,0:T(8,128)S(1)}, u32[]{:S(2)}, u32[]{:S(2)}) collective-permute-start(f32[8,16,128]{2,1,0:T(8,128)} %get-tuple-element.37), channel_id=1, source_target_pairs={{1,2},{2,1},{5,6},{6,5},{9,10},{10,9},{13,14},{14,13},{17,18},{18,... | collective-permute-start | bytes 196616 | tf_op jit(solution)/shard_map/ppermute | solution.py:666
  10.7 1.4 %collective-permute-done.one_ref = f32[8,16,128]{2,1,0:T(8,128)S(1)} collective-permute-done((f32[8,16,128]{2,1,0:T(8,128)}, f32[8,16,128]{2,1,0:T(8,128)S(1)}, u32[]{:S(2)}, u32[]{:S(2)}) %collective-permute-start) | collective-permute-done | bytes 65568 | tf_op jit(solution)/shard_map/ppermute | solution.py:666
  12.1 0.0 collective-permute-done.1.two_ref
  12.1 0.1 shard_map.65
  12.2 0.3 collective-permute-start.3
  12.5 2.5 %collective-permute-done.3.refs_1_.refs_8_ = f32[4,16,128]{2,1,0:T(8,128)S(1)} collective-permute-done((f32[4,16,128]{2,1,0:T(8,128)S(1)}, f32[4,16,128]{2,1,0:T(8,128)S(1)}, u32[]{:S(2)}, u32[]{:S(2)}) %collective-permute-start.3) | collective-permute-done | bytes 32800 | tf_op jit(solution)/shard_map/ppermute | solution.py:666
  15.0 0.0 collective-permute-done.2.refs_0_.refs_7_
  15.0 0.1 shard_map.66
  15.1 4.5 %collective-permute-start.6 = (f32[37,4,128]{2,1,0:T(4,128)S(1)}, f32[37,4,128]{2,1,0:T(4,128)S(1)}, u32[]{:S(2)}, u32[]{:S(2)}) collective-permute-start(f32[37,4,128]{2,1,0:T(4,128)S(1)} %get-tuple-element.43), channel_id=1, source_target_pairs={{4,8},{8,4},{5,9},{9,5},{6,10},{10,6},{7,11},{11,7},{20,24},{24,20... | collective-permute-start | bytes 227336 | tf_op jit(solution)/shard_map/ppermute | solution.py:666
  19.6 0.1 collective-permute-start.7
  19.8 0.8 %shard_map.67 = (f32[4,4,128]{2,1,0:T(4,128)S(1)}, f32[5,8,8,128]{3,2,1,0:T(8,128)S(1)}) custom-call(s32[1]{0:T(128)} %bitcast.where_ref, f32[16,16,128]{2,1,0:T(8,128)S(1)} %copy-done, f32[16,16,128]{2,1,0:T(8,128)S(1)} %copy-done.1, f32[16,16,128]{2,1,0:T(8,128)S(1)} %copy-done.2, f32[16,16,128]{2,1,0:T(8,128)S(1)} %copy-done.3, ...), custom_call_target="tpu_custom_call" | custom-call | bytes 7200000 | tf_op jit(solution)/shard_map/pallas_call | solution.py:647
  20.6 0.0 collective-permute-done.5.refs_10_
  20.6 1.1 %collective-permute-done.6.refs_11_ = f32[37,4,128]{2,1,0:T(4,128)S(1)} collective-permute-done((f32[37,4,128]{2,1,0:T(4,128)S(1)}, f32[37,4,128]{2,1,0:T(4,128)S(1)}, u32[]{:S(2)}, u32[]{:S(2)}) %collective-permute-start.6) | collective-permute-done | bytes 75808 | tf_op jit(solution)/shard_map/ppermute | solution.py:666
  21.7 0.0 collective-permute-done.7.refs_12_
  21.7 3.9 %shard_map.68 = (f32[5,8,8,128]{3,2,1,0:T(8,128)S(1)}, f32[5,4,8,128]{3,2,1,0:T(8,128)S(1)}, f32[5,8,4,128]{3,2,1,0:T(4,128)S(1)}, f32[5,8,4,128]{3,2,1,0:T(4,12...) custom-call(s32[1]{0:T(128)} %bitcast.where_ref, ...), custom_call_target="tpu_custom_call" | custom-call | bytes 14400000 | tf_op jit(solution)/shard_map/pallas_call | solution.py:647
  25.6 0.3 collective-permute-start.8
  26.0 3.9 %collective-permute-start.9 = (f32[5,8,4,128]{3,2,1,0:T(4,128)S(1)}, f32[5,8,4,128]{3,2,1,0:T(4,128)S(1)}, u32[]{:S(2)}, u32[]{:S(2)}) collective-permute-start(f32[5,8,4,128]{3,2,1,0:T(4,128)S(1)} %get-tuple-element.48), channel_id=1, source_target_pairs={{4,8},{8,4},{5,9},{9,5},{6,10},{10,6},{7,11},{11,7},{20,24},{24,20... | collective-permute-start | bytes 245768 | tf_op jit(solution)/shard_map/ppermute | solution.py:666
  29.9 0.1 collective-permute-start.10
  30.0 0.0 collective-permute-done.8.refs_0_
  30.0 3.8 %collective-permute-start.11 = (f32[25,4,128]{2,1,0:T(4,128)S(1)}, f32[25,4,128]{2,1,0:T(4,128)S(1)}, u32[]{:S(2)}, u32[]{:S(2)}) collective-permute-start(f32[25,4,128]{2,1,0:T(4,128)S(1)} %get-tuple-element.50), channel_id=1, source_target_pairs={{4,8},{8,4},{5,9},{9,5},{6,10},{10,6},{7,11},{11,7},{20,24},{24,20... | collective-permute-start | bytes 153608 | tf_op jit(solution)/shard_map/ppermute | solution.py:666
  33.8 0.1 collective-permute-start.12
  33.9 0.0 collective-permute-done.10.refs_2_
  33.9 1.7 %collective-permute-done.11.refs_3_ = f32[25,4,128]{2,1,0:T(4,128)S(1)} collective-permute-done((f32[25,4,128]{2,1,0:T(4,128)S(1)}, f32[25,4,128]{2,1,0:T(4,128)S(1)}, u32[]{:S(2)}, u32[]{:S(2)}) %collective-permute-start.11) | collective-permute-done | bytes 51232 | tf_op jit(solution)/shard_map/ppermute | solution.py:666
  35.6 0.0 collective-permute-done.12.refs_4_
  35.6 0.4 shard_map.70
  36.0 18.9 %all_to_all.5.gathered = f32[32,5,4,128]{3,2,1,0:T(4,128)S(1)} all-to-all(f32[32,5,4,128]{3,2,1,0:T(4,128)S(1)} %get-tuple-element.53), channel_id=1, replica_groups=mesh['gx'=2,'gy'=4,'gz'=4] {'gx','gy','gz'}, dimensions={0} | all-to-all | bytes 655360 | tf_op jit(solution)/shard_map/all_to_all | solution.py:746
  54.9 5.1 %shard_map.71 = f32[16,16,128]{2,1,0:T(8,128)} custom-call(s32[1]{0:T(128)} %bitcast.where_ref, f32[32,5,4,128]{3,2,1,0:T(4,128)S(1)} %all_to_all.5.gathered, f32[6,16,16,128]{3,2,1,0:T(8,128)S(1)} %get-tuple-element.54.level1, f32[24,24,128]{2,1,0:T(8,128)S(1)} %get-tuple-element.55.refs_0_, f32[24,24,128]{2,1,0:T(8,128)S(1)} %get-tuple-element.56.refs_1_, ...), custom_call_target="tpu_custom_call" | custom-call | bytes 14400000 | tf_op jit(solution)/shard_map/pallas_call | solution.py:647
  (15 shorter events, 0.1 us)
Async XLA Ops:
  0.0 19.7 %copy-start.3 = (f32[16,16,128]{2,1,0:T(8,128)S(1)}, f32[16,16,128]{2,1,0:T(8,128)}, u32[]{:S(2)}) copy-start(f32[16,16,128]{2,1,0:T(8,128)} %refs_3_.5) | copy-start | bytes 393220
  0.0 19.7 %copy-start.4 = (f32[16,16,128]{2,1,0:T(8,128)S(1)}, f32[16,16,128]{2,1,0:T(8,128)}, u32[]{:S(2)}) copy-start(f32[16,16,128]{2,1,0:T(8,128)} %refs_4_.5) | copy-start | bytes 393220
  0.0 19.7 %copy-start.5 = (f32[16,16,128]{2,1,0:T(8,128)S(1)}, f32[16,16,128]{2,1,0:T(8,128)}, u32[]{:S(2)}) copy-start(f32[16,16,128]{2,1,0:T(8,128)} %refs_5_.5) | copy-start | bytes 393220
  2.6 12.4 %collective-permute-start.2 = (f32[6,4,16,128]{3,2,1,0:T(8,128)}, f32[6,4,16,128]{3,2,1,0:T(8,128)S(1)}, u32[]{:S(2)}, u32[]{:S(2)}) collective-permute-start(f32[6,4,16,128]{3,2,1,0:T(8,128)} %get-tuple-element.39), channel_id=1, source_target_pairs={{0,16},{16,0},{1,17},{17,1},{2,18},{18,2},{3,19},{19,3},{4,20},{20... | collective-permute-start | bytes 589832 | tf_op jit(solution)/shard_map/ppermute | solution.py:666
  4.6 15.9 %collective-permute-start.4 = (f32[6,16,4,128]{3,2,1,0:T(4,128)}, f32[6,16,4,128]{3,2,1,0:T(4,128)S(1)}, u32[]{:S(2)}, u32[]{:S(2)}) collective-permute-start(f32[6,16,4,128]{3,2,1,0:T(4,128)} %get-tuple-element.41), channel_id=1, source_target_pairs={{4,8},{8,4},{5,9},{9,5},{6,10},{10,6},{7,11},{11,7},{20,24},{24,20... | collective-permute-start | bytes 589832 | tf_op jit(solution)/shard_map/ppermute | solution.py:666
  8.6 12.0 %collective-permute-start.5 = (f32[6,16,4,128]{3,2,1,0:T(4,128)}, f32[6,16,4,128]{3,2,1,0:T(4,128)S(1)}, u32[]{:S(2)}, u32[]{:S(2)}) collective-permute-start(f32[6,16,4,128]{3,2,1,0:T(4,128)} %get-tuple-element.42), channel_id=1, source_target_pairs={{0,4},{4,0},{8,12},{12,8},{1,5},{5,1},{9,13},{13,9},{2,6},{6,2},{1... | collective-permute-start | bytes 589832 | tf_op jit(solution)/shard_map/ppermute | solution.py:666
  8.7 3.4 %collective-permute-start = (f32[8,16,128]{2,1,0:T(8,128)}, f32[8,16,128]{2,1,0:T(8,128)S(1)}, u32[]{:S(2)}, u32[]{:S(2)}) collective-permute-start(f32[8,16,128]{2,1,0:T(8,128)} %get-tuple-element.36), channel_id=1, source_target_pairs={{0,1},{1,0},{2,3},{3,2},{4,5},{5,4},{6,7},{7,6},{8,9},{9,8},{10,11... | collective-permute-start | bytes 196616 | tf_op jit(solution)/shard_map/ppermute | solution.py:666
  10.1 2.0 %collective-permute-start.1 = (f32[8,16,128]{2,1,0:T(8,128)}, f32[8,16,128]{2,1,0:T(8,128)S(1)}, u32[]{:S(2)}, u32[]{:S(2)}) collective-permute-start(f32[8,16,128]{2,1,0:T(8,128)} %get-tuple-element.37), channel_id=1, source_target_pairs={{1,2},{2,1},{5,6},{6,5},{9,10},{10,9},{13,14},{14,13},{17,18},{18,... | collective-permute-start | bytes 196616 | tf_op jit(solution)/shard_map/ppermute | solution.py:666
  12.1 7.7 %copy-start.2 = (f32[16,16,128]{2,1,0:T(8,128)S(1)}, f32[16,16,128]{2,1,0:T(8,128)}, u32[]{:S(2)}) copy-start(f32[16,16,128]{2,1,0:T(8,128)} %refs_2_.5) | copy-start | bytes 393220
  12.2 2.8 %collective-permute-start.3 = (f32[4,16,128]{2,1,0:T(8,128)S(1)}, f32[4,16,128]{2,1,0:T(8,128)S(1)}, u32[]{:S(2)}, u32[]{:S(2)}) collective-permute-start(f32[4,16,128]{2,1,0:T(8,128)S(1)} %get-tuple-element.40), channel_id=1, source_target_pairs={{0,16},{16,0},{1,17},{17,1},{2,18},{18,2},{3,19},{19,3},{4,20},{20... | collective-permute-start | bytes 98312 | tf_op jit(solution)/shard_map/ppermute | solution.py:666
  15.0 4.7 %copy-start = (f32[16,16,128]{2,1,0:T(8,128)S(1)}, f32[16,16,128]{2,1,0:T(8,128)}, u32[]{:S(2)}) copy-start(f32[16,16,128]{2,1,0:T(8,128)} %refs_0_.5) | copy-start | bytes 393220
  15.0 4.7 %copy-start.1 = (f32[16,16,128]{2,1,0:T(8,128)S(1)}, f32[16,16,128]{2,1,0:T(8,128)}, u32[]{:S(2)}) copy-start(f32[16,16,128]{2,1,0:T(8,128)} %refs_1_.5) | copy-start | bytes 393220
  15.1 6.6 %collective-permute-start.6 = (f32[37,4,128]{2,1,0:T(4,128)S(1)}, f32[37,4,128]{2,1,0:T(4,128)S(1)}, u32[]{:S(2)}, u32[]{:S(2)}) collective-permute-start(f32[37,4,128]{2,1,0:T(4,128)S(1)} %get-tuple-element.43), channel_id=1, source_target_pairs={{4,8},{8,4},{5,9},{9,5},{6,10},{10,6},{7,11},{11,7},{20,24},{24,20... | collective-permute-start | bytes 227336 | tf_op jit(solution)/shard_map/ppermute | solution.py:666
  19.6 2.0 %collective-permute-start.7 = (f32[37,4,128]{2,1,0:T(4,128)S(1)}, f32[37,4,128]{2,1,0:T(4,128)S(1)}, u32[]{:S(2)}, u32[]{:S(2)}) collective-permute-start(f32[37,4,128]{2,1,0:T(4,128)S(1)} %get-tuple-element.44), channel_id=1, source_target_pairs={{0,4},{4,0},{8,12},{12,8},{1,5},{5,1},{9,13},{13,9},{2,6},{6,2},{1... | collective-permute-start | bytes 227336 | tf_op jit(solution)/shard_map/ppermute | solution.py:666
  25.6 4.3 %collective-permute-start.8 = (f32[5,4,8,128]{3,2,1,0:T(8,128)S(1)}, f32[5,4,8,128]{3,2,1,0:T(8,128)S(1)}, u32[]{:S(2)}, u32[]{:S(2)}) collective-permute-start(f32[5,4,8,128]{3,2,1,0:T(8,128)S(1)} %get-tuple-element.47), channel_id=1, source_target_pairs={{0,16},{16,0},{1,17},{17,1},{2,18},{18,2},{3,19},{19,3},{4,20},{20... | collective-permute-start | bytes 245768 | tf_op jit(solution)/shard_map/ppermute | solution.py:666
  26.0 8.0 %collective-permute-start.9 = (f32[5,8,4,128]{3,2,1,0:T(4,128)S(1)}, f32[5,8,4,128]{3,2,1,0:T(4,128)S(1)}, u32[]{:S(2)}, u32[]{:S(2)}) collective-permute-start(f32[5,8,4,128]{3,2,1,0:T(4,128)S(1)} %get-tuple-element.48), channel_id=1, source_target_pairs={{4,8},{8,4},{5,9},{9,5},{6,10},{10,6},{7,11},{11,7},{20,24},{24,20... | collective-permute-start | bytes 245768 | tf_op jit(solution)/shard_map/ppermute | solution.py:666
  29.9 4.0 %collective-permute-start.10 = (f32[5,8,4,128]{3,2,1,0:T(4,128)S(1)}, f32[5,8,4,128]{3,2,1,0:T(4,128)S(1)}, u32[]{:S(2)}, u32[]{:S(2)}) collective-permute-start(f32[5,8,4,128]{3,2,1,0:T(4,128)S(1)} %get-tuple-element.49), channel_id=1, source_target_pairs={{0,4},{4,0},{8,12},{12,8},{1,5},{5,1},{9,13},{13,9},{2,6},{6,2},{1... | collective-permute-start | bytes 245768 | tf_op jit(solution)/shard_map/ppermute | solution.py:666
  30.0 5.6 %collective-permute-start.11 = (f32[25,4,128]{2,1,0:T(4,128)S(1)}, f32[25,4,128]{2,1,0:T(4,128)S(1)}, u32[]{:S(2)}, u32[]{:S(2)}) collective-permute-start(f32[25,4,128]{2,1,0:T(4,128)S(1)} %get-tuple-element.50), channel_id=1, source_target_pairs={{4,8},{8,4},{5,9},{9,5},{6,10},{10,6},{7,11},{11,7},{20,24},{24,20... | collective-permute-start | bytes 153608 | tf_op jit(solution)/shard_map/ppermute | solution.py:666
  33.8 1.8 %collective-permute-start.12 = (f32[25,4,128]{2,1,0:T(4,128)S(1)}, f32[25,4,128]{2,1,0:T(4,128)S(1)}, u32[]{:S(2)}, u32[]{:S(2)}) collective-permute-start(f32[25,4,128]{2,1,0:T(4,128)S(1)} %get-tuple-element.51), channel_id=1, source_target_pairs={{0,4},{4,0},{8,12},{12,8},{1,5},{5,1},{9,13},{13,9},{2,6},{6,2},{1... | collective-permute-start | bytes 153608 | tf_op jit(solution)/shard_map/ppermute | solution.py:666

commit v8 on v7

--- a/solution.py
+++ b/solution.py
@@ -40,10 +40,13 @@
     return jnp.where(jnp.full(yes.shape, flag, jnp.int32) == 1, yes, no)
 
 
-def neighbours(axis_size, odd, one, two):
-    if axis_size == 2:
+def neighbours(count, place, one, two):
+    if count == 2:
         two = jnp.zeros_like(one)
-    return pick(odd, one, two), pick(odd, two, one)
+    else:
+        ends = jnp.full(two.shape, place, jnp.int32)
+        two = jnp.where((ends == 0) | (ends == count - 1), 0.0, two)
+    return pick(place % 2, one, two), pick(place % 2, two, one)
 
 
 def turn(values, shift, axis):
@@ -193,28 +196,28 @@
 
 
 def halo_z_kernel(counts, where_ref, one_ref, two_ref, zpack, *sends):
-    odd_x, _, odd = (place % 2 for place in position(where_ref))
+    at_x, _, at_z = position(where_ref)
     half = one_ref.shape[0]
-    below, above = neighbours(counts[2], odd, one_ref[...], two_ref[...])
+    below, above = neighbours(counts[2], at_z, one_ref[...], two_ref[...])
     lane = lane_of(below.shape)
     zpack[:half] = jnp.where(lane < SIDE, above, turn(below, SIDE, 2))
     zpack[half:] = jnp.where(lane < SIDE, turn(above, SIDE, 2), below)
-    for send, face in zip(sends, faces_x(zpack[...][None], odd_x, len(sends), HALO)):
+    for send, face in zip(sends, faces_x(zpack[...][None], at_x % 2, len(sends), HALO)):
         send[...] = face[0]
 
 
 def corners_kernel(counts, where_ref, zpack, *refs):
     n_x = 1 if counts[0] == 2 else 2
     main_x, halos_x, (two_y, one_y) = refs[:n_x], refs[n_x:2 * n_x], refs[2 * n_x:]
-    odd_x, odd = (place % 2 for place in position(where_ref)[:2])
+    at_x, at_y, _ = position(where_ref)
     for a in range(7):
         if a < 6:
-            below, above = neighbours(counts[0], odd_x, main_x[0][a], main_x[-1][a])
+            below, above = neighbours(counts[0], at_x, main_x[0][a], main_x[-1][a])
         else:
-            below, above = neighbours(counts[0], odd_x, halos_x[0][...], halos_x[-1][...])
-        for n, pair in enumerate(corner_sends(below, above, odd, False)):
+            below, above = neighbours(counts[0], at_x, halos_x[0][...], halos_x[-1][...])
+        for n, pair in enumerate(corner_sends(below, above, at_y % 2, False)):
             one_y[3 * a + n], two_y[3 * a + n] = pair
-    one_y[21:], two_y[21:] = faces_y(zpack[...], odd, HALO)
+    one_y[21:], two_y[21:] = faces_y(zpack[...], at_y % 2, HALO)
 
 
 def each(first, last, step, body):
@@ -287,14 +290,14 @@
     main_x, halos_x = refs[:n_x], refs[n_x:2 * n_x]
     coarse2, coeffs1, halo, sums, pairing = refs[2 * n_x:]
     sx, sy, sz = ins[0].shape
-    odd_x = position(where_ref)[0] % 2
+    at_x = position(where_ref)[0]
     x1, y1 = sx // 2, sy // 2
     lane = lane_of((sx, sy, LANES))
     lanes = [slice(k * LANES, (k + 1) * LANES) for k in range(2)]
     edge_lane = lane_of((1, sy, LANES))
     last = slice(HALO - 1, HALO)
-    below, _ = neighbours(counts[0], odd_x, main_x[0][3, last], main_x[-1][3, last])
-    packed, _ = neighbours(counts[0], odd_x, halos_x[0][last], halos_x[-1][last])
+    below, _ = neighbours(counts[0], at_x, main_x[0][3, last], main_x[-1][3, last])
+    packed, _ = neighbours(counts[0], at_x, halos_x[0][last], halos_x[-1][last])
     for k, edge in enumerate((below, unpacked(packed, 3, edge_lane))):
         halo[k, 0:1] = edge
         sums[4, 0, :, lanes[k]] = rows_of(halo.at[k], 0, (0,), BOTH)
@@ -339,19 +342,19 @@
     arrays = (field, rhs, alpha, bx, by, bz)
     sx, sy, sz = ins[0].shape
     ex, ey = sx + 2 * HALO, sy + 2 * HALO
-    odd_x, odd_y = (place % 2 for place in position(where_ref)[:2])
-
-    rest = neighbours(counts[1], odd_y, rest_one[...], rest_two[...])
+    at_x, at_y, _ = position(where_ref)
+
+    rest = neighbours(counts[1], at_y, rest_one[...], rest_two[...])
     rest = jnp.concatenate(rest[::-1], axis=1)
     for a in range(7):
         if a < 6:
             to = arrays[a][0]
-            below, above = neighbours(counts[0], odd_x, main_x[0][a], main_x[-1][a])
-            rows = neighbours(counts[1], odd_y, main_one[a], main_two[a])
+            below, above = neighbours(counts[0], at_x, main_x[0][a], main_x[-1][a])
+            rows = neighbours(counts[1], at_y, main_one[a], main_two[a])
             rows = jnp.concatenate(rows[::-1], axis=1)
         else:
             to = packs
-            below, above = neighbours(counts[0], odd_x, halos_x[0][...], halos_x[-1][...])
+            below, above = neighbours(counts[0], at_x, halos_x[0][...], halos_x[-1][...])
             rows = rest[21:]
         to[:HALO, :sy] = below
         to[HALO:HALO + sx, :sy] = ins[a][...]
@@ -418,9 +421,9 @@
     weight1 = relaxer(coeffs1[0], coeffs1[1] + low_y)
     for n, values in enumerate((2.0 * rhs1, weight1, coeffs1[2], coeffs1[3], coeffs1[4])):
         own1[n] = values
-        for send, face in zip(sends, faces_x(values[None], odd_x, n_x, NEAR)):
+        for send, face in zip(sends, faces_x(values[None], at_x % 2, n_x, NEAR)):
             send[n] = face[0]
-        near_one[n], near_two[n] = faces_y(values, odd_y, NEAR)
+        near_one[n], near_two[n] = faces_y(values, at_y % 2, NEAR)
 
 
 def level2_rows(source, odd_axes, factor, x2, y2, z2):
@@ -444,10 +447,10 @@
 
 def near_corners_kernel(counts, where_ref, *refs):
     halos_x, (two_y, one_y) = refs[:-2], refs[-2:]
-    odd_x, odd = (place % 2 for place in position(where_ref)[:2])
+    at_x, at_y, _ = position(where_ref)
     for a in range(halos_x[0].shape[0]):
-        below, above = neighbours(counts[0], odd_x, halos_x[0][a], halos_x[-1][a])
-        for n, pair in enumerate(corner_sends(below, above, odd, True)):
+        below, above = neighbours(counts[0], at_x, halos_x[0][a], halos_x[-1][a])
+        for n, pair in enumerate(corner_sends(below, above, at_y % 2, True)):
             one_y[5 * a + n], two_y[5 * a + n] = pair
 
 
@@ -456,13 +459,13 @@
     halos_x = refs[:n_x]
     main_two, main_one, rest_two, rest_one, coarse2, copies, level1, left = refs[n_x:]
     n, bx1, by1, _ = ring.shape
-    odd_x, odd_y = (place % 2 for place in position(where_ref)[:2])
-    rest = neighbours(counts[1], odd_y, rest_one[...], rest_two[...])
+    at_x, at_y, _ = position(where_ref)
+    rest = neighbours(counts[1], at_y, rest_one[...], rest_two[...])
     rest = jnp.concatenate(rest[::-1], axis=1)
     whole = []
     for a in range(n):
-        below, above = neighbours(counts[0], odd_x, halos_x[0][a], halos_x[-1][a])
-        rows = neighbours(counts[1], odd_y, main_one[a], main_two[a])
+        below, above = neighbours(counts[0], at_x, halos_x[0][a], halos_x[-1][a])
+        rows = neighbours(counts[1], at_y, main_one[a], main_two[a])
         rows = jnp.concatenate(rows[::-1], axis=1)
         low, high = corner_tiles([rest[5 * a + k] for k in range(5)])
         rows = jnp.concatenate(
@@ -660,11 +663,11 @@
 def swaps(axis, sends):
     count = lax.axis_size(axis)
     got = []
-    for k, block in reversed(list(enumerate(sends))):
-        pairs = [(i, i + 1) for i in range(k, count - 1, 2)]
+    for k, block in enumerate(sends):
+        pairs = [(i, (i + 1) % count) for i in range(k, count, 2)]
         pairs = [pair for low, high in pairs for pair in ((low, high), (high, low))]
         got.append(lax.ppermute(block, axis, pairs))
-    return got[::-1]
+    return got
 
 
 def local(initial, right_side, alpha, beta_x, beta_y, beta_z):

time: 60.3 us -> 55.7 us (0.924)
  blocking collectives: 18.9 us -> 14.8 us
  starting transfers between devices: 21.2 us -> 17.2 us
  waiting for transfers between devices: 6.69 us -> 10.3 us
    all_to_all x1, blocking collectives: 18.9 us -> 14.8 us  [local(): gathered = lax.all_to_all(copies, axes, 0, 0, tiled=True)]
    ppermute x13, starting transfers between devices: 21.2 us -> 17.2 us  [swaps(): got.append(lax.ppermute(block, axis, pairs))]
    ppermute x13, waiting for transfers between devices: 6.69 us -> 10.3 us  [swaps(): got.append(lax.ppermute(block, axis, pairs))]
  transfers between devices with their start and end apart: 13 -> 13, of which waited for: 4 -> 6; matrix products, arithmetic and copies ran while one was open for 0% -> 0% of each run, Pallas kernels for 2% -> 2%
where the time goes in v8:
time: 55.7 us; the launch traced here: 55.5 us
  starting transfers between devices  17.2 us (31%)
  blocking collectives  14.8 us (27%)
  Pallas kernels  13 us (23%)
  waiting for transfers between devices  10.3 us (18%)
    ppermute x13, starting transfers between devices, swaps(): got.append(lax.ppermute(block, axis, pairs))  17.2 us
    all_to_all x1, blocking collectives, local(): gathered = lax.all_to_all(copies, axes, 0, 0, tiled=True)  14.8 us
    pallas_call x8, Pallas kernels, run(): pl.pallas_call(kernel, out_shape=tuple((jax.ShapeDtypeStruct(shape, F32)...  13 us
    ppermute x13, waiting for transfers between devices, swaps(): got.append(lax.ppermute(block, axis, pairs))  10.3 us
  transfers between devices with their start and end apart: 13, of which 6 were waited for; matrix products, arithmetic and copies ran while one was open for 0% of the time, Pallas kernels for 2%

profile of v8, /device:TPU:1, one launch (start us, length us, event | category | flops | bytes accessed | tf_op | source)
XLA Modules:
  0.0 55.5 jit_solution(17046549498530650562)
XLA Ops:
  0.0 2.6 %shard_map.64 = (f32[6,4,16,128]{3,2,1,0:T(8,128)}, f32[6,16,4,128]{3,2,1,0:T(4,128)}, f32[6,16,4,128]{3,2,1,0:T(4,128)}, f32[8,16,128]{2,1,0:T(8,128)}, f32[8,16,128]{2,1,0:T(8,128)}) custom-call(s32[1]{0:T(128)} %bitcast.where_ref, f32[16,16,128]{2,1,0:T(8,128)} %refs_0_.5, f32[16,16,128]{2,1,0:T(8,128)} %refs_1_.5, f32[16,16,128]{2,1,0:T(8,128)} %refs_2_.5, ...), custom_call_target="tpu_custom_call" | custom-call | bytes 3600000 | tf_op jit(solution)/shard_map/pallas_call | solution.py:650
  2.6 2.0 %collective-permute-start.2 = (f32[6,4,16,128]{3,2,1,0:T(8,128)}, f32[6,4,16,128]{3,2,1,0:T(8,128)S(1)}, u32[]{:S(2)}, u32[]{:S(2)}) collective-permute-start(f32[6,4,16,128]{3,2,1,0:T(8,128)} %get-tuple-element.39), channel_id=1, source_target_pairs={{0,16},{16,0},{1,17},{17,1},{2,18},{18,2},{3,19},{19,3},{4,20},{20... | collective-permute-start | bytes 589832 | tf_op jit(solution)/shard_map/ppermute | solution.py:669
  4.6 2.1 %collective-permute-start.4 = (f32[6,16,4,128]{3,2,1,0:T(4,128)}, f32[6,16,4,128]{3,2,1,0:T(4,128)S(1)}, u32[]{:S(2)}, u32[]{:S(2)}) collective-permute-start(f32[6,16,4,128]{3,2,1,0:T(4,128)} %get-tuple-element.41), channel_id=1, source_target_pairs={{4,8},{8,4},{12,0},{0,12},{5,9},{9,5},{13,1},{1,13},{6,10},{10,6},... | collective-permute-start | bytes 589832 | tf_op jit(solution)/shard_map/ppermute | solution.py:669
  6.7 0.0 collective-permute-start.5
  6.7 1.3 %collective-permute-start = (f32[8,16,128]{2,1,0:T(8,128)}, f32[8,16,128]{2,1,0:T(8,128)S(1)}, u32[]{:S(2)}, u32[]{:S(2)}) collective-permute-start(f32[8,16,128]{2,1,0:T(8,128)} %get-tuple-element.36), channel_id=1, source_target_pairs={{0,1},{1,0},{2,3},{3,2},{4,5},{5,4},{6,7},{7,6},{8,9},{9,8},{10,11... | collective-permute-start | bytes 196616 | tf_op jit(solution)/shard_map/ppermute | solution.py:669
  8.0 2.2 %collective-permute-start.1 = (f32[8,16,128]{2,1,0:T(8,128)}, f32[8,16,128]{2,1,0:T(8,128)S(1)}, u32[]{:S(2)}, u32[]{:S(2)}) collective-permute-start(f32[8,16,128]{2,1,0:T(8,128)} %get-tuple-element.37), channel_id=1, source_target_pairs={{1,2},{2,1},{3,0},{0,3},{5,6},{6,5},{7,4},{4,7},{9,10},{10,9},{11,... | collective-permute-start | bytes 196616 | tf_op jit(solution)/shard_map/ppermute | solution.py:669
  10.2 0.1 collective-permute-done.one_ref
  10.3 3.7 %collective-permute-done.1.two_ref = f32[8,16,128]{2,1,0:T(8,128)S(1)} collective-permute-done((f32[8,16,128]{2,1,0:T(8,128)}, f32[8,16,128]{2,1,0:T(8,128)S(1)}, u32[]{:S(2)}, u32[]{:S(2)}) %collective-permute-start.1) | collective-permute-done | bytes 65568 | tf_op jit(solution)/shard_map/ppermute | solution.py:669
  14.1 0.1 shard_map.65
  14.2 0.3 collective-permute-start.3
  14.5 2.5 %collective-permute-done.3.refs_1_.refs_8_ = f32[4,16,128]{2,1,0:T(8,128)S(1)} collective-permute-done((f32[4,16,128]{2,1,0:T(8,128)S(1)}, f32[4,16,128]{2,1,0:T(8,128)S(1)}, u32[]{:S(2)}, u32[]{:S(2)}) %collective-permute-start.3) | collective-permute-done | bytes 32800 | tf_op jit(solution)/shard_map/ppermute | solution.py:669
  17.0 0.0 collective-permute-done.2.refs_0_.refs_7_
  17.0 0.1 shard_map.66
  17.1 2.5 %collective-permute-start.6 = (f32[37,4,128]{2,1,0:T(4,128)S(1)}, f32[37,4,128]{2,1,0:T(4,128)S(1)}, u32[]{:S(2)}, u32[]{:S(2)}) collective-permute-start(f32[37,4,128]{2,1,0:T(4,128)S(1)} %get-tuple-element.43), channel_id=1, source_target_pairs={{4,8},{8,4},{12,0},{0,12},{5,9},{9,5},{13,1},{1,13},{6,10},{10,6},... | collective-permute-start | bytes 227336 | tf_op jit(solution)/shard_map/ppermute | solution.py:669
  19.6 0.0 collective-permute-start.7
  19.6 0.8 %shard_map.67 = (f32[4,4,128]{2,1,0:T(4,128)S(1)}, f32[5,8,8,128]{3,2,1,0:T(8,128)S(1)}) custom-call(s32[1]{0:T(128)} %bitcast.where_ref, f32[16,16,128]{2,1,0:T(8,128)S(1)} %copy-done, f32[16,16,128]{2,1,0:T(8,128)S(1)} %copy-done.1, f32[16,16,128]{2,1,0:T(8,128)S(1)} %copy-done.2, f32[16,16,128]{2,1,0:T(8,128)S(1)} %copy-done.3, ...), custom_call_target="tpu_custom_call" | custom-call | bytes 7200000 | tf_op jit(solution)/shard_map/pallas_call | solution.py:650
  20.4 0.0 collective-permute-done.4.refs_9_
  20.4 0.0 collective-permute-done.5.refs_10_
  20.4 1.2 %collective-permute-done.6.refs_11_ = f32[37,4,128]{2,1,0:T(4,128)S(1)} collective-permute-done((f32[37,4,128]{2,1,0:T(4,128)S(1)}, f32[37,4,128]{2,1,0:T(4,128)S(1)}, u32[]{:S(2)}, u32[]{:S(2)}) %collective-permute-start.6) | collective-permute-done | bytes 75808 | tf_op jit(solution)/shard_map/ppermute | solution.py:669
  21.6 0.0 collective-permute-done.7.refs_12_
  21.6 3.9 %shard_map.68 = (f32[5,8,8,128]{3,2,1,0:T(8,128)S(1)}, f32[5,4,8,128]{3,2,1,0:T(8,128)S(1)}, f32[5,8,4,128]{3,2,1,0:T(4,128)S(1)}, f32[5,8,4,128]{3,2,1,0:T(4,12...) custom-call(s32[1]{0:T(128)} %bitcast.where_ref, ...), custom_call_target="tpu_custom_call" | custom-call | bytes 14400000 | tf_op jit(solution)/shard_map/pallas_call | solution.py:650
  25.6 0.3 collective-permute-start.8
  25.9 2.8 %collective-permute-start.9 = (f32[5,8,4,128]{3,2,1,0:T(4,128)S(1)}, f32[5,8,4,128]{3,2,1,0:T(4,128)S(1)}, u32[]{:S(2)}, u32[]{:S(2)}) collective-permute-start(f32[5,8,4,128]{3,2,1,0:T(4,128)S(1)} %get-tuple-element.48), channel_id=1, source_target_pairs={{4,8},{8,4},{12,0},{0,12},{5,9},{9,5},{13,1},{1,13},{6,10},{10,6},... | collective-permute-start | bytes 245768 | tf_op jit(solution)/shard_map/ppermute | solution.py:669
  28.7 0.0 collective-permute-start.10
  28.7 0.3 collective-permute-done.8.refs_0_
  29.0 3.7 %collective-permute-start.11 = (f32[25,4,128]{2,1,0:T(4,128)S(1)}, f32[25,4,128]{2,1,0:T(4,128)S(1)}, u32[]{:S(2)}, u32[]{:S(2)}) collective-permute-start(f32[25,4,128]{2,1,0:T(4,128)S(1)} %get-tuple-element.50), channel_id=1, source_target_pairs={{4,8},{8,4},{12,0},{0,12},{5,9},{9,5},{13,1},{1,13},{6,10},{10,6},... | collective-permute-start | bytes 153608 | tf_op jit(solution)/shard_map/ppermute | solution.py:669
  32.7 0.0 collective-permute-done.10.refs_2_
  32.7 2.4 %collective-permute-done.11.refs_3_ = f32[25,4,128]{2,1,0:T(4,128)S(1)} collective-permute-done((f32[25,4,128]{2,1,0:T(4,128)S(1)}, f32[25,4,128]{2,1,0:T(4,128)S(1)}, u32[]{:S(2)}, u32[]{:S(2)}) %collective-permute-start.11) | collective-permute-done | bytes 51232 | tf_op jit(solution)/shard_map/ppermute | solution.py:669
  35.2 0.0 collective-permute-done.12.refs_4_
  35.2 0.4 shard_map.70
  35.6 14.8 %all_to_all.5.gathered = f32[32,5,4,128]{3,2,1,0:T(4,128)S(1)} all-to-all(f32[32,5,4,128]{3,2,1,0:T(4,128)S(1)} %get-tuple-element.53), channel_id=1, replica_groups=mesh['gx'=2,'gy'=4,'gz'=4] {'gx','gy','gz'}, dimensions={0} | all-to-all | bytes 655360 | tf_op jit(solution)/shard_map/all_to_all | solution.py:749
  50.4 5.1 %shard_map.71 = f32[16,16,128]{2,1,0:T(8,128)} custom-call(s32[1]{0:T(128)} %bitcast.where_ref, f32[32,5,4,128]{3,2,1,0:T(4,128)S(1)} %all_to_all.5.gathered, f32[6,16,16,128]{3,2,1,0:T(8,128)S(1)} %get-tuple-element.54.level1, f32[24,24,128]{2,1,0:T(8,128)S(1)} %get-tuple-element.55.refs_0_, f32[24,24,128]{2,1,0:T(8,128)S(1)} %get-tuple-element.56.refs_1_, ...), custom_call_target="tpu_custom_call" | custom-call | bytes 14400000 | tf_op jit(solution)/shard_map/pallas_call | solution.py:650
  (15 shorter events, 0.1 us)
Async XLA Ops:
  0.0 19.6 %copy-start.3 = (f32[16,16,128]{2,1,0:T(8,128)S(1)}, f32[16,16,128]{2,1,0:T(8,128)}, u32[]{:S(2)}) copy-start(f32[16,16,128]{2,1,0:T(8,128)} %refs_3_.5) | copy-start | bytes 393220
  0.0 19.6 %copy-start.4 = (f32[16,16,128]{2,1,0:T(8,128)S(1)}, f32[16,16,128]{2,1,0:T(8,128)}, u32[]{:S(2)}) copy-start(f32[16,16,128]{2,1,0:T(8,128)} %refs_4_.5) | copy-start | bytes 393220
  0.0 19.6 %copy-start.5 = (f32[16,16,128]{2,1,0:T(8,128)S(1)}, f32[16,16,128]{2,1,0:T(8,128)}, u32[]{:S(2)}) copy-start(f32[16,16,128]{2,1,0:T(8,128)} %refs_5_.5) | copy-start | bytes 393220
  2.6 14.4 %collective-permute-start.2 = (f32[6,4,16,128]{3,2,1,0:T(8,128)}, f32[6,4,16,128]{3,2,1,0:T(8,128)S(1)}, u32[]{:S(2)}, u32[]{:S(2)}) collective-permute-start(f32[6,4,16,128]{3,2,1,0:T(8,128)} %get-tuple-element.39), channel_id=1, source_target_pairs={{0,16},{16,0},{1,17},{17,1},{2,18},{18,2},{3,19},{19,3},{4,20},{20... | collective-permute-start | bytes 589832 | tf_op jit(solution)/shard_map/ppermute | solution.py:669
  4.6 15.8 %collective-permute-start.4 = (f32[6,16,4,128]{3,2,1,0:T(4,128)}, f32[6,16,4,128]{3,2,1,0:T(4,128)S(1)}, u32[]{:S(2)}, u32[]{:S(2)}) collective-permute-start(f32[6,16,4,128]{3,2,1,0:T(4,128)} %get-tuple-element.41), channel_id=1, source_target_pairs={{4,8},{8,4},{12,0},{0,12},{5,9},{9,5},{13,1},{1,13},{6,10},{10,6},... | collective-permute-start | bytes 589832 | tf_op jit(solution)/shard_map/ppermute | solution.py:669
  6.7 13.7 %collective-permute-start.5 = (f32[6,16,4,128]{3,2,1,0:T(4,128)}, f32[6,16,4,128]{3,2,1,0:T(4,128)S(1)}, u32[]{:S(2)}, u32[]{:S(2)}) collective-permute-start(f32[6,16,4,128]{3,2,1,0:T(4,128)} %get-tuple-element.42), channel_id=1, source_target_pairs={{0,4},{4,0},{8,12},{12,8},{1,5},{5,1},{9,13},{13,9},{2,6},{6,2},{1... | collective-permute-start | bytes 589832 | tf_op jit(solution)/shard_map/ppermute | solution.py:669
  6.7 3.6 %collective-permute-start = (f32[8,16,128]{2,1,0:T(8,128)}, f32[8,16,128]{2,1,0:T(8,128)S(1)}, u32[]{:S(2)}, u32[]{:S(2)}) collective-permute-start(f32[8,16,128]{2,1,0:T(8,128)} %get-tuple-element.36), channel_id=1, source_target_pairs={{0,1},{1,0},{2,3},{3,2},{4,5},{5,4},{6,7},{7,6},{8,9},{9,8},{10,11... | collective-permute-start | bytes 196616 | tf_op jit(solution)/shard_map/ppermute | solution.py:669
  8.0 6.0 %collective-permute-start.1 = (f32[8,16,128]{2,1,0:T(8,128)}, f32[8,16,128]{2,1,0:T(8,128)S(1)}, u32[]{:S(2)}, u32[]{:S(2)}) collective-permute-start(f32[8,16,128]{2,1,0:T(8,128)} %get-tuple-element.37), channel_id=1, source_target_pairs={{1,2},{2,1},{3,0},{0,3},{5,6},{6,5},{7,4},{4,7},{9,10},{10,9},{11,... | collective-permute-start | bytes 196616 | tf_op jit(solution)/shard_map/ppermute | solution.py:669
  14.1 5.5 %copy-start.2 = (f32[16,16,128]{2,1,0:T(8,128)S(1)}, f32[16,16,128]{2,1,0:T(8,128)}, u32[]{:S(2)}) copy-start(f32[16,16,128]{2,1,0:T(8,128)} %refs_2_.5) | copy-start | bytes 393220
  14.2 2.8 %collective-permute-start.3 = (f32[4,16,128]{2,1,0:T(8,128)S(1)}, f32[4,16,128]{2,1,0:T(8,128)S(1)}, u32[]{:S(2)}, u32[]{:S(2)}) collective-permute-start(f32[4,16,128]{2,1,0:T(8,128)S(1)} %get-tuple-element.40), channel_id=1, source_target_pairs={{0,16},{16,0},{1,17},{17,1},{2,18},{18,2},{3,19},{19,3},{4,20},{20... | collective-permute-start | bytes 98312 | tf_op jit(solution)/shard_map/ppermute | solution.py:669
  17.0 2.6 %copy-start = (f32[16,16,128]{2,1,0:T(8,128)S(1)}, f32[16,16,128]{2,1,0:T(8,128)}, u32[]{:S(2)}) copy-start(f32[16,16,128]{2,1,0:T(8,128)} %refs_0_.5) | copy-start | bytes 393220
  17.0 2.6 %copy-start.1 = (f32[16,16,128]{2,1,0:T(8,128)S(1)}, f32[16,16,128]{2,1,0:T(8,128)}, u32[]{:S(2)}) copy-start(f32[16,16,128]{2,1,0:T(8,128)} %refs_1_.5) | copy-start | bytes 393220
  17.1 4.6 %collective-permute-start.6 = (f32[37,4,128]{2,1,0:T(4,128)S(1)}, f32[37,4,128]{2,1,0:T(4,128)S(1)}, u32[]{:S(2)}, u32[]{:S(2)}) collective-permute-start(f32[37,4,128]{2,1,0:T(4,128)S(1)} %get-tuple-element.43), channel_id=1, source_target_pairs={{4,8},{8,4},{12,0},{0,12},{5,9},{9,5},{13,1},{1,13},{6,10},{10,6},... | collective-permute-start | bytes 227336 | tf_op jit(solution)/shard_map/ppermute | solution.py:669
  19.6 2.1 %collective-permute-start.7 = (f32[37,4,128]{2,1,0:T(4,128)S(1)}, f32[37,4,128]{2,1,0:T(4,128)S(1)}, u32[]{:S(2)}, u32[]{:S(2)}) collective-permute-start(f32[37,4,128]{2,1,0:T(4,128)S(1)} %get-tuple-element.44), channel_id=1, source_target_pairs={{0,4},{4,0},{8,12},{12,8},{1,5},{5,1},{9,13},{13,9},{2,6},{6,2},{1... | collective-permute-start | bytes 227336 | tf_op jit(solution)/shard_map/ppermute | solution.py:669
  25.6 3.4 %collective-permute-start.8 = (f32[5,4,8,128]{3,2,1,0:T(8,128)S(1)}, f32[5,4,8,128]{3,2,1,0:T(8,128)S(1)}, u32[]{:S(2)}, u32[]{:S(2)}) collective-permute-start(f32[5,4,8,128]{3,2,1,0:T(8,128)S(1)} %get-tuple-element.47), channel_id=1, source_target_pairs={{0,16},{16,0},{1,17},{17,1},{2,18},{18,2},{3,19},{19,3},{4,20},{20... | collective-permute-start | bytes 245768 | tf_op jit(solution)/shard_map/ppermute | solution.py:669
  25.9 6.8 %collective-permute-start.9 = (f32[5,8,4,128]{3,2,1,0:T(4,128)S(1)}, f32[5,8,4,128]{3,2,1,0:T(4,128)S(1)}, u32[]{:S(2)}, u32[]{:S(2)}) collective-permute-start(f32[5,8,4,128]{3,2,1,0:T(4,128)S(1)} %get-tuple-element.48), channel_id=1, source_target_pairs={{4,8},{8,4},{12,0},{0,12},{5,9},{9,5},{13,1},{1,13},{6,10},{10,6},... | collective-permute-start | bytes 245768 | tf_op jit(solution)/shard_map/ppermute | solution.py:669
  28.7 4.0 %collective-permute-start.10 = (f32[5,8,4,128]{3,2,1,0:T(4,128)S(1)}, f32[5,8,4,128]{3,2,1,0:T(4,128)S(1)}, u32[]{:S(2)}, u32[]{:S(2)}) collective-permute-start(f32[5,8,4,128]{3,2,1,0:T(4,128)S(1)} %get-tuple-element.49), channel_id=1, source_target_pairs={{0,4},{4,0},{8,12},{12,8},{1,5},{5,1},{9,13},{13,9},{2,6},{6,2},{1... | collective-permute-start | bytes 245768 | tf_op jit(solution)/shard_map/ppermute | solution.py:669
  29.0 6.2 %collective-permute-start.11 = (f32[25,4,128]{2,1,0:T(4,128)S(1)}, f32[25,4,128]{2,1,0:T(4,128)S(1)}, u32[]{:S(2)}, u32[]{:S(2)}) collective-permute-start(f32[25,4,128]{2,1,0:T(4,128)S(1)} %get-tuple-element.50), channel_id=1, source_target_pairs={{4,8},{8,4},{12,0},{0,12},{5,9},{9,5},{13,1},{1,13},{6,10},{10,6},... | collective-permute-start | bytes 153608 | tf_op jit(solution)/shard_map/ppermute | solution.py:669
  32.7 2.5 %collective-permute-start.12 = (f32[25,4,128]{2,1,0:T(4,128)S(1)}, f32[25,4,128]{2,1,0:T(4,128)S(1)}, u32[]{:S(2)}, u32[]{:S(2)}) collective-permute-start(f32[25,4,128]{2,1,0:T(4,128)S(1)} %get-tuple-element.51), channel_id=1, source_target_pairs={{0,4},{4,0},{8,12},{12,8},{1,5},{5,1},{9,13},{13,9},{2,6},{6,2},{1... | collective-permute-start | bytes 153608 | tf_op jit(solution)/shard_map/ppermute | solution.py:669

commit v9 on v8

--- a/solution.py
+++ b/solution.py
@@ -664,9 +664,10 @@
     count = lax.axis_size(axis)
     got = []
     for k, block in enumerate(sends):
-        pairs = [(i, (i + 1) % count) for i in range(k, count, 2)]
-        pairs = [pair for low, high in pairs for pair in ((low, high), (high, low))]
-        got.append(lax.ppermute(block, axis, pairs))
+        partner = list(range(count))
+        for low in range(k, count - 1, 2):
+            partner[low], partner[low + 1] = low + 1, low
+        got.append(lax.ppermute(block, axis, list(enumerate(partner))))
     return got
 
 

time: 55.7 us -> 60.3 us (1.083)
  starting transfers between devices: 17.2 us -> 22 us
  waiting for transfers between devices: 10.3 us -> 5.86 us
  blocking collectives: 14.8 us -> 18.9 us
    ppermute x13, starting transfers between devices: 17.2 us -> 22 us  [swaps(): got.append(lax.ppermute(block, axis, list(enumerate(partner))))]
    ppermute x13, waiting for transfers between devices: 10.3 us -> 5.86 us  [swaps(): got.append(lax.ppermute(block, axis, list(enumerate(partner))))]
    all_to_all x1, blocking collectives: 14.8 us -> 18.9 us  [local(): gathered = lax.all_to_all(copies, axes, 0, 0, tiled=True)]
  transfers between devices with their start and end apart: 13 -> 13, of which waited for: 6 -> 4; matrix products, arithmetic and copies ran while one was open for 0% -> 0% of each run, Pallas kernels for 2% -> 2%
where the time goes in v9:
time: 60.3 us; the launch traced here: 60.1 us
  starting transfers between devices  22 us (36%)
  blocking collectives  18.9 us (31%)
  Pallas kernels  13 us (22%)
  waiting for transfers between devices  5.86 us (10%)
    ppermute x13, starting transfers between devices, swaps(): got.append(lax.ppermute(block, axis, list(enumerate(partner))))  22 us
    all_to_all x1, blocking collectives, local(): gathered = lax.all_to_all(copies, axes, 0, 0, tiled=True)  18.9 us
    pallas_call x8, Pallas kernels, run(): pl.pallas_call(kernel, out_shape=tuple((jax.ShapeDtypeStruct(shape, F32)...  13 us
    ppermute x13, waiting for transfers between devices, swaps(): got.append(lax.ppermute(block, axis, list(enumerate(partner))))  5.86 us
  transfers between devices with their start and end apart: 13, of which 4 were waited for; matrix products, arithmetic and copies ran while one was open for 0% of the time, Pallas kernels for 2%

profile of v9, /device:TPU:1, one launch (start us, length us, event | category | flops | bytes accessed | tf_op | source)
XLA Modules:
  0.0 60.1 jit_solution(11975554088463156242)
XLA Ops:
  0.0 2.6 %shard_map.64 = (f32[6,4,16,128]{3,2,1,0:T(8,128)}, f32[6,16,4,128]{3,2,1,0:T(4,128)}, f32[6,16,4,128]{3,2,1,0:T(4,128)}, f32[8,16,128]{2,1,0:T(8,128)}, f32[8,16,128]{2,1,0:T(8,128)}) custom-call(s32[1]{0:T(128)} %bitcast.where_ref, f32[16,16,128]{2,1,0:T(8,128)} %refs_0_.5, f32[16,16,128]{2,1,0:T(8,128)} %refs_1_.5, f32[16,16,128]{2,1,0:T(8,128)} %refs_2_.5, ...), custom_call_target="tpu_custom_call" | custom-call | bytes 3600000 | tf_op jit(solution)/shard_map/pallas_call | solution.py:650
  2.6 2.0 %collective-permute-start.2 = (f32[6,4,16,128]{3,2,1,0:T(8,128)}, f32[6,4,16,128]{3,2,1,0:T(8,128)S(1)}, u32[]{:S(2)}, u32[]{:S(2)}) collective-permute-start(f32[6,4,16,128]{3,2,1,0:T(8,128)} %get-tuple-element.39), channel_id=1, source_target_pairs={{0,16},{16,0},{1,17},{17,1},{2,18},{18,2},{3,19},{19,3},{4,20},{20... | collective-permute-start | bytes 589832 | tf_op jit(solution)/shard_map/ppermute | solution.py:670
  4.6 4.0 %collective-permute-start.4 = (f32[6,16,4,128]{3,2,1,0:T(4,128)}, f32[6,16,4,128]{3,2,1,0:T(4,128)S(1)}, u32[]{:S(2)}, u32[]{:S(2)}) collective-permute-start(f32[6,16,4,128]{3,2,1,0:T(4,128)} %get-tuple-element.41), channel_id=1, source_target_pairs={{0,0},{4,8},{8,4},{12,12},{1,1},{5,9},{9,5},{13,13},{2,2},{6,10},{... | collective-permute-start | bytes 589832 | tf_op jit(solution)/shard_map/ppermute | solution.py:670
  8.6 0.1 collective-permute-start.5
  8.7 1.4 %collective-permute-start = (f32[8,16,128]{2,1,0:T(8,128)}, f32[8,16,128]{2,1,0:T(8,128)S(1)}, u32[]{:S(2)}, u32[]{:S(2)}) collective-permute-start(f32[8,16,128]{2,1,0:T(8,128)} %get-tuple-element.36), channel_id=1, source_target_pairs={{0,1},{1,0},{2,3},{3,2},{4,5},{5,4},{6,7},{7,6},{8,9},{9,8},{10,11... | collective-permute-start | bytes 196616 | tf_op jit(solution)/shard_map/ppermute | solution.py:670
  10.1 1.5 %collective-permute-start.1 = (f32[8,16,128]{2,1,0:T(8,128)}, f32[8,16,128]{2,1,0:T(8,128)S(1)}, u32[]{:S(2)}, u32[]{:S(2)}) collective-permute-start(f32[8,16,128]{2,1,0:T(8,128)} %get-tuple-element.37), channel_id=1, source_target_pairs={{0,0},{1,2},{2,1},{3,3},{4,4},{5,6},{6,5},{7,7},{8,8},{9,10},{10,9... | collective-permute-start | bytes 196616 | tf_op jit(solution)/shard_map/ppermute | solution.py:670
  11.5 0.5 collective-permute-done.one_ref
  12.1 0.0 collective-permute-done.1.two_ref
  12.1 0.1 shard_map.65
  12.2 0.3 collective-permute-start.3
  12.5 2.5 %collective-permute-done.3.refs_1_.refs_8_ = f32[4,16,128]{2,1,0:T(8,128)S(1)} collective-permute-done((f32[4,16,128]{2,1,0:T(8,128)S(1)}, f32[4,16,128]{2,1,0:T(8,128)S(1)}, u32[]{:S(2)}, u32[]{:S(2)}) %collective-permute-start.3) | collective-permute-done | bytes 32800 | tf_op jit(solution)/shard_map/ppermute | solution.py:670
  15.0 0.0 collective-permute-done.2.refs_0_.refs_7_
  15.0 0.1 shard_map.66
  15.1 4.5 %collective-permute-start.6 = (f32[37,4,128]{2,1,0:T(4,128)S(1)}, f32[37,4,128]{2,1,0:T(4,128)S(1)}, u32[]{:S(2)}, u32[]{:S(2)}) collective-permute-start(f32[37,4,128]{2,1,0:T(4,128)S(1)} %get-tuple-element.43), channel_id=1, source_target_pairs={{0,0},{4,8},{8,4},{12,12},{1,1},{5,9},{9,5},{13,13},{2,2},{6,10},{... | collective-permute-start | bytes 227336 | tf_op jit(solution)/shard_map/ppermute | solution.py:670
  19.6 0.1 collective-permute-start.7
  19.8 0.8 %shard_map.67 = (f32[4,4,128]{2,1,0:T(4,128)S(1)}, f32[5,8,8,128]{3,2,1,0:T(8,128)S(1)}) custom-call(s32[1]{0:T(128)} %bitcast.where_ref, f32[16,16,128]{2,1,0:T(8,128)S(1)} %copy-done, f32[16,16,128]{2,1,0:T(8,128)S(1)} %copy-done.1, f32[16,16,128]{2,1,0:T(8,128)S(1)} %copy-done.2, f32[16,16,128]{2,1,0:T(8,128)S(1)} %copy-done.3, ...), custom_call_target="tpu_custom_call" | custom-call | bytes 7200000 | tf_op jit(solution)/shard_map/pallas_call | solution.py:650
  20.6 0.0 collective-permute-done.4.refs_9_
  20.6 0.0 collective-permute-done.5.refs_10_
  20.6 1.1 %collective-permute-done.6.refs_11_ = f32[37,4,128]{2,1,0:T(4,128)S(1)} collective-permute-done((f32[37,4,128]{2,1,0:T(4,128)S(1)}, f32[37,4,128]{2,1,0:T(4,128)S(1)}, u32[]{:S(2)}, u32[]{:S(2)}) %collective-permute-start.6) | collective-permute-done | bytes 75808 | tf_op jit(solution)/shard_map/ppermute | solution.py:670
  21.7 0.0 collective-permute-done.7.refs_12_
  21.7 3.9 %shard_map.68 = (f32[5,8,8,128]{3,2,1,0:T(8,128)S(1)}, f32[5,4,8,128]{3,2,1,0:T(8,128)S(1)}, f32[5,8,4,128]{3,2,1,0:T(4,128)S(1)}, f32[5,8,4,128]{3,2,1,0:T(4,12...) custom-call(s32[1]{0:T(128)} %bitcast.where_ref, ...), custom_call_target="tpu_custom_call" | custom-call | bytes 14400000 | tf_op jit(solution)/shard_map/pallas_call | solution.py:650
  25.6 0.3 collective-permute-start.8
  26.0 3.9 %collective-permute-start.9 = (f32[5,8,4,128]{3,2,1,0:T(4,128)S(1)}, f32[5,8,4,128]{3,2,1,0:T(4,128)S(1)}, u32[]{:S(2)}, u32[]{:S(2)}) collective-permute-start(f32[5,8,4,128]{3,2,1,0:T(4,128)S(1)} %get-tuple-element.48), channel_id=1, source_target_pairs={{0,0},{4,8},{8,4},{12,12},{1,1},{5,9},{9,5},{13,13},{2,2},{6,10},{... | collective-permute-start | bytes 245768 | tf_op jit(solution)/shard_map/ppermute | solution.py:670
  29.9 0.1 collective-permute-start.10
  30.0 3.8 %collective-permute-start.11 = (f32[25,4,128]{2,1,0:T(4,128)S(1)}, f32[25,4,128]{2,1,0:T(4,128)S(1)}, u32[]{:S(2)}, u32[]{:S(2)}) collective-permute-start(f32[25,4,128]{2,1,0:T(4,128)S(1)} %get-tuple-element.50), channel_id=1, source_target_pairs={{0,0},{4,8},{8,4},{12,12},{1,1},{5,9},{9,5},{13,13},{2,2},{6,10},{... | collective-permute-start | bytes 153608 | tf_op jit(solution)/shard_map/ppermute | solution.py:670
  33.8 0.1 collective-permute-start.12
  33.9 0.0 collective-permute-done.10.refs_2_
  33.9 1.7 %collective-permute-done.11.refs_3_ = f32[25,4,128]{2,1,0:T(4,128)S(1)} collective-permute-done((f32[25,4,128]{2,1,0:T(4,128)S(1)}, f32[25,4,128]{2,1,0:T(4,128)S(1)}, u32[]{:S(2)}, u32[]{:S(2)}) %collective-permute-start.11) | collective-permute-done | bytes 51232 | tf_op jit(solution)/shard_map/ppermute | solution.py:670
  35.6 0.0 collective-permute-done.12.refs_4_
  35.6 0.4 shard_map.70
  36.0 18.9 %all_to_all.5.gathered = f32[32,5,4,128]{3,2,1,0:T(4,128)S(1)} all-to-all(f32[32,5,4,128]{3,2,1,0:T(4,128)S(1)} %get-tuple-element.53), channel_id=1, replica_groups=mesh['gx'=2,'gy'=4,'gz'=4] {'gx','gy','gz'}, dimensions={0} | all-to-all | bytes 655360 | tf_op jit(solution)/shard_map/all_to_all | solution.py:750
  54.9 5.1 %shard_map.71 = f32[16,16,128]{2,1,0:T(8,128)} custom-call(s32[1]{0:T(128)} %bitcast.where_ref, f32[32,5,4,128]{3,2,1,0:T(4,128)S(1)} %all_to_all.5.gathered, f32[6,16,16,128]{3,2,1,0:T(8,128)S(1)} %get-tuple-element.54.level1, f32[24,24,128]{2,1,0:T(8,128)S(1)} %get-tuple-element.55.refs_0_, f32[24,24,128]{2,1,0:T(8,128)S(1)} %get-tuple-element.56.refs_1_, ...), custom_call_target="tpu_custom_call" | custom-call | bytes 14400000 | tf_op jit(solution)/shard_map/pallas_call | solution.py:650
  (15 shorter events, 0.1 us)
Async XLA Ops:
  0.0 19.7 %copy-start.3 = (f32[16,16,128]{2,1,0:T(8,128)S(1)}, f32[16,16,128]{2,1,0:T(8,128)}, u32[]{:S(2)}) copy-start(f32[16,16,128]{2,1,0:T(8,128)} %refs_3_.5) | copy-start | bytes 393220
  0.0 19.7 %copy-start.4 = (f32[16,16,128]{2,1,0:T(8,128)S(1)}, f32[16,16,128]{2,1,0:T(8,128)}, u32[]{:S(2)}) copy-start(f32[16,16,128]{2,1,0:T(8,128)} %refs_4_.5) | copy-start | bytes 393220
  0.0 19.7 %copy-start.5 = (f32[16,16,128]{2,1,0:T(8,128)S(1)}, f32[16,16,128]{2,1,0:T(8,128)}, u32[]{:S(2)}) copy-start(f32[16,16,128]{2,1,0:T(8,128)} %refs_5_.5) | copy-start | bytes 393220
  2.6 12.4 %collective-permute-start.2 = (f32[6,4,16,128]{3,2,1,0:T(8,128)}, f32[6,4,16,128]{3,2,1,0:T(8,128)S(1)}, u32[]{:S(2)}, u32[]{:S(2)}) collective-permute-start(f32[6,4,16,128]{3,2,1,0:T(8,128)} %get-tuple-element.39), channel_id=1, source_target_pairs={{0,16},{16,0},{1,17},{17,1},{2,18},{18,2},{3,19},{19,3},{4,20},{20... | collective-permute-start | bytes 589832 | tf_op jit(solution)/shard_map/ppermute | solution.py:670
  4.6 15.9 %collective-permute-start.4 = (f32[6,16,4,128]{3,2,1,0:T(4,128)}, f32[6,16,4,128]{3,2,1,0:T(4,128)S(1)}, u32[]{:S(2)}, u32[]{:S(2)}) collective-permute-start(f32[6,16,4,128]{3,2,1,0:T(4,128)} %get-tuple-element.41), channel_id=1, source_target_pairs={{0,0},{4,8},{8,4},{12,12},{1,1},{5,9},{9,5},{13,13},{2,2},{6,10},{... | collective-permute-start | bytes 589832 | tf_op jit(solution)/shard_map/ppermute | solution.py:670
  8.6 12.0 %collective-permute-start.5 = (f32[6,16,4,128]{3,2,1,0:T(4,128)}, f32[6,16,4,128]{3,2,1,0:T(4,128)S(1)}, u32[]{:S(2)}, u32[]{:S(2)}) collective-permute-start(f32[6,16,4,128]{3,2,1,0:T(4,128)} %get-tuple-element.42), channel_id=1, source_target_pairs={{0,4},{4,0},{8,12},{12,8},{1,5},{5,1},{9,13},{13,9},{2,6},{6,2},{1... | collective-permute-start | bytes 589832 | tf_op jit(solution)/shard_map/ppermute | solution.py:670
  8.7 3.4 %collective-permute-start = (f32[8,16,128]{2,1,0:T(8,128)}, f32[8,16,128]{2,1,0:T(8,128)S(1)}, u32[]{:S(2)}, u32[]{:S(2)}) collective-permute-start(f32[8,16,128]{2,1,0:T(8,128)} %get-tuple-element.36), channel_id=1, source_target_pairs={{0,1},{1,0},{2,3},{3,2},{4,5},{5,4},{6,7},{7,6},{8,9},{9,8},{10,11... | collective-permute-start | bytes 196616 | tf_op jit(solution)/shard_map/ppermute | solution.py:670
  10.1 2.0 %collective-permute-start.1 = (f32[8,16,128]{2,1,0:T(8,128)}, f32[8,16,128]{2,1,0:T(8,128)S(1)}, u32[]{:S(2)}, u32[]{:S(2)}) collective-permute-start(f32[8,16,128]{2,1,0:T(8,128)} %get-tuple-element.37), channel_id=1, source_target_pairs={{0,0},{1,2},{2,1},{3,3},{4,4},{5,6},{6,5},{7,7},{8,8},{9,10},{10,9... | collective-permute-start | bytes 196616 | tf_op jit(solution)/shard_map/ppermute | solution.py:670
  12.1 7.7 %copy-start.2 = (f32[16,16,128]{2,1,0:T(8,128)S(1)}, f32[16,16,128]{2,1,0:T(8,128)}, u32[]{:S(2)}) copy-start(f32[16,16,128]{2,1,0:T(8,128)} %refs_2_.5) | copy-start | bytes 393220
  12.2 2.8 %collective-permute-start.3 = (f32[4,16,128]{2,1,0:T(8,128)S(1)}, f32[4,16,128]{2,1,0:T(8,128)S(1)}, u32[]{:S(2)}, u32[]{:S(2)}) collective-permute-start(f32[4,16,128]{2,1,0:T(8,128)S(1)} %get-tuple-element.40), channel_id=1, source_target_pairs={{0,16},{16,0},{1,17},{17,1},{2,18},{18,2},{3,19},{19,3},{4,20},{20... | collective-permute-start | bytes 98312 | tf_op jit(solution)/shard_map/ppermute | solution.py:670
  15.0 4.7 %copy-start = (f32[16,16,128]{2,1,0:T(8,128)S(1)}, f32[16,16,128]{2,1,0:T(8,128)}, u32[]{:S(2)}) copy-start(f32[16,16,128]{2,1,0:T(8,128)} %refs_0_.5) | copy-start | bytes 393220
  15.0 4.7 %copy-start.1 = (f32[16,16,128]{2,1,0:T(8,128)S(1)}, f32[16,16,128]{2,1,0:T(8,128)}, u32[]{:S(2)}) copy-start(f32[16,16,128]{2,1,0:T(8,128)} %refs_1_.5) | copy-start | bytes 393220
  15.1 6.6 %collective-permute-start.6 = (f32[37,4,128]{2,1,0:T(4,128)S(1)}, f32[37,4,128]{2,1,0:T(4,128)S(1)}, u32[]{:S(2)}, u32[]{:S(2)}) collective-permute-start(f32[37,4,128]{2,1,0:T(4,128)S(1)} %get-tuple-element.43), channel_id=1, source_target_pairs={{0,0},{4,8},{8,4},{12,12},{1,1},{5,9},{9,5},{13,13},{2,2},{6,10},{... | collective-permute-start | bytes 227336 | tf_op jit(solution)/shard_map/ppermute | solution.py:670
  19.6 2.0 %collective-permute-start.7 = (f32[37,4,128]{2,1,0:T(4,128)S(1)}, f32[37,4,128]{2,1,0:T(4,128)S(1)}, u32[]{:S(2)}, u32[]{:S(2)}) collective-permute-start(f32[37,4,128]{2,1,0:T(4,128)S(1)} %get-tuple-element.44), channel_id=1, source_target_pairs={{0,4},{4,0},{8,12},{12,8},{1,5},{5,1},{9,13},{13,9},{2,6},{6,2},{1... | collective-permute-start | bytes 227336 | tf_op jit(solution)/shard_map/ppermute | solution.py:670
  25.6 4.3 %collective-permute-start.8 = (f32[5,4,8,128]{3,2,1,0:T(8,128)S(1)}, f32[5,4,8,128]{3,2,1,0:T(8,128)S(1)}, u32[]{:S(2)}, u32[]{:S(2)}) collective-permute-start(f32[5,4,8,128]{3,2,1,0:T(8,128)S(1)} %get-tuple-element.47), channel_id=1, source_target_pairs={{0,16},{16,0},{1,17},{17,1},{2,18},{18,2},{3,19},{19,3},{4,20},{20... | collective-permute-start | bytes 245768 | tf_op jit(solution)/shard_map/ppermute | solution.py:670
  26.0 8.0 %collective-permute-start.9 = (f32[5,8,4,128]{3,2,1,0:T(4,128)S(1)}, f32[5,8,4,128]{3,2,1,0:T(4,128)S(1)}, u32[]{:S(2)}, u32[]{:S(2)}) collective-permute-start(f32[5,8,4,128]{3,2,1,0:T(4,128)S(1)} %get-tuple-element.48), channel_id=1, source_target_pairs={{0,0},{4,8},{8,4},{12,12},{1,1},{5,9},{9,5},{13,13},{2,2},{6,10},{... | collective-permute-start | bytes 245768 | tf_op jit(solution)/shard_map/ppermute | solution.py:670
  29.9 4.0 %collective-permute-start.10 = (f32[5,8,4,128]{3,2,1,0:T(4,128)S(1)}, f32[5,8,4,128]{3,2,1,0:T(4,128)S(1)}, u32[]{:S(2)}, u32[]{:S(2)}) collective-permute-start(f32[5,8,4,128]{3,2,1,0:T(4,128)S(1)} %get-tuple-element.49), channel_id=1, source_target_pairs={{0,4},{4,0},{8,12},{12,8},{1,5},{5,1},{9,13},{13,9},{2,6},{6,2},{1... | collective-permute-start | bytes 245768 | tf_op jit(solution)/shard_map/ppermute | solution.py:670
  30.0 5.6 %collective-permute-start.11 = (f32[25,4,128]{2,1,0:T(4,128)S(1)}, f32[25,4,128]{2,1,0:T(4,128)S(1)}, u32[]{:S(2)}, u32[]{:S(2)}) collective-permute-start(f32[25,4,128]{2,1,0:T(4,128)S(1)} %get-tuple-element.50), channel_id=1, source_target_pairs={{0,0},{4,8},{8,4},{12,12},{1,1},{5,9},{9,5},{13,13},{2,2},{6,10},{... | collective-permute-start | bytes 153608 | tf_op jit(solution)/shard_map/ppermute | solution.py:670
  33.8 1.8 %collective-permute-start.12 = (f32[25,4,128]{2,1,0:T(4,128)S(1)}, f32[25,4,128]{2,1,0:T(4,128)S(1)}, u32[]{:S(2)}, u32[]{:S(2)}) collective-permute-start(f32[25,4,128]{2,1,0:T(4,128)S(1)} %get-tuple-element.51), channel_id=1, source_target_pairs={{0,4},{4,0},{8,12},{12,8},{1,5},{5,1},{9,13},{13,9},{2,6},{6,2},{1... | collective-permute-start | bytes 153608 | tf_op jit(solution)/shard_map/ppermute | solution.py:670

commit v10 on v9

--- a/solution.py
+++ b/solution.py
@@ -660,14 +660,26 @@
     )(*where, *arrays)
 
 
-def swaps(axis, sends):
+def swaps(axis, sends, other=None):
     count = lax.axis_size(axis)
     got = []
     for k, block in enumerate(sends):
         partner = list(range(count))
         for low in range(k, count - 1, 2):
             partner[low], partner[low + 1] = low + 1, low
-        got.append(lax.ppermute(block, axis, list(enumerate(partner))))
+        if k == 0:
+            got.append(lax.ppermute(block, axis, list(enumerate(partner))))
+            continue
+        rows = lax.axis_size(other)
+        pairs = []
+        for row in range(rows):
+            for i in range(count):
+                ends = [(row, i), (min(row ^ 1, rows - 1) if partner[i] == i else row, partner[i])]
+                if axis < other:
+                    pairs.append(tuple(at * rows + line for line, at in ends))
+                else:
+                    pairs.append(tuple(line * count + at for line, at in ends))
+        got.append(lax.ppermute(block, tuple(sorted((axis, other))), pairs))
     return got
 
 
@@ -692,23 +704,23 @@
         ins,
         grant=60,
     )
-    main_x = tuple(swaps("gx", sends_x))
-    main_y = tuple(swaps("gy", (one_y, two_y))[::-1])
-    got = swaps("gz", (first, second))
+    main_x = tuple(swaps("gx", sends_x, "gy"))
+    main_y = tuple(swaps("gy", (one_y, two_y), "gz")[::-1])
+    got = swaps("gz", (first, second), "gy")
     zpack, *sends = run(
         functools.partial(halo_z_kernel, counts),
         [(sx, sy, LANES)] + [(HALO, sy, LANES)] * n_x,
         where,
         tuple(got),
     )
-    halos_x = tuple(swaps("gx", sends))
+    halos_x = tuple(swaps("gx", sends, "gy"))
     two_y, one_y = run(
         functools.partial(corners_kernel, counts),
         [(21 + sx, HALO, LANES)] * 2,
         where,
         (zpack,) + main_x + halos_x,
     )
-    rest_y = tuple(swaps("gy", (one_y, two_y))[::-1])
+    rest_y = tuple(swaps("gy", (one_y, two_y), "gz")[::-1])
     x1, y1 = sx // 2, sy // 2
     ins = ins + (zpack,)
     coarse2, coeffs1 = run(
@@ -733,12 +745,12 @@
     )
     sends_x, (two_y, one_y), fine_arrays = outs[:n_x], outs[n_x:n_x + 2], outs[n_x + 2:]
 
-    near_x = tuple(swaps("gx", sends_x))
-    near_y = tuple(swaps("gy", (one_y, two_y))[::-1])
+    near_x = tuple(swaps("gx", sends_x, "gy"))
+    near_y = tuple(swaps("gy", (one_y, two_y), "gz")[::-1])
     two_y, one_y = run(
         functools.partial(near_corners_kernel, counts), [(25, NEAR, LANES)] * 2, where, near_x
     )
-    rest_y = tuple(swaps("gy", (one_y, two_y))[::-1])
+    rest_y = tuple(swaps("gy", (one_y, two_y), "gz")[::-1])
     copies, level1 = run(
         functools.partial(near_kernel, counts, devices),
         [(devices, 5, y1 // 2, LANES), (6, x1 + 2 * NEAR, y1 + 2 * NEAR, LANES)],

time: 60.3 us -> 54.9 us (0.910)
  starting transfers between devices: 22 us -> 18.8 us
  blocking collectives: 18.9 us -> 16.7 us
    ppermute x13 -> x8, starting transfers between devices: 22 us -> 10.8 us  [swaps(): got.append(lax.ppermute(block, axis, list(enumerate(partner))))]
    ppermute x0 -> x5, starting transfers between devices: none -> 8 us  [swaps(): got.append(lax.ppermute(block, tuple(sorted((axis, other))), pairs))]
    all_to_all x1, blocking collectives: 18.9 us -> 16.7 us  [local(): gathered = lax.all_to_all(copies, axes, 0, 0, tiled=True)]
    ppermute x13 -> x8, waiting for transfers between devices: 5.86 us -> 6.11 us  [swaps(): got.append(lax.ppermute(block, axis, list(enumerate(partner))))]
where the time goes in v10:
time: 54.9 us; the launch traced here: 54.8 us
  starting transfers between devices  18.8 us (34%)
  blocking collectives  16.7 us (30%)
  Pallas kernels  13 us (24%)
  waiting for transfers between devices  6.12 us (11%)
    all_to_all x1, blocking collectives, local(): gathered = lax.all_to_all(copies, axes, 0, 0, tiled=True)  16.7 us
    pallas_call x8, Pallas kernels, run(): pl.pallas_call(kernel, out_shape=tuple((jax.ShapeDtypeStruct(shape, F32)...  13 us
    ppermute x8, starting transfers between devices, swaps(): got.append(lax.ppermute(block, axis, list(enumerate(partner))))  10.8 us
    ppermute x5, starting transfers between devices, swaps(): got.append(lax.ppermute(block, tuple(sorted((axis, other))), pairs))  8 us
    ppermute x8, waiting for transfers between devices, swaps(): got.append(lax.ppermute(block, axis, list(enumerate(partner))))  6.11 us
  transfers between devices with their start and end apart: 13, of which 4 were waited for; matrix products, arithmetic and copies ran while one was open for 0% of the time, Pallas kernels for 2%

profile of v10, /device:TPU:1, one launch (start us, length us, event | category | flops | bytes accessed | tf_op | source)
XLA Modules:
  0.0 54.8 jit_solution(11118933983369986455)
XLA Ops:
  0.0 2.6 %shard_map.64 = (f32[6,4,16,128]{3,2,1,0:T(8,128)}, f32[6,16,4,128]{3,2,1,0:T(4,128)}, f32[6,16,4,128]{3,2,1,0:T(4,128)}, f32[8,16,128]{2,1,0:T(8,128)}, f32[8,16,128]{2,1,0:T(8,128)}) custom-call(s32[1]{0:T(128)} %bitcast.where_ref, f32[16,16,128]{2,1,0:T(8,128)} %refs_0_.5, f32[16,16,128]{2,1,0:T(8,128)} %refs_1_.5, f32[16,16,128]{2,1,0:T(8,128)} %refs_2_.5, ...), custom_call_target="tpu_custom_call" | custom-call | bytes 3600000 | tf_op jit(solution)/shard_map/pallas_call | solution.py:650
  2.6 2.0 %collective-permute-start.2 = (f32[6,4,16,128]{3,2,1,0:T(8,128)}, f32[6,4,16,128]{3,2,1,0:T(8,128)S(1)}, u32[]{:S(2)}, u32[]{:S(2)}) collective-permute-start(f32[6,4,16,128]{3,2,1,0:T(8,128)} %get-tuple-element.39), channel_id=1, source_target_pairs={{0,16},{16,0},{1,17},{17,1},{2,18},{18,2},{3,19},{19,3},{4,20},{20... | collective-permute-start | bytes 589832 | tf_op jit(solution)/shard_map/ppermute | solution.py:671
  4.6 2.1 %collective-permute-start.4 = (f32[6,16,4,128]{3,2,1,0:T(4,128)}, f32[6,16,4,128]{3,2,1,0:T(4,128)S(1)}, u32[]{:S(2)}, u32[]{:S(2)}) collective-permute-start(f32[6,16,4,128]{3,2,1,0:T(4,128)} %get-tuple-element.41), channel_id=1, source_target_pairs={{0,1},{4,8},{8,4},{12,13},{1,0},{5,9},{9,5},{13,12},{2,3},{6,10},{... | collective-permute-start | bytes 589832 | tf_op jit(solution)/shard_map/ppermute | solution.py:682
  6.7 0.5 collective-permute-start.5
  7.2 0.8 %collective-permute-start = (f32[8,16,128]{2,1,0:T(8,128)}, f32[8,16,128]{2,1,0:T(8,128)S(1)}, u32[]{:S(2)}, u32[]{:S(2)}) collective-permute-start(f32[8,16,128]{2,1,0:T(8,128)} %get-tuple-element.36), channel_id=1, source_target_pairs={{0,1},{1,0},{2,3},{3,2},{4,5},{5,4},{6,7},{7,6},{8,9},{9,8},{10,11... | collective-permute-start | bytes 196616 | tf_op jit(solution)/shard_map/ppermute | solution.py:671
  8.0 0.8 %collective-permute-start.1 = (f32[8,16,128]{2,1,0:T(8,128)}, f32[8,16,128]{2,1,0:T(8,128)S(1)}, u32[]{:S(2)}, u32[]{:S(2)}) collective-permute-start(f32[8,16,128]{2,1,0:T(8,128)} %get-tuple-element.37), channel_id=1, source_target_pairs={{0,4},{1,2},{2,1},{3,7},{4,0},{5,6},{6,5},{7,3},{8,12},{9,10},{10,... | collective-permute-start | bytes 196616 | tf_op jit(solution)/shard_map/ppermute | solution.py:682
  8.8 2.7 %collective-permute-done.one_ref = f32[8,16,128]{2,1,0:T(8,128)S(1)} collective-permute-done((f32[8,16,128]{2,1,0:T(8,128)}, f32[8,16,128]{2,1,0:T(8,128)S(1)}, u32[]{:S(2)}, u32[]{:S(2)}) %collective-permute-start) | collective-permute-done | bytes 65568 | tf_op jit(solution)/shard_map/ppermute | solution.py:671
  11.5 0.0 collective-permute-done.1.two_ref
  11.5 0.1 shard_map.65
  11.6 0.4 collective-permute-start.3
  12.0 2.5 %collective-permute-done.3.refs_1_.refs_8_ = f32[4,16,128]{2,1,0:T(8,128)S(1)} collective-permute-done((f32[4,16,128]{2,1,0:T(8,128)S(1)}, f32[4,16,128]{2,1,0:T(8,128)S(1)}, u32[]{:S(2)}, u32[]{:S(2)}) %collective-permute-start.3) | collective-permute-done | bytes 32800 | tf_op jit(solution)/shard_map/ppermute | solution.py:671
  14.5 0.1 shard_map.66
  14.5 2.3 %collective-permute-start.6 = (f32[37,4,128]{2,1,0:T(4,128)S(1)}, f32[37,4,128]{2,1,0:T(4,128)S(1)}, u32[]{:S(2)}, u32[]{:S(2)}) collective-permute-start(f32[37,4,128]{2,1,0:T(4,128)S(1)} %get-tuple-element.43), channel_id=1, source_target_pairs={{0,1},{4,8},{8,4},{12,13},{1,0},{5,9},{9,5},{13,12},{2,3},{6,10},{... | collective-permute-start | bytes 227336 | tf_op jit(solution)/shard_map/ppermute | solution.py:682
  16.8 1.9 %collective-permute-start.7 = (f32[37,4,128]{2,1,0:T(4,128)S(1)}, f32[37,4,128]{2,1,0:T(4,128)S(1)}, u32[]{:S(2)}, u32[]{:S(2)}) collective-permute-start(f32[37,4,128]{2,1,0:T(4,128)S(1)} %get-tuple-element.44), channel_id=1, source_target_pairs={{0,4},{4,0},{8,12},{12,8},{1,5},{5,1},{9,13},{13,9},{2,6},{6,2},{1... | collective-permute-start | bytes 227336 | tf_op jit(solution)/shard_map/ppermute | solution.py:671
  18.7 0.8 %shard_map.67 = (f32[4,4,128]{2,1,0:T(4,128)S(1)}, f32[5,8,8,128]{3,2,1,0:T(8,128)S(1)}) custom-call(s32[1]{0:T(128)} %bitcast.where_ref, f32[16,16,128]{2,1,0:T(8,128)S(1)} %copy-done, f32[16,16,128]{2,1,0:T(8,128)S(1)} %copy-done.1, f32[16,16,128]{2,1,0:T(8,128)S(1)} %copy-done.2, f32[16,16,128]{2,1,0:T(8,128)S(1)} %copy-done.3, ...), custom_call_target="tpu_custom_call" | custom-call | bytes 7200000 | tf_op jit(solution)/shard_map/pallas_call | solution.py:650
  19.5 0.0 collective-permute-done.4.refs_9_
  19.5 0.0 collective-permute-done.5.refs_10_
  19.5 0.1 collective-permute-done.7.refs_12_
  19.6 3.9 %shard_map.68 = (f32[5,8,8,128]{3,2,1,0:T(8,128)S(1)}, f32[5,4,8,128]{3,2,1,0:T(8,128)S(1)}, f32[5,8,4,128]{3,2,1,0:T(4,128)S(1)}, f32[5,8,4,128]{3,2,1,0:T(4,12...) custom-call(s32[1]{0:T(128)} %bitcast.where_ref, ...), custom_call_target="tpu_custom_call" | custom-call | bytes 14400000 | tf_op jit(solution)/shard_map/pallas_call | solution.py:650
  23.5 0.3 collective-permute-start.8
  23.9 1.3 %collective-permute-start.9 = (f32[5,8,4,128]{3,2,1,0:T(4,128)S(1)}, f32[5,8,4,128]{3,2,1,0:T(4,128)S(1)}, u32[]{:S(2)}, u32[]{:S(2)}) collective-permute-start(f32[5,8,4,128]{3,2,1,0:T(4,128)S(1)} %get-tuple-element.48), channel_id=1, source_target_pairs={{0,1},{4,8},{8,4},{12,13},{1,0},{5,9},{9,5},{13,12},{2,3},{6,10},{... | collective-permute-start | bytes 245768 | tf_op jit(solution)/shard_map/ppermute | solution.py:682
  25.2 2.4 %collective-permute-start.10 = (f32[5,8,4,128]{3,2,1,0:T(4,128)S(1)}, f32[5,8,4,128]{3,2,1,0:T(4,128)S(1)}, u32[]{:S(2)}, u32[]{:S(2)}) collective-permute-start(f32[5,8,4,128]{3,2,1,0:T(4,128)S(1)} %get-tuple-element.49), channel_id=1, source_target_pairs={{0,4},{4,0},{8,12},{12,8},{1,5},{5,1},{9,13},{13,9},{2,6},{6,2},{1... | collective-permute-start | bytes 245768 | tf_op jit(solution)/shard_map/ppermute | solution.py:671
  27.6 0.0 collective-permute-done.8.refs_0_
  27.7 1.5 %collective-permute-start.11 = (f32[25,4,128]{2,1,0:T(4,128)S(1)}, f32[25,4,128]{2,1,0:T(4,128)S(1)}, u32[]{:S(2)}, u32[]{:S(2)}) collective-permute-start(f32[25,4,128]{2,1,0:T(4,128)S(1)} %get-tuple-element.50), channel_id=1, source_target_pairs={{0,1},{4,8},{8,4},{12,13},{1,0},{5,9},{9,5},{13,12},{2,3},{6,10},{... | collective-permute-start | bytes 153608 | tf_op jit(solution)/shard_map/ppermute | solution.py:682
  29.2 2.4 %collective-permute-start.12 = (f32[25,4,128]{2,1,0:T(4,128)S(1)}, f32[25,4,128]{2,1,0:T(4,128)S(1)}, u32[]{:S(2)}, u32[]{:S(2)}) collective-permute-start(f32[25,4,128]{2,1,0:T(4,128)S(1)} %get-tuple-element.51), channel_id=1, source_target_pairs={{0,4},{4,0},{8,12},{12,8},{1,5},{5,1},{9,13},{13,9},{2,6},{6,2},{1... | collective-permute-start | bytes 153608 | tf_op jit(solution)/shard_map/ppermute | solution.py:671
  31.6 0.0 collective-permute-done.9.refs_1_
  31.6 0.0 collective-permute-done.10.refs_2_
  31.6 0.0 collective-permute-done.11.refs_3_
  31.6 0.9 %collective-permute-done.12.refs_4_ = f32[25,4,128]{2,1,0:T(4,128)S(1)} collective-permute-done((f32[25,4,128]{2,1,0:T(4,128)S(1)}, f32[25,4,128]{2,1,0:T(4,128)S(1)}, u32[]{:S(2)}, u32[]{:S(2)}) %collective-permute-start.12) | collective-permute-done | bytes 51232 | tf_op jit(solution)/shard_map/ppermute | solution.py:671
  32.5 0.4 shard_map.70
  32.9 16.7 %all_to_all.5.gathered = f32[32,5,4,128]{3,2,1,0:T(4,128)S(1)} all-to-all(f32[32,5,4,128]{3,2,1,0:T(4,128)S(1)} %get-tuple-element.53), channel_id=1, replica_groups=mesh['gx'=2,'gy'=4,'gz'=4] {'gx','gy','gz'}, dimensions={0} | all-to-all | bytes 655360 | tf_op jit(solution)/shard_map/all_to_all | solution.py:762
  49.7 5.1 %shard_map.71 = f32[16,16,128]{2,1,0:T(8,128)} custom-call(s32[1]{0:T(128)} %bitcast.where_ref, f32[32,5,4,128]{3,2,1,0:T(4,128)S(1)} %all_to_all.5.gathered, f32[6,16,16,128]{3,2,1,0:T(8,128)S(1)} %get-tuple-element.54.level1, f32[24,24,128]{2,1,0:T(8,128)S(1)} %get-tuple-element.55.refs_0_, f32[24,24,128]{2,1,0:T(8,128)S(1)} %get-tuple-element.56.refs_1_, ...), custom_call_target="tpu_custom_call" | custom-call | bytes 14400000 | tf_op jit(solution)/shard_map/pallas_call | solution.py:650
  (15 shorter events, 0.1 us)
Async XLA Ops:
  0.0 18.7 %copy-start.3 = (f32[16,16,128]{2,1,0:T(8,128)S(1)}, f32[16,16,128]{2,1,0:T(8,128)}, u32[]{:S(2)}) copy-start(f32[16,16,128]{2,1,0:T(8,128)} %refs_3_.5) | copy-start | bytes 393220
  0.0 18.7 %copy-start.4 = (f32[16,16,128]{2,1,0:T(8,128)S(1)}, f32[16,16,128]{2,1,0:T(8,128)}, u32[]{:S(2)}) copy-start(f32[16,16,128]{2,1,0:T(8,128)} %refs_4_.5) | copy-start | bytes 393220
  0.0 18.7 %copy-start.5 = (f32[16,16,128]{2,1,0:T(8,128)S(1)}, f32[16,16,128]{2,1,0:T(8,128)}, u32[]{:S(2)}) copy-start(f32[16,16,128]{2,1,0:T(8,128)} %refs_5_.5) | copy-start | bytes 393220
  2.6 11.9 %collective-permute-start.2 = (f32[6,4,16,128]{3,2,1,0:T(8,128)}, f32[6,4,16,128]{3,2,1,0:T(8,128)S(1)}, u32[]{:S(2)}, u32[]{:S(2)}) collective-permute-start(f32[6,4,16,128]{3,2,1,0:T(8,128)} %get-tuple-element.39), channel_id=1, source_target_pairs={{0,16},{16,0},{1,17},{17,1},{2,18},{18,2},{3,19},{19,3},{4,20},{20... | collective-permute-start | bytes 589832 | tf_op jit(solution)/shard_map/ppermute | solution.py:671
  4.6 14.9 %collective-permute-start.4 = (f32[6,16,4,128]{3,2,1,0:T(4,128)}, f32[6,16,4,128]{3,2,1,0:T(4,128)S(1)}, u32[]{:S(2)}, u32[]{:S(2)}) collective-permute-start(f32[6,16,4,128]{3,2,1,0:T(4,128)} %get-tuple-element.41), channel_id=1, source_target_pairs={{0,1},{4,8},{8,4},{12,13},{1,0},{5,9},{9,5},{13,12},{2,3},{6,10},{... | collective-permute-start | bytes 589832 | tf_op jit(solution)/shard_map/ppermute | solution.py:682
  6.7 12.8 %collective-permute-start.5 = (f32[6,16,4,128]{3,2,1,0:T(4,128)}, f32[6,16,4,128]{3,2,1,0:T(4,128)S(1)}, u32[]{:S(2)}, u32[]{:S(2)}) collective-permute-start(f32[6,16,4,128]{3,2,1,0:T(4,128)} %get-tuple-element.42), channel_id=1, source_target_pairs={{0,4},{4,0},{8,12},{12,8},{1,5},{5,1},{9,13},{13,9},{2,6},{6,2},{1... | collective-permute-start | bytes 589832 | tf_op jit(solution)/shard_map/ppermute | solution.py:671
  7.2 4.3 %collective-permute-start = (f32[8,16,128]{2,1,0:T(8,128)}, f32[8,16,128]{2,1,0:T(8,128)S(1)}, u32[]{:S(2)}, u32[]{:S(2)}) collective-permute-start(f32[8,16,128]{2,1,0:T(8,128)} %get-tuple-element.36), channel_id=1, source_target_pairs={{0,1},{1,0},{2,3},{3,2},{4,5},{5,4},{6,7},{7,6},{8,9},{9,8},{10,11... | collective-permute-start | bytes 196616 | tf_op jit(solution)/shard_map/ppermute | solution.py:671
  8.0 3.5 %collective-permute-start.1 = (f32[8,16,128]{2,1,0:T(8,128)}, f32[8,16,128]{2,1,0:T(8,128)S(1)}, u32[]{:S(2)}, u32[]{:S(2)}) collective-permute-start(f32[8,16,128]{2,1,0:T(8,128)} %get-tuple-element.37), channel_id=1, source_target_pairs={{0,4},{1,2},{2,1},{3,7},{4,0},{5,6},{6,5},{7,3},{8,12},{9,10},{10,... | collective-permute-start | bytes 196616 | tf_op jit(solution)/shard_map/ppermute | solution.py:682
  11.5 7.2 %copy-start.2 = (f32[16,16,128]{2,1,0:T(8,128)S(1)}, f32[16,16,128]{2,1,0:T(8,128)}, u32[]{:S(2)}) copy-start(f32[16,16,128]{2,1,0:T(8,128)} %refs_2_.5) | copy-start | bytes 393220
  11.6 2.8 %collective-permute-start.3 = (f32[4,16,128]{2,1,0:T(8,128)S(1)}, f32[4,16,128]{2,1,0:T(8,128)S(1)}, u32[]{:S(2)}, u32[]{:S(2)}) collective-permute-start(f32[4,16,128]{2,1,0:T(8,128)S(1)} %get-tuple-element.40), channel_id=1, source_target_pairs={{0,16},{16,0},{1,17},{17,1},{2,18},{18,2},{3,19},{19,3},{4,20},{20... | collective-permute-start | bytes 98312 | tf_op jit(solution)/shard_map/ppermute | solution.py:671
  14.5 4.2 %copy-start = (f32[16,16,128]{2,1,0:T(8,128)S(1)}, f32[16,16,128]{2,1,0:T(8,128)}, u32[]{:S(2)}) copy-start(f32[16,16,128]{2,1,0:T(8,128)} %refs_0_.5) | copy-start | bytes 393220
  14.5 4.3 %copy-start.1 = (f32[16,16,128]{2,1,0:T(8,128)S(1)}, f32[16,16,128]{2,1,0:T(8,128)}, u32[]{:S(2)}) copy-start(f32[16,16,128]{2,1,0:T(8,128)} %refs_1_.5) | copy-start | bytes 393220
  14.5 5.0 %collective-permute-start.6 = (f32[37,4,128]{2,1,0:T(4,128)S(1)}, f32[37,4,128]{2,1,0:T(4,128)S(1)}, u32[]{:S(2)}, u32[]{:S(2)}) collective-permute-start(f32[37,4,128]{2,1,0:T(4,128)S(1)} %get-tuple-element.43), channel_id=1, source_target_pairs={{0,1},{4,8},{8,4},{12,13},{1,0},{5,9},{9,5},{13,12},{2,3},{6,10},{... | collective-permute-start | bytes 227336 | tf_op jit(solution)/shard_map/ppermute | solution.py:682
  16.8 2.8 %collective-permute-start.7 = (f32[37,4,128]{2,1,0:T(4,128)S(1)}, f32[37,4,128]{2,1,0:T(4,128)S(1)}, u32[]{:S(2)}, u32[]{:S(2)}) collective-permute-start(f32[37,4,128]{2,1,0:T(4,128)S(1)} %get-tuple-element.44), channel_id=1, source_target_pairs={{0,4},{4,0},{8,12},{12,8},{1,5},{5,1},{9,13},{13,9},{2,6},{6,2},{1... | collective-permute-start | bytes 227336 | tf_op jit(solution)/shard_map/ppermute | solution.py:671
  23.5 4.1 %collective-permute-start.8 = (f32[5,4,8,128]{3,2,1,0:T(8,128)S(1)}, f32[5,4,8,128]{3,2,1,0:T(8,128)S(1)}, u32[]{:S(2)}, u32[]{:S(2)}) collective-permute-start(f32[5,4,8,128]{3,2,1,0:T(8,128)S(1)} %get-tuple-element.47), channel_id=1, source_target_pairs={{0,16},{16,0},{1,17},{17,1},{2,18},{18,2},{3,19},{19,3},{4,20},{20... | collective-permute-start | bytes 245768 | tf_op jit(solution)/shard_map/ppermute | solution.py:671
  23.9 7.8 %collective-permute-start.9 = (f32[5,8,4,128]{3,2,1,0:T(4,128)S(1)}, f32[5,8,4,128]{3,2,1,0:T(4,128)S(1)}, u32[]{:S(2)}, u32[]{:S(2)}) collective-permute-start(f32[5,8,4,128]{3,2,1,0:T(4,128)S(1)} %get-tuple-element.48), channel_id=1, source_target_pairs={{0,1},{4,8},{8,4},{12,13},{1,0},{5,9},{9,5},{13,12},{2,3},{6,10},{... | collective-permute-start | bytes 245768 | tf_op jit(solution)/shard_map/ppermute | solution.py:682
  25.2 6.5 %collective-permute-start.10 = (f32[5,8,4,128]{3,2,1,0:T(4,128)S(1)}, f32[5,8,4,128]{3,2,1,0:T(4,128)S(1)}, u32[]{:S(2)}, u32[]{:S(2)}) collective-permute-start(f32[5,8,4,128]{3,2,1,0:T(4,128)S(1)} %get-tuple-element.49), channel_id=1, source_target_pairs={{0,4},{4,0},{8,12},{12,8},{1,5},{5,1},{9,13},{13,9},{2,6},{6,2},{1... | collective-permute-start | bytes 245768 | tf_op jit(solution)/shard_map/ppermute | solution.py:671
  27.7 4.0 %collective-permute-start.11 = (f32[25,4,128]{2,1,0:T(4,128)S(1)}, f32[25,4,128]{2,1,0:T(4,128)S(1)}, u32[]{:S(2)}, u32[]{:S(2)}) collective-permute-start(f32[25,4,128]{2,1,0:T(4,128)S(1)} %get-tuple-element.50), channel_id=1, source_target_pairs={{0,1},{4,8},{8,4},{12,13},{1,0},{5,9},{9,5},{13,12},{2,3},{6,10},{... | collective-permute-start | bytes 153608 | tf_op jit(solution)/shard_map/ppermute | solution.py:682
  29.2 3.3 %collective-permute-start.12 = (f32[25,4,128]{2,1,0:T(4,128)S(1)}, f32[25,4,128]{2,1,0:T(4,128)S(1)}, u32[]{:S(2)}, u32[]{:S(2)}) collective-permute-start(f32[25,4,128]{2,1,0:T(4,128)S(1)} %get-tuple-element.51), channel_id=1, source_target_pairs={{0,4},{4,0},{8,12},{12,8},{1,5},{5,1},{9,13},{13,9},{2,6},{6,2},{1... | collective-permute-start | bytes 153608 | tf_op jit(solution)/shard_map/ppermute | solution.py:671

commit v11 on v10

--- a/solution.py
+++ b/solution.py
@@ -208,7 +208,7 @@
 
 def corners_kernel(counts, where_ref, zpack, *refs):
     n_x = 1 if counts[0] == 2 else 2
-    main_x, halos_x, (two_y, one_y) = refs[:n_x], refs[n_x:2 * n_x], refs[2 * n_x:]
+    main_x, halos_x, (two_y, one_y) = refs[:n_x], refs[n_x:2 * n_x], refs[2 * n_x + 1:]
     at_x, at_y, _ = position(where_ref)
     for a in range(7):
         if a < 6:
@@ -266,11 +266,11 @@
     return jnp.where(lane < depth, right, jnp.where(lane >= LANES - depth, left, 0.0))
 
 
-def rows_of(source, x, firsts, seconds):
+def rows_of(source, x, count, firsts, seconds):
     total = None
     for p in firsts:
         for q in seconds:
-            term = source[x + p, pl.ds(q, source.shape[1] // 2, stride=2), :]
+            term = source[x + p, pl.ds(q, count, stride=2), :]
             total = term if total is None else total + term
     return total
 
@@ -285,34 +285,34 @@
 
 
 def coefficient_kernel(counts, where_ref, *refs):
-    ins, refs = refs[2:7], refs[7:]
+    ins, refs = refs[:7], refs[7:]
     n_x = 1 if counts[0] == 2 else 2
-    main_x, halos_x = refs[:n_x], refs[n_x:2 * n_x]
-    coarse2, coeffs1, halo, sums, pairing = refs[2 * n_x:]
+    main_x, refs = refs[:n_x], refs[n_x:]
+    arrays, (coarse2, coeffs1, sums, pairing) = refs[:12], refs[12:]
     sx, sy, sz = ins[0].shape
     at_x = position(where_ref)[0]
     x1, y1 = sx // 2, sy // 2
     lane = lane_of((sx, sy, LANES))
     lanes = [slice(k * LANES, (k + 1) * LANES) for k in range(2)]
-    edge_lane = lane_of((1, sy, LANES))
-    last = slice(HALO - 1, HALO)
-    below, _ = neighbours(counts[0], at_x, main_x[0][3, last], main_x[-1][3, last])
-    packed, _ = neighbours(counts[0], at_x, halos_x[0][last], halos_x[-1][last])
-    for k, edge in enumerate((below, unpacked(packed, 3, edge_lane))):
-        halo[k, 0:1] = edge
-        sums[4, 0, :, lanes[k]] = rows_of(halo.at[k], 0, (0,), BOTH)
+    mine = slice(HALO, HALO + sx)
+    for a in range(6):
+        to = arrays[2 * a]
+        below, above = neighbours(counts[0], at_x, main_x[0][a], main_x[-1][a])
+        to[:HALO, :sy] = below
+        to[mine, :sy] = ins[a][...]
+        to[HALO + sx:, :sy] = above
+        arrays[2 * a + 1][mine, :sy] = unpacked(ins[6][...], a, lane)
     for n, (firsts, seconds) in enumerate(((BOTH, BOTH), (ODD, BOTH), (BOTH, ODD), (BOTH, BOTH))):
-        halo[0] = unpacked(ins[4][...], n + 2, lane)
-        for i in range(x1):
-            sums[n, i, :, lanes[0]] = rows_of(ins[n], 2 * i, firsts, seconds)
-            sums[n, i, :, lanes[1]] = rows_of(halo.at[0], 2 * i, firsts, seconds)
+        for k in range(2):
+            for i in range(x1):
+                source = arrays[2 * (n + 2) + k]
+                sums[n, i, :, lanes[k]] = rows_of(source, HALO + 2 * i, y1, firsts, seconds)
     pairs = pair_table(2 * LANES, LANES, False)
     odds = pair_table(2 * LANES, LANES, True)
     paired = to_level1(sums, 0, 3, pairs, 0.0625)
     mass1 = (2.0 * WEIGHT) * paired[0]
     faces1 = (paired[1], paired[2], to_level1(sums, 3, 1, odds, 0.0625)[0])
-    edge = 0.0625 * times_table(sums[4, 0], pairs)[None]
-    diag1 = mass1 + faces1[0] + jnp.concatenate([edge, faces1[0][:-1]], axis=0)
+    diag1 = mass1 + faces1[0] + below_x(faces1[0])
     diag1 = diag1 + faces1[1] + faces1[2] + turn(faces1[2], 1, 2)
     for n, values in enumerate((mass1, diag1) + faces1):
         coeffs1[n] = values
@@ -327,20 +327,19 @@
         coarse2[n] = level2_rows(pairing.at[n], odd_axes, factor, x1 // 2, y1 // 2, sz // 4)
 
 
-def down_kernel(counts, where_ref, *refs):
-    ins, refs = refs[:7], refs[7:]
+def down_kernel(counts, where_ref, zpack, *refs):
+    refs = refs[12:]
     n_x = 1 if counts[0] == 2 else 2
-    main_x, halos_x = refs[:n_x], refs[n_x:2 * n_x]
-    main_two, main_one, rest_two, rest_one, coeffs1, own1 = refs[2 * n_x:6 + 2 * n_x]
-    refs = refs[6 + 2 * n_x:]
+    halos_x = refs[:n_x]
+    main_two, main_one, rest_two, rest_one, coeffs1 = refs[n_x:5 + n_x]
+    flat, refs = refs[5 + n_x:17 + n_x], refs[17 + n_x:]
+    arrays = tuple(zip(flat[::2], flat[1::2]))
+    own1, refs = refs[0], refs[1:]
     sends, near_two, near_one, refs = refs[:n_x], refs[n_x], refs[n_x + 1], refs[n_x + 2:]
     kept_m, kept_h, weight_m, weight_h = refs[:4]
-    faces_out, scratch = refs[4:12], refs[12:]
-    rhs, bx, by, bz = zip(faces_out[::2], faces_out[1::2])
-    field, alpha = scratch[:2], scratch[2:4]
-    packs, half_m, half_h, diag_m, diag_h, sums, left = scratch[4:]
-    arrays = (field, rhs, alpha, bx, by, bz)
-    sx, sy, sz = ins[0].shape
+    packs, half_m, half_h, diag_m, diag_h, sums, left = refs[4:]
+    field, rhs, alpha, bx, by, bz = arrays
+    sx, sy, sz = zpack.shape
     ex, ey = sx + 2 * HALO, sy + 2 * HALO
     at_x, at_y, _ = position(where_ref)
 
@@ -349,29 +348,35 @@
     for a in range(7):
         if a < 6:
             to = arrays[a][0]
-            below, above = neighbours(counts[0], at_x, main_x[0][a], main_x[-1][a])
             rows = neighbours(counts[1], at_y, main_one[a], main_two[a])
             rows = jnp.concatenate(rows[::-1], axis=1)
         else:
             to = packs
+            rows = rest[21:]
             below, above = neighbours(counts[0], at_x, halos_x[0][...], halos_x[-1][...])
-            rows = rest[21:]
-        to[:HALO, :sy] = below
-        to[HALO:HALO + sx, :sy] = ins[a][...]
-        to[HALO + sx:, :sy] = above
+            to[:HALO, :sy] = below
+            to[HALO + sx:, :sy] = above
         to[HALO:HALO + sx, sy:] = rows
         low, high = corner_tiles([rest[3 * a + n] for n in range(3)])
         for n in range(HALO):
             to[n, sy:] = low[n]
             to[HALO + sx + n, sy:] = high[n]
     lane = lane_of((ey, LANES))
+    lane_low = lane_of((2 * HALO, LANES))
+
+    def unpack_rows(x):
+        packed = packs[x, sy:]
+        for a in range(6):
+            arrays[a][1][x, sy:] = unpacked(packed, a, lane_low)
 
     def unpack(x):
         packed = packs[x]
         for a in range(6):
             arrays[a][1][x] = unpacked(packed, a, lane)
 
-    each(0, ex, 4, unpack)
+    each(0, HALO, HALO, unpack)
+    each(HALO, HALO + sx, 8, unpack_rows)
+    each(HALO + sx, ex, HALO, unpack)
     halfway, weight, kept = (half_m, half_h), (weight_m, weight_h), (kept_m, kept_h)
     diag = (diag_m, diag_h)
 
@@ -409,16 +414,13 @@
         lanes = slice(k * LANES, (k + 1) * LANES)
         for i in range(x1):
             x = HALO + 2 * i
-            total = None
-            for p in BOTH:
-                for q in BOTH:
-                    term = halfway[k][x + p, pl.ds(q, y1, stride=2), :]
-                    total = term if total is None else total + term
-            sums[0, i, :, lanes] = total
+            sums[0, i, :, lanes] = rows_of(halfway[k], x, y1, BOTH, BOTH)
             left[...] = turn(by[k][x] + by[k][x + 1], 1, 0)
             sums[1, i, :, lanes] = left[pl.ds(0, y1, stride=2), :]
-    rhs1, low_y = to_level1(sums, 0, 2, pair_table(2 * LANES, LANES, False), 0.0625)
-    weight1 = relaxer(coeffs1[0], coeffs1[1] + low_y)
+        sums[2, 0, :, lanes] = rows_of(bx[k], HALO - 1, y1, (0,), BOTH)
+        sums[2, 1:, :, lanes] = jnp.zeros((x1 - 1, y1, LANES), F32)
+    rhs1, low_y, low_x = to_level1(sums, 0, 3, pair_table(2 * LANES, LANES, False), 0.0625)
+    weight1 = relaxer(coeffs1[0], coeffs1[1] + low_y + low_x)
     for n, values in enumerate((2.0 * rhs1, weight1, coeffs1[2], coeffs1[3], coeffs1[4])):
         own1[n] = values
         for send, face in zip(sends, faces_x(values[None], at_x % 2, n_x, NEAR)):
@@ -646,12 +648,13 @@
     each(HALO, ex - HALO, 4, sweep_own)
 
 
-def run(kernel, outs, where, arrays, scratch=(), grant=16, micros=1):
+def run(kernel, outs, where, arrays, scratch=(), grant=16, micros=1, aliases={}):
     return pl.pallas_call(
         kernel,
         out_shape=tuple(jax.ShapeDtypeStruct(shape, F32) for shape in outs),
         in_specs=[SM] * len(where) + [VM] * len(arrays),
         out_specs=tuple(VM for _ in outs),
+        input_output_aliases=aliases,
         scratch_shapes=[pltpu.VMEM(shape, F32) for shape in scratch],
         compiler_params=pltpu.CompilerParams(vmem_limit_bytes=grant * 1024 * 1024),
         cost_estimate=pl.CostEstimate(
@@ -714,36 +717,39 @@
         tuple(got),
     )
     halos_x = tuple(swaps("gx", sends, "gy"))
+    x1, y1 = sx // 2, sy // 2
+    *laid, coarse2, coeffs1 = run(
+        functools.partial(coefficient_kernel, counts),
+        [fine] * 12 + [(4, y1 // 2, LANES), (5, x1, y1, LANES)],
+        where,
+        ins + (zpack,) + main_x,
+        [(4, x1, y1, 2 * LANES), (4, x1, y1, LANES)],
+        micros=2,
+    )
     two_y, one_y = run(
         functools.partial(corners_kernel, counts),
         [(21 + sx, HALO, LANES)] * 2,
         where,
-        (zpack,) + main_x + halos_x,
+        (zpack,) + main_x + halos_x + (coarse2,),
     )
     rest_y = tuple(swaps("gy", (one_y, two_y), "gz")[::-1])
-    x1, y1 = sx // 2, sy // 2
-    ins = ins + (zpack,)
-    coarse2, coeffs1 = run(
-        functools.partial(coefficient_kernel, counts),
-        [(4, y1 // 2, LANES), (5, x1, y1, LANES)],
-        where,
-        ins + main_x + halos_x,
-        [(2, sx, sy, LANES), (5, x1, y1, 2 * LANES), (4, x1, y1, LANES)],
-        micros=2,
-    )
-    own1, *outs = run(
+    outs = run(
         functools.partial(down_kernel, counts),
-        [(5, x1, y1, LANES)]
+        [fine] * 12
+        + [(5, x1, y1, LANES)]
         + [(5, NEAR, y1, LANES)] * n_x
         + [(5, x1, NEAR, LANES)] * 2
-        + [fine] * 12,
+        + [fine] * 4,
         where,
-        ins + main_x + halos_x + main_y + rest_y + (coeffs1,),
-        [fine] * 9 + [(2, x1, y1, 2 * LANES), (ey, LANES)],
+        (zpack,) + tuple(laid) + halos_x + main_y + rest_y + (coeffs1,),
+        [fine] * 5 + [(3, x1, y1, 2 * LANES), (ey, LANES)],
         24,
         micros=4,
-    )
+        aliases={n + 2: n for n in range(12)},
+    )
+    laid, own1, outs = outs[:12], outs[12], outs[13:]
     sends_x, (two_y, one_y), fine_arrays = outs[:n_x], outs[n_x:n_x + 2], outs[n_x + 2:]
+    fine_arrays = tuple(fine_arrays) + tuple(laid[2:4]) + tuple(laid[6:])
 
     near_x = tuple(swaps("gx", sends_x, "gy"))
     near_y = tuple(swaps("gy", (one_y, two_y), "gz")[::-1])

time: 54.9 us -> 54.5 us (level)
  transfers between devices with their start and end apart: 13 -> 13, of which waited for: 4 -> 5; matrix products, arithmetic and copies ran while one was open for 0% -> 0% of each run, Pallas kernels for 2% -> 2%
where the time goes in v11:
time: 54.5 us; the launch traced here: 54.3 us
  starting transfers between devices  18.8 us (34%)
  blocking collectives  16.7 us (31%)
  Pallas kernels  12.5 us (23%)
  waiting for transfers between devices  6.14 us (11%)
    all_to_all x1, blocking collectives, local(): gathered = lax.all_to_all(copies, axes, 0, 0, tiled=True)  16.7 us
    pallas_call x8, Pallas kernels, run(): pl.pallas_call(kernel, out_shape=tuple((jax.ShapeDtypeStruct(shape, F32)...  12.5 us
    ppermute x8, starting transfers between devices, swaps(): got.append(lax.ppermute(block, axis, list(enumerate(partner))))  10.8 us
    ppermute x5, starting transfers between devices, swaps(): got.append(lax.ppermute(block, tuple(sorted((axis, other))), pairs))  7.99 us
    ppermute x8, waiting for transfers between devices, swaps(): got.append(lax.ppermute(block, axis, list(enumerate(partner))))  5.94 us
  transfers between devices with their start and end apart: 13, of which 5 were waited for; matrix products, arithmetic and copies ran while one was open for 0% of the time, Pallas kernels for 2%

profile of v11, /device:TPU:1, one launch (start us, length us, event | category | flops | bytes accessed | tf_op | source)
XLA Modules:
  0.0 54.3 jit_solution(8081666947767246789)
XLA Ops:
  0.0 2.6 %shard_map.64 = (f32[6,4,16,128]{3,2,1,0:T(8,128)}, f32[6,16,4,128]{3,2,1,0:T(4,128)}, f32[6,16,4,128]{3,2,1,0:T(4,128)}, f32[8,16,128]{2,1,0:T(8,128)}, f32[8,16,128]{2,1,0:T(8,128)}) custom-call(s32[1]{0:T(128)} %bitcast.where_ref, f32[16,16,128]{2,1,0:T(8,128)} %refs_0_.3, f32[16,16,128]{2,1,0:T(8,128)} %refs_1_.3, f32[16,16,128]{2,1,0:T(8,128)} %refs_2_.3, ...), custom_call_target="tpu_custom_call" | custom-call | bytes 3600000 | tf_op jit(solution)/shard_map/pallas_call | solution.py:652
  2.6 2.0 %collective-permute-start.2 = (f32[6,4,16,128]{3,2,1,0:T(8,128)}, f32[6,4,16,128]{3,2,1,0:T(8,128)S(1)}, u32[]{:S(2)}, u32[]{:S(2)}) collective-permute-start(f32[6,4,16,128]{3,2,1,0:T(8,128)} %get-tuple-element.51), channel_id=1, source_target_pairs={{0,16},{16,0},{1,17},{17,1},{2,18},{18,2},{3,19},{19,3},{4,20},{20... | collective-permute-start | bytes 589832 | tf_op jit(solution)/shard_map/ppermute | solution.py:674
  4.7 2.1 %collective-permute-start.4 = (f32[6,16,4,128]{3,2,1,0:T(4,128)}, f32[6,16,4,128]{3,2,1,0:T(4,128)S(1)}, u32[]{:S(2)}, u32[]{:S(2)}) collective-permute-start(f32[6,16,4,128]{3,2,1,0:T(4,128)} %get-tuple-element.65), channel_id=1, source_target_pairs={{0,1},{4,8},{8,4},{12,13},{1,0},{5,9},{9,5},{13,12},{2,3},{6,10},{... | collective-permute-start | bytes 589832 | tf_op jit(solution)/shard_map/ppermute | solution.py:685
  6.7 0.5 collective-permute-start.5
  7.2 0.8 %collective-permute-start = (f32[8,16,128]{2,1,0:T(8,128)}, f32[8,16,128]{2,1,0:T(8,128)S(1)}, u32[]{:S(2)}, u32[]{:S(2)}) collective-permute-start(f32[8,16,128]{2,1,0:T(8,128)} %get-tuple-element.48), channel_id=1, source_target_pairs={{0,1},{1,0},{2,3},{3,2},{4,5},{5,4},{6,7},{7,6},{8,9},{9,8},{10,11... | collective-permute-start | bytes 196616 | tf_op jit(solution)/shard_map/ppermute | solution.py:674
  8.0 0.8 %collective-permute-start.1 = (f32[8,16,128]{2,1,0:T(8,128)}, f32[8,16,128]{2,1,0:T(8,128)S(1)}, u32[]{:S(2)}, u32[]{:S(2)}) collective-permute-start(f32[8,16,128]{2,1,0:T(8,128)} %get-tuple-element.49), channel_id=1, source_target_pairs={{0,4},{1,2},{2,1},{3,7},{4,0},{5,6},{6,5},{7,3},{8,12},{9,10},{10,... | collective-permute-start | bytes 196616 | tf_op jit(solution)/shard_map/ppermute | solution.py:685
  8.8 2.7 %collective-permute-done.one_ref = f32[8,16,128]{2,1,0:T(8,128)S(1)} collective-permute-done((f32[8,16,128]{2,1,0:T(8,128)}, f32[8,16,128]{2,1,0:T(8,128)S(1)}, u32[]{:S(2)}, u32[]{:S(2)}) %collective-permute-start) | collective-permute-done | bytes 65568 | tf_op jit(solution)/shard_map/ppermute | solution.py:674
  11.5 0.0 collective-permute-done.1.two_ref
  11.5 0.1 shard_map.65
  11.7 0.4 collective-permute-start.3
  12.0 0.0 collective-permute-done.2.refs_7_.refs_0_
  12.1 0.8 %shard_map.66 = (f32[24,24,128]{2,1,0:T(8,128)S(1)}, f32[24,24,128]{2,1,0:T(8,128)S(1)}, f32[24,24,128]{2,1,0:T(8,128)S(1)}, f32[24,24,128]{2,1,0:T(8,128)S(1)},...) custom-call(s32[1]{0:T(128)} %bitcast.where_ref, ...), custom_call_target="tpu_custom_call" | custom-call | bytes 7200000 | tf_op jit(solution)/shard_map/pallas_call | solution.py:652
  12.8 1.6 %collective-permute-done.3.refs_1_.refs_12_ = f32[4,16,128]{2,1,0:T(8,128)S(1)} collective-permute-done((f32[4,16,128]{2,1,0:T(8,128)S(1)}, f32[4,16,128]{2,1,0:T(8,128)S(1)}, u32[]{:S(2)}, u32[]{:S(2)}) %collective-permute-start.3) | collective-permute-done | bytes 32800 | tf_op jit(solution)/shard_map/ppermute | solution.py:674
  14.5 0.1 shard_map.67
  14.5 2.3 %collective-permute-start.6 = (f32[37,4,128]{2,1,0:T(4,128)S(1)}, f32[37,4,128]{2,1,0:T(4,128)S(1)}, u32[]{:S(2)}, u32[]{:S(2)}) collective-permute-start(f32[37,4,128]{2,1,0:T(4,128)S(1)} %get-tuple-element.68), channel_id=1, source_target_pairs={{0,1},{4,8},{8,4},{12,13},{1,0},{5,9},{9,5},{13,12},{2,3},{6,10},{... | collective-permute-start | bytes 227336 | tf_op jit(solution)/shard_map/ppermute | solution.py:685
  16.8 1.9 %collective-permute-start.7 = (f32[37,4,128]{2,1,0:T(4,128)S(1)}, f32[37,4,128]{2,1,0:T(4,128)S(1)}, u32[]{:S(2)}, u32[]{:S(2)}) collective-permute-start(f32[37,4,128]{2,1,0:T(4,128)S(1)} %get-tuple-element.69), channel_id=1, source_target_pairs={{0,4},{4,0},{8,12},{12,8},{1,5},{5,1},{9,13},{13,9},{2,6},{6,2},{1... | collective-permute-start | bytes 227336 | tf_op jit(solution)/shard_map/ppermute | solution.py:674
  18.7 0.0 collective-permute-done.4.refs_13_
  18.7 0.0 collective-permute-done.5.refs_14_
  18.7 0.2 collective-permute-done.6.refs_15_
  18.9 0.7 %collective-permute-done.7.refs_16_ = f32[37,4,128]{2,1,0:T(4,128)S(1)} collective-permute-done((f32[37,4,128]{2,1,0:T(4,128)S(1)}, f32[37,4,128]{2,1,0:T(4,128)S(1)}, u32[]{:S(2)}, u32[]{:S(2)}) %collective-permute-start.7) | collective-permute-done | bytes 75808 | tf_op jit(solution)/shard_map/ppermute | solution.py:674
  19.6 3.4 %shard_map.68 = (f32[24,24,128]{2,1,0:T(8,128)S(1)}, f32[24,24,128]{2,1,0:T(8,128)S(1)}, f32[24,24,128]{2,1,0:T(8,128)S(1)}, f32[24,24,128]{2,1,0:T(8,128)S(1)},...) custom-call(s32[1]{0:T(128)} %bitcast.where_ref, ...), custom_call_target="tpu_custom_call", output_to_operand_aliasing={{0}: (2, {}), {1}: (3, {}), {2}: (4, {}), {3}: (5, {}), {4}... | custom-call | bytes 14400000 | tf_op jit(solution)/shard_map/pallas_call | solution.py:652
  23.1 0.3 collective-permute-start.8
  23.4 1.3 %collective-permute-start.9 = (f32[5,8,4,128]{3,2,1,0:T(4,128)S(1)}, f32[5,8,4,128]{3,2,1,0:T(4,128)S(1)}, u32[]{:S(2)}, u32[]{:S(2)}) collective-permute-start(f32[5,8,4,128]{3,2,1,0:T(4,128)S(1)} %get-tuple-element.73), channel_id=1, source_target_pairs={{0,1},{4,8},{8,4},{12,13},{1,0},{5,9},{9,5},{13,12},{2,3},{6,10},{... | collective-permute-start | bytes 245768 | tf_op jit(solution)/shard_map/ppermute | solution.py:685
  24.7 2.4 %collective-permute-start.10 = (f32[5,8,4,128]{3,2,1,0:T(4,128)S(1)}, f32[5,8,4,128]{3,2,1,0:T(4,128)S(1)}, u32[]{:S(2)}, u32[]{:S(2)}) collective-permute-start(f32[5,8,4,128]{3,2,1,0:T(4,128)S(1)} %get-tuple-element.74), channel_id=1, source_target_pairs={{0,4},{4,0},{8,12},{12,8},{1,5},{5,1},{9,13},{13,9},{2,6},{6,2},{1... | collective-permute-start | bytes 245768 | tf_op jit(solution)/shard_map/ppermute | solution.py:674
  27.2 1.5 %collective-permute-start.11 = (f32[25,4,128]{2,1,0:T(4,128)S(1)}, f32[25,4,128]{2,1,0:T(4,128)S(1)}, u32[]{:S(2)}, u32[]{:S(2)}) collective-permute-start(f32[25,4,128]{2,1,0:T(4,128)S(1)} %get-tuple-element.75), channel_id=1, source_target_pairs={{0,1},{4,8},{8,4},{12,13},{1,0},{5,9},{9,5},{13,12},{2,3},{6,10},{... | collective-permute-start | bytes 153608 | tf_op jit(solution)/shard_map/ppermute | solution.py:685
  28.7 2.4 %collective-permute-start.12 = (f32[25,4,128]{2,1,0:T(4,128)S(1)}, f32[25,4,128]{2,1,0:T(4,128)S(1)}, u32[]{:S(2)}, u32[]{:S(2)}) collective-permute-start(f32[25,4,128]{2,1,0:T(4,128)S(1)} %get-tuple-element.76), channel_id=1, source_target_pairs={{0,4},{4,0},{8,12},{12,8},{1,5},{5,1},{9,13},{13,9},{2,6},{6,2},{1... | collective-permute-start | bytes 153608 | tf_op jit(solution)/shard_map/ppermute | solution.py:674
  31.1 0.0 collective-permute-done.10.refs_2_
  31.1 0.0 collective-permute-done.11.refs_3_
  31.1 0.9 %collective-permute-done.12.refs_4_ = f32[25,4,128]{2,1,0:T(4,128)S(1)} collective-permute-done((f32[25,4,128]{2,1,0:T(4,128)S(1)}, f32[25,4,128]{2,1,0:T(4,128)S(1)}, u32[]{:S(2)}, u32[]{:S(2)}) %collective-permute-start.12) | collective-permute-done | bytes 51232 | tf_op jit(solution)/shard_map/ppermute | solution.py:674
  32.0 0.4 shard_map.70
  32.4 16.7 %all_to_all.5.gathered = f32[32,5,4,128]{3,2,1,0:T(4,128)S(1)} all-to-all(f32[32,5,4,128]{3,2,1,0:T(4,128)S(1)} %get-tuple-element.77), channel_id=1, replica_groups=mesh['gx'=2,'gy'=4,'gz'=4] {'gx','gy','gz'}, dimensions={0} | all-to-all | bytes 655360 | tf_op jit(solution)/shard_map/all_to_all | solution.py:768
  49.2 5.1 %shard_map.71 = f32[16,16,128]{2,1,0:T(8,128)} custom-call(s32[1]{0:T(128)} %bitcast.where_ref, f32[32,5,4,128]{3,2,1,0:T(4,128)S(1)} %all_to_all.5.gathered, f32[6,16,16,128]{3,2,1,0:T(8,128)S(1)} %get-tuple-element.78.level1, f32[24,24,128]{2,1,0:T(8,128)S(1)} %get-tuple-element.79.refs_0_, f32[24,24,128]{2,1,0:T(8,128)S(1)} %get-tuple-element.80.refs_1_, ...), custom_call_target="tpu_custom_call" | custom-call | bytes 14400000 | tf_op jit(solution)/shard_map/pallas_call | solution.py:652
  (15 shorter events, 0.1 us)
Async XLA Ops:
  0.0 12.0 %copy-start.1 = (f32[16,16,128]{2,1,0:T(8,128)S(1)}, f32[16,16,128]{2,1,0:T(8,128)}, u32[]{:S(2)}) copy-start(f32[16,16,128]{2,1,0:T(8,128)} %refs_1_.3) | copy-start | bytes 393220
  0.0 12.0 %copy-start.2 = (f32[16,16,128]{2,1,0:T(8,128)S(1)}, f32[16,16,128]{2,1,0:T(8,128)}, u32[]{:S(2)}) copy-start(f32[16,16,128]{2,1,0:T(8,128)} %refs_2_.3) | copy-start | bytes 393220
  0.0 12.0 %copy-start.3 = (f32[16,16,128]{2,1,0:T(8,128)S(1)}, f32[16,16,128]{2,1,0:T(8,128)}, u32[]{:S(2)}) copy-start(f32[16,16,128]{2,1,0:T(8,128)} %refs_3_.3) | copy-start | bytes 393220
  0.0 12.0 %copy-start.4 = (f32[16,16,128]{2,1,0:T(8,128)S(1)}, f32[16,16,128]{2,1,0:T(8,128)}, u32[]{:S(2)}) copy-start(f32[16,16,128]{2,1,0:T(8,128)} %refs_4_.3) | copy-start | bytes 393220
  0.0 12.0 %copy-start.5 = (f32[16,16,128]{2,1,0:T(8,128)S(1)}, f32[16,16,128]{2,1,0:T(8,128)}, u32[]{:S(2)}) copy-start(f32[16,16,128]{2,1,0:T(8,128)} %refs_5_.3) | copy-start | bytes 393220
  2.6 9.4 %copy-start = (f32[16,16,128]{2,1,0:T(8,128)S(1)}, f32[16,16,128]{2,1,0:T(8,128)}, u32[]{:S(2)}) copy-start(f32[16,16,128]{2,1,0:T(8,128)} %refs_0_.3) | copy-start | bytes 393220
  2.6 9.4 %collective-permute-start.2 = (f32[6,4,16,128]{3,2,1,0:T(8,128)}, f32[6,4,16,128]{3,2,1,0:T(8,128)S(1)}, u32[]{:S(2)}, u32[]{:S(2)}) collective-permute-start(f32[6,4,16,128]{3,2,1,0:T(8,128)} %get-tuple-element.51), channel_id=1, source_target_pairs={{0,16},{16,0},{1,17},{17,1},{2,18},{18,2},{3,19},{19,3},{4,20},{20... | collective-permute-start | bytes 589832 | tf_op jit(solution)/shard_map/ppermute | solution.py:674
  4.7 14.0 %collective-permute-start.4 = (f32[6,16,4,128]{3,2,1,0:T(4,128)}, f32[6,16,4,128]{3,2,1,0:T(4,128)S(1)}, u32[]{:S(2)}, u32[]{:S(2)}) collective-permute-start(f32[6,16,4,128]{3,2,1,0:T(4,128)} %get-tuple-element.65), channel_id=1, source_target_pairs={{0,1},{4,8},{8,4},{12,13},{1,0},{5,9},{9,5},{13,12},{2,3},{6,10},{... | collective-permute-start | bytes 589832 | tf_op jit(solution)/shard_map/ppermute | solution.py:685
  6.7 12.0 %collective-permute-start.5 = (f32[6,16,4,128]{3,2,1,0:T(4,128)}, f32[6,16,4,128]{3,2,1,0:T(4,128)S(1)}, u32[]{:S(2)}, u32[]{:S(2)}) collective-permute-start(f32[6,16,4,128]{3,2,1,0:T(4,128)} %get-tuple-element.66), channel_id=1, source_target_pairs={{0,4},{4,0},{8,12},{12,8},{1,5},{5,1},{9,13},{13,9},{2,6},{6,2},{1... | collective-permute-start | bytes 589832 | tf_op jit(solution)/shard_map/ppermute | solution.py:674
  7.2 4.3 %collective-permute-start = (f32[8,16,128]{2,1,0:T(8,128)}, f32[8,16,128]{2,1,0:T(8,128)S(1)}, u32[]{:S(2)}, u32[]{:S(2)}) collective-permute-start(f32[8,16,128]{2,1,0:T(8,128)} %get-tuple-element.48), channel_id=1, source_target_pairs={{0,1},{1,0},{2,3},{3,2},{4,5},{5,4},{6,7},{7,6},{8,9},{9,8},{10,11... | collective-permute-start | bytes 196616 | tf_op jit(solution)/shard_map/ppermute | solution.py:674
  8.0 3.5 %collective-permute-start.1 = (f32[8,16,128]{2,1,0:T(8,128)}, f32[8,16,128]{2,1,0:T(8,128)S(1)}, u32[]{:S(2)}, u32[]{:S(2)}) collective-permute-start(f32[8,16,128]{2,1,0:T(8,128)} %get-tuple-element.49), channel_id=1, source_target_pairs={{0,4},{1,2},{2,1},{3,7},{4,0},{5,6},{6,5},{7,3},{8,12},{9,10},{10,... | collective-permute-start | bytes 196616 | tf_op jit(solution)/shard_map/ppermute | solution.py:685
  11.7 2.8 %collective-permute-start.3 = (f32[4,16,128]{2,1,0:T(8,128)S(1)}, f32[4,16,128]{2,1,0:T(8,128)S(1)}, u32[]{:S(2)}, u32[]{:S(2)}) collective-permute-start(f32[4,16,128]{2,1,0:T(8,128)S(1)} %get-tuple-element.64), channel_id=1, source_target_pairs={{0,16},{16,0},{1,17},{17,1},{2,18},{18,2},{3,19},{19,3},{4,20},{20... | collective-permute-start | bytes 98312 | tf_op jit(solution)/shard_map/ppermute | solution.py:674
  14.5 4.4 %collective-permute-start.6 = (f32[37,4,128]{2,1,0:T(4,128)S(1)}, f32[37,4,128]{2,1,0:T(4,128)S(1)}, u32[]{:S(2)}, u32[]{:S(2)}) collective-permute-start(f32[37,4,128]{2,1,0:T(4,128)S(1)} %get-tuple-element.68), channel_id=1, source_target_pairs={{0,1},{4,8},{8,4},{12,13},{1,0},{5,9},{9,5},{13,12},{2,3},{6,10},{... | collective-permute-start | bytes 227336 | tf_op jit(solution)/shard_map/ppermute | solution.py:685
  16.8 2.8 %collective-permute-start.7 = (f32[37,4,128]{2,1,0:T(4,128)S(1)}, f32[37,4,128]{2,1,0:T(4,128)S(1)}, u32[]{:S(2)}, u32[]{:S(2)}) collective-permute-start(f32[37,4,128]{2,1,0:T(4,128)S(1)} %get-tuple-element.69), channel_id=1, source_target_pairs={{0,4},{4,0},{8,12},{12,8},{1,5},{5,1},{9,13},{13,9},{2,6},{6,2},{1... | collective-permute-start | bytes 227336 | tf_op jit(solution)/shard_map/ppermute | solution.py:674
  23.1 4.1 %collective-permute-start.8 = (f32[5,4,8,128]{3,2,1,0:T(8,128)S(1)}, f32[5,4,8,128]{3,2,1,0:T(8,128)S(1)}, u32[]{:S(2)}, u32[]{:S(2)}) collective-permute-start(f32[5,4,8,128]{3,2,1,0:T(8,128)S(1)} %get-tuple-element.72), channel_id=1, source_target_pairs={{0,16},{16,0},{1,17},{17,1},{2,18},{18,2},{3,19},{19,3},{4,20},{20... | collective-permute-start | bytes 245768 | tf_op jit(solution)/shard_map/ppermute | solution.py:674
  23.4 7.8 %collective-permute-start.9 = (f32[5,8,4,128]{3,2,1,0:T(4,128)S(1)}, f32[5,8,4,128]{3,2,1,0:T(4,128)S(1)}, u32[]{:S(2)}, u32[]{:S(2)}) collective-permute-start(f32[5,8,4,128]{3,2,1,0:T(4,128)S(1)} %get-tuple-element.73), channel_id=1, source_target_pairs={{0,1},{4,8},{8,4},{12,13},{1,0},{5,9},{9,5},{13,12},{2,3},{6,10},{... | collective-permute-start | bytes 245768 | tf_op jit(solution)/shard_map/ppermute | solution.py:685
  24.7 6.5 %collective-permute-start.10 = (f32[5,8,4,128]{3,2,1,0:T(4,128)S(1)}, f32[5,8,4,128]{3,2,1,0:T(4,128)S(1)}, u32[]{:S(2)}, u32[]{:S(2)}) collective-permute-start(f32[5,8,4,128]{3,2,1,0:T(4,128)S(1)} %get-tuple-element.74), channel_id=1, source_target_pairs={{0,4},{4,0},{8,12},{12,8},{1,5},{5,1},{9,13},{13,9},{2,6},{6,2},{1... | collective-permute-start | bytes 245768 | tf_op jit(solution)/shard_map/ppermute | solution.py:674
  27.2 4.0 %collective-permute-start.11 = (f32[25,4,128]{2,1,0:T(4,128)S(1)}, f32[25,4,128]{2,1,0:T(4,128)S(1)}, u32[]{:S(2)}, u32[]{:S(2)}) collective-permute-start(f32[25,4,128]{2,1,0:T(4,128)S(1)} %get-tuple-element.75), channel_id=1, source_target_pairs={{0,1},{4,8},{8,4},{12,13},{1,0},{5,9},{9,5},{13,12},{2,3},{6,10},{... | collective-permute-start | bytes 153608 | tf_op jit(solution)/shard_map/ppermute | solution.py:685
  28.7 3.3 %collective-permute-start.12 = (f32[25,4,128]{2,1,0:T(4,128)S(1)}, f32[25,4,128]{2,1,0:T(4,128)S(1)}, u32[]{:S(2)}, u32[]{:S(2)}) collective-permute-start(f32[25,4,128]{2,1,0:T(4,128)S(1)} %get-tuple-element.76), channel_id=1, source_target_pairs={{0,4},{4,0},{8,12},{12,8},{1,5},{5,1},{9,13},{13,9},{2,6},{6,2},{1... | collective-permute-start | bytes 153608 | tf_op jit(solution)/shard_map/ppermute | solution.py:674

commit v12 on v11

--- a/solution.py
+++ b/solution.py
@@ -134,41 +134,57 @@
     return pick(odd, head, tail), pick(odd, tail, head)
 
 
-def corner_sends(below, above, odd, corners):
+def corner_sends(below, above, odd):
     packs = []
     for rows, sign in ((slice(0, 8), 1), (slice(below.shape[1] - 8, below.shape[1]), -1)):
-        low = [below[3 - i, rows] for i in range(4)]
-        high = [above[i, rows] for i in range(4)]
-        pack = []
-        if corners:
-            pack = [low[0], high[0]]
-            low, high = low[1:], high[1:]
+        low = [below[3 - i, rows] for i in range(3)]
+        high = [above[i, rows] for i in range(3)]
         row = iota2(low[0].shape, 0)
         row = row if sign == 1 else 7 - row
-        pack += [
+        pack = (
             jnp.where(row < 3, low[0], turn(low[2], 3 * sign, 0)),
             jnp.where(row < 2, low[1], turn(high[1], 2 * sign, 0)),
             jnp.where(row < 3, high[0], turn(high[2], 3 * sign, 0)),
-        ]
+        )
         packs.append([p[:4] if sign == 1 else p[4:] for p in pack])
     return [(pick(odd, h, t), pick(odd, t, h)) for h, t in zip(*packs)]
 
 
-def corner_tiles(tiles):
-    first, second, third = tiles[-3:]
-    upper = iota2(first.shape, 0) < 4
-
-    def inner(tile, by):
-        return jnp.where(upper, turn(tile, -by, 0), turn(tile, by, 0))
-
-    low = [first, second, inner(first, 3)]
-    high = [third, inner(second, 2), inner(third, 3)]
-    if len(tiles) == 5:
-        low, high = tiles[:1] + low, tiles[1:2] + high
-    else:
-        zero = jnp.zeros_like(first)
-        low, high = low + [zero], high + [zero]
-    return low[::-1], high
+def inner_rows(tile, by):
+    upper = iota2(tile.shape, 0) < 4
+    return jnp.where(upper, turn(tile, -by, 0), turn(tile, by, 0))
+
+
+def corner_tiles(first, second, third):
+    zero = jnp.zeros_like(first)
+    low = (zero, inner_rows(first, 3), second, first)
+    return low, (third, inner_rows(second, 2), inner_rows(third, 3), zero)
+
+
+def diagonal_sends(values, n_x, odd_x, odd_y):
+    corners = []
+    for slabs in ([values[i] for i in range(4)], [values[values.shape[0] - 1 - i] for i in range(4)]):
+        for sign in (1, -1):
+            row = iota2(slabs[0].shape, 0)
+            row = row if sign == 1 else 7 - row
+            tiles = (slabs[0], jnp.where(row < 3, slabs[1], turn(slabs[3], 3 * sign, 0)), slabs[2])
+            corners.append([t[:4] if sign == 1 else t[4:] for t in tiles])
+    sends = []
+    for k_x in range(n_x):
+        for k_y in range(2):
+            head_x = odd_x if k_x == 0 else 1 - odd_x
+            head_y = odd_y if k_y == 0 else 1 - odd_y
+            sends.append(
+                [
+                    pick(head_x, pick(head_y, hh, ht), pick(head_y, th, tt))
+                    for hh, ht, th, tt in zip(*corners)
+                ]
+            )
+    return sends
+
+
+def diagonal_tiles(first, second, third):
+    return [first, second, third, inner_rows(second, 3)]
 
 
 def faces_kernel(counts, where_ref, *refs):
@@ -215,7 +231,7 @@
             below, above = neighbours(counts[0], at_x, main_x[0][a], main_x[-1][a])
         else:
             below, above = neighbours(counts[0], at_x, halos_x[0][...], halos_x[-1][...])
-        for n, pair in enumerate(corner_sends(below, above, at_y % 2, False)):
+        for n, pair in enumerate(corner_sends(below, above, at_y % 2)):
             one_y[3 * a + n], two_y[3 * a + n] = pair
     one_y[21:], two_y[21:] = faces_y(zpack[...], at_y % 2, HALO)
 
@@ -336,6 +352,7 @@
     arrays = tuple(zip(flat[::2], flat[1::2]))
     own1, refs = refs[0], refs[1:]
     sends, near_two, near_one, refs = refs[:n_x], refs[n_x], refs[n_x + 1], refs[n_x + 2:]
+    sends_xy, refs = refs[:2 * n_x], refs[2 * n_x:]
     kept_m, kept_h, weight_m, weight_h = refs[:4]
     packs, half_m, half_h, diag_m, diag_h, sums, left = refs[4:]
     field, rhs, alpha, bx, by, bz = arrays
@@ -357,7 +374,7 @@
             to[:HALO, :sy] = below
             to[HALO + sx:, :sy] = above
         to[HALO:HALO + sx, sy:] = rows
-        low, high = corner_tiles([rest[3 * a + n] for n in range(3)])
+        low, high = corner_tiles(*(rest[3 * a + n] for n in range(3)))
         for n in range(HALO):
             to[n, sy:] = low[n]
             to[HALO + sx + n, sy:] = high[n]
@@ -426,6 +443,9 @@
         for send, face in zip(sends, faces_x(values[None], at_x % 2, n_x, NEAR)):
             send[n] = face[0]
         near_one[n], near_two[n] = faces_y(values, at_y % 2, NEAR)
+        for send, tiles in zip(sends_xy, diagonal_sends(values, n_x, at_x % 2, at_y % 2)):
+            for t in range(3):
+                send[3 * n + t] = tiles[t]
 
 
 def level2_rows(source, odd_axes, factor, x2, y2, z2):
@@ -447,29 +467,27 @@
     return packed
 
 
-def near_corners_kernel(counts, where_ref, *refs):
-    halos_x, (two_y, one_y) = refs[:-2], refs[-2:]
-    at_x, at_y, _ = position(where_ref)
-    for a in range(halos_x[0].shape[0]):
-        below, above = neighbours(counts[0], at_x, halos_x[0][a], halos_x[-1][a])
-        for n, pair in enumerate(corner_sends(below, above, at_y % 2, True)):
-            one_y[5 * a + n], two_y[5 * a + n] = pair
-
-
 def near_kernel(counts, devices, where_ref, ring, *refs):
     n_x = 1 if counts[0] == 2 else 2
     halos_x = refs[:n_x]
-    main_two, main_one, rest_two, rest_one, coarse2, copies, level1, left = refs[n_x:]
+    main_two, main_one = refs[n_x:n_x + 2]
+    diagonals, (coarse2, copies, level1, left) = refs[n_x + 2:3 * n_x + 2], refs[3 * n_x + 2:]
     n, bx1, by1, _ = ring.shape
     at_x, at_y, _ = position(where_ref)
-    rest = neighbours(counts[1], at_y, rest_one[...], rest_two[...])
-    rest = jnp.concatenate(rest[::-1], axis=1)
+    sides = [
+        neighbours(counts[0], at_x, diagonals[k][...], diagonals[k - 2][...]) for k in range(2)
+    ]
+    rest = []
+    for one, two in zip(*sides):
+        rows = neighbours(counts[1], at_y, one, two)
+        rest.append(jnp.concatenate(rows[::-1], axis=1))
     whole = []
     for a in range(n):
         below, above = neighbours(counts[0], at_x, halos_x[0][a], halos_x[-1][a])
         rows = neighbours(counts[1], at_y, main_one[a], main_two[a])
         rows = jnp.concatenate(rows[::-1], axis=1)
-        low, high = corner_tiles([rest[5 * a + k] for k in range(5)])
+        low, high = (diagonal_tiles(*(side[3 * a + k] for k in range(3))) for side in rest)
+        low = low[::-1]
         rows = jnp.concatenate(
             [tile[None] for tile in low] + [rows] + [tile[None] for tile in high], axis=0
         )
@@ -663,14 +681,21 @@
     )(*where, *arrays)
 
 
+def partners(count, k):
+    partner = list(range(count))
+    for low in range(k, count - 1, 2):
+        partner[low], partner[low + 1] = low + 1, low
+    return partner
+
+
 def swaps(axis, sends, other=None):
     count = lax.axis_size(axis)
     got = []
     for k, block in enumerate(sends):
-        partner = list(range(count))
-        for low in range(k, count - 1, 2):
-            partner[low], partner[low + 1] = low + 1, low
-        if k == 0:
+        partner = partners(count, k)
+        if k == 1 and other is None:
+            partner[0], partner[-1] = count - 1, 0
+        if k == 0 or other is None:
             got.append(lax.ppermute(block, axis, list(enumerate(partner))))
             continue
         rows = lax.axis_size(other)
@@ -686,6 +711,20 @@
     return got
 
 
+def diagonal_swaps(sends):
+    count_x, count_y = lax.axis_size("gx"), lax.axis_size("gy")
+    got = []
+    for n, block in enumerate(sends):
+        xs, ys = partners(count_x, n // 2), partners(count_y, n % 2)
+        pairs = [
+            (x * count_y + y, xs[x] * count_y + ys[y])
+            for x in range(count_x)
+            for y in range(count_y)
+        ]
+        got.append(lax.ppermute(block, ("gx", "gy"), pairs))
+    return got
+
+
 def local(initial, right_side, alpha, beta_x, beta_y, beta_z):
     axes = ("gx", "gy", "gz")
     counts = tuple(lax.axis_size(axis) for axis in axes)
@@ -708,7 +747,7 @@
         grant=60,
     )
     main_x = tuple(swaps("gx", sends_x, "gy"))
-    main_y = tuple(swaps("gy", (one_y, two_y), "gz")[::-1])
+    main_y = tuple(swaps("gy", (one_y, two_y))[::-1])
     got = swaps("gz", (first, second), "gy")
     zpack, *sends = run(
         functools.partial(halo_z_kernel, counts),
@@ -739,6 +778,7 @@
         + [(5, x1, y1, LANES)]
         + [(5, NEAR, y1, LANES)] * n_x
         + [(5, x1, NEAR, LANES)] * 2
+        + [(15, NEAR, LANES)] * (2 * n_x)
         + [fine] * 4,
         where,
         (zpack,) + tuple(laid) + halos_x + main_y + rest_y + (coeffs1,),
@@ -748,20 +788,18 @@
         aliases={n + 2: n for n in range(12)},
     )
     laid, own1, outs = outs[:12], outs[12], outs[13:]
-    sends_x, (two_y, one_y), fine_arrays = outs[:n_x], outs[n_x:n_x + 2], outs[n_x + 2:]
+    sends_x, (two_y, one_y), outs = outs[:n_x], outs[n_x:n_x + 2], outs[n_x + 2:]
+    sends_xy, fine_arrays = outs[:2 * n_x], outs[2 * n_x:]
     fine_arrays = tuple(fine_arrays) + tuple(laid[2:4]) + tuple(laid[6:])
 
     near_x = tuple(swaps("gx", sends_x, "gy"))
     near_y = tuple(swaps("gy", (one_y, two_y), "gz")[::-1])
-    two_y, one_y = run(
-        functools.partial(near_corners_kernel, counts), [(25, NEAR, LANES)] * 2, where, near_x
-    )
-    rest_y = tuple(swaps("gy", (one_y, two_y), "gz")[::-1])
+    near_xy = tuple(diagonal_swaps(sends_xy))
     copies, level1 = run(
         functools.partial(near_kernel, counts, devices),
         [(devices, 5, y1 // 2, LANES), (6, x1 + 2 * NEAR, y1 + 2 * NEAR, LANES)],
         where,
-        (own1,) + near_x + near_y + rest_y + (coarse2,),
+        (own1,) + near_x + near_y + near_xy + (coarse2,),
         [(x1, y1 + 2 * NEAR, LANES)],
     )
 

time: 54.5 us -> 52.7 us (0.967)
  waiting for transfers between devices: 6.14 us -> 8.37 us
  blocking collectives: 16.7 us -> 14.6 us
  starting transfers between devices: 18.8 us -> 17 us
    ppermute x5 -> x3, starting transfers between devices: 7.99 us -> 3.68 us  [swaps(): got.append(lax.ppermute(block, tuple(sorted((axis, other))), pairs))]
    ppermute x0 -> x2, waiting for transfers between devices: none -> 4.21 us  [diagonal_swaps(): got.append(lax.ppermute(block, ('gx', 'gy'), pairs))]
    all_to_all x1, blocking collectives: 16.7 us -> 14.6 us  [local(): gathered = lax.all_to_all(copies, axes, 0, 0, tiled=True)]
    ppermute x8, waiting for transfers between devices: 5.94 us -> 4.15 us  [swaps(): got.append(lax.ppermute(block, axis, list(enumerate(partner))))]
    ppermute x8, starting transfers between devices: 10.8 us -> 12.2 us  [swaps(): got.append(lax.ppermute(block, axis, list(enumerate(partner))))]
    ppermute x0 -> x2, starting transfers between devices: none -> 1.1 us  [diagonal_swaps(): got.append(lax.ppermute(block, ('gx', 'gy'), pairs))]
    pallas_call x8 -> x7, Pallas kernels: 12.5 us -> 12.5 us  [run(): pl.pallas_call(kernel, out_shape=tuple((jax.ShapeDtypeStruct(shape, F32)...]
where the time goes in v12:
time: 52.7 us; the launch traced here: 52.6 us
  starting transfers between devices  17 us (32%)
  blocking collectives  14.6 us (28%)
  Pallas kernels  12.5 us (24%)
  waiting for transfers between devices  8.37 us (16%)
    all_to_all x1, blocking collectives, local(): gathered = lax.all_to_all(copies, axes, 0, 0, tiled=True)  14.6 us
    pallas_call x7, Pallas kernels, run(): pl.pallas_call(kernel, out_shape=tuple((jax.ShapeDtypeStruct(shape, F32)...  12.5 us
    ppermute x8, starting transfers between devices, swaps(): got.append(lax.ppermute(block, axis, list(enumerate(partner))))  12.2 us
    ppermute x2, waiting for transfers between devices, diagonal_swaps(): got.append(lax.ppermute(block, ('gx', 'gy'), pairs))  4.21 us
    ppermute x8, waiting for transfers between devices, swaps(): got.append(lax.ppermute(block, axis, list(enumerate(partner))))  4.15 us
    ppermute x3, starting transfers between devices, swaps(): got.append(lax.ppermute(block, tuple(sorted((axis, other))), pairs))  3.68 us
    ppermute x2, starting transfers between devices, diagonal_swaps(): got.append(lax.ppermute(block, ('gx', 'gy'), pairs))  1.1 us
  transfers between devices with their start and end apart: 13, of which 5 were waited for; matrix products, arithmetic and copies ran while one was open for 0% of the time, Pallas kernels for 2%

profile of v12, /device:TPU:1, one launch (start us, length us, event | category | flops | bytes accessed | tf_op | source)
XLA Modules:
  0.0 52.6 jit_solution(16393850170866839249)
XLA Ops:
  0.0 2.6 %shard_map.64 = (f32[6,4,16,128]{3,2,1,0:T(8,128)}, f32[6,16,4,128]{3,2,1,0:T(4,128)}, f32[6,16,4,128]{3,2,1,0:T(4,128)}, f32[8,16,128]{2,1,0:T(8,128)}, f32[8,16,128]{2,1,0:T(8,128)}) custom-call(s32[1]{0:T(128)} %bitcast.where_ref, f32[16,16,128]{2,1,0:T(8,128)} %refs_0_.3, f32[16,16,128]{2,1,0:T(8,128)} %refs_1_.3, f32[16,16,128]{2,1,0:T(8,128)} %refs_2_.3, ...), custom_call_target="tpu_custom_call" | custom-call | bytes 3600000 | tf_op jit(solution)/shard_map/pallas_call | solution.py:670
  2.6 2.0 %collective-permute-start.2 = (f32[6,4,16,128]{3,2,1,0:T(8,128)}, f32[6,4,16,128]{3,2,1,0:T(8,128)S(1)}, u32[]{:S(2)}, u32[]{:S(2)}) collective-permute-start(f32[6,4,16,128]{3,2,1,0:T(8,128)} %get-tuple-element.51), channel_id=1, source_target_pairs={{0,16},{16,0},{1,17},{17,1},{2,18},{18,2},{3,19},{19,3},{4,20},{20... | collective-permute-start | bytes 589832 | tf_op jit(solution)/shard_map/ppermute | solution.py:699
  4.7 2.1 %collective-permute-start.4 = (f32[6,16,4,128]{3,2,1,0:T(4,128)}, f32[6,16,4,128]{3,2,1,0:T(4,128)S(1)}, u32[]{:S(2)}, u32[]{:S(2)}) collective-permute-start(f32[6,16,4,128]{3,2,1,0:T(4,128)} %get-tuple-element.65), channel_id=1, source_target_pairs={{0,12},{4,8},{8,4},{12,0},{1,13},{5,9},{9,5},{13,1},{2,14},{6,10},... | collective-permute-start | bytes 589832 | tf_op jit(solution)/shard_map/ppermute | solution.py:699
  6.8 0.0 collective-permute-start.5
  6.8 1.3 %collective-permute-start = (f32[8,16,128]{2,1,0:T(8,128)}, f32[8,16,128]{2,1,0:T(8,128)S(1)}, u32[]{:S(2)}, u32[]{:S(2)}) collective-permute-start(f32[8,16,128]{2,1,0:T(8,128)} %get-tuple-element.48), channel_id=1, source_target_pairs={{0,1},{1,0},{2,3},{3,2},{4,5},{5,4},{6,7},{7,6},{8,9},{9,8},{10,11... | collective-permute-start | bytes 196616 | tf_op jit(solution)/shard_map/ppermute | solution.py:699
  8.1 0.8 %collective-permute-start.1 = (f32[8,16,128]{2,1,0:T(8,128)}, f32[8,16,128]{2,1,0:T(8,128)S(1)}, u32[]{:S(2)}, u32[]{:S(2)}) collective-permute-start(f32[8,16,128]{2,1,0:T(8,128)} %get-tuple-element.49), channel_id=1, source_target_pairs={{0,4},{1,2},{2,1},{3,7},{4,0},{5,6},{6,5},{7,3},{8,12},{9,10},{10,... | collective-permute-start | bytes 196616 | tf_op jit(solution)/shard_map/ppermute | solution.py:710
  8.8 1.5 %collective-permute-done.one_ref = f32[8,16,128]{2,1,0:T(8,128)S(1)} collective-permute-done((f32[8,16,128]{2,1,0:T(8,128)}, f32[8,16,128]{2,1,0:T(8,128)S(1)}, u32[]{:S(2)}, u32[]{:S(2)}) %collective-permute-start) | collective-permute-done | bytes 65568 | tf_op jit(solution)/shard_map/ppermute | solution.py:699
  10.4 0.0 collective-permute-done.1.two_ref
  10.4 0.1 shard_map.65
  10.5 0.3 collective-permute-start.3
  10.8 0.0 collective-permute-done.2.refs_7_.refs_0_
  10.9 0.8 %shard_map.66 = (f32[24,24,128]{2,1,0:T(8,128)S(1)}, f32[24,24,128]{2,1,0:T(8,128)S(1)}, f32[24,24,128]{2,1,0:T(8,128)S(1)}, f32[24,24,128]{2,1,0:T(8,128)S(1)},...) custom-call(s32[1]{0:T(128)} %bitcast.where_ref, ...), custom_call_target="tpu_custom_call" | custom-call | bytes 7200000 | tf_op jit(solution)/shard_map/pallas_call | solution.py:670
  11.6 1.7 %collective-permute-done.3.refs_1_.refs_12_ = f32[4,16,128]{2,1,0:T(8,128)S(1)} collective-permute-done((f32[4,16,128]{2,1,0:T(8,128)S(1)}, f32[4,16,128]{2,1,0:T(8,128)S(1)}, u32[]{:S(2)}, u32[]{:S(2)}) %collective-permute-start.3) | collective-permute-done | bytes 32800 | tf_op jit(solution)/shard_map/ppermute | solution.py:699
  13.3 0.1 shard_map.67
  13.4 2.7 %collective-permute-start.6 = (f32[37,4,128]{2,1,0:T(4,128)S(1)}, f32[37,4,128]{2,1,0:T(4,128)S(1)}, u32[]{:S(2)}, u32[]{:S(2)}) collective-permute-start(f32[37,4,128]{2,1,0:T(4,128)S(1)} %get-tuple-element.68), channel_id=1, source_target_pairs={{0,1},{4,8},{8,4},{12,13},{1,0},{5,9},{9,5},{13,12},{2,3},{6,10},{... | collective-permute-start | bytes 227336 | tf_op jit(solution)/shard_map/ppermute | solution.py:710
  16.1 2.6 %collective-permute-start.7 = (f32[37,4,128]{2,1,0:T(4,128)S(1)}, f32[37,4,128]{2,1,0:T(4,128)S(1)}, u32[]{:S(2)}, u32[]{:S(2)}) collective-permute-start(f32[37,4,128]{2,1,0:T(4,128)S(1)} %get-tuple-element.69), channel_id=1, source_target_pairs={{0,4},{4,0},{8,12},{12,8},{1,5},{5,1},{9,13},{13,9},{2,6},{6,2},{1... | collective-permute-start | bytes 227336 | tf_op jit(solution)/shard_map/ppermute | solution.py:699
  18.7 0.0 collective-permute-done.4.refs_13_
  18.7 0.0 collective-permute-done.5.refs_14_
  18.7 0.0 collective-permute-done.6.refs_15_
  18.7 0.9 %collective-permute-done.7.refs_16_ = f32[37,4,128]{2,1,0:T(4,128)S(1)} collective-permute-done((f32[37,4,128]{2,1,0:T(4,128)S(1)}, f32[37,4,128]{2,1,0:T(4,128)S(1)}, u32[]{:S(2)}, u32[]{:S(2)}) %collective-permute-start.7) | collective-permute-done | bytes 75808 | tf_op jit(solution)/shard_map/ppermute | solution.py:699
  19.6 3.5 %shard_map.68 = (f32[24,24,128]{2,1,0:T(8,128)S(1)}, f32[24,24,128]{2,1,0:T(8,128)S(1)}, f32[24,24,128]{2,1,0:T(8,128)S(1)}, f32[24,24,128]{2,1,0:T(8,128)S(1)},...) custom-call(s32[1]{0:T(128)} %bitcast.where_ref, ...), custom_call_target="tpu_custom_call", output_to_operand_aliasing={{0}: (2, {}), {1}: (3, {}), {2}: (4, {}), {3}: (5, {}), {4}... | custom-call | bytes 14400000 | tf_op jit(solution)/shard_map/pallas_call | solution.py:670
  23.0 0.3 collective-permute-start.8
  23.4 0.2 collective-permute-start.9
  23.6 3.5 %collective-permute-start.10 = (f32[5,8,4,128]{3,2,1,0:T(4,128)S(1)}, f32[5,8,4,128]{3,2,1,0:T(4,128)S(1)}, u32[]{:S(2)}, u32[]{:S(2)}) collective-permute-start(f32[5,8,4,128]{3,2,1,0:T(4,128)S(1)} %get-tuple-element.74), channel_id=1, source_target_pairs={{0,4},{4,0},{8,12},{12,8},{1,5},{5,1},{9,13},{13,9},{2,6},{6,2},{1... | collective-permute-start | bytes 245768 | tf_op jit(solution)/shard_map/ppermute | solution.py:699
  27.1 1.1 %collective-permute-start.11 = (f32[15,4,128]{2,1,0:T(4,128)S(1)}, f32[15,4,128]{2,1,0:T(4,128)S(1)}, u32[]{:S(2)}, u32[]{:S(2)}) collective-permute-start(f32[15,4,128]{2,1,0:T(4,128)S(1)} %get-tuple-element.75), channel_id=1, source_target_pairs={{0,20},{4,16},{8,28},{12,24},{16,4},{20,0},{24,12},{28,8},{1,21},{... | collective-permute-start | bytes 92168 | tf_op jit(solution)/shard_map/ppermute | solution.py:724
  28.2 0.0 collective-permute-start.12
  28.2 2.2 %collective-permute-done.11.refs_3_ = f32[15,4,128]{2,1,0:T(4,128)S(1)} collective-permute-done((f32[15,4,128]{2,1,0:T(4,128)S(1)}, f32[15,4,128]{2,1,0:T(4,128)S(1)}, u32[]{:S(2)}, u32[]{:S(2)}) %collective-permute-start.11) | collective-permute-done | bytes 30752 | tf_op jit(solution)/shard_map/ppermute | solution.py:724
  30.4 2.0 %collective-permute-done.12.refs_4_ = f32[15,4,128]{2,1,0:T(4,128)S(1)} collective-permute-done((f32[15,4,128]{2,1,0:T(4,128)S(1)}, f32[15,4,128]{2,1,0:T(4,128)S(1)}, u32[]{:S(2)}, u32[]{:S(2)}) %collective-permute-start.12) | collective-permute-done | bytes 30752 | tf_op jit(solution)/shard_map/ppermute | solution.py:724
  32.4 0.0 collective-permute-done.8.refs_0_
  32.4 0.4 shard_map.69
  32.9 14.6 %all_to_all.5.gathered = f32[32,5,4,128]{3,2,1,0:T(4,128)S(1)} all-to-all(f32[32,5,4,128]{3,2,1,0:T(4,128)S(1)} %get-tuple-element.77), channel_id=1, replica_groups=mesh['gx'=2,'gy'=4,'gz'=4] {'gx','gy','gz'}, dimensions={0} | all-to-all | bytes 655360 | tf_op jit(solution)/shard_map/all_to_all | solution.py:806
  47.4 5.1 %shard_map.70 = f32[16,16,128]{2,1,0:T(8,128)} custom-call(s32[1]{0:T(128)} %bitcast.where_ref, f32[32,5,4,128]{3,2,1,0:T(4,128)S(1)} %all_to_all.5.gathered, f32[6,16,16,128]{3,2,1,0:T(8,128)S(1)} %get-tuple-element.78.level1, f32[24,24,128]{2,1,0:T(8,128)S(1)} %get-tuple-element.79.refs_0_, f32[24,24,128]{2,1,0:T(8,128)S(1)} %get-tuple-element.80.refs_1_, ...), custom_call_target="tpu_custom_call" | custom-call | bytes 14400000 | tf_op jit(solution)/shard_map/pallas_call | solution.py:670
  (14 shorter events, 0.0 us)
Async XLA Ops:
  0.0 10.8 %copy-start.1 = (f32[16,16,128]{2,1,0:T(8,128)S(1)}, f32[16,16,128]{2,1,0:T(8,128)}, u32[]{:S(2)}) copy-start(f32[16,16,128]{2,1,0:T(8,128)} %refs_1_.3) | copy-start | bytes 393220
  0.0 10.8 %copy-start.2 = (f32[16,16,128]{2,1,0:T(8,128)S(1)}, f32[16,16,128]{2,1,0:T(8,128)}, u32[]{:S(2)}) copy-start(f32[16,16,128]{2,1,0:T(8,128)} %refs_2_.3) | copy-start | bytes 393220
  0.0 10.8 %copy-start.3 = (f32[16,16,128]{2,1,0:T(8,128)S(1)}, f32[16,16,128]{2,1,0:T(8,128)}, u32[]{:S(2)}) copy-start(f32[16,16,128]{2,1,0:T(8,128)} %refs_3_.3) | copy-start | bytes 393220
  0.0 10.8 %copy-start.4 = (f32[16,16,128]{2,1,0:T(8,128)S(1)}, f32[16,16,128]{2,1,0:T(8,128)}, u32[]{:S(2)}) copy-start(f32[16,16,128]{2,1,0:T(8,128)} %refs_4_.3) | copy-start | bytes 393220
  0.0 10.8 %copy-start.5 = (f32[16,16,128]{2,1,0:T(8,128)S(1)}, f32[16,16,128]{2,1,0:T(8,128)}, u32[]{:S(2)}) copy-start(f32[16,16,128]{2,1,0:T(8,128)} %refs_5_.3) | copy-start | bytes 393220
  2.6 8.2 %copy-start = (f32[16,16,128]{2,1,0:T(8,128)S(1)}, f32[16,16,128]{2,1,0:T(8,128)}, u32[]{:S(2)}) copy-start(f32[16,16,128]{2,1,0:T(8,128)} %refs_0_.3) | copy-start | bytes 393220
  2.6 8.2 %collective-permute-start.2 = (f32[6,4,16,128]{3,2,1,0:T(8,128)}, f32[6,4,16,128]{3,2,1,0:T(8,128)S(1)}, u32[]{:S(2)}, u32[]{:S(2)}) collective-permute-start(f32[6,4,16,128]{3,2,1,0:T(8,128)} %get-tuple-element.51), channel_id=1, source_target_pairs={{0,16},{16,0},{1,17},{17,1},{2,18},{18,2},{3,19},{19,3},{4,20},{20... | collective-permute-start | bytes 589832 | tf_op jit(solution)/shard_map/ppermute | solution.py:699
  4.7 14.0 %collective-permute-start.4 = (f32[6,16,4,128]{3,2,1,0:T(4,128)}, f32[6,16,4,128]{3,2,1,0:T(4,128)S(1)}, u32[]{:S(2)}, u32[]{:S(2)}) collective-permute-start(f32[6,16,4,128]{3,2,1,0:T(4,128)} %get-tuple-element.65), channel_id=1, source_target_pairs={{0,12},{4,8},{8,4},{12,0},{1,13},{5,9},{9,5},{13,1},{2,14},{6,10},... | collective-permute-start | bytes 589832 | tf_op jit(solution)/shard_map/ppermute | solution.py:699
  6.8 11.9 %collective-permute-start.5 = (f32[6,16,4,128]{3,2,1,0:T(4,128)}, f32[6,16,4,128]{3,2,1,0:T(4,128)S(1)}, u32[]{:S(2)}, u32[]{:S(2)}) collective-permute-start(f32[6,16,4,128]{3,2,1,0:T(4,128)} %get-tuple-element.66), channel_id=1, source_target_pairs={{0,4},{4,0},{8,12},{12,8},{1,5},{5,1},{9,13},{13,9},{2,6},{6,2},{1... | collective-permute-start | bytes 589832 | tf_op jit(solution)/shard_map/ppermute | solution.py:699
  6.8 3.6 %collective-permute-start = (f32[8,16,128]{2,1,0:T(8,128)}, f32[8,16,128]{2,1,0:T(8,128)S(1)}, u32[]{:S(2)}, u32[]{:S(2)}) collective-permute-start(f32[8,16,128]{2,1,0:T(8,128)} %get-tuple-element.48), channel_id=1, source_target_pairs={{0,1},{1,0},{2,3},{3,2},{4,5},{5,4},{6,7},{7,6},{8,9},{9,8},{10,11... | collective-permute-start | bytes 196616 | tf_op jit(solution)/shard_map/ppermute | solution.py:699
  8.1 2.3 %collective-permute-start.1 = (f32[8,16,128]{2,1,0:T(8,128)}, f32[8,16,128]{2,1,0:T(8,128)S(1)}, u32[]{:S(2)}, u32[]{:S(2)}) collective-permute-start(f32[8,16,128]{2,1,0:T(8,128)} %get-tuple-element.49), channel_id=1, source_target_pairs={{0,4},{1,2},{2,1},{3,7},{4,0},{5,6},{6,5},{7,3},{8,12},{9,10},{10,... | collective-permute-start | bytes 196616 | tf_op jit(solution)/shard_map/ppermute | solution.py:710
  10.5 2.8 %collective-permute-start.3 = (f32[4,16,128]{2,1,0:T(8,128)S(1)}, f32[4,16,128]{2,1,0:T(8,128)S(1)}, u32[]{:S(2)}, u32[]{:S(2)}) collective-permute-start(f32[4,16,128]{2,1,0:T(8,128)S(1)} %get-tuple-element.64), channel_id=1, source_target_pairs={{0,16},{16,0},{1,17},{17,1},{2,18},{18,2},{3,19},{19,3},{4,20},{20... | collective-permute-start | bytes 98312 | tf_op jit(solution)/shard_map/ppermute | solution.py:699
  13.4 5.3 %collective-permute-start.6 = (f32[37,4,128]{2,1,0:T(4,128)S(1)}, f32[37,4,128]{2,1,0:T(4,128)S(1)}, u32[]{:S(2)}, u32[]{:S(2)}) collective-permute-start(f32[37,4,128]{2,1,0:T(4,128)S(1)} %get-tuple-element.68), channel_id=1, source_target_pairs={{0,1},{4,8},{8,4},{12,13},{1,0},{5,9},{9,5},{13,12},{2,3},{6,10},{... | collective-permute-start | bytes 227336 | tf_op jit(solution)/shard_map/ppermute | solution.py:710
  16.1 3.5 %collective-permute-start.7 = (f32[37,4,128]{2,1,0:T(4,128)S(1)}, f32[37,4,128]{2,1,0:T(4,128)S(1)}, u32[]{:S(2)}, u32[]{:S(2)}) collective-permute-start(f32[37,4,128]{2,1,0:T(4,128)S(1)} %get-tuple-element.69), channel_id=1, source_target_pairs={{0,4},{4,0},{8,12},{12,8},{1,5},{5,1},{9,13},{13,9},{2,6},{6,2},{1... | collective-permute-start | bytes 227336 | tf_op jit(solution)/shard_map/ppermute | solution.py:699
  23.0 9.4 %collective-permute-start.8 = (f32[5,4,8,128]{3,2,1,0:T(8,128)S(1)}, f32[5,4,8,128]{3,2,1,0:T(8,128)S(1)}, u32[]{:S(2)}, u32[]{:S(2)}) collective-permute-start(f32[5,4,8,128]{3,2,1,0:T(8,128)S(1)} %get-tuple-element.72), channel_id=1, source_target_pairs={{0,16},{16,0},{1,17},{17,1},{2,18},{18,2},{3,19},{19,3},{4,20},{20... | collective-permute-start | bytes 245768 | tf_op jit(solution)/shard_map/ppermute | solution.py:699
  23.4 9.1 %collective-permute-start.9 = (f32[5,8,4,128]{3,2,1,0:T(4,128)S(1)}, f32[5,8,4,128]{3,2,1,0:T(4,128)S(1)}, u32[]{:S(2)}, u32[]{:S(2)}) collective-permute-start(f32[5,8,4,128]{3,2,1,0:T(4,128)S(1)} %get-tuple-element.73), channel_id=1, source_target_pairs={{0,1},{4,8},{8,4},{12,13},{1,0},{5,9},{9,5},{13,12},{2,3},{6,10},{... | collective-permute-start | bytes 245768 | tf_op jit(solution)/shard_map/ppermute | solution.py:710
  23.6 8.9 %collective-permute-start.10 = (f32[5,8,4,128]{3,2,1,0:T(4,128)S(1)}, f32[5,8,4,128]{3,2,1,0:T(4,128)S(1)}, u32[]{:S(2)}, u32[]{:S(2)}) collective-permute-start(f32[5,8,4,128]{3,2,1,0:T(4,128)S(1)} %get-tuple-element.74), channel_id=1, source_target_pairs={{0,4},{4,0},{8,12},{12,8},{1,5},{5,1},{9,13},{13,9},{2,6},{6,2},{1... | collective-permute-start | bytes 245768 | tf_op jit(solution)/shard_map/ppermute | solution.py:699
  27.1 3.3 %collective-permute-start.11 = (f32[15,4,128]{2,1,0:T(4,128)S(1)}, f32[15,4,128]{2,1,0:T(4,128)S(1)}, u32[]{:S(2)}, u32[]{:S(2)}) collective-permute-start(f32[15,4,128]{2,1,0:T(4,128)S(1)} %get-tuple-element.75), channel_id=1, source_target_pairs={{0,20},{4,16},{8,28},{12,24},{16,4},{20,0},{24,12},{28,8},{1,21},{... | collective-permute-start | bytes 92168 | tf_op jit(solution)/shard_map/ppermute | solution.py:724
  28.2 4.2 %collective-permute-start.12 = (f32[15,4,128]{2,1,0:T(4,128)S(1)}, f32[15,4,128]{2,1,0:T(4,128)S(1)}, u32[]{:S(2)}, u32[]{:S(2)}) collective-permute-start(f32[15,4,128]{2,1,0:T(4,128)S(1)} %get-tuple-element.76), channel_id=1, source_target_pairs={{0,16},{4,24},{8,20},{12,28},{16,0},{20,8},{24,4},{28,12},{1,17},{... | collective-permute-start | bytes 92168 | tf_op jit(solution)/shard_map/ppermute | solution.py:724

commit v13 on v12

--- a/solution.py
+++ b/solution.py
@@ -183,6 +183,42 @@
     return sends
 
 
+def halo_lanes(n):
+    return SIDE + 2 * NEAR * n
+
+
+def pack_level1(values):
+    lane = lane_of(values[0].shape)
+    axis = values[0].ndim - 1
+    packs = [
+        jnp.where(lane < SIDE, values[0], turn(values[1], SIDE, axis)),
+        jnp.where(lane < SIDE, values[2], turn(values[3], SIDE, axis)),
+    ]
+    last = jnp.where(lane < SIDE, values[4], 0.0)
+    for n, array in enumerate(values):
+        at = halo_lanes(n)
+        right = turn(array, at - SIDE, axis)
+        left = turn(array, at + 2 * NEAR, axis)
+        last = jnp.where((lane >= at) & (lane < at + NEAR), right, last)
+        last = jnp.where((lane >= at + NEAR) & (lane < at + 2 * NEAR), left, last)
+    return packs + [last]
+
+
+def unpack_level1(packs):
+    first, second, last = packs
+    lane = lane_of(first.shape)
+    axis = first.ndim - 1
+    blocks = (first, turn(first, SIDE, axis), second, turn(second, SIDE, axis), last)
+    values = []
+    for n, block in enumerate(blocks):
+        at = halo_lanes(n)
+        right = turn(last, SIDE - at, axis)
+        left = turn(last, -at - 2 * NEAR, axis)
+        halo = jnp.where(lane < SIDE + NEAR, right, jnp.where(lane >= LANES - NEAR, left, 0.0))
+        values.append(jnp.where(lane < SIDE, block, halo))
+    return values
+
+
 def diagonal_tiles(first, second, third):
     return [first, second, third, inner_rows(second, 3)]
 
@@ -190,7 +226,7 @@
 def faces_kernel(counts, where_ref, *refs):
     ins, refs = refs[:6], refs[6:]
     n_x = 1 if counts[0] == 2 else 2
-    sends_x, (two_y, one_y, first, second) = refs[:n_x], refs[n_x:]
+    sends_x, (two_y, one_y, first, second), sends_xz = refs[:n_x], refs[n_x:n_x + 4], refs[n_x + 4:]
     odd_x, odd_y, odd = (place % 2 for place in position(where_ref))
     sx, sy, sz = ins[0].shape
     half = sx // 2
@@ -207,33 +243,45 @@
             mask = (lane >= at) & (lane < at + DEPTH[a])
             head = jnp.where(mask, turn(values, at, 2), head)
             tail = jnp.where(mask, turn(values, at + DEPTH[a], 2), tail)
-    first[...] = pick(odd, head, tail)
-    second[...] = pick(odd, tail, head)
-
-
-def halo_z_kernel(counts, where_ref, one_ref, two_ref, zpack, *sends):
-    at_x, _, at_z = position(where_ref)
+    swapped = (pick(odd, head, tail), pick(odd, tail, head))
+    first[...], second[...] = swapped
+    lane = lane_of((2, sy, LANES))
+    for k_z, values in enumerate(swapped):
+        low = jnp.where(lane < SIDE, values[:2], turn(values[2:4], SIDE, 2))
+        high = jnp.where(lane < SIDE, turn(values[half - 4:half - 2], SIDE, 2), values[half - 2:])
+        for k_x in range(n_x):
+            sends_xz[2 * k_x + k_z][...] = pick(odd_x if k_x == 0 else 1 - odd_x, low, high)
+
+
+def halo_z_kernel(counts, where_ref, one_ref, two_ref, *refs):
+    n_x = 1 if counts[0] == 2 else 2
+    diagonals, main_x = refs[:2 * n_x], refs[2 * n_x:3 * n_x]
+    zpack, two_y, one_y = refs[3 * n_x:]
+    at_x, at_y, at_z = position(where_ref)
     half = one_ref.shape[0]
+    sx = 2 * half
     below, above = neighbours(counts[2], at_z, one_ref[...], two_ref[...])
     lane = lane_of(below.shape)
-    zpack[:half] = jnp.where(lane < SIDE, above, turn(below, SIDE, 2))
-    zpack[half:] = jnp.where(lane < SIDE, turn(above, SIDE, 2), below)
-    for send, face in zip(sends, faces_x(zpack[...][None], at_x % 2, len(sends), HALO)):
-        send[...] = face[0]
-
-
-def corners_kernel(counts, where_ref, zpack, *refs):
-    n_x = 1 if counts[0] == 2 else 2
-    main_x, halos_x, (two_y, one_y) = refs[:n_x], refs[n_x:2 * n_x], refs[2 * n_x + 1:]
-    at_x, at_y, _ = position(where_ref)
+    own = slice(HALO, HALO + half), slice(HALO + half, HALO + sx)
+    zpack[own[0]] = jnp.where(lane < SIDE, above, turn(below, SIDE, 2))
+    zpack[own[1]] = jnp.where(lane < SIDE, turn(above, SIDE, 2), below)
+    sides = [
+        neighbours(counts[0], at_x, diagonals[k][...], diagonals[k - 2][...]) for k in range(2)
+    ]
+    lane = lane_of(sides[0][0].shape)
+    for at, (one, two) in zip((0, HALO + sx), zip(*sides)):
+        below, above = neighbours(counts[2], at_z, one, two)
+        zpack[at:at + 2] = jnp.where(lane < SIDE, above, turn(below, SIDE, 2))
+        zpack[at + 2:at + 4] = jnp.where(lane < SIDE, turn(above, SIDE, 2), below)
+    odd = at_y % 2
     for a in range(7):
         if a < 6:
             below, above = neighbours(counts[0], at_x, main_x[0][a], main_x[-1][a])
         else:
-            below, above = neighbours(counts[0], at_x, halos_x[0][...], halos_x[-1][...])
-        for n, pair in enumerate(corner_sends(below, above, at_y % 2)):
+            below, above = zpack[:HALO], zpack[HALO + sx:]
+        for n, pair in enumerate(corner_sends(below, above, odd)):
             one_y[3 * a + n], two_y[3 * a + n] = pair
-    one_y[21:], two_y[21:] = faces_y(zpack[...], at_y % 2, HALO)
+    one_y[21:], two_y[21:] = faces_y(zpack[HALO:HALO + sx], odd, HALO)
 
 
 def each(first, last, step, body):
@@ -301,14 +349,14 @@
 
 
 def coefficient_kernel(counts, where_ref, *refs):
-    ins, refs = refs[:7], refs[7:]
+    ins, zpack, refs = refs[:6], refs[6], refs[7:]
     n_x = 1 if counts[0] == 2 else 2
     main_x, refs = refs[:n_x], refs[n_x:]
     arrays, (coarse2, coeffs1, sums, pairing) = refs[:12], refs[12:]
     sx, sy, sz = ins[0].shape
     at_x = position(where_ref)[0]
     x1, y1 = sx // 2, sy // 2
-    lane = lane_of((sx, sy, LANES))
+    lane = lane_of(zpack.shape)
     lanes = [slice(k * LANES, (k + 1) * LANES) for k in range(2)]
     mine = slice(HALO, HALO + sx)
     for a in range(6):
@@ -317,7 +365,7 @@
         to[:HALO, :sy] = below
         to[mine, :sy] = ins[a][...]
         to[HALO + sx:, :sy] = above
-        arrays[2 * a + 1][mine, :sy] = unpacked(ins[6][...], a, lane)
+        arrays[2 * a + 1][:, :sy] = unpacked(zpack[...], a, lane)
     for n, (firsts, seconds) in enumerate(((BOTH, BOTH), (ODD, BOTH), (BOTH, ODD), (BOTH, BOTH))):
         for k in range(2):
             for i in range(x1):
@@ -343,12 +391,11 @@
         coarse2[n] = level2_rows(pairing.at[n], odd_axes, factor, x1 // 2, y1 // 2, sz // 4)
 
 
-def down_kernel(counts, where_ref, zpack, *refs):
+def down_kernel(counts, where_ref, *refs):
     refs = refs[12:]
     n_x = 1 if counts[0] == 2 else 2
-    halos_x = refs[:n_x]
-    main_two, main_one, rest_two, rest_one, coeffs1 = refs[n_x:5 + n_x]
-    flat, refs = refs[5 + n_x:17 + n_x], refs[17 + n_x:]
+    main_two, main_one, rest_two, rest_one, coeffs1 = refs[:5]
+    flat, refs = refs[5:17], refs[17:]
     arrays = tuple(zip(flat[::2], flat[1::2]))
     own1, refs = refs[0], refs[1:]
     sends, near_two, near_one, refs = refs[:n_x], refs[n_x], refs[n_x + 1], refs[n_x + 2:]
@@ -356,8 +403,8 @@
     kept_m, kept_h, weight_m, weight_h = refs[:4]
     packs, half_m, half_h, diag_m, diag_h, sums, left = refs[4:]
     field, rhs, alpha, bx, by, bz = arrays
-    sx, sy, sz = zpack.shape
-    ex, ey = sx + 2 * HALO, sy + 2 * HALO
+    ex, ey, _ = flat[0].shape
+    sx, sy = ex - 2 * HALO, ey - 2 * HALO
     at_x, at_y, _ = position(where_ref)
 
     rest = neighbours(counts[1], at_y, rest_one[...], rest_two[...])
@@ -370,30 +417,21 @@
         else:
             to = packs
             rows = rest[21:]
-            below, above = neighbours(counts[0], at_x, halos_x[0][...], halos_x[-1][...])
-            to[:HALO, :sy] = below
-            to[HALO + sx:, :sy] = above
-        to[HALO:HALO + sx, sy:] = rows
+        first = 0 if a == 6 else sy
+        to[HALO:HALO + sx, first:] = rows
         low, high = corner_tiles(*(rest[3 * a + n] for n in range(3)))
         for n in range(HALO):
-            to[n, sy:] = low[n]
-            to[HALO + sx + n, sy:] = high[n]
+            to[n, first:] = low[n]
+            to[HALO + sx + n, first:] = high[n]
     lane = lane_of((ey, LANES))
     lane_low = lane_of((2 * HALO, LANES))
-
-    def unpack_rows(x):
-        packed = packs[x, sy:]
-        for a in range(6):
-            arrays[a][1][x, sy:] = unpacked(packed, a, lane_low)
 
     def unpack(x):
         packed = packs[x]
         for a in range(6):
-            arrays[a][1][x] = unpacked(packed, a, lane)
-
-    each(0, HALO, HALO, unpack)
-    each(HALO, HALO + sx, 8, unpack_rows)
-    each(HALO + sx, ex, HALO, unpack)
+            arrays[a][1][x, sy:] = unpacked(packed, a, lane_low)
+
+    each(0, ex, 8, unpack)
     halfway, weight, kept = (half_m, half_h), (weight_m, weight_h), (kept_m, kept_h)
     diag = (diag_m, diag_h)
 
@@ -438,7 +476,8 @@
         sums[2, 1:, :, lanes] = jnp.zeros((x1 - 1, y1, LANES), F32)
     rhs1, low_y, low_x = to_level1(sums, 0, 3, pair_table(2 * LANES, LANES, False), 0.0625)
     weight1 = relaxer(coeffs1[0], coeffs1[1] + low_y + low_x)
-    for n, values in enumerate((2.0 * rhs1, weight1, coeffs1[2], coeffs1[3], coeffs1[4])):
+    packed = pack_level1((2.0 * rhs1, weight1, coeffs1[2], coeffs1[3], coeffs1[4]))
+    for n, values in enumerate(packed):
         own1[n] = values
         for send, face in zip(sends, faces_x(values[None], at_x % 2, n_x, NEAR)):
             send[n] = face[0]
@@ -493,6 +532,7 @@
         )
         block = jnp.concatenate([below, ring[a], above], axis=0)
         whole.append(jnp.concatenate([block, rows], axis=1))
+    whole = unpack_level1(whole)
     rhs1, weight1 = whole[:2]
     faces1 = tuple(whole[2:])
     field1 = weight1 * rhs1
@@ -507,7 +547,7 @@
     packed = level2_rows(left, (False,) * 3, 0.125, bx1 // 2, by1 // 2, LANES // 4)
     for d in range(devices):
         copies[d, 0] = packed
-        for a in range(n - 1):
+        for a in range(4):
             copies[d, a + 1] = coarse2[a]
 
 
@@ -711,17 +751,15 @@
     return got
 
 
-def diagonal_swaps(sends):
-    count_x, count_y = lax.axis_size("gx"), lax.axis_size("gy")
+def diagonal_swaps(sends, other):
+    count_x, count = lax.axis_size("gx"), lax.axis_size(other)
     got = []
     for n, block in enumerate(sends):
-        xs, ys = partners(count_x, n // 2), partners(count_y, n % 2)
+        xs, others = partners(count_x, n // 2), partners(count, n % 2)
         pairs = [
-            (x * count_y + y, xs[x] * count_y + ys[y])
-            for x in range(count_x)
-            for y in range(count_y)
+            (x * count + y, xs[x] * count + others[y]) for x in range(count_x) for y in range(count)
         ]
-        got.append(lax.ppermute(block, ("gx", "gy"), pairs))
+        got.append(lax.ppermute(block, ("gx", other), pairs))
     return got
 
 
@@ -737,25 +775,26 @@
     ex, ey = sx + 2 * HALO, sy + 2 * HALO
     fine = (ex, ey, LANES)
 
-    *sends_x, two_y, one_y, first, second = run(
+    sends = run(
         functools.partial(faces_kernel, counts),
         [(6, HALO, sy, LANES)] * n_x
         + [(6, sx, HALO, LANES)] * 2
-        + [(sx // 2, sy, LANES)] * 2,
+        + [(sx // 2, sy, LANES)] * 2
+        + [(2, sy, LANES)] * (2 * n_x),
         where,
         ins,
         grant=60,
     )
-    main_x = tuple(swaps("gx", sends_x, "gy"))
-    main_y = tuple(swaps("gy", (one_y, two_y))[::-1])
-    got = swaps("gz", (first, second), "gy")
-    zpack, *sends = run(
+    main_x = tuple(swaps("gx", sends[:n_x], "gy"))
+    main_y = tuple(swaps("gy", sends[n_x:n_x + 2][::-1])[::-1])
+    got = tuple(swaps("gz", sends[n_x + 2:n_x + 4], "gy"))
+    got_xz = tuple(diagonal_swaps(sends[n_x + 4:], "gz"))
+    zpack, two_y, one_y = run(
         functools.partial(halo_z_kernel, counts),
-        [(sx, sy, LANES)] + [(HALO, sy, LANES)] * n_x,
+        [(ex, sy, LANES)] + [(21 + sx, HALO, LANES)] * 2,
         where,
-        tuple(got),
+        got + got_xz + main_x,
     )
-    halos_x = tuple(swaps("gx", sends, "gy"))
     x1, y1 = sx // 2, sy // 2
     *laid, coarse2, coeffs1 = run(
         functools.partial(coefficient_kernel, counts),
@@ -765,27 +804,21 @@
         [(4, x1, y1, 2 * LANES), (4, x1, y1, LANES)],
         micros=2,
     )
-    two_y, one_y = run(
-        functools.partial(corners_kernel, counts),
-        [(21 + sx, HALO, LANES)] * 2,
-        where,
-        (zpack,) + main_x + halos_x + (coarse2,),
-    )
     rest_y = tuple(swaps("gy", (one_y, two_y), "gz")[::-1])
     outs = run(
         functools.partial(down_kernel, counts),
         [fine] * 12
-        + [(5, x1, y1, LANES)]
-        + [(5, NEAR, y1, LANES)] * n_x
-        + [(5, x1, NEAR, LANES)] * 2
-        + [(15, NEAR, LANES)] * (2 * n_x)
+        + [(3, x1, y1, LANES)]
+        + [(3, NEAR, y1, LANES)] * n_x
+        + [(3, x1, NEAR, LANES)] * 2
+        + [(9, NEAR, LANES)] * (2 * n_x)
         + [fine] * 4,
         where,
-        (zpack,) + tuple(laid) + halos_x + main_y + rest_y + (coeffs1,),
-        [fine] * 5 + [(3, x1, y1, 2 * LANES), (ey, LANES)],
+        tuple(laid) + main_y + rest_y + (coeffs1,),
+        [(ex, 2 * HALO, LANES)] + [fine] * 4 + [(3, x1, y1, 2 * LANES), (ey, LANES)],
         24,
         micros=4,
-        aliases={n + 2: n for n in range(12)},
+        aliases={n + 1: n for n in range(12)},
     )
     laid, own1, outs = outs[:12], outs[12], outs[13:]
     sends_x, (two_y, one_y), outs = outs[:n_x], outs[n_x:n_x + 2], outs[n_x + 2:]
@@ -794,7 +827,7 @@
 
     near_x = tuple(swaps("gx", sends_x, "gy"))
     near_y = tuple(swaps("gy", (one_y, two_y), "gz")[::-1])
-    near_xy = tuple(diagonal_swaps(sends_xy))
+    near_xy = tuple(diagonal_swaps(sends_xy, "gy"))
     copies, level1 = run(
         functools.partial(near_kernel, counts, devices),
         [(devices, 5, y1 // 2, LANES), (6, x1 + 2 * NEAR, y1 + 2 * NEAR, LANES)],

time: 52.7 us -> 54.4 us (1.032)
  starting transfers between devices: 17 us -> 19.4 us
  waiting for transfers between devices: 8.37 us -> 6.44 us
  blocking collectives: 14.6 us -> 15.5 us
    ppermute x8 -> x7, waiting for transfers between devices: 4.15 us -> 0.09 us  [swaps(): got.append(lax.ppermute(block, axis, list(enumerate(partner))))]
    ppermute x2 -> x4, starting transfers between devices: 1.1 us -> 2.65 us  [diagonal_swaps(): got.append(lax.ppermute(block, ('gx', other), pairs))]
    ppermute x2 -> x4, waiting for transfers between devices: 4.21 us -> 5.3 us  [diagonal_swaps(): got.append(lax.ppermute(block, ('gx', other), pairs))]
    ppermute x3, waiting for transfers between devices: 0.01 us -> 1.04 us  [swaps(): got.append(lax.ppermute(block, tuple(sorted((axis, other))), pairs))]
    all_to_all x1, blocking collectives: 14.6 us -> 15.5 us  [local(): gathered = lax.all_to_all(copies, axes, 0, 0, tiled=True)]
    ppermute x8 -> x7, starting transfers between devices: 12.2 us -> 12.8 us  [swaps(): got.append(lax.ppermute(block, axis, list(enumerate(partner))))]
    pallas_call x7 -> x6, Pallas kernels: 12.5 us -> 12.7 us  [run(): pl.pallas_call(kernel, out_shape=tuple((jax.ShapeDtypeStruct(shape, F32)...]
  transfers between devices with their start and end apart: 13 -> 14, of which waited for: 5 -> 5; matrix products, arithmetic and copies ran while one was open for 0% -> 0% of each run, Pallas kernels for 2% -> 2%
where the time goes in v13:
time: 54.4 us; the launch traced here: 54.2 us
  starting transfers between devices  19.4 us (36%)
  blocking collectives  15.5 us (28%)
  Pallas kernels  12.7 us (23%)
  waiting for transfers between devices  6.44 us (12%)
    all_to_all x1, blocking collectives, local(): gathered = lax.all_to_all(copies, axes, 0, 0, tiled=True)  15.5 us
    ppermute x7, starting transfers between devices, swaps(): got.append(lax.ppermute(block, axis, list(enumerate(partner))))  12.8 us
    pallas_call x6, Pallas kernels, run(): pl.pallas_call(kernel, out_shape=tuple((jax.ShapeDtypeStruct(shape, F32)...  12.7 us
    ppermute x4, waiting for transfers between devices, diagonal_swaps(): got.append(lax.ppermute(block, ('gx', other), pairs))  5.3 us
    ppermute x3, starting transfers between devices, swaps(): got.append(lax.ppermute(block, tuple(sorted((axis, other))), pairs))  3.99 us
    ppermute x4, starting transfers between devices, diagonal_swaps(): got.append(lax.ppermute(block, ('gx', other), pairs))  2.65 us
  transfers between devices with their start and end apart: 14, of which 5 were waited for; matrix products, arithmetic and copies ran while one was open for 0% of the time, Pallas kernels for 2%

profile of v13, /device:TPU:1, one launch (start us, length us, event | category | flops | bytes accessed | tf_op | source)
XLA Modules:
  0.0 54.2 jit_solution(5784786002963831511)
XLA Ops:
  0.0 2.6 %shard_map.64 = (f32[6,4,16,128]{3,2,1,0:T(8,128)}, f32[6,16,4,128]{3,2,1,0:T(4,128)}, f32[6,16,4,128]{3,2,1,0:T(4,128)}, f32[8,16,128]{2,1,0:T(8,128)}, f32[8,1...) custom-call(s32[1]{0:T(128)} %bitcast.where_ref, f32[16,16,128]{2,1,0:T(8,128)} %refs_0_.3, ...), custom_call_target="tpu_custom_call" | custom-call | bytes 3600000 | tf_op jit(solution)/shard_map/pallas_call | solution.py:710
  2.6 2.0 %collective-permute-start.4 = (f32[6,4,16,128]{3,2,1,0:T(8,128)}, f32[6,4,16,128]{3,2,1,0:T(8,128)S(1)}, u32[]{:S(2)}, u32[]{:S(2)}) collective-permute-start(f32[6,4,16,128]{3,2,1,0:T(8,128)} %get-tuple-element.53), channel_id=1, source_target_pairs={{0,16},{16,0},{1,17},{17,1},{2,18},{18,2},{3,19},{19,3},{4,20},{20... | collective-permute-start | bytes 589832 | tf_op jit(solution)/shard_map/ppermute | solution.py:739
  4.7 2.1 %collective-permute-start.5 = (f32[6,16,4,128]{3,2,1,0:T(4,128)}, f32[6,16,4,128]{3,2,1,0:T(4,128)S(1)}, u32[]{:S(2)}, u32[]{:S(2)}) collective-permute-start(f32[6,16,4,128]{3,2,1,0:T(4,128)} %get-tuple-element.67), channel_id=1, source_target_pairs={{0,12},{4,8},{8,4},{12,0},{1,13},{5,9},{9,5},{13,1},{2,14},{6,10},... | collective-permute-start | bytes 589832 | tf_op jit(solution)/shard_map/ppermute | solution.py:739
  6.7 0.0 collective-permute-start.6
  6.7 1.3 %collective-permute-start.2 = (f32[2,16,128]{2,1,0:T(8,128)}, f32[2,16,128]{2,1,0:T(8,128)S(1)}, u32[]{:S(2)}, u32[]{:S(2)}) collective-permute-start(f32[2,16,128]{2,1,0:T(8,128)} %get-tuple-element.51), channel_id=1, source_target_pairs={{0,17},{1,16},{2,19},{3,18},{16,1},{17,0},{18,3},{19,2},{4,21},{5,... | collective-permute-start | bytes 49160 | tf_op jit(solution)/shard_map/ppermute | solution.py:762
  8.0 1.2 %collective-permute-start.3 = (f32[2,16,128]{2,1,0:T(8,128)}, f32[2,16,128]{2,1,0:T(8,128)S(1)}, u32[]{:S(2)}, u32[]{:S(2)}) collective-permute-start(f32[2,16,128]{2,1,0:T(8,128)} %get-tuple-element.52), channel_id=1, source_target_pairs={{0,16},{1,18},{2,17},{3,19},{16,0},{17,2},{18,1},{19,3},{4,20},{5,... | collective-permute-start | bytes 49160 | tf_op jit(solution)/shard_map/ppermute | solution.py:762
  9.2 1.2 %collective-permute-done.2.refs_0_ = f32[2,16,128]{2,1,0:T(8,128)S(1)} collective-permute-done((f32[2,16,128]{2,1,0:T(8,128)}, f32[2,16,128]{2,1,0:T(8,128)S(1)}, u32[]{:S(2)}, u32[]{:S(2)}) %collective-permute-start.2) | collective-permute-done | bytes 16416 | tf_op jit(solution)/shard_map/ppermute | solution.py:762
  10.4 1.3 %collective-permute-start = (f32[8,16,128]{2,1,0:T(8,128)}, f32[8,16,128]{2,1,0:T(8,128)S(1)}, u32[]{:S(2)}, u32[]{:S(2)}) collective-permute-start(f32[8,16,128]{2,1,0:T(8,128)} %get-tuple-element.49), channel_id=1, source_target_pairs={{0,1},{1,0},{2,3},{3,2},{4,5},{5,4},{6,7},{7,6},{8,9},{9,8},{10,11... | collective-permute-start | bytes 196616 | tf_op jit(solution)/shard_map/ppermute | solution.py:739
  11.8 0.0 collective-permute-done.3.refs_1_
  11.8 1.9 %collective-permute-start.1 = (f32[8,16,128]{2,1,0:T(8,128)}, f32[8,16,128]{2,1,0:T(8,128)S(1)}, u32[]{:S(2)}, u32[]{:S(2)}) collective-permute-start(f32[8,16,128]{2,1,0:T(8,128)} %get-tuple-element.50), channel_id=1, source_target_pairs={{0,4},{1,2},{2,1},{3,7},{4,0},{5,6},{6,5},{7,3},{8,12},{9,10},{10,... | collective-permute-start | bytes 196616 | tf_op jit(solution)/shard_map/ppermute | solution.py:750
  13.7 0.1 collective-permute-done.one_ref
  13.8 1.0 %collective-permute-done.1.two_ref = f32[8,16,128]{2,1,0:T(8,128)S(1)} collective-permute-done((f32[8,16,128]{2,1,0:T(8,128)}, f32[8,16,128]{2,1,0:T(8,128)S(1)}, u32[]{:S(2)}, u32[]{:S(2)}) %collective-permute-start.1) | collective-permute-done | bytes 65568 | tf_op jit(solution)/shard_map/ppermute | solution.py:750
  14.8 0.0 collective-permute-done.4.refs_2_.refs_7_
  14.8 0.1 shard_map.65
  14.9 2.1 %collective-permute-start.7 = (f32[37,4,128]{2,1,0:T(4,128)S(1)}, f32[37,4,128]{2,1,0:T(4,128)S(1)}, u32[]{:S(2)}, u32[]{:S(2)}) collective-permute-start(f32[37,4,128]{2,1,0:T(4,128)S(1)} %get-tuple-element.69), channel_id=1, source_target_pairs={{0,1},{4,8},{8,4},{12,13},{1,0},{5,9},{9,5},{13,12},{2,3},{6,10},{... | collective-permute-start | bytes 227336 | tf_op jit(solution)/shard_map/ppermute | solution.py:750
  17.0 2.5 %collective-permute-start.8 = (f32[37,4,128]{2,1,0:T(4,128)S(1)}, f32[37,4,128]{2,1,0:T(4,128)S(1)}, u32[]{:S(2)}, u32[]{:S(2)}) collective-permute-start(f32[37,4,128]{2,1,0:T(4,128)S(1)} %get-tuple-element.70), channel_id=1, source_target_pairs={{0,4},{4,0},{8,12},{12,8},{1,5},{5,1},{9,13},{13,9},{2,6},{6,2},{1... | collective-permute-start | bytes 227336 | tf_op jit(solution)/shard_map/ppermute | solution.py:739
  19.5 0.9 %shard_map.66 = (f32[24,24,128]{2,1,0:T(8,128)S(1)}, f32[24,24,128]{2,1,0:T(8,128)S(1)}, f32[24,24,128]{2,1,0:T(8,128)S(1)}, f32[24,24,128]{2,1,0:T(8,128)S(1)},...) custom-call(s32[1]{0:T(128)} %bitcast.where_ref, ...), custom_call_target="tpu_custom_call" | custom-call | bytes 7200000 | tf_op jit(solution)/shard_map/pallas_call | solution.py:710
  20.4 0.0 collective-permute-done.6.refs_13_
  20.5 0.0 collective-permute-done.7.refs_14_
  20.5 3.3 %shard_map.67 = (f32[24,24,128]{2,1,0:T(8,128)S(1)}, f32[24,24,128]{2,1,0:T(8,128)S(1)}, f32[24,24,128]{2,1,0:T(8,128)S(1)}, f32[24,24,128]{2,1,0:T(8,128)S(1)},...) custom-call(s32[1]{0:T(128)} %bitcast.where_ref, ...), custom_call_target="tpu_custom_call", output_to_operand_aliasing={{0}: (1, {}), {1}: (2, {}), {2}: (3, {}), {3}: (4, {}), {4}... | custom-call | bytes 14400000 | tf_op jit(solution)/shard_map/pallas_call | solution.py:710
  23.8 1.2 %collective-permute-start.9 = (f32[3,4,8,128]{3,2,1,0:T(8,128)S(1)}, f32[3,4,8,128]{3,2,1,0:T(8,128)S(1)}, u32[]{:S(2)}, u32[]{:S(2)}) collective-permute-start(f32[3,4,8,128]{3,2,1,0:T(8,128)S(1)} %get-tuple-element.73), channel_id=1, source_target_pairs={{0,16},{16,0},{1,17},{17,1},{2,18},{18,2},{3,19},{19,3},{4,20},{20... | collective-permute-start | bytes 147464 | tf_op jit(solution)/shard_map/ppermute | solution.py:739
  25.0 0.0 collective-permute-start.10
  25.0 3.6 %collective-permute-start.11 = (f32[3,8,4,128]{3,2,1,0:T(4,128)S(1)}, f32[3,8,4,128]{3,2,1,0:T(4,128)S(1)}, u32[]{:S(2)}, u32[]{:S(2)}) collective-permute-start(f32[3,8,4,128]{3,2,1,0:T(4,128)S(1)} %get-tuple-element.75), channel_id=1, source_target_pairs={{0,4},{4,0},{8,12},{12,8},{1,5},{5,1},{9,13},{13,9},{2,6},{6,2},{1... | collective-permute-start | bytes 147464 | tf_op jit(solution)/shard_map/ppermute | solution.py:739
  28.6 0.2 collective-permute-start.12
  28.8 0.0 collective-permute-start.13
  28.8 3.0 %collective-permute-done.12.refs_3_ = f32[9,4,128]{2,1,0:T(4,128)S(1)} collective-permute-done((f32[9,4,128]{2,1,0:T(4,128)S(1)}, f32[9,4,128]{2,1,0:T(4,128)S(1)}, u32[]{:S(2)}, u32[]{:S(2)}) %collective-permute-start.12) | collective-permute-done | bytes 18464 | tf_op jit(solution)/shard_map/ppermute | solution.py:762
  31.8 1.1 %collective-permute-done.13.refs_4_ = f32[9,4,128]{2,1,0:T(4,128)S(1)} collective-permute-done((f32[9,4,128]{2,1,0:T(4,128)S(1)}, f32[9,4,128]{2,1,0:T(4,128)S(1)}, u32[]{:S(2)}, u32[]{:S(2)}) %collective-permute-start.13) | collective-permute-done | bytes 18464 | tf_op jit(solution)/shard_map/ppermute | solution.py:762
  32.9 0.0 collective-permute-done.10.refs_1_
  32.9 0.0 collective-permute-done.11.refs_2_
  32.9 0.7 %shard_map.68 = (f32[32,5,4,128]{3,2,1,0:T(4,128)S(1)}, f32[6,16,16,128]{3,2,1,0:T(8,128)S(1)}) custom-call(s32[1]{0:T(128)} %bitcast.where_ref, f32[3,8,8,128]{3,2,1,0:T(8,128)S(1)} %get-tuple-element.72.ring, f32[3,4,8,128]{3,2,1,0:T(8,128)S(1)} %collective-permute-done.9.refs_0_, f32[3,8,4,128]{3,2,1,0:T(4,128)S(1)} %collective-permute-done.10.refs_1_, ...), custom_call_target="tpu_custom_call" | custom-call | bytes 3600000 | tf_op jit(solution)/shard_map/pallas_call | solution.py:710
  33.6 15.5 %all_to_all.5.gathered = f32[32,5,4,128]{3,2,1,0:T(4,128)S(1)} all-to-all(f32[32,5,4,128]{3,2,1,0:T(4,128)S(1)} %get-tuple-element.79), channel_id=1, replica_groups=mesh['gx'=2,'gy'=4,'gz'=4] {'gx','gy','gz'}, dimensions={0} | all-to-all | bytes 655360 | tf_op jit(solution)/shard_map/all_to_all | solution.py:839
  49.1 5.1 %shard_map.69 = f32[16,16,128]{2,1,0:T(8,128)} custom-call(s32[1]{0:T(128)} %bitcast.where_ref, f32[32,5,4,128]{3,2,1,0:T(4,128)S(1)} %all_to_all.5.gathered, f32[6,16,16,128]{3,2,1,0:T(8,128)S(1)} %get-tuple-element.80.level1, f32[24,24,128]{2,1,0:T(8,128)S(1)} %get-tuple-element.81.refs_0_, f32[24,24,128]{2,1,0:T(8,128)S(1)} %get-tuple-element.82.refs_1_, ...), custom_call_target="tpu_custom_call" | custom-call | bytes 14400000 | tf_op jit(solution)/shard_map/pallas_call | solution.py:710
  (15 shorter events, 0.0 us)
Async XLA Ops:
  0.0 19.5 %copy-start.2 = (f32[16,16,128]{2,1,0:T(8,128)S(1)}, f32[16,16,128]{2,1,0:T(8,128)}, u32[]{:S(2)}) copy-start(f32[16,16,128]{2,1,0:T(8,128)} %refs_2_.3) | copy-start | bytes 393220
  0.0 19.5 %copy-start.3 = (f32[16,16,128]{2,1,0:T(8,128)S(1)}, f32[16,16,128]{2,1,0:T(8,128)}, u32[]{:S(2)}) copy-start(f32[16,16,128]{2,1,0:T(8,128)} %refs_3_.3) | copy-start | bytes 393220
  0.0 19.5 %copy-start.4 = (f32[16,16,128]{2,1,0:T(8,128)S(1)}, f32[16,16,128]{2,1,0:T(8,128)}, u32[]{:S(2)}) copy-start(f32[16,16,128]{2,1,0:T(8,128)} %refs_4_.3) | copy-start | bytes 393220
  0.0 19.5 %copy-start.5 = (f32[16,16,128]{2,1,0:T(8,128)S(1)}, f32[16,16,128]{2,1,0:T(8,128)}, u32[]{:S(2)}) copy-start(f32[16,16,128]{2,1,0:T(8,128)} %refs_5_.3) | copy-start | bytes 393220
  2.6 12.2 %collective-permute-start.4 = (f32[6,4,16,128]{3,2,1,0:T(8,128)}, f32[6,4,16,128]{3,2,1,0:T(8,128)S(1)}, u32[]{:S(2)}, u32[]{:S(2)}) collective-permute-start(f32[6,4,16,128]{3,2,1,0:T(8,128)} %get-tuple-element.53), channel_id=1, source_target_pairs={{0,16},{16,0},{1,17},{17,1},{2,18},{18,2},{3,19},{19,3},{4,20},{20... | collective-permute-start | bytes 589832 | tf_op jit(solution)/shard_map/ppermute | solution.py:739
  4.7 15.8 %collective-permute-start.5 = (f32[6,16,4,128]{3,2,1,0:T(4,128)}, f32[6,16,4,128]{3,2,1,0:T(4,128)S(1)}, u32[]{:S(2)}, u32[]{:S(2)}) collective-permute-start(f32[6,16,4,128]{3,2,1,0:T(4,128)} %get-tuple-element.67), channel_id=1, source_target_pairs={{0,12},{4,8},{8,4},{12,0},{1,13},{5,9},{9,5},{13,1},{2,14},{6,10},... | collective-permute-start | bytes 589832 | tf_op jit(solution)/shard_map/ppermute | solution.py:739
  6.7 13.7 %collective-permute-start.6 = (f32[6,16,4,128]{3,2,1,0:T(4,128)}, f32[6,16,4,128]{3,2,1,0:T(4,128)S(1)}, u32[]{:S(2)}, u32[]{:S(2)}) collective-permute-start(f32[6,16,4,128]{3,2,1,0:T(4,128)} %get-tuple-element.68), channel_id=1, source_target_pairs={{0,4},{4,0},{8,12},{12,8},{1,5},{5,1},{9,13},{13,9},{2,6},{6,2},{1... | collective-permute-start | bytes 589832 | tf_op jit(solution)/shard_map/ppermute | solution.py:739
  6.7 3.7 %collective-permute-start.2 = (f32[2,16,128]{2,1,0:T(8,128)}, f32[2,16,128]{2,1,0:T(8,128)S(1)}, u32[]{:S(2)}, u32[]{:S(2)}) collective-permute-start(f32[2,16,128]{2,1,0:T(8,128)} %get-tuple-element.51), channel_id=1, source_target_pairs={{0,17},{1,16},{2,19},{3,18},{16,1},{17,0},{18,3},{19,2},{4,21},{5,... | collective-permute-start | bytes 49160 | tf_op jit(solution)/shard_map/ppermute | solution.py:762
  8.0 3.7 %collective-permute-start.3 = (f32[2,16,128]{2,1,0:T(8,128)}, f32[2,16,128]{2,1,0:T(8,128)S(1)}, u32[]{:S(2)}, u32[]{:S(2)}) collective-permute-start(f32[2,16,128]{2,1,0:T(8,128)} %get-tuple-element.52), channel_id=1, source_target_pairs={{0,16},{1,18},{2,17},{3,19},{16,0},{17,2},{18,1},{19,3},{4,20},{5,... | collective-permute-start | bytes 49160 | tf_op jit(solution)/shard_map/ppermute | solution.py:762
  10.4 3.3 %collective-permute-start = (f32[8,16,128]{2,1,0:T(8,128)}, f32[8,16,128]{2,1,0:T(8,128)S(1)}, u32[]{:S(2)}, u32[]{:S(2)}) collective-permute-start(f32[8,16,128]{2,1,0:T(8,128)} %get-tuple-element.49), channel_id=1, source_target_pairs={{0,1},{1,0},{2,3},{3,2},{4,5},{5,4},{6,7},{7,6},{8,9},{9,8},{10,11... | collective-permute-start | bytes 196616 | tf_op jit(solution)/shard_map/ppermute | solution.py:739
  11.8 7.7 %copy-start = (f32[16,16,128]{2,1,0:T(8,128)S(1)}, f32[16,16,128]{2,1,0:T(8,128)}, u32[]{:S(2)}) copy-start(f32[16,16,128]{2,1,0:T(8,128)} %refs_0_.3) | copy-start | bytes 393220
  11.8 7.8 %copy-start.1 = (f32[16,16,128]{2,1,0:T(8,128)S(1)}, f32[16,16,128]{2,1,0:T(8,128)}, u32[]{:S(2)}) copy-start(f32[16,16,128]{2,1,0:T(8,128)} %refs_1_.3) | copy-start | bytes 393220
  11.8 3.0 %collective-permute-start.1 = (f32[8,16,128]{2,1,0:T(8,128)}, f32[8,16,128]{2,1,0:T(8,128)S(1)}, u32[]{:S(2)}, u32[]{:S(2)}) collective-permute-start(f32[8,16,128]{2,1,0:T(8,128)} %get-tuple-element.50), channel_id=1, source_target_pairs={{0,4},{1,2},{2,1},{3,7},{4,0},{5,6},{6,5},{7,3},{8,12},{9,10},{10,... | collective-permute-start | bytes 196616 | tf_op jit(solution)/shard_map/ppermute | solution.py:750
  14.9 5.5 %collective-permute-start.7 = (f32[37,4,128]{2,1,0:T(4,128)S(1)}, f32[37,4,128]{2,1,0:T(4,128)S(1)}, u32[]{:S(2)}, u32[]{:S(2)}) collective-permute-start(f32[37,4,128]{2,1,0:T(4,128)S(1)} %get-tuple-element.69), channel_id=1, source_target_pairs={{0,1},{4,8},{8,4},{12,13},{1,0},{5,9},{9,5},{13,12},{2,3},{6,10},{... | collective-permute-start | bytes 227336 | tf_op jit(solution)/shard_map/ppermute | solution.py:750
  17.0 3.5 %collective-permute-start.8 = (f32[37,4,128]{2,1,0:T(4,128)S(1)}, f32[37,4,128]{2,1,0:T(4,128)S(1)}, u32[]{:S(2)}, u32[]{:S(2)}) collective-permute-start(f32[37,4,128]{2,1,0:T(4,128)S(1)} %get-tuple-element.70), channel_id=1, source_target_pairs={{0,4},{4,0},{8,12},{12,8},{1,5},{5,1},{9,13},{13,9},{2,6},{6,2},{1... | collective-permute-start | bytes 227336 | tf_op jit(solution)/shard_map/ppermute | solution.py:739
  23.8 9.1 %collective-permute-start.9 = (f32[3,4,8,128]{3,2,1,0:T(8,128)S(1)}, f32[3,4,8,128]{3,2,1,0:T(8,128)S(1)}, u32[]{:S(2)}, u32[]{:S(2)}) collective-permute-start(f32[3,4,8,128]{3,2,1,0:T(8,128)S(1)} %get-tuple-element.73), channel_id=1, source_target_pairs={{0,16},{16,0},{1,17},{17,1},{2,18},{18,2},{3,19},{19,3},{4,20},{20... | collective-permute-start | bytes 147464 | tf_op jit(solution)/shard_map/ppermute | solution.py:739
  25.0 7.9 %collective-permute-start.10 = (f32[3,8,4,128]{3,2,1,0:T(4,128)S(1)}, f32[3,8,4,128]{3,2,1,0:T(4,128)S(1)}, u32[]{:S(2)}, u32[]{:S(2)}) collective-permute-start(f32[3,8,4,128]{3,2,1,0:T(4,128)S(1)} %get-tuple-element.74), channel_id=1, source_target_pairs={{0,1},{4,8},{8,4},{12,13},{1,0},{5,9},{9,5},{13,12},{2,3},{6,10},{... | collective-permute-start | bytes 147464 | tf_op jit(solution)/shard_map/ppermute | solution.py:750
  25.0 7.9 %collective-permute-start.11 = (f32[3,8,4,128]{3,2,1,0:T(4,128)S(1)}, f32[3,8,4,128]{3,2,1,0:T(4,128)S(1)}, u32[]{:S(2)}, u32[]{:S(2)}) collective-permute-start(f32[3,8,4,128]{3,2,1,0:T(4,128)S(1)} %get-tuple-element.75), channel_id=1, source_target_pairs={{0,4},{4,0},{8,12},{12,8},{1,5},{5,1},{9,13},{13,9},{2,6},{6,2},{1... | collective-permute-start | bytes 147464 | tf_op jit(solution)/shard_map/ppermute | solution.py:739
  28.6 3.2 %collective-permute-start.12 = (f32[9,4,128]{2,1,0:T(4,128)S(1)}, f32[9,4,128]{2,1,0:T(4,128)S(1)}, u32[]{:S(2)}, u32[]{:S(2)}) collective-permute-start(f32[9,4,128]{2,1,0:T(4,128)S(1)} %get-tuple-element.76), channel_id=1, source_target_pairs={{0,20},{4,16},{8,28},{12,24},{16,4},{20,0},{24,12},{28,8},{1,21},{... | collective-permute-start | bytes 55304 | tf_op jit(solution)/shard_map/ppermute | solution.py:762
  28.8 4.1 %collective-permute-start.13 = (f32[9,4,128]{2,1,0:T(4,128)S(1)}, f32[9,4,128]{2,1,0:T(4,128)S(1)}, u32[]{:S(2)}, u32[]{:S(2)}) collective-permute-start(f32[9,4,128]{2,1,0:T(4,128)S(1)} %get-tuple-element.77), channel_id=1, source_target_pairs={{0,16},{4,24},{8,20},{12,28},{16,0},{20,8},{24,4},{28,12},{1,17},{... | collective-permute-start | bytes 55304 | tf_op jit(solution)/shard_map/ppermute | solution.py:762

commit v14 on v12

--- a/solution.py
+++ b/solution.py
@@ -189,18 +189,16 @@
 
 def faces_kernel(counts, where_ref, *refs):
     ins, refs = refs[:6], refs[6:]
-    n_x = 1 if counts[0] == 2 else 2
-    sends_x, (two_y, one_y, first, second) = refs[:n_x], refs[n_x:]
-    odd_x, odd_y, odd = (place % 2 for place in position(where_ref))
+    sends_x, (first, second) = refs[:-2], refs[-2:]
+    odd_x, _, odd = (place % 2 for place in position(where_ref))
     sx, sy, sz = ins[0].shape
     half = sx // 2
     lane = lane_of((half, sy, LANES))
     head = jnp.zeros((half, sy, LANES), F32)
     tail = head
     for a, ref in enumerate(ins):
-        for send, face in zip(sends_x, faces_x(ref[...][None], odd_x, n_x, HALO)):
+        for send, face in zip(sends_x, faces_x(ref[...][None], odd_x, len(sends_x), HALO)):
             send[a] = face[0]
-        one_y[a], two_y[a] = faces_y(ref[...], odd_y, HALO)
         for g in range(2):
             values = ref[g * half:(g + 1) * half]
             at = SIDE * g + PLACE[a]
@@ -304,9 +302,10 @@
     ins, refs = refs[:7], refs[7:]
     n_x = 1 if counts[0] == 2 else 2
     main_x, refs = refs[:n_x], refs[n_x:]
+    two_y, one_y, refs = refs[0], refs[1], refs[2:]
     arrays, (coarse2, coeffs1, sums, pairing) = refs[:12], refs[12:]
     sx, sy, sz = ins[0].shape
-    at_x = position(where_ref)[0]
+    at_x, at_y, _ = position(where_ref)
     x1, y1 = sx // 2, sy // 2
     lane = lane_of((sx, sy, LANES))
     lanes = [slice(k * LANES, (k + 1) * LANES) for k in range(2)]
@@ -318,6 +317,7 @@
         to[mine, :sy] = ins[a][...]
         to[HALO + sx:, :sy] = above
         arrays[2 * a + 1][mine, :sy] = unpacked(ins[6][...], a, lane)
+        one_y[a], two_y[a] = faces_y(ins[a][...], at_y % 2, HALO)
     for n, (firsts, seconds) in enumerate(((BOTH, BOTH), (ODD, BOTH), (BOTH, ODD), (BOTH, BOTH))):
         for k in range(2):
             for i in range(x1):
@@ -737,17 +737,14 @@
     ex, ey = sx + 2 * HALO, sy + 2 * HALO
     fine = (ex, ey, LANES)
 
-    *sends_x, two_y, one_y, first, second = run(
+    *sends_x, first, second = run(
         functools.partial(faces_kernel, counts),
-        [(6, HALO, sy, LANES)] * n_x
-        + [(6, sx, HALO, LANES)] * 2
-        + [(sx // 2, sy, LANES)] * 2,
+        [(6, HALO, sy, LANES)] * n_x + [(sx // 2, sy, LANES)] * 2,
         where,
         ins,
         grant=60,
     )
     main_x = tuple(swaps("gx", sends_x, "gy"))
-    main_y = tuple(swaps("gy", (one_y, two_y))[::-1])
     got = swaps("gz", (first, second), "gy")
     zpack, *sends = run(
         functools.partial(halo_z_kernel, counts),
@@ -757,14 +754,15 @@
     )
     halos_x = tuple(swaps("gx", sends, "gy"))
     x1, y1 = sx // 2, sy // 2
-    *laid, coarse2, coeffs1 = run(
+    two_y, one_y, *laid, coarse2, coeffs1 = run(
         functools.partial(coefficient_kernel, counts),
-        [fine] * 12 + [(4, y1 // 2, LANES), (5, x1, y1, LANES)],
+        [(6, sx, HALO, LANES)] * 2 + [fine] * 12 + [(4, y1 // 2, LANES), (5, x1, y1, LANES)],
         where,
         ins + (zpack,) + main_x,
         [(4, x1, y1, 2 * LANES), (4, x1, y1, LANES)],
         micros=2,
     )
+    main_y = tuple(swaps("gy", (one_y, two_y), "gz")[::-1])
     two_y, one_y = run(
         functools.partial(corners_kernel, counts),
         [(21 + sx, HALO, LANES)] * 2,

time: 52.7 us -> 53.6 us (1.017)
  waiting for transfers between devices: 8.37 us -> 10.3 us
  starting transfers between devices: 17 us -> 15.9 us
    ppermute x8 -> x7, starting transfers between devices: 12.2 us -> 10.4 us  [swaps(): got.append(lax.ppermute(block, axis, list(enumerate(partner))))]
    ppermute x3 -> x4, waiting for transfers between devices: 0.01 us -> 1.63 us  [swaps(): got.append(lax.ppermute(block, tuple(sorted((axis, other))), pairs))]
    ppermute x3 -> x4, starting transfers between devices: 3.68 us -> 4.98 us  [swaps(): got.append(lax.ppermute(block, tuple(sorted((axis, other))), pairs))]
    ppermute x2, starting transfers between devices: 1.1 us -> 0.53 us  [diagonal_swaps(): got.append(lax.ppermute(block, ('gx', 'gy'), pairs))]
    ppermute x8 -> x7, waiting for transfers between devices: 4.15 us -> 4.41 us  [swaps(): got.append(lax.ppermute(block, axis, list(enumerate(partner))))]
  transfers between devices with their start and end apart: 13 -> 13, of which waited for: 5 -> 6; matrix products, arithmetic and copies ran while one was open for 0% -> 0% of each run, Pallas kernels for 2% -> 0%
where the time goes in v14:
time: 53.6 us; the launch traced here: 53.5 us
  starting transfers between devices  15.9 us (30%)
  blocking collectives  14.8 us (28%)
  Pallas kernels  12.4 us (23%)
  waiting for transfers between devices  10.3 us (19%)
    all_to_all x1, blocking collectives, local(): gathered = lax.all_to_all(copies, axes, 0, 0, tiled=True)  14.8 us
    pallas_call x7, Pallas kernels, run(): pl.pallas_call(kernel, out_shape=tuple((jax.ShapeDtypeStruct(shape, F32)...  12.4 us
    ppermute x7, starting transfers between devices, swaps(): got.append(lax.ppermute(block, axis, list(enumerate(partner))))  10.4 us
    ppermute x4, starting transfers between devices, swaps(): got.append(lax.ppermute(block, tuple(sorted((axis, other))), pairs))  4.98 us
    ppermute x7, waiting for transfers between devices, swaps(): got.append(lax.ppermute(block, axis, list(enumerate(partner))))  4.41 us
    ppermute x2, waiting for transfers between devices, diagonal_swaps(): got.append(lax.ppermute(block, ('gx', 'gy'), pairs))  4.21 us
    ppermute x4, waiting for transfers between devices, swaps(): got.append(lax.ppermute(block, tuple(sorted((axis, other))), pairs))  1.63 us
  transfers between devices with their start and end apart: 13, of which 6 were waited for; matrix products, arithmetic and copies ran while one was open for 0% of the time, Pallas kernels for 0%

profile of v14, /device:TPU:1, one launch (start us, length us, event | category | flops | bytes accessed | tf_op | source)
XLA Modules:
  0.0 53.5 jit_solution(13491674962973235630)
XLA Ops:
  0.0 2.4 %shard_map.64 = (f32[6,4,16,128]{3,2,1,0:T(8,128)}, f32[8,16,128]{2,1,0:T(8,128)}, f32[8,16,128]{2,1,0:T(8,128)}) custom-call(s32[1]{0:T(128)} %bitcast.where_ref, f32[16,16,128]{2,1,0:T(8,128)} %refs_0_.3, f32[16,16,128]{2,1,0:T(8,128)} %refs_1_.3, f32[16,16,128]{2,1,0:T(8,128)} %refs_2_.3, f32[16,16,128]{2,1,0:T(8,128)} %refs_3_.3, ...), custom_call_target="tpu_custom_call" | custom-call | bytes 3600000 | tf_op jit(solution)/shard_map/pallas_call | solution.py:670
  2.4 2.0 %collective-permute-start.2 = (f32[6,4,16,128]{3,2,1,0:T(8,128)}, f32[6,4,16,128]{3,2,1,0:T(8,128)S(1)}, u32[]{:S(2)}, u32[]{:S(2)}) collective-permute-start(f32[6,4,16,128]{3,2,1,0:T(8,128)} %get-tuple-element.51), channel_id=1, source_target_pairs={{0,16},{16,0},{1,17},{17,1},{2,18},{18,2},{3,19},{19,3},{4,20},{20... | collective-permute-start | bytes 589832 | tf_op jit(solution)/shard_map/ppermute | solution.py:699
  4.5 1.3 %collective-permute-start = (f32[8,16,128]{2,1,0:T(8,128)}, f32[8,16,128]{2,1,0:T(8,128)S(1)}, u32[]{:S(2)}, u32[]{:S(2)}) collective-permute-start(f32[8,16,128]{2,1,0:T(8,128)} %get-tuple-element.48), channel_id=1, source_target_pairs={{0,1},{1,0},{2,3},{3,2},{4,5},{5,4},{6,7},{7,6},{8,9},{9,8},{10,11... | collective-permute-start | bytes 196616 | tf_op jit(solution)/shard_map/ppermute | solution.py:699
  5.8 1.2 %collective-permute-start.1 = (f32[8,16,128]{2,1,0:T(8,128)}, f32[8,16,128]{2,1,0:T(8,128)S(1)}, u32[]{:S(2)}, u32[]{:S(2)}) collective-permute-start(f32[8,16,128]{2,1,0:T(8,128)} %get-tuple-element.49), channel_id=1, source_target_pairs={{0,4},{1,2},{2,1},{3,7},{4,0},{5,6},{6,5},{7,3},{8,12},{9,10},{10,... | collective-permute-start | bytes 196616 | tf_op jit(solution)/shard_map/ppermute | solution.py:710
  7.0 1.1 %collective-permute-done.one_ref = f32[8,16,128]{2,1,0:T(8,128)S(1)} collective-permute-done((f32[8,16,128]{2,1,0:T(8,128)}, f32[8,16,128]{2,1,0:T(8,128)S(1)}, u32[]{:S(2)}, u32[]{:S(2)}) %collective-permute-start) | collective-permute-done | bytes 65568 | tf_op jit(solution)/shard_map/ppermute | solution.py:699
  8.1 0.0 collective-permute-done.1.two_ref
  8.1 0.1 shard_map.65
  8.2 1.1 %collective-permute-done.2.refs_7_.refs_0_ = f32[6,4,16,128]{3,2,1,0:T(8,128)S(1)} collective-permute-done((f32[6,4,16,128]{3,2,1,0:T(8,128)}, f32[6,4,16,128]{3,2,1,0:T(8,128)S(1)}, u32[]{:S(2)}, u32[]{:S(2)}) %collective-permute-start.2) | collective-permute-done | bytes 196640 | tf_op jit(solution)/shard_map/ppermute | solution.py:699
  9.3 0.8 %shard_map.66 = (f32[6,16,4,128]{3,2,1,0:T(4,128)S(1)}, f32[6,16,4,128]{3,2,1,0:T(4,128)S(1)}, f32[24,24,128]{2,1,0:T(8,128)S(1)}, f32[24,24,128]{2,1,0:T(8,128)...) custom-call(s32[1]{0:T(128)} %bitcast.where_ref, ...), custom_call_target="tpu_custom_call" | custom-call | bytes 7200000 | tf_op jit(solution)/shard_map/pallas_call | solution.py:670
  10.1 2.6 %collective-permute-start.4 = (f32[6,16,4,128]{3,2,1,0:T(4,128)S(1)}, f32[6,16,4,128]{3,2,1,0:T(4,128)S(1)}, u32[]{:S(2)}, u32[]{:S(2)}) collective-permute-start(f32[6,16,4,128]{3,2,1,0:T(4,128)S(1)} %get-tuple-element.65), channel_id=1, source_target_pairs={{0,1},{4,8},{8,4},{12,13},{1,0},{5,9},{9,5},{13,12},{2,3},{6,10},{... | collective-permute-start | bytes 589832 | tf_op jit(solution)/shard_map/ppermute | solution.py:710
  12.8 0.8 %collective-permute-start.5 = (f32[6,16,4,128]{3,2,1,0:T(4,128)S(1)}, f32[6,16,4,128]{3,2,1,0:T(4,128)S(1)}, u32[]{:S(2)}, u32[]{:S(2)}) collective-permute-start(f32[6,16,4,128]{3,2,1,0:T(4,128)S(1)} %get-tuple-element.66), channel_id=1, source_target_pairs={{0,4},{4,0},{8,12},{12,8},{1,5},{5,1},{9,13},{13,9},{2,6},{6,2},{1... | collective-permute-start | bytes 589832 | tf_op jit(solution)/shard_map/ppermute | solution.py:699
  13.6 0.8 %collective-permute-start.3 = (f32[4,16,128]{2,1,0:T(8,128)S(1)}, f32[4,16,128]{2,1,0:T(8,128)S(1)}, u32[]{:S(2)}, u32[]{:S(2)}) collective-permute-start(f32[4,16,128]{2,1,0:T(8,128)S(1)} %get-tuple-element.64), channel_id=1, source_target_pairs={{0,16},{16,0},{1,17},{17,1},{2,18},{18,2},{3,19},{19,3},{4,20},{20... | collective-permute-start | bytes 98312 | tf_op jit(solution)/shard_map/ppermute | solution.py:699
  14.4 2.2 %collective-permute-done.3.refs_1_.refs_12_ = f32[4,16,128]{2,1,0:T(8,128)S(1)} collective-permute-done((f32[4,16,128]{2,1,0:T(8,128)S(1)}, f32[4,16,128]{2,1,0:T(8,128)S(1)}, u32[]{:S(2)}, u32[]{:S(2)}) %collective-permute-start.3) | collective-permute-done | bytes 32800 | tf_op jit(solution)/shard_map/ppermute | solution.py:699
  16.7 0.1 shard_map.67
  16.7 0.5 collective-permute-start.6
  17.2 2.1 %collective-permute-start.7 = (f32[37,4,128]{2,1,0:T(4,128)S(1)}, f32[37,4,128]{2,1,0:T(4,128)S(1)}, u32[]{:S(2)}, u32[]{:S(2)}) collective-permute-start(f32[37,4,128]{2,1,0:T(4,128)S(1)} %get-tuple-element.69), channel_id=1, source_target_pairs={{0,4},{4,0},{8,12},{12,8},{1,5},{5,1},{9,13},{13,9},{2,6},{6,2},{1... | collective-permute-start | bytes 227336 | tf_op jit(solution)/shard_map/ppermute | solution.py:699
  19.3 1.6 %collective-permute-done.6.refs_15_ = f32[37,4,128]{2,1,0:T(4,128)S(1)} collective-permute-done((f32[37,4,128]{2,1,0:T(4,128)S(1)}, f32[37,4,128]{2,1,0:T(4,128)S(1)}, u32[]{:S(2)}, u32[]{:S(2)}) %collective-permute-start.6) | collective-permute-done | bytes 75808 | tf_op jit(solution)/shard_map/ppermute | solution.py:710
  20.9 0.0 collective-permute-done.7.refs_16_
  20.9 0.0 collective-permute-done.4.refs_13_
  20.9 0.0 collective-permute-done.5.refs_14_
  20.9 3.5 %shard_map.68 = (f32[24,24,128]{2,1,0:T(8,128)S(1)}, f32[24,24,128]{2,1,0:T(8,128)S(1)}, f32[24,24,128]{2,1,0:T(8,128)S(1)}, f32[24,24,128]{2,1,0:T(8,128)S(1)},...) custom-call(s32[1]{0:T(128)} %bitcast.where_ref, ...), custom_call_target="tpu_custom_call", output_to_operand_aliasing={{0}: (2, {}), {1}: (3, {}), {2}: (4, {}), {3}: (5, {}), {4}... | custom-call | bytes 14400000 | tf_op jit(solution)/shard_map/pallas_call | solution.py:670
  24.4 0.9 %collective-permute-start.8 = (f32[5,4,8,128]{3,2,1,0:T(8,128)S(1)}, f32[5,4,8,128]{3,2,1,0:T(8,128)S(1)}, u32[]{:S(2)}, u32[]{:S(2)}) collective-permute-start(f32[5,4,8,128]{3,2,1,0:T(8,128)S(1)} %get-tuple-element.72), channel_id=1, source_target_pairs={{0,16},{16,0},{1,17},{17,1},{2,18},{18,2},{3,19},{19,3},{4,20},{20... | collective-permute-start | bytes 245768 | tf_op jit(solution)/shard_map/ppermute | solution.py:699
  25.3 0.6 %collective-permute-start.9 = (f32[5,8,4,128]{3,2,1,0:T(4,128)S(1)}, f32[5,8,4,128]{3,2,1,0:T(4,128)S(1)}, u32[]{:S(2)}, u32[]{:S(2)}) collective-permute-start(f32[5,8,4,128]{3,2,1,0:T(4,128)S(1)} %get-tuple-element.73), channel_id=1, source_target_pairs={{0,1},{4,8},{8,4},{12,13},{1,0},{5,9},{9,5},{13,12},{2,3},{6,10},{... | collective-permute-start | bytes 245768 | tf_op jit(solution)/shard_map/ppermute | solution.py:710
  25.9 2.4 %collective-permute-start.10 = (f32[5,8,4,128]{3,2,1,0:T(4,128)S(1)}, f32[5,8,4,128]{3,2,1,0:T(4,128)S(1)}, u32[]{:S(2)}, u32[]{:S(2)}) collective-permute-start(f32[5,8,4,128]{3,2,1,0:T(4,128)S(1)} %get-tuple-element.74), channel_id=1, source_target_pairs={{0,4},{4,0},{8,12},{12,8},{1,5},{5,1},{9,13},{13,9},{2,6},{6,2},{1... | collective-permute-start | bytes 245768 | tf_op jit(solution)/shard_map/ppermute | solution.py:699
  28.3 0.5 collective-permute-start.11
  28.9 0.0 collective-permute-start.12
  28.9 2.8 %collective-permute-done.11.refs_3_ = f32[15,4,128]{2,1,0:T(4,128)S(1)} collective-permute-done((f32[15,4,128]{2,1,0:T(4,128)S(1)}, f32[15,4,128]{2,1,0:T(4,128)S(1)}, u32[]{:S(2)}, u32[]{:S(2)}) %collective-permute-start.11) | collective-permute-done | bytes 30752 | tf_op jit(solution)/shard_map/ppermute | solution.py:724
  31.7 1.4 %collective-permute-done.12.refs_4_ = f32[15,4,128]{2,1,0:T(4,128)S(1)} collective-permute-done((f32[15,4,128]{2,1,0:T(4,128)S(1)}, f32[15,4,128]{2,1,0:T(4,128)S(1)}, u32[]{:S(2)}, u32[]{:S(2)}) %collective-permute-start.12) | collective-permute-done | bytes 30752 | tf_op jit(solution)/shard_map/ppermute | solution.py:724
  33.1 0.0 collective-permute-done.8.refs_0_
  33.1 0.4 shard_map.69
  33.5 14.8 %all_to_all.5.gathered = f32[32,5,4,128]{3,2,1,0:T(4,128)S(1)} all-to-all(f32[32,5,4,128]{3,2,1,0:T(4,128)S(1)} %get-tuple-element.77), channel_id=1, replica_groups=mesh['gx'=2,'gy'=4,'gz'=4] {'gx','gy','gz'}, dimensions={0} | all-to-all | bytes 655360 | tf_op jit(solution)/shard_map/all_to_all | solution.py:804
  48.3 5.1 %shard_map.70 = f32[16,16,128]{2,1,0:T(8,128)} custom-call(s32[1]{0:T(128)} %bitcast.where_ref, f32[32,5,4,128]{3,2,1,0:T(4,128)S(1)} %all_to_all.5.gathered, f32[6,16,16,128]{3,2,1,0:T(8,128)S(1)} %get-tuple-element.78.level1, f32[24,24,128]{2,1,0:T(8,128)S(1)} %get-tuple-element.79.refs_0_, f32[24,24,128]{2,1,0:T(8,128)S(1)} %get-tuple-element.80.refs_1_, ...), custom_call_target="tpu_custom_call" | custom-call | bytes 14400000 | tf_op jit(solution)/shard_map/pallas_call | solution.py:670
  (14 shorter events, 0.0 us)
Async XLA Ops:
  0.0 9.3 %copy-start.1 = (f32[16,16,128]{2,1,0:T(8,128)S(1)}, f32[16,16,128]{2,1,0:T(8,128)}, u32[]{:S(2)}) copy-start(f32[16,16,128]{2,1,0:T(8,128)} %refs_1_.3) | copy-start | bytes 393220
  0.0 9.3 %copy-start.2 = (f32[16,16,128]{2,1,0:T(8,128)S(1)}, f32[16,16,128]{2,1,0:T(8,128)}, u32[]{:S(2)}) copy-start(f32[16,16,128]{2,1,0:T(8,128)} %refs_2_.3) | copy-start | bytes 393220
  0.0 9.3 %copy-start.3 = (f32[16,16,128]{2,1,0:T(8,128)S(1)}, f32[16,16,128]{2,1,0:T(8,128)}, u32[]{:S(2)}) copy-start(f32[16,16,128]{2,1,0:T(8,128)} %refs_3_.3) | copy-start | bytes 393220
  0.0 9.3 %copy-start.4 = (f32[16,16,128]{2,1,0:T(8,128)S(1)}, f32[16,16,128]{2,1,0:T(8,128)}, u32[]{:S(2)}) copy-start(f32[16,16,128]{2,1,0:T(8,128)} %refs_4_.3) | copy-start | bytes 393220
  0.0 9.3 %copy-start.5 = (f32[16,16,128]{2,1,0:T(8,128)S(1)}, f32[16,16,128]{2,1,0:T(8,128)}, u32[]{:S(2)}) copy-start(f32[16,16,128]{2,1,0:T(8,128)} %refs_5_.3) | copy-start | bytes 393220
  2.4 6.9 %copy-start = (f32[16,16,128]{2,1,0:T(8,128)S(1)}, f32[16,16,128]{2,1,0:T(8,128)}, u32[]{:S(2)}) copy-start(f32[16,16,128]{2,1,0:T(8,128)} %refs_0_.3) | copy-start | bytes 393220
  2.4 6.9 %collective-permute-start.2 = (f32[6,4,16,128]{3,2,1,0:T(8,128)}, f32[6,4,16,128]{3,2,1,0:T(8,128)S(1)}, u32[]{:S(2)}, u32[]{:S(2)}) collective-permute-start(f32[6,4,16,128]{3,2,1,0:T(8,128)} %get-tuple-element.51), channel_id=1, source_target_pairs={{0,16},{16,0},{1,17},{17,1},{2,18},{18,2},{3,19},{19,3},{4,20},{20... | collective-permute-start | bytes 589832 | tf_op jit(solution)/shard_map/ppermute | solution.py:699
  4.5 3.6 %collective-permute-start = (f32[8,16,128]{2,1,0:T(8,128)}, f32[8,16,128]{2,1,0:T(8,128)S(1)}, u32[]{:S(2)}, u32[]{:S(2)}) collective-permute-start(f32[8,16,128]{2,1,0:T(8,128)} %get-tuple-element.48), channel_id=1, source_target_pairs={{0,1},{1,0},{2,3},{3,2},{4,5},{5,4},{6,7},{7,6},{8,9},{9,8},{10,11... | collective-permute-start | bytes 196616 | tf_op jit(solution)/shard_map/ppermute | solution.py:699
  5.8 2.3 %collective-permute-start.1 = (f32[8,16,128]{2,1,0:T(8,128)}, f32[8,16,128]{2,1,0:T(8,128)S(1)}, u32[]{:S(2)}, u32[]{:S(2)}) collective-permute-start(f32[8,16,128]{2,1,0:T(8,128)} %get-tuple-element.49), channel_id=1, source_target_pairs={{0,4},{1,2},{2,1},{3,7},{4,0},{5,6},{6,5},{7,3},{8,12},{9,10},{10,... | collective-permute-start | bytes 196616 | tf_op jit(solution)/shard_map/ppermute | solution.py:710
  10.1 10.8 %collective-permute-start.4 = (f32[6,16,4,128]{3,2,1,0:T(4,128)S(1)}, f32[6,16,4,128]{3,2,1,0:T(4,128)S(1)}, u32[]{:S(2)}, u32[]{:S(2)}) collective-permute-start(f32[6,16,4,128]{3,2,1,0:T(4,128)S(1)} %get-tuple-element.65), channel_id=1, source_target_pairs={{0,1},{4,8},{8,4},{12,13},{1,0},{5,9},{9,5},{13,12},{2,3},{6,10},{... | collective-permute-start | bytes 589832 | tf_op jit(solution)/shard_map/ppermute | solution.py:710
  12.8 8.1 %collective-permute-start.5 = (f32[6,16,4,128]{3,2,1,0:T(4,128)S(1)}, f32[6,16,4,128]{3,2,1,0:T(4,128)S(1)}, u32[]{:S(2)}, u32[]{:S(2)}) collective-permute-start(f32[6,16,4,128]{3,2,1,0:T(4,128)S(1)} %get-tuple-element.66), channel_id=1, source_target_pairs={{0,4},{4,0},{8,12},{12,8},{1,5},{5,1},{9,13},{13,9},{2,6},{6,2},{1... | collective-permute-start | bytes 589832 | tf_op jit(solution)/shard_map/ppermute | solution.py:699
  13.6 3.1 %collective-permute-start.3 = (f32[4,16,128]{2,1,0:T(8,128)S(1)}, f32[4,16,128]{2,1,0:T(8,128)S(1)}, u32[]{:S(2)}, u32[]{:S(2)}) collective-permute-start(f32[4,16,128]{2,1,0:T(8,128)S(1)} %get-tuple-element.64), channel_id=1, source_target_pairs={{0,16},{16,0},{1,17},{17,1},{2,18},{18,2},{3,19},{19,3},{4,20},{20... | collective-permute-start | bytes 98312 | tf_op jit(solution)/shard_map/ppermute | solution.py:699
  16.7 4.2 %collective-permute-start.6 = (f32[37,4,128]{2,1,0:T(4,128)S(1)}, f32[37,4,128]{2,1,0:T(4,128)S(1)}, u32[]{:S(2)}, u32[]{:S(2)}) collective-permute-start(f32[37,4,128]{2,1,0:T(4,128)S(1)} %get-tuple-element.68), channel_id=1, source_target_pairs={{0,1},{4,8},{8,4},{12,13},{1,0},{5,9},{9,5},{13,12},{2,3},{6,10},{... | collective-permute-start | bytes 227336 | tf_op jit(solution)/shard_map/ppermute | solution.py:710
  17.2 3.7 %collective-permute-start.7 = (f32[37,4,128]{2,1,0:T(4,128)S(1)}, f32[37,4,128]{2,1,0:T(4,128)S(1)}, u32[]{:S(2)}, u32[]{:S(2)}) collective-permute-start(f32[37,4,128]{2,1,0:T(4,128)S(1)} %get-tuple-element.69), channel_id=1, source_target_pairs={{0,4},{4,0},{8,12},{12,8},{1,5},{5,1},{9,13},{13,9},{2,6},{6,2},{1... | collective-permute-start | bytes 227336 | tf_op jit(solution)/shard_map/ppermute | solution.py:699
  24.4 8.7 %collective-permute-start.8 = (f32[5,4,8,128]{3,2,1,0:T(8,128)S(1)}, f32[5,4,8,128]{3,2,1,0:T(8,128)S(1)}, u32[]{:S(2)}, u32[]{:S(2)}) collective-permute-start(f32[5,4,8,128]{3,2,1,0:T(8,128)S(1)} %get-tuple-element.72), channel_id=1, source_target_pairs={{0,16},{16,0},{1,17},{17,1},{2,18},{18,2},{3,19},{19,3},{4,20},{20... | collective-permute-start | bytes 245768 | tf_op jit(solution)/shard_map/ppermute | solution.py:699
  25.3 7.8 %collective-permute-start.9 = (f32[5,8,4,128]{3,2,1,0:T(4,128)S(1)}, f32[5,8,4,128]{3,2,1,0:T(4,128)S(1)}, u32[]{:S(2)}, u32[]{:S(2)}) collective-permute-start(f32[5,8,4,128]{3,2,1,0:T(4,128)S(1)} %get-tuple-element.73), channel_id=1, source_target_pairs={{0,1},{4,8},{8,4},{12,13},{1,0},{5,9},{9,5},{13,12},{2,3},{6,10},{... | collective-permute-start | bytes 245768 | tf_op jit(solution)/shard_map/ppermute | solution.py:710
  25.9 7.2 %collective-permute-start.10 = (f32[5,8,4,128]{3,2,1,0:T(4,128)S(1)}, f32[5,8,4,128]{3,2,1,0:T(4,128)S(1)}, u32[]{:S(2)}, u32[]{:S(2)}) collective-permute-start(f32[5,8,4,128]{3,2,1,0:T(4,128)S(1)} %get-tuple-element.74), channel_id=1, source_target_pairs={{0,4},{4,0},{8,12},{12,8},{1,5},{5,1},{9,13},{13,9},{2,6},{6,2},{1... | collective-permute-start | bytes 245768 | tf_op jit(solution)/shard_map/ppermute | solution.py:699
  28.3 3.3 %collective-permute-start.11 = (f32[15,4,128]{2,1,0:T(4,128)S(1)}, f32[15,4,128]{2,1,0:T(4,128)S(1)}, u32[]{:S(2)}, u32[]{:S(2)}) collective-permute-start(f32[15,4,128]{2,1,0:T(4,128)S(1)} %get-tuple-element.75), channel_id=1, source_target_pairs={{0,20},{4,16},{8,28},{12,24},{16,4},{20,0},{24,12},{28,8},{1,21},{... | collective-permute-start | bytes 92168 | tf_op jit(solution)/shard_map/ppermute | solution.py:724
  28.9 4.2 %collective-permute-start.12 = (f32[15,4,128]{2,1,0:T(4,128)S(1)}, f32[15,4,128]{2,1,0:T(4,128)S(1)}, u32[]{:S(2)}, u32[]{:S(2)}) collective-permute-start(f32[15,4,128]{2,1,0:T(4,128)S(1)} %get-tuple-element.76), channel_id=1, source_target_pairs={{0,16},{4,24},{8,20},{12,28},{16,0},{20,8},{24,4},{28,12},{1,17},{... | collective-permute-start | bytes 92168 | tf_op jit(solution)/shard_map/ppermute | solution.py:724

commit v15 on v12

--- a/solution.py
+++ b/solution.py
@@ -55,10 +55,7 @@
 
 def parts_of(values):
     high = values.astype(jnp.bfloat16)
-    rest = values - high.astype(F32)
-    middle = rest.astype(jnp.bfloat16)
-    low = (rest - middle.astype(F32)).astype(jnp.bfloat16)
-    return high, middle, low
+    return high, (values - high.astype(F32)).astype(jnp.bfloat16)
 
 
 def times_table(values, table):
@@ -410,21 +407,21 @@
             weight[k][x] = w
             halfway[k][x] = KEEP * centre[k] + w * (rhs[k][x] + near[k])
 
-    each(1, ex - 1, 4, first_sweep)
+    each(1, ex - 1, 11, first_sweep)
 
     def second_sweep(x):
         centre, near = pull_slab(halfway, bx, by, bz, x, lane)
         for k in range(2):
             kept[k][x] = KEEP * centre[k] + weight[k][x] * (rhs[k][x] + near[k])
 
-    each(2, ex - 2, 4, second_sweep)
+    each(2, ex - 2, 10, second_sweep)
 
     def residual(x):
         centre, near = pull_slab(kept, bx, by, bz, x, lane)
         for k in range(2):
             halfway[k][x] = rhs[k][x] - diag[k][x] * centre[k] + near[k]
 
-    each(HALO, ex - HALO, 4, residual)
+    each(HALO, ex - HALO, 8, residual)
 
     x1, y1 = sx // 2, sy // 2
     for k in range(2):
@@ -505,10 +502,23 @@
     remain = rhs1[mine] - diag1 * field1[mine] + pull(field1, faces1)[mine]
     left[...] = remain
     packed = level2_rows(left, (False,) * 3, 0.125, bx1 // 2, by1 // 2, LANES // 4)
+    blocks = LANES // (LANES // 4)
+    shift = position(where_ref)[2] % blocks * (LANES // blocks)
+    slots = [pltpu.roll(values, shift, 1) for values in [packed] + [coarse2[a] for a in range(4)]]
     for d in range(devices):
-        copies[d, 0] = packed
-        for a in range(n - 1):
-            copies[d, a + 1] = coarse2[a]
+        for a in range(n):
+            copies[d, a] = slots[a]
+
+
+def inner_sweep(values, rhs, weight, faces, first):
+    part = slice(first, rhs.shape[0] - first)
+    below = slice(first - 1, rhs.shape[0] - first - 1)
+    bx, by, bz = faces
+    centre = values[1:-1]
+    near = bx[part] * values[2:] + bx[below] * values[:-2]
+    near = near + (by[part] * turn(centre, -1, 1) + turn(by[part] * centre, 1, 1))
+    near = near + (bz[part] * turn(centre, -1, 2) + turn(bz[part] * centre, 1, 2))
+    return KEEP * centre + weight[part] * (rhs[part] + near)
 
 
 def halve(values, odd_axis, step):
@@ -537,14 +547,15 @@
         bx, by, bz = faces
         row = lax.broadcasted_iota(jnp.int32, by.shape, 1)
         lane = lane_of(bz.shape)
-        coupled = (
+        upper = (
             bx,
             jnp.where(row == (y - 1) * step, 0.0, by),
             jnp.where(lane == (z - 1) * step, 0.0, bz),
         )
+        lower = (below_x(bx), turn(upper[1], step, 1), turn(upper[2], step, 2))
         mass = jnp.where((row % step == 0) & (lane % step == 0), mass, 0.0)
-        diag = diagonal(mass, faces, coupled, step)
-        levels.append((diag, relaxer(mass, diag), coupled))
+        diag = mass + bx + lower[0] + by + lower[1] + bz + lower[2]
+        levels.append((diag, relaxer(mass, diag), upper, lower))
         if level < LEVELS - 1:
             faces = tuple(0.0625 * halve(face, axis, step) for axis, face in enumerate(faces))
             mass = 0.125 * halve(mass, -1, step)
@@ -552,21 +563,34 @@
     return levels
 
 
+def coupled(values, upper, lower, step):
+    ups = (above_x(values), turn(values, -step, 1), turn(values, -step, 2))
+    downs = (below_x(values), turn(values, step, 1), turn(values, step, 2))
+    x, y, z = (u * up + l * down for u, up, l, down in zip(upper, ups, lower, downs))
+    return (y + z) + x if values.shape[0] > 1 else y + z
+
+
 def coarse_cycle(level, rhs, levels):
     step = 2 ** (level - 2)
-    diag, weight, faces = levels[level - 2]
-    field = weight * rhs
+    diag, weight, upper, lower = levels[level - 2]
+    scaled = tuple(tuple(weight * b for b in faces) for faces in (upper, lower))
+    source = weight * rhs
+
+    def relax(field):
+        return (KEEP * field + source) + coupled(field, *scaled, step)
+
+    field = source
     if level == LEVELS - 1:
         for _ in range(BOTTOM - 1):
-            field = sweep(field, rhs, weight, faces, step)
+            field = relax(field)
         return field
     for _ in range(SWEEPS - 1):
-        field = sweep(field, rhs, weight, faces, step)
-    remain = rhs - diag * field + pull(field, faces, step)
+        field = relax(field)
+    remain = (rhs - diag * field) + coupled(field, upper, lower, step)
     correction = coarse_cycle(level + 1, 0.125 * halve(remain, -1, step), levels)
     field = field + double(correction, step)
     for _ in range(SWEEPS):
-        field = sweep(field, rhs, weight, faces, step)
+        field = relax(field)
     return field
 
 
@@ -580,13 +604,18 @@
         for j in range(gy):
             for x in range(x2):
                 for part in range(whole.shape[2] // LANES):
-                    total = jnp.zeros((y2, LANES), F32)
+                    total = None
                     for k in range(LANES // z2):
                         column = part * (LANES // z2) + k
                         if column < gz:
                             block = slots[(i * gy + j) * gz + column]
-                            mask = (lane >= k * z2) & (lane < (k + 1) * z2)
-                            total = jnp.where(mask, turn(block, (k - x) * z2, 1), total)
+                            at = (x + k) * z2 % LANES
+                            mask = (lane >= at) & (lane < at + z2)
+                            if total is None:
+                                total = jnp.where(mask, block, 0.0)
+                            total = jnp.where(mask, block, total)
+                    if x:
+                        total = turn(total, -x * z2, 1)
                     lanes = slice(part * LANES, (part + 1) * LANES)
                     whole[i * x2 + x, j * y2:(j + 1) * y2, lanes] = total
 
@@ -626,12 +655,12 @@
     lifted = jnp.concatenate([blocks[i // 2] for i in range(ex1)], axis=0)
     field1, rhs1, weight1 = level1[0], level1[1], level1[2]
     faces1 = (level1[3], level1[4], level1[5])
-    field1 = field1 + jnp.where(weight1 > 0.0, lifted, 0.0)
-    for _ in range(SWEEPS):
-        field1 = sweep(field1, rhs1, weight1, faces1)
+    field1 = (field1 + jnp.where(weight1 > 0.0, lifted, 0.0))[1:-1]
+    for n in range(SWEEPS):
+        field1 = inner_sweep(field1, rhs1, weight1, faces1, 2 + n)
 
     ex, ey = sx + 2 * HALO, sy + 2 * HALO
-    near = field1[NEAR - 1:NEAR + x1 + 1].reshape((x1 + 2) * ey1, LANES)
+    near = field1.reshape((x1 + 2) * ey1, LANES)
     row = iota2((LANES, 2 * LANES), 0)
     col = iota2((LANES, 2 * LANES), 1)
     lifted = times_table(near, (col // 2 == row).astype(F32))
@@ -656,14 +685,14 @@
         for k in range(2):
             after[k][x] = KEEP * centre[k] + weight[k][x] * (rhs[k][x] + around[k])
 
-    each(first + 1, ex - first - 1, 4, sweep_out)
+    each(first + 1, ex - first - 1, 9, sweep_out)
 
     def sweep_own(x):
         centre, around = pull_slab(after, bx, by, bz, x, lane)
         value = KEEP * centre[0] + weight[0][x] * (rhs[0][x] + around[0])
         out[x - HALO] = value[:sy]
 
-    each(HALO, ex - HALO, 4, sweep_own)
+    each(HALO, ex - HALO, 8, sweep_own)
 
 
 def run(kernel, outs, where, arrays, scratch=(), grant=16, micros=1, aliases={}):

time: 52.7 us -> 51.5 us (0.977)
  Pallas kernels: 12.5 us -> 11.3 us
    pallas_call x7, Pallas kernels: 12.5 us -> 11.3 us  [run(): pl.pallas_call(kernel, out_shape=tuple((jax.ShapeDtypeStruct(shape, F32)...]
where the time goes in v15:
time: 51.5 us; the launch traced here: 51.4 us
  starting transfers between devices  17 us (33%)
  blocking collectives  14.6 us (28%)
  Pallas kernels  11.3 us (22%)
  waiting for transfers between devices  8.42 us (16%)
    all_to_all x1, blocking collectives, local(): gathered = lax.all_to_all(copies, axes, 0, 0, tiled=True)  14.6 us
    ppermute x8, starting transfers between devices, swaps(): got.append(lax.ppermute(block, axis, list(enumerate(partner))))  12.2 us
    pallas_call x7, Pallas kernels, run(): pl.pallas_call(kernel, out_shape=tuple((jax.ShapeDtypeStruct(shape, F32)...  11.3 us
    ppermute x2, waiting for transfers between devices, diagonal_swaps(): got.append(lax.ppermute(block, ('gx', 'gy'), pairs))  4.21 us
    ppermute x8, waiting for transfers between devices, swaps(): got.append(lax.ppermute(block, axis, list(enumerate(partner))))  4.2 us
    ppermute x3, starting transfers between devices, swaps(): got.append(lax.ppermute(block, tuple(sorted((axis, other))), pairs))  3.67 us
    ppermute x2, starting transfers between devices, diagonal_swaps(): got.append(lax.ppermute(block, ('gx', 'gy'), pairs))  1.1 us
  transfers between devices with their start and end apart: 13, of which 5 were waited for; matrix products, arithmetic and copies ran while one was open for 0% of the time, Pallas kernels for 2%

profile of v15, /device:TPU:1, one launch (start us, length us, event | category | flops | bytes accessed | tf_op | source)
XLA Modules:
  0.0 51.4 jit_solution(13958132896711236324)
XLA Ops:
  0.0 2.6 %shard_map.64 = (f32[6,4,16,128]{3,2,1,0:T(8,128)}, f32[6,16,4,128]{3,2,1,0:T(4,128)}, f32[6,16,4,128]{3,2,1,0:T(4,128)}, f32[8,16,128]{2,1,0:T(8,128)}, f32[8,16,128]{2,1,0:T(8,128)}) custom-call(s32[1]{0:T(128)} %bitcast.where_ref, f32[16,16,128]{2,1,0:T(8,128)} %refs_0_.3, f32[16,16,128]{2,1,0:T(8,128)} %refs_1_.3, f32[16,16,128]{2,1,0:T(8,128)} %refs_2_.3, ...), custom_call_target="tpu_custom_call" | custom-call | bytes 3600000 | tf_op jit(solution)/shard_map/pallas_call | solution.py:699
  2.6 2.0 %collective-permute-start.2 = (f32[6,4,16,128]{3,2,1,0:T(8,128)}, f32[6,4,16,128]{3,2,1,0:T(8,128)S(1)}, u32[]{:S(2)}, u32[]{:S(2)}) collective-permute-start(f32[6,4,16,128]{3,2,1,0:T(8,128)} %get-tuple-element.51), channel_id=1, source_target_pairs={{0,16},{16,0},{1,17},{17,1},{2,18},{18,2},{3,19},{19,3},{4,20},{20... | collective-permute-start | bytes 589832 | tf_op jit(solution)/shard_map/ppermute | solution.py:728
  4.7 2.1 %collective-permute-start.4 = (f32[6,16,4,128]{3,2,1,0:T(4,128)}, f32[6,16,4,128]{3,2,1,0:T(4,128)S(1)}, u32[]{:S(2)}, u32[]{:S(2)}) collective-permute-start(f32[6,16,4,128]{3,2,1,0:T(4,128)} %get-tuple-element.65), channel_id=1, source_target_pairs={{0,12},{4,8},{8,4},{12,0},{1,13},{5,9},{9,5},{13,1},{2,14},{6,10},... | collective-permute-start | bytes 589832 | tf_op jit(solution)/shard_map/ppermute | solution.py:728
  6.8 0.0 collective-permute-start.5
  6.8 1.3 %collective-permute-start = (f32[8,16,128]{2,1,0:T(8,128)}, f32[8,16,128]{2,1,0:T(8,128)S(1)}, u32[]{:S(2)}, u32[]{:S(2)}) collective-permute-start(f32[8,16,128]{2,1,0:T(8,128)} %get-tuple-element.48), channel_id=1, source_target_pairs={{0,1},{1,0},{2,3},{3,2},{4,5},{5,4},{6,7},{7,6},{8,9},{9,8},{10,11... | collective-permute-start | bytes 196616 | tf_op jit(solution)/shard_map/ppermute | solution.py:728
  8.1 0.8 %collective-permute-start.1 = (f32[8,16,128]{2,1,0:T(8,128)}, f32[8,16,128]{2,1,0:T(8,128)S(1)}, u32[]{:S(2)}, u32[]{:S(2)}) collective-permute-start(f32[8,16,128]{2,1,0:T(8,128)} %get-tuple-element.49), channel_id=1, source_target_pairs={{0,4},{1,2},{2,1},{3,7},{4,0},{5,6},{6,5},{7,3},{8,12},{9,10},{10,... | collective-permute-start | bytes 196616 | tf_op jit(solution)/shard_map/ppermute | solution.py:739
  8.8 1.5 %collective-permute-done.one_ref = f32[8,16,128]{2,1,0:T(8,128)S(1)} collective-permute-done((f32[8,16,128]{2,1,0:T(8,128)}, f32[8,16,128]{2,1,0:T(8,128)S(1)}, u32[]{:S(2)}, u32[]{:S(2)}) %collective-permute-start) | collective-permute-done | bytes 65568 | tf_op jit(solution)/shard_map/ppermute | solution.py:728
  10.4 0.0 collective-permute-done.1.two_ref
  10.4 0.1 shard_map.65
  10.5 0.3 collective-permute-start.3
  10.8 0.0 collective-permute-done.2.refs_7_.refs_0_
  10.9 0.7 %shard_map.66 = (f32[24,24,128]{2,1,0:T(8,128)S(1)}, f32[24,24,128]{2,1,0:T(8,128)S(1)}, f32[24,24,128]{2,1,0:T(8,128)S(1)}, f32[24,24,128]{2,1,0:T(8,128)S(1)},...) custom-call(s32[1]{0:T(128)} %bitcast.where_ref, ...), custom_call_target="tpu_custom_call" | custom-call | bytes 7200000 | tf_op jit(solution)/shard_map/pallas_call | solution.py:699
  11.6 1.7 %collective-permute-done.3.refs_1_.refs_12_ = f32[4,16,128]{2,1,0:T(8,128)S(1)} collective-permute-done((f32[4,16,128]{2,1,0:T(8,128)S(1)}, f32[4,16,128]{2,1,0:T(8,128)S(1)}, u32[]{:S(2)}, u32[]{:S(2)}) %collective-permute-start.3) | collective-permute-done | bytes 32800 | tf_op jit(solution)/shard_map/ppermute | solution.py:728
  13.3 0.1 shard_map.67
  13.4 2.7 %collective-permute-start.6 = (f32[37,4,128]{2,1,0:T(4,128)S(1)}, f32[37,4,128]{2,1,0:T(4,128)S(1)}, u32[]{:S(2)}, u32[]{:S(2)}) collective-permute-start(f32[37,4,128]{2,1,0:T(4,128)S(1)} %get-tuple-element.68), channel_id=1, source_target_pairs={{0,1},{4,8},{8,4},{12,13},{1,0},{5,9},{9,5},{13,12},{2,3},{6,10},{... | collective-permute-start | bytes 227336 | tf_op jit(solution)/shard_map/ppermute | solution.py:739
  16.1 2.6 %collective-permute-start.7 = (f32[37,4,128]{2,1,0:T(4,128)S(1)}, f32[37,4,128]{2,1,0:T(4,128)S(1)}, u32[]{:S(2)}, u32[]{:S(2)}) collective-permute-start(f32[37,4,128]{2,1,0:T(4,128)S(1)} %get-tuple-element.69), channel_id=1, source_target_pairs={{0,4},{4,0},{8,12},{12,8},{1,5},{5,1},{9,13},{13,9},{2,6},{6,2},{1... | collective-permute-start | bytes 227336 | tf_op jit(solution)/shard_map/ppermute | solution.py:728
  18.7 0.0 collective-permute-done.4.refs_13_
  18.7 0.0 collective-permute-done.5.refs_14_
  18.7 0.0 collective-permute-done.6.refs_15_
  18.7 0.9 %collective-permute-done.7.refs_16_ = f32[37,4,128]{2,1,0:T(4,128)S(1)} collective-permute-done((f32[37,4,128]{2,1,0:T(4,128)S(1)}, f32[37,4,128]{2,1,0:T(4,128)S(1)}, u32[]{:S(2)}, u32[]{:S(2)}) %collective-permute-start.7) | collective-permute-done | bytes 75808 | tf_op jit(solution)/shard_map/ppermute | solution.py:728
  19.6 3.0 %shard_map.68 = (f32[24,24,128]{2,1,0:T(8,128)S(1)}, f32[24,24,128]{2,1,0:T(8,128)S(1)}, f32[24,24,128]{2,1,0:T(8,128)S(1)}, f32[24,24,128]{2,1,0:T(8,128)S(1)},...) custom-call(s32[1]{0:T(128)} %bitcast.where_ref, ...), custom_call_target="tpu_custom_call", output_to_operand_aliasing={{0}: (2, {}), {1}: (3, {}), {2}: (4, {}), {3}: (5, {}), {4}... | custom-call | bytes 14400000 | tf_op jit(solution)/shard_map/pallas_call | solution.py:699
  22.6 0.3 collective-permute-start.8
  22.9 0.2 collective-permute-start.9
  23.1 3.5 %collective-permute-start.10 = (f32[5,8,4,128]{3,2,1,0:T(4,128)S(1)}, f32[5,8,4,128]{3,2,1,0:T(4,128)S(1)}, u32[]{:S(2)}, u32[]{:S(2)}) collective-permute-start(f32[5,8,4,128]{3,2,1,0:T(4,128)S(1)} %get-tuple-element.74), channel_id=1, source_target_pairs={{0,4},{4,0},{8,12},{12,8},{1,5},{5,1},{9,13},{13,9},{2,6},{6,2},{1... | collective-permute-start | bytes 245768 | tf_op jit(solution)/shard_map/ppermute | solution.py:728
  26.6 1.1 %collective-permute-start.11 = (f32[15,4,128]{2,1,0:T(4,128)S(1)}, f32[15,4,128]{2,1,0:T(4,128)S(1)}, u32[]{:S(2)}, u32[]{:S(2)}) collective-permute-start(f32[15,4,128]{2,1,0:T(4,128)S(1)} %get-tuple-element.75), channel_id=1, source_target_pairs={{0,20},{4,16},{8,28},{12,24},{16,4},{20,0},{24,12},{28,8},{1,21},{... | collective-permute-start | bytes 92168 | tf_op jit(solution)/shard_map/ppermute | solution.py:753
  27.7 0.0 collective-permute-start.12
  27.7 2.2 %collective-permute-done.11.refs_3_ = f32[15,4,128]{2,1,0:T(4,128)S(1)} collective-permute-done((f32[15,4,128]{2,1,0:T(4,128)S(1)}, f32[15,4,128]{2,1,0:T(4,128)S(1)}, u32[]{:S(2)}, u32[]{:S(2)}) %collective-permute-start.11) | collective-permute-done | bytes 30752 | tf_op jit(solution)/shard_map/ppermute | solution.py:753
  30.0 2.0 %collective-permute-done.12.refs_4_ = f32[15,4,128]{2,1,0:T(4,128)S(1)} collective-permute-done((f32[15,4,128]{2,1,0:T(4,128)S(1)}, f32[15,4,128]{2,1,0:T(4,128)S(1)}, u32[]{:S(2)}, u32[]{:S(2)}) %collective-permute-start.12) | collective-permute-done | bytes 30752 | tf_op jit(solution)/shard_map/ppermute | solution.py:753
  32.0 0.0 collective-permute-done.8.refs_0_
  32.0 0.5 shard_map.69
  32.4 14.6 %all_to_all.5.gathered = f32[32,5,4,128]{3,2,1,0:T(4,128)S(1)} all-to-all(f32[32,5,4,128]{3,2,1,0:T(4,128)S(1)} %get-tuple-element.77), channel_id=1, replica_groups=mesh['gx'=2,'gy'=4,'gz'=4] {'gx','gy','gz'}, dimensions={0} | all-to-all | bytes 655360 | tf_op jit(solution)/shard_map/all_to_all | solution.py:835
  47.0 4.4 %shard_map.70 = f32[16,16,128]{2,1,0:T(8,128)} custom-call(s32[1]{0:T(128)} %bitcast.where_ref, f32[32,5,4,128]{3,2,1,0:T(4,128)S(1)} %all_to_all.5.gathered, f32[6,16,16,128]{3,2,1,0:T(8,128)S(1)} %get-tuple-element.78.level1, f32[24,24,128]{2,1,0:T(8,128)S(1)} %get-tuple-element.79.refs_0_, f32[24,24,128]{2,1,0:T(8,128)S(1)} %get-tuple-element.80.refs_1_, ...), custom_call_target="tpu_custom_call" | custom-call | bytes 14400000 | tf_op jit(solution)/shard_map/pallas_call | solution.py:699
  (14 shorter events, 0.0 us)
Async XLA Ops:
  0.0 10.8 %copy-start.1 = (f32[16,16,128]{2,1,0:T(8,128)S(1)}, f32[16,16,128]{2,1,0:T(8,128)}, u32[]{:S(2)}) copy-start(f32[16,16,128]{2,1,0:T(8,128)} %refs_1_.3) | copy-start | bytes 393220
  0.0 10.8 %copy-start.2 = (f32[16,16,128]{2,1,0:T(8,128)S(1)}, f32[16,16,128]{2,1,0:T(8,128)}, u32[]{:S(2)}) copy-start(f32[16,16,128]{2,1,0:T(8,128)} %refs_2_.3) | copy-start | bytes 393220
  0.0 10.8 %copy-start.3 = (f32[16,16,128]{2,1,0:T(8,128)S(1)}, f32[16,16,128]{2,1,0:T(8,128)}, u32[]{:S(2)}) copy-start(f32[16,16,128]{2,1,0:T(8,128)} %refs_3_.3) | copy-start | bytes 393220
  0.0 10.8 %copy-start.4 = (f32[16,16,128]{2,1,0:T(8,128)S(1)}, f32[16,16,128]{2,1,0:T(8,128)}, u32[]{:S(2)}) copy-start(f32[16,16,128]{2,1,0:T(8,128)} %refs_4_.3) | copy-start | bytes 393220
  0.0 10.8 %copy-start.5 = (f32[16,16,128]{2,1,0:T(8,128)S(1)}, f32[16,16,128]{2,1,0:T(8,128)}, u32[]{:S(2)}) copy-start(f32[16,16,128]{2,1,0:T(8,128)} %refs_5_.3) | copy-start | bytes 393220
  2.6 8.2 %copy-start = (f32[16,16,128]{2,1,0:T(8,128)S(1)}, f32[16,16,128]{2,1,0:T(8,128)}, u32[]{:S(2)}) copy-start(f32[16,16,128]{2,1,0:T(8,128)} %refs_0_.3) | copy-start | bytes 393220
  2.6 8.2 %collective-permute-start.2 = (f32[6,4,16,128]{3,2,1,0:T(8,128)}, f32[6,4,16,128]{3,2,1,0:T(8,128)S(1)}, u32[]{:S(2)}, u32[]{:S(2)}) collective-permute-start(f32[6,4,16,128]{3,2,1,0:T(8,128)} %get-tuple-element.51), channel_id=1, source_target_pairs={{0,16},{16,0},{1,17},{17,1},{2,18},{18,2},{3,19},{19,3},{4,20},{20... | collective-permute-start | bytes 589832 | tf_op jit(solution)/shard_map/ppermute | solution.py:728
  4.7 14.0 %collective-permute-start.4 = (f32[6,16,4,128]{3,2,1,0:T(4,128)}, f32[6,16,4,128]{3,2,1,0:T(4,128)S(1)}, u32[]{:S(2)}, u32[]{:S(2)}) collective-permute-start(f32[6,16,4,128]{3,2,1,0:T(4,128)} %get-tuple-element.65), channel_id=1, source_target_pairs={{0,12},{4,8},{8,4},{12,0},{1,13},{5,9},{9,5},{13,1},{2,14},{6,10},... | collective-permute-start | bytes 589832 | tf_op jit(solution)/shard_map/ppermute | solution.py:728
  6.8 11.9 %collective-permute-start.5 = (f32[6,16,4,128]{3,2,1,0:T(4,128)}, f32[6,16,4,128]{3,2,1,0:T(4,128)S(1)}, u32[]{:S(2)}, u32[]{:S(2)}) collective-permute-start(f32[6,16,4,128]{3,2,1,0:T(4,128)} %get-tuple-element.66), channel_id=1, source_target_pairs={{0,4},{4,0},{8,12},{12,8},{1,5},{5,1},{9,13},{13,9},{2,6},{6,2},{1... | collective-permute-start | bytes 589832 | tf_op jit(solution)/shard_map/ppermute | solution.py:728
  6.8 3.6 %collective-permute-start = (f32[8,16,128]{2,1,0:T(8,128)}, f32[8,16,128]{2,1,0:T(8,128)S(1)}, u32[]{:S(2)}, u32[]{:S(2)}) collective-permute-start(f32[8,16,128]{2,1,0:T(8,128)} %get-tuple-element.48), channel_id=1, source_target_pairs={{0,1},{1,0},{2,3},{3,2},{4,5},{5,4},{6,7},{7,6},{8,9},{9,8},{10,11... | collective-permute-start | bytes 196616 | tf_op jit(solution)/shard_map/ppermute | solution.py:728
  8.1 2.3 %collective-permute-start.1 = (f32[8,16,128]{2,1,0:T(8,128)}, f32[8,16,128]{2,1,0:T(8,128)S(1)}, u32[]{:S(2)}, u32[]{:S(2)}) collective-permute-start(f32[8,16,128]{2,1,0:T(8,128)} %get-tuple-element.49), channel_id=1, source_target_pairs={{0,4},{1,2},{2,1},{3,7},{4,0},{5,6},{6,5},{7,3},{8,12},{9,10},{10,... | collective-permute-start | bytes 196616 | tf_op jit(solution)/shard_map/ppermute | solution.py:739
  10.5 2.8 %collective-permute-start.3 = (f32[4,16,128]{2,1,0:T(8,128)S(1)}, f32[4,16,128]{2,1,0:T(8,128)S(1)}, u32[]{:S(2)}, u32[]{:S(2)}) collective-permute-start(f32[4,16,128]{2,1,0:T(8,128)S(1)} %get-tuple-element.64), channel_id=1, source_target_pairs={{0,16},{16,0},{1,17},{17,1},{2,18},{18,2},{3,19},{19,3},{4,20},{20... | collective-permute-start | bytes 98312 | tf_op jit(solution)/shard_map/ppermute | solution.py:728
  13.4 5.3 %collective-permute-start.6 = (f32[37,4,128]{2,1,0:T(4,128)S(1)}, f32[37,4,128]{2,1,0:T(4,128)S(1)}, u32[]{:S(2)}, u32[]{:S(2)}) collective-permute-start(f32[37,4,128]{2,1,0:T(4,128)S(1)} %get-tuple-element.68), channel_id=1, source_target_pairs={{0,1},{4,8},{8,4},{12,13},{1,0},{5,9},{9,5},{13,12},{2,3},{6,10},{... | collective-permute-start | bytes 227336 | tf_op jit(solution)/shard_map/ppermute | solution.py:739
  16.1 3.5 %collective-permute-start.7 = (f32[37,4,128]{2,1,0:T(4,128)S(1)}, f32[37,4,128]{2,1,0:T(4,128)S(1)}, u32[]{:S(2)}, u32[]{:S(2)}) collective-permute-start(f32[37,4,128]{2,1,0:T(4,128)S(1)} %get-tuple-element.69), channel_id=1, source_target_pairs={{0,4},{4,0},{8,12},{12,8},{1,5},{5,1},{9,13},{13,9},{2,6},{6,2},{1... | collective-permute-start | bytes 227336 | tf_op jit(solution)/shard_map/ppermute | solution.py:728
  22.6 9.4 %collective-permute-start.8 = (f32[5,4,8,128]{3,2,1,0:T(8,128)S(1)}, f32[5,4,8,128]{3,2,1,0:T(8,128)S(1)}, u32[]{:S(2)}, u32[]{:S(2)}) collective-permute-start(f32[5,4,8,128]{3,2,1,0:T(8,128)S(1)} %get-tuple-element.72), channel_id=1, source_target_pairs={{0,16},{16,0},{1,17},{17,1},{2,18},{18,2},{3,19},{19,3},{4,20},{20... | collective-permute-start | bytes 245768 | tf_op jit(solution)/shard_map/ppermute | solution.py:728
  22.9 9.1 %collective-permute-start.9 = (f32[5,8,4,128]{3,2,1,0:T(4,128)S(1)}, f32[5,8,4,128]{3,2,1,0:T(4,128)S(1)}, u32[]{:S(2)}, u32[]{:S(2)}) collective-permute-start(f32[5,8,4,128]{3,2,1,0:T(4,128)S(1)} %get-tuple-element.73), channel_id=1, source_target_pairs={{0,1},{4,8},{8,4},{12,13},{1,0},{5,9},{9,5},{13,12},{2,3},{6,10},{... | collective-permute-start | bytes 245768 | tf_op jit(solution)/shard_map/ppermute | solution.py:739
  23.1 8.9 %collective-permute-start.10 = (f32[5,8,4,128]{3,2,1,0:T(4,128)S(1)}, f32[5,8,4,128]{3,2,1,0:T(4,128)S(1)}, u32[]{:S(2)}, u32[]{:S(2)}) collective-permute-start(f32[5,8,4,128]{3,2,1,0:T(4,128)S(1)} %get-tuple-element.74), channel_id=1, source_target_pairs={{0,4},{4,0},{8,12},{12,8},{1,5},{5,1},{9,13},{13,9},{2,6},{6,2},{1... | collective-permute-start | bytes 245768 | tf_op jit(solution)/shard_map/ppermute | solution.py:728
  26.6 3.3 %collective-permute-start.11 = (f32[15,4,128]{2,1,0:T(4,128)S(1)}, f32[15,4,128]{2,1,0:T(4,128)S(1)}, u32[]{:S(2)}, u32[]{:S(2)}) collective-permute-start(f32[15,4,128]{2,1,0:T(4,128)S(1)} %get-tuple-element.75), channel_id=1, source_target_pairs={{0,20},{4,16},{8,28},{12,24},{16,4},{20,0},{24,12},{28,8},{1,21},{... | collective-permute-start | bytes 92168 | tf_op jit(solution)/shard_map/ppermute | solution.py:753
  27.7 4.2 %collective-permute-start.12 = (f32[15,4,128]{2,1,0:T(4,128)S(1)}, f32[15,4,128]{2,1,0:T(4,128)S(1)}, u32[]{:S(2)}, u32[]{:S(2)}) collective-permute-start(f32[15,4,128]{2,1,0:T(4,128)S(1)} %get-tuple-element.76), channel_id=1, source_target_pairs={{0,16},{4,24},{8,20},{12,28},{16,0},{20,8},{24,4},{28,12},{1,17},{... | collective-permute-start | bytes 92168 | tf_op jit(solution)/shard_map/ppermute | solution.py:753

commit v16 on v15

--- a/solution.py
+++ b/solution.py
@@ -233,17 +233,8 @@
     one_y[21:], two_y[21:] = faces_y(zpack[...], at_y % 2, HALO)
 
 
-def each(first, last, step, body):
-    rounds = (last - first) // step
-
-    def go(i, carry):
-        for j in range(step):
-            body(first + i * step + j)
-        return carry
-
-    if rounds:
-        lax.fori_loop(0, rounds, go, 0)
-    for x in range(first + rounds * step, last):
+def each(first, last, body):
+    for x in range(first, last):
         body(x)
 
 
@@ -388,9 +379,9 @@
         for a in range(6):
             arrays[a][1][x] = unpacked(packed, a, lane)
 
-    each(0, HALO, HALO, unpack)
-    each(HALO, HALO + sx, 8, unpack_rows)
-    each(HALO + sx, ex, HALO, unpack)
+    each(0, HALO, unpack)
+    each(HALO, HALO + sx, unpack_rows)
+    each(HALO + sx, ex, unpack)
     halfway, weight, kept = (half_m, half_h), (weight_m, weight_h), (kept_m, kept_h)
     diag = (diag_m, diag_h)
 
@@ -407,21 +398,21 @@
             weight[k][x] = w
             halfway[k][x] = KEEP * centre[k] + w * (rhs[k][x] + near[k])
 
-    each(1, ex - 1, 11, first_sweep)
+    each(1, ex - 1, first_sweep)
 
     def second_sweep(x):
         centre, near = pull_slab(halfway, bx, by, bz, x, lane)
         for k in range(2):
             kept[k][x] = KEEP * centre[k] + weight[k][x] * (rhs[k][x] + near[k])
 
-    each(2, ex - 2, 10, second_sweep)
+    each(2, ex - 2, second_sweep)
 
     def residual(x):
         centre, near = pull_slab(kept, bx, by, bz, x, lane)
         for k in range(2):
             halfway[k][x] = rhs[k][x] - diag[k][x] * centre[k] + near[k]
 
-    each(HALO, ex - HALO, 8, residual)
+    each(HALO, ex - HALO, residual)
 
     x1, y1 = sx // 2, sy // 2
     for k in range(2):
@@ -685,14 +676,14 @@
         for k in range(2):
             after[k][x] = KEEP * centre[k] + weight[k][x] * (rhs[k][x] + around[k])
 
-    each(first + 1, ex - first - 1, 9, sweep_out)
+    each(first + 1, ex - first - 1, sweep_out)
 
     def sweep_own(x):
         centre, around = pull_slab(after, bx, by, bz, x, lane)
         value = KEEP * centre[0] + weight[0][x] * (rhs[0][x] + around[0])
         out[x - HALO] = value[:sy]
 
-    each(HALO, ex - HALO, 8, sweep_own)
+    each(HALO, ex - HALO, sweep_own)
 
 
 def run(kernel, outs, where, arrays, scratch=(), grant=16, micros=1, aliases={}):

time: 51.5 us -> 50.5 us (0.981)
  Pallas kernels: 11.3 us -> 10.3 us
    pallas_call x7, Pallas kernels: 11.3 us -> 10.3 us  [run(): pl.pallas_call(kernel, out_shape=tuple((jax.ShapeDtypeStruct(shape, F32)...]
where the time goes in v16:
time: 50.5 us; the launch traced here: 50.4 us
  starting transfers between devices  17 us (34%)
  blocking collectives  14.6 us (29%)
  Pallas kernels  10.3 us (20%)
  waiting for transfers between devices  8.42 us (17%)
    all_to_all x1, blocking collectives, local(): gathered = lax.all_to_all(copies, axes, 0, 0, tiled=True)  14.6 us
    ppermute x8, starting transfers between devices, swaps(): got.append(lax.ppermute(block, axis, list(enumerate(partner))))  12.2 us
    pallas_call x7, Pallas kernels, run(): pl.pallas_call(kernel, out_shape=tuple((jax.ShapeDtypeStruct(shape, F32)...  10.3 us
    ppermute x2, waiting for transfers between devices, diagonal_swaps(): got.append(lax.ppermute(block, ('gx', 'gy'), pairs))  4.21 us
    ppermute x8, waiting for transfers between devices, swaps(): got.append(lax.ppermute(block, axis, list(enumerate(partner))))  4.2 us
    ppermute x3, starting transfers between devices, swaps(): got.append(lax.ppermute(block, tuple(sorted((axis, other))), pairs))  3.68 us
    ppermute x2, starting transfers between devices, diagonal_swaps(): got.append(lax.ppermute(block, ('gx', 'gy'), pairs))  1.1 us
  transfers between devices with their start and end apart: 13, of which 5 were waited for; matrix products, arithmetic and copies ran while one was open for 0% of the time, Pallas kernels for 2%

profile of v16, /device:TPU:1, one launch (start us, length us, event | category | flops | bytes accessed | tf_op | source)
XLA Modules:
  0.0 50.4 jit_solution(6841844920543808651)
XLA Ops:
  0.0 2.6 %shard_map.64 = (f32[6,4,16,128]{3,2,1,0:T(8,128)}, f32[6,16,4,128]{3,2,1,0:T(4,128)}, f32[6,16,4,128]{3,2,1,0:T(4,128)}, f32[8,16,128]{2,1,0:T(8,128)}, f32[8,16,128]{2,1,0:T(8,128)}) custom-call(s32[1]{0:T(128)} %bitcast.where_ref, f32[16,16,128]{2,1,0:T(8,128)} %refs_0_.3, f32[16,16,128]{2,1,0:T(8,128)} %refs_1_.3, f32[16,16,128]{2,1,0:T(8,128)} %refs_2_.3, ...), custom_call_target="tpu_custom_call" | custom-call | bytes 3600000 | tf_op jit(solution)/shard_map/pallas_call | solution.py:690
  2.6 2.0 %collective-permute-start.2 = (f32[6,4,16,128]{3,2,1,0:T(8,128)}, f32[6,4,16,128]{3,2,1,0:T(8,128)S(1)}, u32[]{:S(2)}, u32[]{:S(2)}) collective-permute-start(f32[6,4,16,128]{3,2,1,0:T(8,128)} %get-tuple-element.51), channel_id=1, source_target_pairs={{0,16},{16,0},{1,17},{17,1},{2,18},{18,2},{3,19},{19,3},{4,20},{20... | collective-permute-start | bytes 589832 | tf_op jit(solution)/shard_map/ppermute | solution.py:719
  4.7 2.1 %collective-permute-start.4 = (f32[6,16,4,128]{3,2,1,0:T(4,128)}, f32[6,16,4,128]{3,2,1,0:T(4,128)S(1)}, u32[]{:S(2)}, u32[]{:S(2)}) collective-permute-start(f32[6,16,4,128]{3,2,1,0:T(4,128)} %get-tuple-element.65), channel_id=1, source_target_pairs={{0,12},{4,8},{8,4},{12,0},{1,13},{5,9},{9,5},{13,1},{2,14},{6,10},... | collective-permute-start | bytes 589832 | tf_op jit(solution)/shard_map/ppermute | solution.py:719
  6.8 0.0 collective-permute-start.5
  6.8 1.3 %collective-permute-start = (f32[8,16,128]{2,1,0:T(8,128)}, f32[8,16,128]{2,1,0:T(8,128)S(1)}, u32[]{:S(2)}, u32[]{:S(2)}) collective-permute-start(f32[8,16,128]{2,1,0:T(8,128)} %get-tuple-element.48), channel_id=1, source_target_pairs={{0,1},{1,0},{2,3},{3,2},{4,5},{5,4},{6,7},{7,6},{8,9},{9,8},{10,11... | collective-permute-start | bytes 196616 | tf_op jit(solution)/shard_map/ppermute | solution.py:719
  8.1 0.8 %collective-permute-start.1 = (f32[8,16,128]{2,1,0:T(8,128)}, f32[8,16,128]{2,1,0:T(8,128)S(1)}, u32[]{:S(2)}, u32[]{:S(2)}) collective-permute-start(f32[8,16,128]{2,1,0:T(8,128)} %get-tuple-element.49), channel_id=1, source_target_pairs={{0,4},{1,2},{2,1},{3,7},{4,0},{5,6},{6,5},{7,3},{8,12},{9,10},{10,... | collective-permute-start | bytes 196616 | tf_op jit(solution)/shard_map/ppermute | solution.py:730
  8.8 1.5 %collective-permute-done.one_ref = f32[8,16,128]{2,1,0:T(8,128)S(1)} collective-permute-done((f32[8,16,128]{2,1,0:T(8,128)}, f32[8,16,128]{2,1,0:T(8,128)S(1)}, u32[]{:S(2)}, u32[]{:S(2)}) %collective-permute-start) | collective-permute-done | bytes 65568 | tf_op jit(solution)/shard_map/ppermute | solution.py:719
  10.4 0.0 collective-permute-done.1.two_ref
  10.4 0.1 shard_map.65
  10.5 0.3 collective-permute-start.3
  10.8 0.0 collective-permute-done.2.refs_7_.refs_0_
  10.9 0.7 %shard_map.66 = (f32[24,24,128]{2,1,0:T(8,128)S(1)}, f32[24,24,128]{2,1,0:T(8,128)S(1)}, f32[24,24,128]{2,1,0:T(8,128)S(1)}, f32[24,24,128]{2,1,0:T(8,128)S(1)},...) custom-call(s32[1]{0:T(128)} %bitcast.where_ref, ...), custom_call_target="tpu_custom_call" | custom-call | bytes 7200000 | tf_op jit(solution)/shard_map/pallas_call | solution.py:690
  11.6 1.7 %collective-permute-done.3.refs_1_.refs_12_ = f32[4,16,128]{2,1,0:T(8,128)S(1)} collective-permute-done((f32[4,16,128]{2,1,0:T(8,128)S(1)}, f32[4,16,128]{2,1,0:T(8,128)S(1)}, u32[]{:S(2)}, u32[]{:S(2)}) %collective-permute-start.3) | collective-permute-done | bytes 32800 | tf_op jit(solution)/shard_map/ppermute | solution.py:719
  13.3 0.1 shard_map.67
  13.4 2.7 %collective-permute-start.6 = (f32[37,4,128]{2,1,0:T(4,128)S(1)}, f32[37,4,128]{2,1,0:T(4,128)S(1)}, u32[]{:S(2)}, u32[]{:S(2)}) collective-permute-start(f32[37,4,128]{2,1,0:T(4,128)S(1)} %get-tuple-element.68), channel_id=1, source_target_pairs={{0,1},{4,8},{8,4},{12,13},{1,0},{5,9},{9,5},{13,12},{2,3},{6,10},{... | collective-permute-start | bytes 227336 | tf_op jit(solution)/shard_map/ppermute | solution.py:730
  16.1 2.6 %collective-permute-start.7 = (f32[37,4,128]{2,1,0:T(4,128)S(1)}, f32[37,4,128]{2,1,0:T(4,128)S(1)}, u32[]{:S(2)}, u32[]{:S(2)}) collective-permute-start(f32[37,4,128]{2,1,0:T(4,128)S(1)} %get-tuple-element.69), channel_id=1, source_target_pairs={{0,4},{4,0},{8,12},{12,8},{1,5},{5,1},{9,13},{13,9},{2,6},{6,2},{1... | collective-permute-start | bytes 227336 | tf_op jit(solution)/shard_map/ppermute | solution.py:719
  18.7 0.0 collective-permute-done.4.refs_13_
  18.7 0.0 collective-permute-done.5.refs_14_
  18.7 0.0 collective-permute-done.6.refs_15_
  18.7 0.9 %collective-permute-done.7.refs_16_ = f32[37,4,128]{2,1,0:T(4,128)S(1)} collective-permute-done((f32[37,4,128]{2,1,0:T(4,128)S(1)}, f32[37,4,128]{2,1,0:T(4,128)S(1)}, u32[]{:S(2)}, u32[]{:S(2)}) %collective-permute-start.7) | collective-permute-done | bytes 75808 | tf_op jit(solution)/shard_map/ppermute | solution.py:719
  19.6 2.3 %shard_map.68 = (f32[24,24,128]{2,1,0:T(8,128)S(1)}, f32[24,24,128]{2,1,0:T(8,128)S(1)}, f32[24,24,128]{2,1,0:T(8,128)S(1)}, f32[24,24,128]{2,1,0:T(8,128)S(1)},...) custom-call(s32[1]{0:T(128)} %bitcast.where_ref, ...), custom_call_target="tpu_custom_call", output_to_operand_aliasing={{0}: (2, {}), {1}: (3, {}), {2}: (4, {}), {3}: (5, {}), {4}... | custom-call | bytes 14400000 | tf_op jit(solution)/shard_map/pallas_call | solution.py:690
  21.9 0.3 collective-permute-start.8
  22.2 0.2 collective-permute-start.9
  22.4 3.5 %collective-permute-start.10 = (f32[5,8,4,128]{3,2,1,0:T(4,128)S(1)}, f32[5,8,4,128]{3,2,1,0:T(4,128)S(1)}, u32[]{:S(2)}, u32[]{:S(2)}) collective-permute-start(f32[5,8,4,128]{3,2,1,0:T(4,128)S(1)} %get-tuple-element.74), channel_id=1, source_target_pairs={{0,4},{4,0},{8,12},{12,8},{1,5},{5,1},{9,13},{13,9},{2,6},{6,2},{1... | collective-permute-start | bytes 245768 | tf_op jit(solution)/shard_map/ppermute | solution.py:719
  26.0 1.1 %collective-permute-start.11 = (f32[15,4,128]{2,1,0:T(4,128)S(1)}, f32[15,4,128]{2,1,0:T(4,128)S(1)}, u32[]{:S(2)}, u32[]{:S(2)}) collective-permute-start(f32[15,4,128]{2,1,0:T(4,128)S(1)} %get-tuple-element.75), channel_id=1, source_target_pairs={{0,20},{4,16},{8,28},{12,24},{16,4},{20,0},{24,12},{28,8},{1,21},{... | collective-permute-start | bytes 92168 | tf_op jit(solution)/shard_map/ppermute | solution.py:744
  27.1 0.0 collective-permute-start.12
  27.1 2.2 %collective-permute-done.11.refs_3_ = f32[15,4,128]{2,1,0:T(4,128)S(1)} collective-permute-done((f32[15,4,128]{2,1,0:T(4,128)S(1)}, f32[15,4,128]{2,1,0:T(4,128)S(1)}, u32[]{:S(2)}, u32[]{:S(2)}) %collective-permute-start.11) | collective-permute-done | bytes 30752 | tf_op jit(solution)/shard_map/ppermute | solution.py:744
  29.3 2.0 %collective-permute-done.12.refs_4_ = f32[15,4,128]{2,1,0:T(4,128)S(1)} collective-permute-done((f32[15,4,128]{2,1,0:T(4,128)S(1)}, f32[15,4,128]{2,1,0:T(4,128)S(1)}, u32[]{:S(2)}, u32[]{:S(2)}) %collective-permute-start.12) | collective-permute-done | bytes 30752 | tf_op jit(solution)/shard_map/ppermute | solution.py:744
  31.3 0.0 collective-permute-done.8.refs_0_
  31.3 0.5 shard_map.69
  31.8 14.6 %all_to_all.5.gathered = f32[32,5,4,128]{3,2,1,0:T(4,128)S(1)} all-to-all(f32[32,5,4,128]{3,2,1,0:T(4,128)S(1)} %get-tuple-element.77), channel_id=1, replica_groups=mesh['gx'=2,'gy'=4,'gz'=4] {'gx','gy','gz'}, dimensions={0} | all-to-all | bytes 655360 | tf_op jit(solution)/shard_map/all_to_all | solution.py:826
  46.4 4.0 %shard_map.70 = f32[16,16,128]{2,1,0:T(8,128)} custom-call(s32[1]{0:T(128)} %bitcast.where_ref, f32[32,5,4,128]{3,2,1,0:T(4,128)S(1)} %all_to_all.5.gathered, f32[6,16,16,128]{3,2,1,0:T(8,128)S(1)} %get-tuple-element.78.level1, f32[24,24,128]{2,1,0:T(8,128)S(1)} %get-tuple-element.79.refs_0_, f32[24,24,128]{2,1,0:T(8,128)S(1)} %get-tuple-element.80.refs_1_, ...), custom_call_target="tpu_custom_call" | custom-call | bytes 14400000 | tf_op jit(solution)/shard_map/pallas_call | solution.py:690
  (14 shorter events, 0.0 us)
Async XLA Ops:
  0.0 10.8 %copy-start.1 = (f32[16,16,128]{2,1,0:T(8,128)S(1)}, f32[16,16,128]{2,1,0:T(8,128)}, u32[]{:S(2)}) copy-start(f32[16,16,128]{2,1,0:T(8,128)} %refs_1_.3) | copy-start | bytes 393220
  0.0 10.8 %copy-start.2 = (f32[16,16,128]{2,1,0:T(8,128)S(1)}, f32[16,16,128]{2,1,0:T(8,128)}, u32[]{:S(2)}) copy-start(f32[16,16,128]{2,1,0:T(8,128)} %refs_2_.3) | copy-start | bytes 393220
  0.0 10.8 %copy-start.3 = (f32[16,16,128]{2,1,0:T(8,128)S(1)}, f32[16,16,128]{2,1,0:T(8,128)}, u32[]{:S(2)}) copy-start(f32[16,16,128]{2,1,0:T(8,128)} %refs_3_.3) | copy-start | bytes 393220
  0.0 10.8 %copy-start.4 = (f32[16,16,128]{2,1,0:T(8,128)S(1)}, f32[16,16,128]{2,1,0:T(8,128)}, u32[]{:S(2)}) copy-start(f32[16,16,128]{2,1,0:T(8,128)} %refs_4_.3) | copy-start | bytes 393220
  0.0 10.8 %copy-start.5 = (f32[16,16,128]{2,1,0:T(8,128)S(1)}, f32[16,16,128]{2,1,0:T(8,128)}, u32[]{:S(2)}) copy-start(f32[16,16,128]{2,1,0:T(8,128)} %refs_5_.3) | copy-start | bytes 393220
  2.6 8.2 %copy-start = (f32[16,16,128]{2,1,0:T(8,128)S(1)}, f32[16,16,128]{2,1,0:T(8,128)}, u32[]{:S(2)}) copy-start(f32[16,16,128]{2,1,0:T(8,128)} %refs_0_.3) | copy-start | bytes 393220
  2.6 8.2 %collective-permute-start.2 = (f32[6,4,16,128]{3,2,1,0:T(8,128)}, f32[6,4,16,128]{3,2,1,0:T(8,128)S(1)}, u32[]{:S(2)}, u32[]{:S(2)}) collective-permute-start(f32[6,4,16,128]{3,2,1,0:T(8,128)} %get-tuple-element.51), channel_id=1, source_target_pairs={{0,16},{16,0},{1,17},{17,1},{2,18},{18,2},{3,19},{19,3},{4,20},{20... | collective-permute-start | bytes 589832 | tf_op jit(solution)/shard_map/ppermute | solution.py:719
  4.7 14.0 %collective-permute-start.4 = (f32[6,16,4,128]{3,2,1,0:T(4,128)}, f32[6,16,4,128]{3,2,1,0:T(4,128)S(1)}, u32[]{:S(2)}, u32[]{:S(2)}) collective-permute-start(f32[6,16,4,128]{3,2,1,0:T(4,128)} %get-tuple-element.65), channel_id=1, source_target_pairs={{0,12},{4,8},{8,4},{12,0},{1,13},{5,9},{9,5},{13,1},{2,14},{6,10},... | collective-permute-start | bytes 589832 | tf_op jit(solution)/shard_map/ppermute | solution.py:719
  6.8 11.9 %collective-permute-start.5 = (f32[6,16,4,128]{3,2,1,0:T(4,128)}, f32[6,16,4,128]{3,2,1,0:T(4,128)S(1)}, u32[]{:S(2)}, u32[]{:S(2)}) collective-permute-start(f32[6,16,4,128]{3,2,1,0:T(4,128)} %get-tuple-element.66), channel_id=1, source_target_pairs={{0,4},{4,0},{8,12},{12,8},{1,5},{5,1},{9,13},{13,9},{2,6},{6,2},{1... | collective-permute-start | bytes 589832 | tf_op jit(solution)/shard_map/ppermute | solution.py:719
  6.8 3.6 %collective-permute-start = (f32[8,16,128]{2,1,0:T(8,128)}, f32[8,16,128]{2,1,0:T(8,128)S(1)}, u32[]{:S(2)}, u32[]{:S(2)}) collective-permute-start(f32[8,16,128]{2,1,0:T(8,128)} %get-tuple-element.48), channel_id=1, source_target_pairs={{0,1},{1,0},{2,3},{3,2},{4,5},{5,4},{6,7},{7,6},{8,9},{9,8},{10,11... | collective-permute-start | bytes 196616 | tf_op jit(solution)/shard_map/ppermute | solution.py:719
  8.1 2.3 %collective-permute-start.1 = (f32[8,16,128]{2,1,0:T(8,128)}, f32[8,16,128]{2,1,0:T(8,128)S(1)}, u32[]{:S(2)}, u32[]{:S(2)}) collective-permute-start(f32[8,16,128]{2,1,0:T(8,128)} %get-tuple-element.49), channel_id=1, source_target_pairs={{0,4},{1,2},{2,1},{3,7},{4,0},{5,6},{6,5},{7,3},{8,12},{9,10},{10,... | collective-permute-start | bytes 196616 | tf_op jit(solution)/shard_map/ppermute | solution.py:730
  10.5 2.8 %collective-permute-start.3 = (f32[4,16,128]{2,1,0:T(8,128)S(1)}, f32[4,16,128]{2,1,0:T(8,128)S(1)}, u32[]{:S(2)}, u32[]{:S(2)}) collective-permute-start(f32[4,16,128]{2,1,0:T(8,128)S(1)} %get-tuple-element.64), channel_id=1, source_target_pairs={{0,16},{16,0},{1,17},{17,1},{2,18},{18,2},{3,19},{19,3},{4,20},{20... | collective-permute-start | bytes 98312 | tf_op jit(solution)/shard_map/ppermute | solution.py:719
  13.4 5.3 %collective-permute-start.6 = (f32[37,4,128]{2,1,0:T(4,128)S(1)}, f32[37,4,128]{2,1,0:T(4,128)S(1)}, u32[]{:S(2)}, u32[]{:S(2)}) collective-permute-start(f32[37,4,128]{2,1,0:T(4,128)S(1)} %get-tuple-element.68), channel_id=1, source_target_pairs={{0,1},{4,8},{8,4},{12,13},{1,0},{5,9},{9,5},{13,12},{2,3},{6,10},{... | collective-permute-start | bytes 227336 | tf_op jit(solution)/shard_map/ppermute | solution.py:730
  16.1 3.5 %collective-permute-start.7 = (f32[37,4,128]{2,1,0:T(4,128)S(1)}, f32[37,4,128]{2,1,0:T(4,128)S(1)}, u32[]{:S(2)}, u32[]{:S(2)}) collective-permute-start(f32[37,4,128]{2,1,0:T(4,128)S(1)} %get-tuple-element.69), channel_id=1, source_target_pairs={{0,4},{4,0},{8,12},{12,8},{1,5},{5,1},{9,13},{13,9},{2,6},{6,2},{1... | collective-permute-start | bytes 227336 | tf_op jit(solution)/shard_map/ppermute | solution.py:719
  21.9 9.4 %collective-permute-start.8 = (f32[5,4,8,128]{3,2,1,0:T(8,128)S(1)}, f32[5,4,8,128]{3,2,1,0:T(8,128)S(1)}, u32[]{:S(2)}, u32[]{:S(2)}) collective-permute-start(f32[5,4,8,128]{3,2,1,0:T(8,128)S(1)} %get-tuple-element.72), channel_id=1, source_target_pairs={{0,16},{16,0},{1,17},{17,1},{2,18},{18,2},{3,19},{19,3},{4,20},{20... | collective-permute-start | bytes 245768 | tf_op jit(solution)/shard_map/ppermute | solution.py:719
  22.2 9.1 %collective-permute-start.9 = (f32[5,8,4,128]{3,2,1,0:T(4,128)S(1)}, f32[5,8,4,128]{3,2,1,0:T(4,128)S(1)}, u32[]{:S(2)}, u32[]{:S(2)}) collective-permute-start(f32[5,8,4,128]{3,2,1,0:T(4,128)S(1)} %get-tuple-element.73), channel_id=1, source_target_pairs={{0,1},{4,8},{8,4},{12,13},{1,0},{5,9},{9,5},{13,12},{2,3},{6,10},{... | collective-permute-start | bytes 245768 | tf_op jit(solution)/shard_map/ppermute | solution.py:730
  22.4 8.9 %collective-permute-start.10 = (f32[5,8,4,128]{3,2,1,0:T(4,128)S(1)}, f32[5,8,4,128]{3,2,1,0:T(4,128)S(1)}, u32[]{:S(2)}, u32[]{:S(2)}) collective-permute-start(f32[5,8,4,128]{3,2,1,0:T(4,128)S(1)} %get-tuple-element.74), channel_id=1, source_target_pairs={{0,4},{4,0},{8,12},{12,8},{1,5},{5,1},{9,13},{13,9},{2,6},{6,2},{1... | collective-permute-start | bytes 245768 | tf_op jit(solution)/shard_map/ppermute | solution.py:719
  26.0 3.3 %collective-permute-start.11 = (f32[15,4,128]{2,1,0:T(4,128)S(1)}, f32[15,4,128]{2,1,0:T(4,128)S(1)}, u32[]{:S(2)}, u32[]{:S(2)}) collective-permute-start(f32[15,4,128]{2,1,0:T(4,128)S(1)} %get-tuple-element.75), channel_id=1, source_target_pairs={{0,20},{4,16},{8,28},{12,24},{16,4},{20,0},{24,12},{28,8},{1,21},{... | collective-permute-start | bytes 92168 | tf_op jit(solution)/shard_map/ppermute | solution.py:744
  27.1 4.2 %collective-permute-start.12 = (f32[15,4,128]{2,1,0:T(4,128)S(1)}, f32[15,4,128]{2,1,0:T(4,128)S(1)}, u32[]{:S(2)}, u32[]{:S(2)}) collective-permute-start(f32[15,4,128]{2,1,0:T(4,128)S(1)} %get-tuple-element.76), channel_id=1, source_target_pairs={{0,16},{4,24},{8,20},{12,28},{16,0},{20,8},{24,4},{28,12},{1,17},{... | collective-permute-start | bytes 92168 | tf_op jit(solution)/shard_map/ppermute | solution.py:744

commit v17 on v16

--- a/solution.py
+++ b/solution.py
@@ -63,15 +63,6 @@
     total = None
     for part in reversed(parts_of(values)):
         term = jnp.dot(part, table, preferred_element_type=F32)
-        total = term if total is None else total + term
-    return total
-
-
-def table_times(table, values):
-    table = table.astype(jnp.bfloat16)
-    total = None
-    for part in reversed(parts_of(values)):
-        term = jnp.dot(table, part, preferred_element_type=F32)
         total = term if total is None else total + term
     return total
 
@@ -613,7 +604,7 @@
 
 def up_kernel(counts, where_ref, gathered, level1, *refs):
     kept, weight, rhs, bx, by, bz = zip(refs[0:12:2], refs[1:12:2])
-    out, whole, second, spread_m, spread_h, field_m, field_h, half_m, half_h = refs[12:]
+    out, whole, second, lift, spread_m, spread_h, field_m, field_h, half_m, half_h = refs[12:]
     gx, gy, gz = counts
     at_x, at_y, at_z = position(where_ref)
     sx, sy, sz = out.shape
@@ -633,17 +624,19 @@
     second[half + wide:] = jnp.zeros((half,) + correction.shape[1:], F32)
     window = second[pl.ds(at_x * x2, x2 + NEAR)]
     rows = correction.shape[1]
-    row = iota2((ey1, rows), 0)
-    col = iota2((ey1, rows), 1)
-    place = jnp.where(row < y1 + NEAR, row, row - ey1)
-    table_y = (col == at_y * y2 + lax.shift_right_arithmetic(place, 1)).astype(F32)
     row = iota2((columns, LANES), 0)
     col = iota2((columns, LANES), 1)
     place = jnp.where(col < LANES * 3 // 4, col, col - LANES)
     table_z = (row == at_z * z2 + lax.shift_right_arithmetic(place, 1)).astype(F32)
     flat = times_table(window.reshape((x2 + NEAR) * rows, columns), table_z)
-    blocks = [table_times(table_y, flat[i * rows:(i + 1) * rows])[None] for i in range(x2 + NEAR)]
-    lifted = jnp.concatenate([blocks[i // 2] for i in range(ex1)], axis=0)
+    flat = flat.reshape(x2 + NEAR, rows, LANES)
+    flat = pltpu.roll(flat, (rows - at_y * y2) % rows, 1)
+    for i in range(x2 + NEAR):
+        for q in range(2):
+            lift[i, pl.ds(q, y2, stride=2), :] = flat[i, :y2]
+            lift[i, pl.ds(y1 + q, half, stride=2), :] = flat[i, y2:y2 + half]
+            lift[i, pl.ds(y1 + NEAR + q, half, stride=2), :] = flat[i, rows - half:]
+    lifted = jnp.concatenate([lift[i // 2][None] for i in range(ex1)], axis=0)
     field1, rhs1, weight1 = level1[0], level1[1], level1[2]
     faces1 = (level1[3], level1[4], level1[5])
     field1 = (field1 + jnp.where(weight1 > 0.0, lifted, 0.0))[1:-1]
@@ -832,6 +825,7 @@
         where,
         (gathered, level1) + tuple(fine_arrays),
         [(5, wide, rows, columns), (wide + NEAR, rows, columns)]
+        + [(x1 // 2 + NEAR, y1 + 2 * NEAR, LANES)]
         + [(x1 + 2, ey, LANES)] * 2
         + [fine] * 4,
         24,

time: 50.5 us -> 50.5 us (level)
  no operation moved by 1% of the time
where the time goes in v17:
time: 50.5 us; the launch traced here: 50.3 us
  starting transfers between devices  17 us (34%)
  blocking collectives  14.6 us (29%)
  Pallas kernels  10.2 us (20%)
  waiting for transfers between devices  8.42 us (17%)
    all_to_all x1, blocking collectives, local(): gathered = lax.all_to_all(copies, axes, 0, 0, tiled=True)  14.6 us
    ppermute x8, starting transfers between devices, swaps(): got.append(lax.ppermute(block, axis, list(enumerate(partner))))  12.2 us
    pallas_call x7, Pallas kernels, run(): pl.pallas_call(kernel, out_shape=tuple((jax.ShapeDtypeStruct(shape, F32)...  10.2 us
    ppermute x2, waiting for transfers between devices, diagonal_swaps(): got.append(lax.ppermute(block, ('gx', 'gy'), pairs))  4.21 us
    ppermute x8, waiting for transfers between devices, swaps(): got.append(lax.ppermute(block, axis, list(enumerate(partner))))  4.2 us
    ppermute x3, starting transfers between devices, swaps(): got.append(lax.ppermute(block, tuple(sorted((axis, other))), pairs))  3.68 us
    ppermute x2, starting transfers between devices, diagonal_swaps(): got.append(lax.ppermute(block, ('gx', 'gy'), pairs))  1.1 us
  transfers between devices with their start and end apart: 13, of which 5 were waited for; matrix products, arithmetic and copies ran while one was open for 0% of the time, Pallas kernels for 2%

profile of v17, /device:TPU:1, one launch (start us, length us, event | category | flops | bytes accessed | tf_op | source)
XLA Modules:
  0.0 50.3 jit_solution(13509808302663695273)
XLA Ops:
  0.0 2.6 %shard_map.64 = (f32[6,4,16,128]{3,2,1,0:T(8,128)}, f32[6,16,4,128]{3,2,1,0:T(4,128)}, f32[6,16,4,128]{3,2,1,0:T(4,128)}, f32[8,16,128]{2,1,0:T(8,128)}, f32[8,16,128]{2,1,0:T(8,128)}) custom-call(s32[1]{0:T(128)} %bitcast.where_ref, f32[16,16,128]{2,1,0:T(8,128)} %refs_0_.3, f32[16,16,128]{2,1,0:T(8,128)} %refs_1_.3, f32[16,16,128]{2,1,0:T(8,128)} %refs_2_.3, ...), custom_call_target="tpu_custom_call" | custom-call | bytes 3600000 | tf_op jit(solution)/shard_map/pallas_call | solution.py:683
  2.6 2.0 %collective-permute-start.2 = (f32[6,4,16,128]{3,2,1,0:T(8,128)}, f32[6,4,16,128]{3,2,1,0:T(8,128)S(1)}, u32[]{:S(2)}, u32[]{:S(2)}) collective-permute-start(f32[6,4,16,128]{3,2,1,0:T(8,128)} %get-tuple-element.51), channel_id=1, source_target_pairs={{0,16},{16,0},{1,17},{17,1},{2,18},{18,2},{3,19},{19,3},{4,20},{20... | collective-permute-start | bytes 589832 | tf_op jit(solution)/shard_map/ppermute | solution.py:712
  4.7 2.1 %collective-permute-start.4 = (f32[6,16,4,128]{3,2,1,0:T(4,128)}, f32[6,16,4,128]{3,2,1,0:T(4,128)S(1)}, u32[]{:S(2)}, u32[]{:S(2)}) collective-permute-start(f32[6,16,4,128]{3,2,1,0:T(4,128)} %get-tuple-element.65), channel_id=1, source_target_pairs={{0,12},{4,8},{8,4},{12,0},{1,13},{5,9},{9,5},{13,1},{2,14},{6,10},... | collective-permute-start | bytes 589832 | tf_op jit(solution)/shard_map/ppermute | solution.py:712
  6.8 0.0 collective-permute-start.5
  6.8 1.3 %collective-permute-start = (f32[8,16,128]{2,1,0:T(8,128)}, f32[8,16,128]{2,1,0:T(8,128)S(1)}, u32[]{:S(2)}, u32[]{:S(2)}) collective-permute-start(f32[8,16,128]{2,1,0:T(8,128)} %get-tuple-element.48), channel_id=1, source_target_pairs={{0,1},{1,0},{2,3},{3,2},{4,5},{5,4},{6,7},{7,6},{8,9},{9,8},{10,11... | collective-permute-start | bytes 196616 | tf_op jit(solution)/shard_map/ppermute | solution.py:712
  8.1 0.8 %collective-permute-start.1 = (f32[8,16,128]{2,1,0:T(8,128)}, f32[8,16,128]{2,1,0:T(8,128)S(1)}, u32[]{:S(2)}, u32[]{:S(2)}) collective-permute-start(f32[8,16,128]{2,1,0:T(8,128)} %get-tuple-element.49), channel_id=1, source_target_pairs={{0,4},{1,2},{2,1},{3,7},{4,0},{5,6},{6,5},{7,3},{8,12},{9,10},{10,... | collective-permute-start | bytes 196616 | tf_op jit(solution)/shard_map/ppermute | solution.py:723
  8.8 1.5 %collective-permute-done.one_ref = f32[8,16,128]{2,1,0:T(8,128)S(1)} collective-permute-done((f32[8,16,128]{2,1,0:T(8,128)}, f32[8,16,128]{2,1,0:T(8,128)S(1)}, u32[]{:S(2)}, u32[]{:S(2)}) %collective-permute-start) | collective-permute-done | bytes 65568 | tf_op jit(solution)/shard_map/ppermute | solution.py:712
  10.4 0.1 shard_map.65
  10.5 0.3 collective-permute-start.3
  10.8 0.0 collective-permute-done.2.refs_7_.refs_0_
  10.9 0.7 %shard_map.66 = (f32[24,24,128]{2,1,0:T(8,128)S(1)}, f32[24,24,128]{2,1,0:T(8,128)S(1)}, f32[24,24,128]{2,1,0:T(8,128)S(1)}, f32[24,24,128]{2,1,0:T(8,128)S(1)},...) custom-call(s32[1]{0:T(128)} %bitcast.where_ref, ...), custom_call_target="tpu_custom_call" | custom-call | bytes 7200000 | tf_op jit(solution)/shard_map/pallas_call | solution.py:683
  11.6 1.7 %collective-permute-done.3.refs_1_.refs_12_ = f32[4,16,128]{2,1,0:T(8,128)S(1)} collective-permute-done((f32[4,16,128]{2,1,0:T(8,128)S(1)}, f32[4,16,128]{2,1,0:T(8,128)S(1)}, u32[]{:S(2)}, u32[]{:S(2)}) %collective-permute-start.3) | collective-permute-done | bytes 32800 | tf_op jit(solution)/shard_map/ppermute | solution.py:712
  13.3 0.1 shard_map.67
  13.4 2.7 %collective-permute-start.6 = (f32[37,4,128]{2,1,0:T(4,128)S(1)}, f32[37,4,128]{2,1,0:T(4,128)S(1)}, u32[]{:S(2)}, u32[]{:S(2)}) collective-permute-start(f32[37,4,128]{2,1,0:T(4,128)S(1)} %get-tuple-element.68), channel_id=1, source_target_pairs={{0,1},{4,8},{8,4},{12,13},{1,0},{5,9},{9,5},{13,12},{2,3},{6,10},{... | collective-permute-start | bytes 227336 | tf_op jit(solution)/shard_map/ppermute | solution.py:723
  16.1 2.6 %collective-permute-start.7 = (f32[37,4,128]{2,1,0:T(4,128)S(1)}, f32[37,4,128]{2,1,0:T(4,128)S(1)}, u32[]{:S(2)}, u32[]{:S(2)}) collective-permute-start(f32[37,4,128]{2,1,0:T(4,128)S(1)} %get-tuple-element.69), channel_id=1, source_target_pairs={{0,4},{4,0},{8,12},{12,8},{1,5},{5,1},{9,13},{13,9},{2,6},{6,2},{1... | collective-permute-start | bytes 227336 | tf_op jit(solution)/shard_map/ppermute | solution.py:712
  18.7 0.0 collective-permute-done.4.refs_13_
  18.7 0.0 collective-permute-done.5.refs_14_
  18.7 0.0 collective-permute-done.6.refs_15_
  18.7 0.9 %collective-permute-done.7.refs_16_ = f32[37,4,128]{2,1,0:T(4,128)S(1)} collective-permute-done((f32[37,4,128]{2,1,0:T(4,128)S(1)}, f32[37,4,128]{2,1,0:T(4,128)S(1)}, u32[]{:S(2)}, u32[]{:S(2)}) %collective-permute-start.7) | collective-permute-done | bytes 75808 | tf_op jit(solution)/shard_map/ppermute | solution.py:712
  19.6 2.3 %shard_map.68 = (f32[24,24,128]{2,1,0:T(8,128)S(1)}, f32[24,24,128]{2,1,0:T(8,128)S(1)}, f32[24,24,128]{2,1,0:T(8,128)S(1)}, f32[24,24,128]{2,1,0:T(8,128)S(1)},...) custom-call(s32[1]{0:T(128)} %bitcast.where_ref, ...), custom_call_target="tpu_custom_call", output_to_operand_aliasing={{0}: (2, {}), {1}: (3, {}), {2}: (4, {}), {3}: (5, {}), {4}... | custom-call | bytes 14400000 | tf_op jit(solution)/shard_map/pallas_call | solution.py:683
  21.9 0.3 collective-permute-start.8
  22.2 0.2 collective-permute-start.9
  22.4 3.5 %collective-permute-start.10 = (f32[5,8,4,128]{3,2,1,0:T(4,128)S(1)}, f32[5,8,4,128]{3,2,1,0:T(4,128)S(1)}, u32[]{:S(2)}, u32[]{:S(2)}) collective-permute-start(f32[5,8,4,128]{3,2,1,0:T(4,128)S(1)} %get-tuple-element.74), channel_id=1, source_target_pairs={{0,4},{4,0},{8,12},{12,8},{1,5},{5,1},{9,13},{13,9},{2,6},{6,2},{1... | collective-permute-start | bytes 245768 | tf_op jit(solution)/shard_map/ppermute | solution.py:712
  26.0 1.1 %collective-permute-start.11 = (f32[15,4,128]{2,1,0:T(4,128)S(1)}, f32[15,4,128]{2,1,0:T(4,128)S(1)}, u32[]{:S(2)}, u32[]{:S(2)}) collective-permute-start(f32[15,4,128]{2,1,0:T(4,128)S(1)} %get-tuple-element.75), channel_id=1, source_target_pairs={{0,20},{4,16},{8,28},{12,24},{16,4},{20,0},{24,12},{28,8},{1,21},{... | collective-permute-start | bytes 92168 | tf_op jit(solution)/shard_map/ppermute | solution.py:737
  27.1 0.0 collective-permute-start.12
  27.1 2.2 %collective-permute-done.11.refs_3_ = f32[15,4,128]{2,1,0:T(4,128)S(1)} collective-permute-done((f32[15,4,128]{2,1,0:T(4,128)S(1)}, f32[15,4,128]{2,1,0:T(4,128)S(1)}, u32[]{:S(2)}, u32[]{:S(2)}) %collective-permute-start.11) | collective-permute-done | bytes 30752 | tf_op jit(solution)/shard_map/ppermute | solution.py:737
  29.3 2.0 %collective-permute-done.12.refs_4_ = f32[15,4,128]{2,1,0:T(4,128)S(1)} collective-permute-done((f32[15,4,128]{2,1,0:T(4,128)S(1)}, f32[15,4,128]{2,1,0:T(4,128)S(1)}, u32[]{:S(2)}, u32[]{:S(2)}) %collective-permute-start.12) | collective-permute-done | bytes 30752 | tf_op jit(solution)/shard_map/ppermute | solution.py:737
  31.3 0.0 collective-permute-done.9.refs_1_
  31.3 0.0 collective-permute-done.10.refs_2_
  31.3 0.5 shard_map.69
  31.8 14.6 %all_to_all.5.gathered = f32[32,5,4,128]{3,2,1,0:T(4,128)S(1)} all-to-all(f32[32,5,4,128]{3,2,1,0:T(4,128)S(1)} %get-tuple-element.77), channel_id=1, replica_groups=mesh['gx'=2,'gy'=4,'gz'=4] {'gx','gy','gz'}, dimensions={0} | all-to-all | bytes 655360 | tf_op jit(solution)/shard_map/all_to_all | solution.py:819
  46.4 4.0 %shard_map.70 = f32[16,16,128]{2,1,0:T(8,128)} custom-call(s32[1]{0:T(128)} %bitcast.where_ref, f32[32,5,4,128]{3,2,1,0:T(4,128)S(1)} %all_to_all.5.gathered, f32[6,16,16,128]{3,2,1,0:T(8,128)S(1)} %get-tuple-element.78.level1, f32[24,24,128]{2,1,0:T(8,128)S(1)} %get-tuple-element.79.refs_0_, f32[24,24,128]{2,1,0:T(8,128)S(1)} %get-tuple-element.80.refs_1_, ...), custom_call_target="tpu_custom_call" | custom-call | bytes 14400000 | tf_op jit(solution)/shard_map/pallas_call | solution.py:683
  (14 shorter events, 0.0 us)
Async XLA Ops:
  0.0 10.8 %copy-start.1 = (f32[16,16,128]{2,1,0:T(8,128)S(1)}, f32[16,16,128]{2,1,0:T(8,128)}, u32[]{:S(2)}) copy-start(f32[16,16,128]{2,1,0:T(8,128)} %refs_1_.3) | copy-start | bytes 393220
  0.0 10.8 %copy-start.2 = (f32[16,16,128]{2,1,0:T(8,128)S(1)}, f32[16,16,128]{2,1,0:T(8,128)}, u32[]{:S(2)}) copy-start(f32[16,16,128]{2,1,0:T(8,128)} %refs_2_.3) | copy-start | bytes 393220
  0.0 10.8 %copy-start.3 = (f32[16,16,128]{2,1,0:T(8,128)S(1)}, f32[16,16,128]{2,1,0:T(8,128)}, u32[]{:S(2)}) copy-start(f32[16,16,128]{2,1,0:T(8,128)} %refs_3_.3) | copy-start | bytes 393220
  0.0 10.8 %copy-start.4 = (f32[16,16,128]{2,1,0:T(8,128)S(1)}, f32[16,16,128]{2,1,0:T(8,128)}, u32[]{:S(2)}) copy-start(f32[16,16,128]{2,1,0:T(8,128)} %refs_4_.3) | copy-start | bytes 393220
  0.0 10.8 %copy-start.5 = (f32[16,16,128]{2,1,0:T(8,128)S(1)}, f32[16,16,128]{2,1,0:T(8,128)}, u32[]{:S(2)}) copy-start(f32[16,16,128]{2,1,0:T(8,128)} %refs_5_.3) | copy-start | bytes 393220
  2.6 8.2 %copy-start = (f32[16,16,128]{2,1,0:T(8,128)S(1)}, f32[16,16,128]{2,1,0:T(8,128)}, u32[]{:S(2)}) copy-start(f32[16,16,128]{2,1,0:T(8,128)} %refs_0_.3) | copy-start | bytes 393220
  2.6 8.2 %collective-permute-start.2 = (f32[6,4,16,128]{3,2,1,0:T(8,128)}, f32[6,4,16,128]{3,2,1,0:T(8,128)S(1)}, u32[]{:S(2)}, u32[]{:S(2)}) collective-permute-start(f32[6,4,16,128]{3,2,1,0:T(8,128)} %get-tuple-element.51), channel_id=1, source_target_pairs={{0,16},{16,0},{1,17},{17,1},{2,18},{18,2},{3,19},{19,3},{4,20},{20... | collective-permute-start | bytes 589832 | tf_op jit(solution)/shard_map/ppermute | solution.py:712
  4.7 14.0 %collective-permute-start.4 = (f32[6,16,4,128]{3,2,1,0:T(4,128)}, f32[6,16,4,128]{3,2,1,0:T(4,128)S(1)}, u32[]{:S(2)}, u32[]{:S(2)}) collective-permute-start(f32[6,16,4,128]{3,2,1,0:T(4,128)} %get-tuple-element.65), channel_id=1, source_target_pairs={{0,12},{4,8},{8,4},{12,0},{1,13},{5,9},{9,5},{13,1},{2,14},{6,10},... | collective-permute-start | bytes 589832 | tf_op jit(solution)/shard_map/ppermute | solution.py:712
  6.8 11.9 %collective-permute-start.5 = (f32[6,16,4,128]{3,2,1,0:T(4,128)}, f32[6,16,4,128]{3,2,1,0:T(4,128)S(1)}, u32[]{:S(2)}, u32[]{:S(2)}) collective-permute-start(f32[6,16,4,128]{3,2,1,0:T(4,128)} %get-tuple-element.66), channel_id=1, source_target_pairs={{0,4},{4,0},{8,12},{12,8},{1,5},{5,1},{9,13},{13,9},{2,6},{6,2},{1... | collective-permute-start | bytes 589832 | tf_op jit(solution)/shard_map/ppermute | solution.py:712
  6.8 3.6 %collective-permute-start = (f32[8,16,128]{2,1,0:T(8,128)}, f32[8,16,128]{2,1,0:T(8,128)S(1)}, u32[]{:S(2)}, u32[]{:S(2)}) collective-permute-start(f32[8,16,128]{2,1,0:T(8,128)} %get-tuple-element.48), channel_id=1, source_target_pairs={{0,1},{1,0},{2,3},{3,2},{4,5},{5,4},{6,7},{7,6},{8,9},{9,8},{10,11... | collective-permute-start | bytes 196616 | tf_op jit(solution)/shard_map/ppermute | solution.py:712
  8.1 2.3 %collective-permute-start.1 = (f32[8,16,128]{2,1,0:T(8,128)}, f32[8,16,128]{2,1,0:T(8,128)S(1)}, u32[]{:S(2)}, u32[]{:S(2)}) collective-permute-start(f32[8,16,128]{2,1,0:T(8,128)} %get-tuple-element.49), channel_id=1, source_target_pairs={{0,4},{1,2},{2,1},{3,7},{4,0},{5,6},{6,5},{7,3},{8,12},{9,10},{10,... | collective-permute-start | bytes 196616 | tf_op jit(solution)/shard_map/ppermute | solution.py:723
  10.5 2.8 %collective-permute-start.3 = (f32[4,16,128]{2,1,0:T(8,128)S(1)}, f32[4,16,128]{2,1,0:T(8,128)S(1)}, u32[]{:S(2)}, u32[]{:S(2)}) collective-permute-start(f32[4,16,128]{2,1,0:T(8,128)S(1)} %get-tuple-element.64), channel_id=1, source_target_pairs={{0,16},{16,0},{1,17},{17,1},{2,18},{18,2},{3,19},{19,3},{4,20},{20... | collective-permute-start | bytes 98312 | tf_op jit(solution)/shard_map/ppermute | solution.py:712
  13.4 5.3 %collective-permute-start.6 = (f32[37,4,128]{2,1,0:T(4,128)S(1)}, f32[37,4,128]{2,1,0:T(4,128)S(1)}, u32[]{:S(2)}, u32[]{:S(2)}) collective-permute-start(f32[37,4,128]{2,1,0:T(4,128)S(1)} %get-tuple-element.68), channel_id=1, source_target_pairs={{0,1},{4,8},{8,4},{12,13},{1,0},{5,9},{9,5},{13,12},{2,3},{6,10},{... | collective-permute-start | bytes 227336 | tf_op jit(solution)/shard_map/ppermute | solution.py:723
  16.1 3.5 %collective-permute-start.7 = (f32[37,4,128]{2,1,0:T(4,128)S(1)}, f32[37,4,128]{2,1,0:T(4,128)S(1)}, u32[]{:S(2)}, u32[]{:S(2)}) collective-permute-start(f32[37,4,128]{2,1,0:T(4,128)S(1)} %get-tuple-element.69), channel_id=1, source_target_pairs={{0,4},{4,0},{8,12},{12,8},{1,5},{5,1},{9,13},{13,9},{2,6},{6,2},{1... | collective-permute-start | bytes 227336 | tf_op jit(solution)/shard_map/ppermute | solution.py:712
  21.9 9.4 %collective-permute-start.8 = (f32[5,4,8,128]{3,2,1,0:T(8,128)S(1)}, f32[5,4,8,128]{3,2,1,0:T(8,128)S(1)}, u32[]{:S(2)}, u32[]{:S(2)}) collective-permute-start(f32[5,4,8,128]{3,2,1,0:T(8,128)S(1)} %get-tuple-element.72), channel_id=1, source_target_pairs={{0,16},{16,0},{1,17},{17,1},{2,18},{18,2},{3,19},{19,3},{4,20},{20... | collective-permute-start | bytes 245768 | tf_op jit(solution)/shard_map/ppermute | solution.py:712
  22.2 9.1 %collective-permute-start.9 = (f32[5,8,4,128]{3,2,1,0:T(4,128)S(1)}, f32[5,8,4,128]{3,2,1,0:T(4,128)S(1)}, u32[]{:S(2)}, u32[]{:S(2)}) collective-permute-start(f32[5,8,4,128]{3,2,1,0:T(4,128)S(1)} %get-tuple-element.73), channel_id=1, source_target_pairs={{0,1},{4,8},{8,4},{12,13},{1,0},{5,9},{9,5},{13,12},{2,3},{6,10},{... | collective-permute-start | bytes 245768 | tf_op jit(solution)/shard_map/ppermute | solution.py:723
  22.4 8.9 %collective-permute-start.10 = (f32[5,8,4,128]{3,2,1,0:T(4,128)S(1)}, f32[5,8,4,128]{3,2,1,0:T(4,128)S(1)}, u32[]{:S(2)}, u32[]{:S(2)}) collective-permute-start(f32[5,8,4,128]{3,2,1,0:T(4,128)S(1)} %get-tuple-element.74), channel_id=1, source_target_pairs={{0,4},{4,0},{8,12},{12,8},{1,5},{5,1},{9,13},{13,9},{2,6},{6,2},{1... | collective-permute-start | bytes 245768 | tf_op jit(solution)/shard_map/ppermute | solution.py:712
  26.0 3.3 %collective-permute-start.11 = (f32[15,4,128]{2,1,0:T(4,128)S(1)}, f32[15,4,128]{2,1,0:T(4,128)S(1)}, u32[]{:S(2)}, u32[]{:S(2)}) collective-permute-start(f32[15,4,128]{2,1,0:T(4,128)S(1)} %get-tuple-element.75), channel_id=1, source_target_pairs={{0,20},{4,16},{8,28},{12,24},{16,4},{20,0},{24,12},{28,8},{1,21},{... | collective-permute-start | bytes 92168 | tf_op jit(solution)/shard_map/ppermute | solution.py:737
  27.1 4.2 %collective-permute-start.12 = (f32[15,4,128]{2,1,0:T(4,128)S(1)}, f32[15,4,128]{2,1,0:T(4,128)S(1)}, u32[]{:S(2)}, u32[]{:S(2)}) collective-permute-start(f32[15,4,128]{2,1,0:T(4,128)S(1)} %get-tuple-element.76), channel_id=1, source_target_pairs={{0,16},{4,24},{8,20},{12,28},{16,0},{20,8},{24,4},{28,12},{1,17},{... | collective-permute-start | bytes 92168 | tf_op jit(solution)/shard_map/ppermute | solution.py:737

commit v18 on v17

--- a/solution.py
+++ b/solution.py
@@ -169,6 +169,42 @@
                 ]
             )
     return sends
+
+
+def halo_lanes(n):
+    return SIDE + 2 * NEAR * n
+
+
+def pack_level1(values):
+    lane = lane_of(values[0].shape)
+    axis = values[0].ndim - 1
+    packs = [
+        jnp.where(lane < SIDE, values[0], turn(values[1], SIDE, axis)),
+        jnp.where(lane < SIDE, values[2], turn(values[3], SIDE, axis)),
+    ]
+    last = jnp.where(lane < SIDE, values[4], 0.0)
+    for n, array in enumerate(values):
+        at = halo_lanes(n)
+        right = turn(array, at - SIDE, axis)
+        left = turn(array, at + 2 * NEAR, axis)
+        last = jnp.where((lane >= at) & (lane < at + NEAR), right, last)
+        last = jnp.where((lane >= at + NEAR) & (lane < at + 2 * NEAR), left, last)
+    return packs + [last]
+
+
+def unpack_level1(packs):
+    first, second, last = packs
+    lane = lane_of(first.shape)
+    axis = first.ndim - 1
+    blocks = (first, turn(first, SIDE, axis), second, turn(second, SIDE, axis), last)
+    values = []
+    for n, block in enumerate(blocks):
+        at = halo_lanes(n)
+        right = turn(last, SIDE - at, axis)
+        left = turn(last, -at - 2 * NEAR, axis)
+        halo = jnp.where(lane < SIDE + NEAR, right, jnp.where(lane >= LANES - NEAR, left, 0.0))
+        values.append(jnp.where(lane < SIDE, block, halo))
+    return values
 
 
 def diagonal_tiles(first, second, third):
@@ -417,7 +453,8 @@
         sums[2, 1:, :, lanes] = jnp.zeros((x1 - 1, y1, LANES), F32)
     rhs1, low_y, low_x = to_level1(sums, 0, 3, pair_table(2 * LANES, LANES, False), 0.0625)
     weight1 = relaxer(coeffs1[0], coeffs1[1] + low_y + low_x)
-    for n, values in enumerate((2.0 * rhs1, weight1, coeffs1[2], coeffs1[3], coeffs1[4])):
+    packed = pack_level1((2.0 * rhs1, weight1, coeffs1[2], coeffs1[3], coeffs1[4]))
+    for n, values in enumerate(packed):
         own1[n] = values
         for send, face in zip(sends, faces_x(values[None], at_x % 2, n_x, NEAR)):
             send[n] = face[0]
@@ -472,6 +509,7 @@
         )
         block = jnp.concatenate([below, ring[a], above], axis=0)
         whole.append(jnp.concatenate([block, rows], axis=1))
+    whole = unpack_level1(whole)
     rhs1, weight1 = whole[:2]
     faces1 = tuple(whole[2:])
     field1 = weight1 * rhs1
@@ -488,7 +526,7 @@
     shift = position(where_ref)[2] % blocks * (LANES // blocks)
     slots = [pltpu.roll(values, shift, 1) for values in [packed] + [coarse2[a] for a in range(4)]]
     for d in range(devices):
-        for a in range(n):
+        for a in range(5):
             copies[d, a] = slots[a]
 
 
@@ -788,10 +826,10 @@
     outs = run(
         functools.partial(down_kernel, counts),
         [fine] * 12
-        + [(5, x1, y1, LANES)]
-        + [(5, NEAR, y1, LANES)] * n_x
-        + [(5, x1, NEAR, LANES)] * 2
-        + [(15, NEAR, LANES)] * (2 * n_x)
+        + [(3, x1, y1, LANES)]
+        + [(3, NEAR, y1, LANES)] * n_x
+        + [(3, x1, NEAR, LANES)] * 2
+        + [(9, NEAR, LANES)] * (2 * n_x)
         + [fine] * 4,
         where,
         (zpack,) + tuple(laid) + halos_x + main_y + rest_y + (coeffs1,),

time: 50.5 us -> 50.7 us (level)
  no operation moved by 1% of the time
where the time goes in v18:
time: 50.7 us; the launch traced here: 50.5 us
  starting transfers between devices  17 us (34%)
  blocking collectives  14.6 us (29%)
  Pallas kernels  10.5 us (21%)
  waiting for transfers between devices  8.29 us (16%)
    all_to_all x1, blocking collectives, local(): gathered = lax.all_to_all(copies, axes, 0, 0, tiled=True)  14.6 us
    ppermute x8, starting transfers between devices, swaps(): got.append(lax.ppermute(block, axis, list(enumerate(partner))))  12.2 us
    pallas_call x7, Pallas kernels, run(): pl.pallas_call(kernel, out_shape=tuple((jax.ShapeDtypeStruct(shape, F32)...  10.5 us
    ppermute x8, waiting for transfers between devices, swaps(): got.append(lax.ppermute(block, axis, list(enumerate(partner))))  4.2 us
    ppermute x2, waiting for transfers between devices, diagonal_swaps(): got.append(lax.ppermute(block, ('gx', 'gy'), pairs))  4.08 us
    ppermute x3, starting transfers between devices, swaps(): got.append(lax.ppermute(block, tuple(sorted((axis, other))), pairs))  3.68 us
    ppermute x2, starting transfers between devices, diagonal_swaps(): got.append(lax.ppermute(block, ('gx', 'gy'), pairs))  1.1 us
  transfers between devices with their start and end apart: 13, of which 5 were waited for; matrix products, arithmetic and copies ran while one was open for 0% of the time, Pallas kernels for 2%

profile of v18, /device:TPU:1, one launch (start us, length us, event | category | flops | bytes accessed | tf_op | source)
XLA Modules:
  0.0 50.5 jit_solution(18261850751611114397)
XLA Ops:
  0.0 2.6 %shard_map.64 = (f32[6,4,16,128]{3,2,1,0:T(8,128)}, f32[6,16,4,128]{3,2,1,0:T(4,128)}, f32[6,16,4,128]{3,2,1,0:T(4,128)}, f32[8,16,128]{2,1,0:T(8,128)}, f32[8,16,128]{2,1,0:T(8,128)}) custom-call(s32[1]{0:T(128)} %bitcast.where_ref, f32[16,16,128]{2,1,0:T(8,128)} %refs_0_.3, f32[16,16,128]{2,1,0:T(8,128)} %refs_1_.3, f32[16,16,128]{2,1,0:T(8,128)} %refs_2_.3, ...), custom_call_target="tpu_custom_call" | custom-call | bytes 3600000 | tf_op jit(solution)/shard_map/pallas_call | solution.py:721
  2.6 2.0 %collective-permute-start.2 = (f32[6,4,16,128]{3,2,1,0:T(8,128)}, f32[6,4,16,128]{3,2,1,0:T(8,128)S(1)}, u32[]{:S(2)}, u32[]{:S(2)}) collective-permute-start(f32[6,4,16,128]{3,2,1,0:T(8,128)} %get-tuple-element.51), channel_id=1, source_target_pairs={{0,16},{16,0},{1,17},{17,1},{2,18},{18,2},{3,19},{19,3},{4,20},{20... | collective-permute-start | bytes 589832 | tf_op jit(solution)/shard_map/ppermute | solution.py:750
  4.7 2.1 %collective-permute-start.4 = (f32[6,16,4,128]{3,2,1,0:T(4,128)}, f32[6,16,4,128]{3,2,1,0:T(4,128)S(1)}, u32[]{:S(2)}, u32[]{:S(2)}) collective-permute-start(f32[6,16,4,128]{3,2,1,0:T(4,128)} %get-tuple-element.65), channel_id=1, source_target_pairs={{0,12},{4,8},{8,4},{12,0},{1,13},{5,9},{9,5},{13,1},{2,14},{6,10},... | collective-permute-start | bytes 589832 | tf_op jit(solution)/shard_map/ppermute | solution.py:750
  6.8 0.0 collective-permute-start.5
  6.8 1.3 %collective-permute-start = (f32[8,16,128]{2,1,0:T(8,128)}, f32[8,16,128]{2,1,0:T(8,128)S(1)}, u32[]{:S(2)}, u32[]{:S(2)}) collective-permute-start(f32[8,16,128]{2,1,0:T(8,128)} %get-tuple-element.48), channel_id=1, source_target_pairs={{0,1},{1,0},{2,3},{3,2},{4,5},{5,4},{6,7},{7,6},{8,9},{9,8},{10,11... | collective-permute-start | bytes 196616 | tf_op jit(solution)/shard_map/ppermute | solution.py:750
  8.1 0.8 %collective-permute-start.1 = (f32[8,16,128]{2,1,0:T(8,128)}, f32[8,16,128]{2,1,0:T(8,128)S(1)}, u32[]{:S(2)}, u32[]{:S(2)}) collective-permute-start(f32[8,16,128]{2,1,0:T(8,128)} %get-tuple-element.49), channel_id=1, source_target_pairs={{0,4},{1,2},{2,1},{3,7},{4,0},{5,6},{6,5},{7,3},{8,12},{9,10},{10,... | collective-permute-start | bytes 196616 | tf_op jit(solution)/shard_map/ppermute | solution.py:761
  8.8 1.5 %collective-permute-done.one_ref = f32[8,16,128]{2,1,0:T(8,128)S(1)} collective-permute-done((f32[8,16,128]{2,1,0:T(8,128)}, f32[8,16,128]{2,1,0:T(8,128)S(1)}, u32[]{:S(2)}, u32[]{:S(2)}) %collective-permute-start) | collective-permute-done | bytes 65568 | tf_op jit(solution)/shard_map/ppermute | solution.py:750
  10.4 0.0 collective-permute-done.1.two_ref
  10.4 0.1 shard_map.65
  10.5 0.3 collective-permute-start.3
  10.8 0.0 collective-permute-done.2.refs_7_.refs_0_
  10.9 0.7 %shard_map.66 = (f32[24,24,128]{2,1,0:T(8,128)S(1)}, f32[24,24,128]{2,1,0:T(8,128)S(1)}, f32[24,24,128]{2,1,0:T(8,128)S(1)}, f32[24,24,128]{2,1,0:T(8,128)S(1)},...) custom-call(s32[1]{0:T(128)} %bitcast.where_ref, ...), custom_call_target="tpu_custom_call" | custom-call | bytes 7200000 | tf_op jit(solution)/shard_map/pallas_call | solution.py:721
  11.6 1.7 %collective-permute-done.3.refs_1_.refs_12_ = f32[4,16,128]{2,1,0:T(8,128)S(1)} collective-permute-done((f32[4,16,128]{2,1,0:T(8,128)S(1)}, f32[4,16,128]{2,1,0:T(8,128)S(1)}, u32[]{:S(2)}, u32[]{:S(2)}) %collective-permute-start.3) | collective-permute-done | bytes 32800 | tf_op jit(solution)/shard_map/ppermute | solution.py:750
  13.3 0.1 shard_map.67
  13.4 2.7 %collective-permute-start.6 = (f32[37,4,128]{2,1,0:T(4,128)S(1)}, f32[37,4,128]{2,1,0:T(4,128)S(1)}, u32[]{:S(2)}, u32[]{:S(2)}) collective-permute-start(f32[37,4,128]{2,1,0:T(4,128)S(1)} %get-tuple-element.68), channel_id=1, source_target_pairs={{0,1},{4,8},{8,4},{12,13},{1,0},{5,9},{9,5},{13,12},{2,3},{6,10},{... | collective-permute-start | bytes 227336 | tf_op jit(solution)/shard_map/ppermute | solution.py:761
  16.1 2.6 %collective-permute-start.7 = (f32[37,4,128]{2,1,0:T(4,128)S(1)}, f32[37,4,128]{2,1,0:T(4,128)S(1)}, u32[]{:S(2)}, u32[]{:S(2)}) collective-permute-start(f32[37,4,128]{2,1,0:T(4,128)S(1)} %get-tuple-element.69), channel_id=1, source_target_pairs={{0,4},{4,0},{8,12},{12,8},{1,5},{5,1},{9,13},{13,9},{2,6},{6,2},{1... | collective-permute-start | bytes 227336 | tf_op jit(solution)/shard_map/ppermute | solution.py:750
  18.7 0.0 collective-permute-done.4.refs_13_
  18.7 0.0 collective-permute-done.5.refs_14_
  18.7 0.0 collective-permute-done.6.refs_15_
  18.7 0.9 %collective-permute-done.7.refs_16_ = f32[37,4,128]{2,1,0:T(4,128)S(1)} collective-permute-done((f32[37,4,128]{2,1,0:T(4,128)S(1)}, f32[37,4,128]{2,1,0:T(4,128)S(1)}, u32[]{:S(2)}, u32[]{:S(2)}) %collective-permute-start.7) | collective-permute-done | bytes 75808 | tf_op jit(solution)/shard_map/ppermute | solution.py:750
  19.6 2.4 %shard_map.68 = (f32[24,24,128]{2,1,0:T(8,128)S(1)}, f32[24,24,128]{2,1,0:T(8,128)S(1)}, f32[24,24,128]{2,1,0:T(8,128)S(1)}, f32[24,24,128]{2,1,0:T(8,128)S(1)},...) custom-call(s32[1]{0:T(128)} %bitcast.where_ref, ...), custom_call_target="tpu_custom_call", output_to_operand_aliasing={{0}: (2, {}), {1}: (3, {}), {2}: (4, {}), {3}: (5, {}), {4}... | custom-call | bytes 14400000 | tf_op jit(solution)/shard_map/pallas_call | solution.py:721
  22.0 0.3 collective-permute-start.8
  22.3 0.2 collective-permute-start.9
  22.5 3.5 %collective-permute-start.10 = (f32[3,8,4,128]{3,2,1,0:T(4,128)S(1)}, f32[3,8,4,128]{3,2,1,0:T(4,128)S(1)}, u32[]{:S(2)}, u32[]{:S(2)}) collective-permute-start(f32[3,8,4,128]{3,2,1,0:T(4,128)S(1)} %get-tuple-element.74), channel_id=1, source_target_pairs={{0,4},{4,0},{8,12},{12,8},{1,5},{5,1},{9,13},{13,9},{2,6},{6,2},{1... | collective-permute-start | bytes 147464 | tf_op jit(solution)/shard_map/ppermute | solution.py:750
  26.0 1.1 %collective-permute-start.11 = (f32[9,4,128]{2,1,0:T(4,128)S(1)}, f32[9,4,128]{2,1,0:T(4,128)S(1)}, u32[]{:S(2)}, u32[]{:S(2)}) collective-permute-start(f32[9,4,128]{2,1,0:T(4,128)S(1)} %get-tuple-element.75), channel_id=1, source_target_pairs={{0,20},{4,16},{8,28},{12,24},{16,4},{20,0},{24,12},{28,8},{1,21},{... | collective-permute-start | bytes 55304 | tf_op jit(solution)/shard_map/ppermute | solution.py:775
  27.1 0.0 collective-permute-start.12
  27.1 2.1 %collective-permute-done.11.refs_3_ = f32[9,4,128]{2,1,0:T(4,128)S(1)} collective-permute-done((f32[9,4,128]{2,1,0:T(4,128)S(1)}, f32[9,4,128]{2,1,0:T(4,128)S(1)}, u32[]{:S(2)}, u32[]{:S(2)}) %collective-permute-start.11) | collective-permute-done | bytes 18464 | tf_op jit(solution)/shard_map/ppermute | solution.py:775
  29.2 2.0 %collective-permute-done.12.refs_4_ = f32[9,4,128]{2,1,0:T(4,128)S(1)} collective-permute-done((f32[9,4,128]{2,1,0:T(4,128)S(1)}, f32[9,4,128]{2,1,0:T(4,128)S(1)}, u32[]{:S(2)}, u32[]{:S(2)}) %collective-permute-start.12) | collective-permute-done | bytes 18464 | tf_op jit(solution)/shard_map/ppermute | solution.py:775
  31.2 0.0 collective-permute-done.8.refs_0_
  31.2 0.8 %shard_map.69 = (f32[32,5,4,128]{3,2,1,0:T(4,128)S(1)}, f32[6,16,16,128]{3,2,1,0:T(8,128)S(1)}) custom-call(s32[1]{0:T(128)} %bitcast.where_ref, f32[3,8,8,128]{3,2,1,0:T(8,128)S(1)} %get-tuple-element.71.ring, f32[3,4,8,128]{3,2,1,0:T(8,128)S(1)} %collective-permute-done.8.refs_0_, f32[3,8,4,128]{3,2,1,0:T(4,128)S(1)} %collective-permute-done.9.refs_1_, ...), custom_call_target="tpu_custom_call" | custom-call | bytes 3600000 | tf_op jit(solution)/shard_map/pallas_call | solution.py:721
  32.0 14.6 %all_to_all.5.gathered = f32[32,5,4,128]{3,2,1,0:T(4,128)S(1)} all-to-all(f32[32,5,4,128]{3,2,1,0:T(4,128)S(1)} %get-tuple-element.77), channel_id=1, replica_groups=mesh['gx'=2,'gy'=4,'gz'=4] {'gx','gy','gz'}, dimensions={0} | all-to-all | bytes 655360 | tf_op jit(solution)/shard_map/all_to_all | solution.py:857
  46.6 3.9 %shard_map.70 = f32[16,16,128]{2,1,0:T(8,128)} custom-call(s32[1]{0:T(128)} %bitcast.where_ref, f32[32,5,4,128]{3,2,1,0:T(4,128)S(1)} %all_to_all.5.gathered, f32[6,16,16,128]{3,2,1,0:T(8,128)S(1)} %get-tuple-element.78.level1, f32[24,24,128]{2,1,0:T(8,128)S(1)} %get-tuple-element.79.refs_0_, f32[24,24,128]{2,1,0:T(8,128)S(1)} %get-tuple-element.80.refs_1_, ...), custom_call_target="tpu_custom_call" | custom-call | bytes 14400000 | tf_op jit(solution)/shard_map/pallas_call | solution.py:721
  (14 shorter events, 0.0 us)
Async XLA Ops:
  0.0 10.8 %copy-start.1 = (f32[16,16,128]{2,1,0:T(8,128)S(1)}, f32[16,16,128]{2,1,0:T(8,128)}, u32[]{:S(2)}) copy-start(f32[16,16,128]{2,1,0:T(8,128)} %refs_1_.3) | copy-start | bytes 393220
  0.0 10.8 %copy-start.2 = (f32[16,16,128]{2,1,0:T(8,128)S(1)}, f32[16,16,128]{2,1,0:T(8,128)}, u32[]{:S(2)}) copy-start(f32[16,16,128]{2,1,0:T(8,128)} %refs_2_.3) | copy-start | bytes 393220
  0.0 10.8 %copy-start.3 = (f32[16,16,128]{2,1,0:T(8,128)S(1)}, f32[16,16,128]{2,1,0:T(8,128)}, u32[]{:S(2)}) copy-start(f32[16,16,128]{2,1,0:T(8,128)} %refs_3_.3) | copy-start | bytes 393220
  0.0 10.8 %copy-start.4 = (f32[16,16,128]{2,1,0:T(8,128)S(1)}, f32[16,16,128]{2,1,0:T(8,128)}, u32[]{:S(2)}) copy-start(f32[16,16,128]{2,1,0:T(8,128)} %refs_4_.3) | copy-start | bytes 393220
  0.0 10.8 %copy-start.5 = (f32[16,16,128]{2,1,0:T(8,128)S(1)}, f32[16,16,128]{2,1,0:T(8,128)}, u32[]{:S(2)}) copy-start(f32[16,16,128]{2,1,0:T(8,128)} %refs_5_.3) | copy-start | bytes 393220
  2.6 8.2 %copy-start = (f32[16,16,128]{2,1,0:T(8,128)S(1)}, f32[16,16,128]{2,1,0:T(8,128)}, u32[]{:S(2)}) copy-start(f32[16,16,128]{2,1,0:T(8,128)} %refs_0_.3) | copy-start | bytes 393220
  2.6 8.2 %collective-permute-start.2 = (f32[6,4,16,128]{3,2,1,0:T(8,128)}, f32[6,4,16,128]{3,2,1,0:T(8,128)S(1)}, u32[]{:S(2)}, u32[]{:S(2)}) collective-permute-start(f32[6,4,16,128]{3,2,1,0:T(8,128)} %get-tuple-element.51), channel_id=1, source_target_pairs={{0,16},{16,0},{1,17},{17,1},{2,18},{18,2},{3,19},{19,3},{4,20},{20... | collective-permute-start | bytes 589832 | tf_op jit(solution)/shard_map/ppermute | solution.py:750
  4.7 14.0 %collective-permute-start.4 = (f32[6,16,4,128]{3,2,1,0:T(4,128)}, f32[6,16,4,128]{3,2,1,0:T(4,128)S(1)}, u32[]{:S(2)}, u32[]{:S(2)}) collective-permute-start(f32[6,16,4,128]{3,2,1,0:T(4,128)} %get-tuple-element.65), channel_id=1, source_target_pairs={{0,12},{4,8},{8,4},{12,0},{1,13},{5,9},{9,5},{13,1},{2,14},{6,10},... | collective-permute-start | bytes 589832 | tf_op jit(solution)/shard_map/ppermute | solution.py:750
  6.8 11.9 %collective-permute-start.5 = (f32[6,16,4,128]{3,2,1,0:T(4,128)}, f32[6,16,4,128]{3,2,1,0:T(4,128)S(1)}, u32[]{:S(2)}, u32[]{:S(2)}) collective-permute-start(f32[6,16,4,128]{3,2,1,0:T(4,128)} %get-tuple-element.66), channel_id=1, source_target_pairs={{0,4},{4,0},{8,12},{12,8},{1,5},{5,1},{9,13},{13,9},{2,6},{6,2},{1... | collective-permute-start | bytes 589832 | tf_op jit(solution)/shard_map/ppermute | solution.py:750
  6.8 3.6 %collective-permute-start = (f32[8,16,128]{2,1,0:T(8,128)}, f32[8,16,128]{2,1,0:T(8,128)S(1)}, u32[]{:S(2)}, u32[]{:S(2)}) collective-permute-start(f32[8,16,128]{2,1,0:T(8,128)} %get-tuple-element.48), channel_id=1, source_target_pairs={{0,1},{1,0},{2,3},{3,2},{4,5},{5,4},{6,7},{7,6},{8,9},{9,8},{10,11... | collective-permute-start | bytes 196616 | tf_op jit(solution)/shard_map/ppermute | solution.py:750
  8.1 2.3 %collective-permute-start.1 = (f32[8,16,128]{2,1,0:T(8,128)}, f32[8,16,128]{2,1,0:T(8,128)S(1)}, u32[]{:S(2)}, u32[]{:S(2)}) collective-permute-start(f32[8,16,128]{2,1,0:T(8,128)} %get-tuple-element.49), channel_id=1, source_target_pairs={{0,4},{1,2},{2,1},{3,7},{4,0},{5,6},{6,5},{7,3},{8,12},{9,10},{10,... | collective-permute-start | bytes 196616 | tf_op jit(solution)/shard_map/ppermute | solution.py:761
  10.5 2.8 %collective-permute-start.3 = (f32[4,16,128]{2,1,0:T(8,128)S(1)}, f32[4,16,128]{2,1,0:T(8,128)S(1)}, u32[]{:S(2)}, u32[]{:S(2)}) collective-permute-start(f32[4,16,128]{2,1,0:T(8,128)S(1)} %get-tuple-element.64), channel_id=1, source_target_pairs={{0,16},{16,0},{1,17},{17,1},{2,18},{18,2},{3,19},{19,3},{4,20},{20... | collective-permute-start | bytes 98312 | tf_op jit(solution)/shard_map/ppermute | solution.py:750
  13.4 5.3 %collective-permute-start.6 = (f32[37,4,128]{2,1,0:T(4,128)S(1)}, f32[37,4,128]{2,1,0:T(4,128)S(1)}, u32[]{:S(2)}, u32[]{:S(2)}) collective-permute-start(f32[37,4,128]{2,1,0:T(4,128)S(1)} %get-tuple-element.68), channel_id=1, source_target_pairs={{0,1},{4,8},{8,4},{12,13},{1,0},{5,9},{9,5},{13,12},{2,3},{6,10},{... | collective-permute-start | bytes 227336 | tf_op jit(solution)/shard_map/ppermute | solution.py:761
  16.1 3.5 %collective-permute-start.7 = (f32[37,4,128]{2,1,0:T(4,128)S(1)}, f32[37,4,128]{2,1,0:T(4,128)S(1)}, u32[]{:S(2)}, u32[]{:S(2)}) collective-permute-start(f32[37,4,128]{2,1,0:T(4,128)S(1)} %get-tuple-element.69), channel_id=1, source_target_pairs={{0,4},{4,0},{8,12},{12,8},{1,5},{5,1},{9,13},{13,9},{2,6},{6,2},{1... | collective-permute-start | bytes 227336 | tf_op jit(solution)/shard_map/ppermute | solution.py:750
  22.0 9.3 %collective-permute-start.8 = (f32[3,4,8,128]{3,2,1,0:T(8,128)S(1)}, f32[3,4,8,128]{3,2,1,0:T(8,128)S(1)}, u32[]{:S(2)}, u32[]{:S(2)}) collective-permute-start(f32[3,4,8,128]{3,2,1,0:T(8,128)S(1)} %get-tuple-element.72), channel_id=1, source_target_pairs={{0,16},{16,0},{1,17},{17,1},{2,18},{18,2},{3,19},{19,3},{4,20},{20... | collective-permute-start | bytes 147464 | tf_op jit(solution)/shard_map/ppermute | solution.py:750
  22.3 8.9 %collective-permute-start.9 = (f32[3,8,4,128]{3,2,1,0:T(4,128)S(1)}, f32[3,8,4,128]{3,2,1,0:T(4,128)S(1)}, u32[]{:S(2)}, u32[]{:S(2)}) collective-permute-start(f32[3,8,4,128]{3,2,1,0:T(4,128)S(1)} %get-tuple-element.73), channel_id=1, source_target_pairs={{0,1},{4,8},{8,4},{12,13},{1,0},{5,9},{9,5},{13,12},{2,3},{6,10},{... | collective-permute-start | bytes 147464 | tf_op jit(solution)/shard_map/ppermute | solution.py:761
  22.5 8.7 %collective-permute-start.10 = (f32[3,8,4,128]{3,2,1,0:T(4,128)S(1)}, f32[3,8,4,128]{3,2,1,0:T(4,128)S(1)}, u32[]{:S(2)}, u32[]{:S(2)}) collective-permute-start(f32[3,8,4,128]{3,2,1,0:T(4,128)S(1)} %get-tuple-element.74), channel_id=1, source_target_pairs={{0,4},{4,0},{8,12},{12,8},{1,5},{5,1},{9,13},{13,9},{2,6},{6,2},{1... | collective-permute-start | bytes 147464 | tf_op jit(solution)/shard_map/ppermute | solution.py:750
  26.0 3.2 %collective-permute-start.11 = (f32[9,4,128]{2,1,0:T(4,128)S(1)}, f32[9,4,128]{2,1,0:T(4,128)S(1)}, u32[]{:S(2)}, u32[]{:S(2)}) collective-permute-start(f32[9,4,128]{2,1,0:T(4,128)S(1)} %get-tuple-element.75), channel_id=1, source_target_pairs={{0,20},{4,16},{8,28},{12,24},{16,4},{20,0},{24,12},{28,8},{1,21},{... | collective-permute-start | bytes 55304 | tf_op jit(solution)/shard_map/ppermute | solution.py:775
  27.1 4.1 %collective-permute-start.12 = (f32[9,4,128]{2,1,0:T(4,128)S(1)}, f32[9,4,128]{2,1,0:T(4,128)S(1)}, u32[]{:S(2)}, u32[]{:S(2)}) collective-permute-start(f32[9,4,128]{2,1,0:T(4,128)S(1)} %get-tuple-element.76), channel_id=1, source_target_pairs={{0,16},{4,24},{8,20},{12,28},{16,0},{20,8},{24,4},{28,12},{1,17},{... | collective-permute-start | bytes 55304 | tf_op jit(solution)/shard_map/ppermute | solution.py:775

commit v19 on v17

--- a/solution.py
+++ b/solution.py
@@ -784,7 +784,7 @@
         where,
         (zpack,) + main_x + halos_x + (coarse2,),
     )
-    rest_y = tuple(swaps("gy", (one_y, two_y), "gz")[::-1])
+    rest_y = tuple(swaps("gy", (one_y, two_y), "gx")[::-1])
     outs = run(
         functools.partial(down_kernel, counts),
         [fine] * 12
@@ -806,7 +806,7 @@
     fine_arrays = tuple(fine_arrays) + tuple(laid[2:4]) + tuple(laid[6:])
 
     near_x = tuple(swaps("gx", sends_x, "gy"))
-    near_y = tuple(swaps("gy", (one_y, two_y), "gz")[::-1])
+    near_y = tuple(swaps("gy", (one_y, two_y))[::-1])
     near_xy = tuple(diagonal_swaps(sends_xy))
     copies, level1 = run(
         functools.partial(near_kernel, counts, devices),

time: 50.5 us -> 50.4 us (level)
  blocking collectives: 14.6 us -> 16.9 us
  starting transfers between devices: 17 us -> 15.3 us
  waiting for transfers between devices: 8.42 us -> 7.74 us
    ppermute x8 -> x9, starting transfers between devices: 12.2 us -> 8.97 us  [swaps(): got.append(lax.ppermute(block, axis, list(enumerate(partner))))]
    all_to_all x1, blocking collectives: 14.6 us -> 16.9 us  [local(): gathered = lax.all_to_all(copies, axes, 0, 0, tiled=True)]
    ppermute x2, starting transfers between devices: 1.1 us -> 2.81 us  [diagonal_swaps(): got.append(lax.ppermute(block, ('gx', 'gy'), pairs))]
    ppermute x3 -> x2, waiting for transfers between devices: 0.01 us -> 1.63 us  [swaps(): got.append(lax.ppermute(block, tuple(sorted((axis, other))), pairs))]
    ppermute x2, waiting for transfers between devices: 4.21 us -> 2.81 us  [diagonal_swaps(): got.append(lax.ppermute(block, ('gx', 'gy'), pairs))]
    ppermute x8 -> x9, waiting for transfers between devices: 4.2 us -> 3.3 us  [swaps(): got.append(lax.ppermute(block, axis, list(enumerate(partner))))]
    ppermute x3 -> x2, starting transfers between devices: 3.68 us -> 3.48 us  [swaps(): got.append(lax.ppermute(block, tuple(sorted((axis, other))), pairs))]
where the time goes in v19:
time: 50.4 us; the launch traced here: 50.3 us
  blocking collectives  16.9 us (34%)
  starting transfers between devices  15.3 us (30%)
  Pallas kernels  10.2 us (20%)
  waiting for transfers between devices  7.74 us (15%)
    all_to_all x1, blocking collectives, local(): gathered = lax.all_to_all(copies, axes, 0, 0, tiled=True)  16.9 us
    pallas_call x7, Pallas kernels, run(): pl.pallas_call(kernel, out_shape=tuple((jax.ShapeDtypeStruct(shape, F32)...  10.2 us
    ppermute x9, starting transfers between devices, swaps(): got.append(lax.ppermute(block, axis, list(enumerate(partner))))  8.97 us
    ppermute x2, starting transfers between devices, swaps(): got.append(lax.ppermute(block, tuple(sorted((axis, other))), pairs))  3.48 us
    ppermute x9, waiting for transfers between devices, swaps(): got.append(lax.ppermute(block, axis, list(enumerate(partner))))  3.3 us
    ppermute x2, starting transfers between devices, diagonal_swaps(): got.append(lax.ppermute(block, ('gx', 'gy'), pairs))  2.81 us
    ppermute x2, waiting for transfers between devices, diagonal_swaps(): got.append(lax.ppermute(block, ('gx', 'gy'), pairs))  2.81 us
    ppermute x2, waiting for transfers between devices, swaps(): got.append(lax.ppermute(block, tuple(sorted((axis, other))), pairs))  1.63 us
  transfers between devices with their start and end apart: 13, of which 5 were waited for; matrix products, arithmetic and copies ran while one was open for 0% of the time, Pallas kernels for 2%

profile of v19, /device:TPU:1, one launch (start us, length us, event | category | flops | bytes accessed | tf_op | source)
XLA Modules:
  0.0 50.3 jit_solution(4531213283204069105)
XLA Ops:
  0.0 2.6 %shard_map.64 = (f32[6,4,16,128]{3,2,1,0:T(8,128)}, f32[6,16,4,128]{3,2,1,0:T(4,128)}, f32[6,16,4,128]{3,2,1,0:T(4,128)}, f32[8,16,128]{2,1,0:T(8,128)}, f32[8,16,128]{2,1,0:T(8,128)}) custom-call(s32[1]{0:T(128)} %bitcast.where_ref, f32[16,16,128]{2,1,0:T(8,128)} %refs_0_.3, f32[16,16,128]{2,1,0:T(8,128)} %refs_1_.3, f32[16,16,128]{2,1,0:T(8,128)} %refs_2_.3, ...), custom_call_target="tpu_custom_call" | custom-call | bytes 3600000 | tf_op jit(solution)/shard_map/pallas_call | solution.py:683
  2.6 2.0 %collective-permute-start.2 = (f32[6,4,16,128]{3,2,1,0:T(8,128)}, f32[6,4,16,128]{3,2,1,0:T(8,128)S(1)}, u32[]{:S(2)}, u32[]{:S(2)}) collective-permute-start(f32[6,4,16,128]{3,2,1,0:T(8,128)} %get-tuple-element.51), channel_id=1, source_target_pairs={{0,16},{16,0},{1,17},{17,1},{2,18},{18,2},{3,19},{19,3},{4,20},{20... | collective-permute-start | bytes 589832 | tf_op jit(solution)/shard_map/ppermute | solution.py:712
  4.7 2.1 %collective-permute-start.4 = (f32[6,16,4,128]{3,2,1,0:T(4,128)}, f32[6,16,4,128]{3,2,1,0:T(4,128)S(1)}, u32[]{:S(2)}, u32[]{:S(2)}) collective-permute-start(f32[6,16,4,128]{3,2,1,0:T(4,128)} %get-tuple-element.65), channel_id=1, source_target_pairs={{0,12},{4,8},{8,4},{12,0},{1,13},{5,9},{9,5},{13,1},{2,14},{6,10},... | collective-permute-start | bytes 589832 | tf_op jit(solution)/shard_map/ppermute | solution.py:712
  6.8 0.0 collective-permute-start.5
  6.8 1.3 %collective-permute-start = (f32[8,16,128]{2,1,0:T(8,128)}, f32[8,16,128]{2,1,0:T(8,128)S(1)}, u32[]{:S(2)}, u32[]{:S(2)}) collective-permute-start(f32[8,16,128]{2,1,0:T(8,128)} %get-tuple-element.48), channel_id=1, source_target_pairs={{0,1},{1,0},{2,3},{3,2},{4,5},{5,4},{6,7},{7,6},{8,9},{9,8},{10,11... | collective-permute-start | bytes 196616 | tf_op jit(solution)/shard_map/ppermute | solution.py:712
  8.1 0.8 %collective-permute-start.1 = (f32[8,16,128]{2,1,0:T(8,128)}, f32[8,16,128]{2,1,0:T(8,128)S(1)}, u32[]{:S(2)}, u32[]{:S(2)}) collective-permute-start(f32[8,16,128]{2,1,0:T(8,128)} %get-tuple-element.49), channel_id=1, source_target_pairs={{0,4},{1,2},{2,1},{3,7},{4,0},{5,6},{6,5},{7,3},{8,12},{9,10},{10,... | collective-permute-start | bytes 196616 | tf_op jit(solution)/shard_map/ppermute | solution.py:723
  8.8 1.5 %collective-permute-done.one_ref = f32[8,16,128]{2,1,0:T(8,128)S(1)} collective-permute-done((f32[8,16,128]{2,1,0:T(8,128)}, f32[8,16,128]{2,1,0:T(8,128)S(1)}, u32[]{:S(2)}, u32[]{:S(2)}) %collective-permute-start) | collective-permute-done | bytes 65568 | tf_op jit(solution)/shard_map/ppermute | solution.py:712
  10.4 0.0 collective-permute-done.1.two_ref
  10.4 0.1 shard_map.65
  10.5 0.3 collective-permute-start.3
  10.8 0.0 collective-permute-done.2.refs_7_.refs_0_
  10.9 0.7 %shard_map.66 = (f32[24,24,128]{2,1,0:T(8,128)S(1)}, f32[24,24,128]{2,1,0:T(8,128)S(1)}, f32[24,24,128]{2,1,0:T(8,128)S(1)}, f32[24,24,128]{2,1,0:T(8,128)S(1)},...) custom-call(s32[1]{0:T(128)} %bitcast.where_ref, ...), custom_call_target="tpu_custom_call" | custom-call | bytes 7200000 | tf_op jit(solution)/shard_map/pallas_call | solution.py:683
  11.6 1.7 %collective-permute-done.3.refs_1_.refs_12_ = f32[4,16,128]{2,1,0:T(8,128)S(1)} collective-permute-done((f32[4,16,128]{2,1,0:T(8,128)S(1)}, f32[4,16,128]{2,1,0:T(8,128)S(1)}, u32[]{:S(2)}, u32[]{:S(2)}) %collective-permute-start.3) | collective-permute-done | bytes 32800 | tf_op jit(solution)/shard_map/ppermute | solution.py:712
  13.3 0.1 shard_map.67
  13.4 2.7 %collective-permute-start.6 = (f32[37,4,128]{2,1,0:T(4,128)S(1)}, f32[37,4,128]{2,1,0:T(4,128)S(1)}, u32[]{:S(2)}, u32[]{:S(2)}) collective-permute-start(f32[37,4,128]{2,1,0:T(4,128)S(1)} %get-tuple-element.68), channel_id=1, source_target_pairs={{0,16},{4,8},{8,4},{12,28},{16,0},{20,24},{24,20},{28,12},{1,17},{... | collective-permute-start | bytes 227336 | tf_op jit(solution)/shard_map/ppermute | solution.py:723
  16.1 0.4 collective-permute-start.7
  16.5 0.0 collective-permute-done.4.refs_13_
  16.5 1.6 %collective-permute-done.6.refs_15_ = f32[37,4,128]{2,1,0:T(4,128)S(1)} collective-permute-done((f32[37,4,128]{2,1,0:T(4,128)S(1)}, f32[37,4,128]{2,1,0:T(4,128)S(1)}, u32[]{:S(2)}, u32[]{:S(2)}) %collective-permute-start.6) | collective-permute-done | bytes 75808 | tf_op jit(solution)/shard_map/ppermute | solution.py:723
  18.1 2.3 %shard_map.68 = (f32[24,24,128]{2,1,0:T(8,128)S(1)}, f32[24,24,128]{2,1,0:T(8,128)S(1)}, f32[24,24,128]{2,1,0:T(8,128)S(1)}, f32[24,24,128]{2,1,0:T(8,128)S(1)},...) custom-call(s32[1]{0:T(128)} %bitcast.where_ref, ...), custom_call_target="tpu_custom_call", output_to_operand_aliasing={{0}: (2, {}), {1}: (3, {}), {2}: (4, {}), {3}: (5, {}), {4}... | custom-call | bytes 14400000 | tf_op jit(solution)/shard_map/pallas_call | solution.py:683
  20.5 0.6 %collective-permute-start.8 = (f32[5,4,8,128]{3,2,1,0:T(8,128)S(1)}, f32[5,4,8,128]{3,2,1,0:T(8,128)S(1)}, u32[]{:S(2)}, u32[]{:S(2)}) collective-permute-start(f32[5,4,8,128]{3,2,1,0:T(8,128)S(1)} %get-tuple-element.72), channel_id=1, source_target_pairs={{0,16},{16,0},{1,17},{17,1},{2,18},{18,2},{3,19},{19,3},{4,20},{20... | collective-permute-start | bytes 245768 | tf_op jit(solution)/shard_map/ppermute | solution.py:712
  21.0 1.4 %collective-permute-start.9 = (f32[5,8,4,128]{3,2,1,0:T(4,128)S(1)}, f32[5,8,4,128]{3,2,1,0:T(4,128)S(1)}, u32[]{:S(2)}, u32[]{:S(2)}) collective-permute-start(f32[5,8,4,128]{3,2,1,0:T(4,128)S(1)} %get-tuple-element.73), channel_id=1, source_target_pairs={{0,12},{4,8},{8,4},{12,0},{1,13},{5,9},{9,5},{13,1},{2,14},{6,10},... | collective-permute-start | bytes 245768 | tf_op jit(solution)/shard_map/ppermute | solution.py:712
  22.4 0.8 %collective-permute-start.10 = (f32[5,8,4,128]{3,2,1,0:T(4,128)S(1)}, f32[5,8,4,128]{3,2,1,0:T(4,128)S(1)}, u32[]{:S(2)}, u32[]{:S(2)}) collective-permute-start(f32[5,8,4,128]{3,2,1,0:T(4,128)S(1)} %get-tuple-element.74), channel_id=1, source_target_pairs={{0,4},{4,0},{8,12},{12,8},{1,5},{5,1},{9,13},{13,9},{2,6},{6,2},{1... | collective-permute-start | bytes 245768 | tf_op jit(solution)/shard_map/ppermute | solution.py:712
  23.3 1.1 %collective-permute-start.11 = (f32[15,4,128]{2,1,0:T(4,128)S(1)}, f32[15,4,128]{2,1,0:T(4,128)S(1)}, u32[]{:S(2)}, u32[]{:S(2)}) collective-permute-start(f32[15,4,128]{2,1,0:T(4,128)S(1)} %get-tuple-element.75), channel_id=1, source_target_pairs={{0,20},{4,16},{8,28},{12,24},{16,4},{20,0},{24,12},{28,8},{1,21},{... | collective-permute-start | bytes 92168 | tf_op jit(solution)/shard_map/ppermute | solution.py:737
  24.4 1.7 %collective-permute-start.12 = (f32[15,4,128]{2,1,0:T(4,128)S(1)}, f32[15,4,128]{2,1,0:T(4,128)S(1)}, u32[]{:S(2)}, u32[]{:S(2)}) collective-permute-start(f32[15,4,128]{2,1,0:T(4,128)S(1)} %get-tuple-element.76), channel_id=1, source_target_pairs={{0,16},{4,24},{8,20},{12,28},{16,0},{20,8},{24,4},{28,12},{1,17},{... | collective-permute-start | bytes 92168 | tf_op jit(solution)/shard_map/ppermute | solution.py:737
  26.1 1.0 %collective-permute-done.11.refs_3_ = f32[15,4,128]{2,1,0:T(4,128)S(1)} collective-permute-done((f32[15,4,128]{2,1,0:T(4,128)S(1)}, f32[15,4,128]{2,1,0:T(4,128)S(1)}, u32[]{:S(2)}, u32[]{:S(2)}) %collective-permute-start.11) | collective-permute-done | bytes 30752 | tf_op jit(solution)/shard_map/ppermute | solution.py:737
  27.1 1.8 %collective-permute-done.12.refs_4_ = f32[15,4,128]{2,1,0:T(4,128)S(1)} collective-permute-done((f32[15,4,128]{2,1,0:T(4,128)S(1)}, f32[15,4,128]{2,1,0:T(4,128)S(1)}, u32[]{:S(2)}, u32[]{:S(2)}) %collective-permute-start.12) | collective-permute-done | bytes 30752 | tf_op jit(solution)/shard_map/ppermute | solution.py:737
  28.9 0.0 collective-permute-done.8.refs_0_
  28.9 0.0 collective-permute-done.9.refs_1_
  28.9 0.0 collective-permute-done.10.refs_2_
  28.9 0.5 shard_map.69
  29.4 16.9 %all_to_all.5.gathered = f32[32,5,4,128]{3,2,1,0:T(4,128)S(1)} all-to-all(f32[32,5,4,128]{3,2,1,0:T(4,128)S(1)} %get-tuple-element.77), channel_id=1, replica_groups=mesh['gx'=2,'gy'=4,'gz'=4] {'gx','gy','gz'}, dimensions={0} | all-to-all | bytes 655360 | tf_op jit(solution)/shard_map/all_to_all | solution.py:819
  46.3 4.0 %shard_map.70 = f32[16,16,128]{2,1,0:T(8,128)} custom-call(s32[1]{0:T(128)} %bitcast.where_ref, f32[32,5,4,128]{3,2,1,0:T(4,128)S(1)} %all_to_all.5.gathered, f32[6,16,16,128]{3,2,1,0:T(8,128)S(1)} %get-tuple-element.78.level1, f32[24,24,128]{2,1,0:T(8,128)S(1)} %get-tuple-element.79.refs_0_, f32[24,24,128]{2,1,0:T(8,128)S(1)} %get-tuple-element.80.refs_1_, ...), custom_call_target="tpu_custom_call" | custom-call | bytes 14400000 | tf_op jit(solution)/shard_map/pallas_call | solution.py:683
  (14 shorter events, 0.0 us)
Async XLA Ops:
  0.0 10.8 %copy-start.1 = (f32[16,16,128]{2,1,0:T(8,128)S(1)}, f32[16,16,128]{2,1,0:T(8,128)}, u32[]{:S(2)}) copy-start(f32[16,16,128]{2,1,0:T(8,128)} %refs_1_.3) | copy-start | bytes 393220
  0.0 10.8 %copy-start.2 = (f32[16,16,128]{2,1,0:T(8,128)S(1)}, f32[16,16,128]{2,1,0:T(8,128)}, u32[]{:S(2)}) copy-start(f32[16,16,128]{2,1,0:T(8,128)} %refs_2_.3) | copy-start | bytes 393220
  0.0 10.8 %copy-start.3 = (f32[16,16,128]{2,1,0:T(8,128)S(1)}, f32[16,16,128]{2,1,0:T(8,128)}, u32[]{:S(2)}) copy-start(f32[16,16,128]{2,1,0:T(8,128)} %refs_3_.3) | copy-start | bytes 393220
  0.0 10.8 %copy-start.4 = (f32[16,16,128]{2,1,0:T(8,128)S(1)}, f32[16,16,128]{2,1,0:T(8,128)}, u32[]{:S(2)}) copy-start(f32[16,16,128]{2,1,0:T(8,128)} %refs_4_.3) | copy-start | bytes 393220
  0.0 10.8 %copy-start.5 = (f32[16,16,128]{2,1,0:T(8,128)S(1)}, f32[16,16,128]{2,1,0:T(8,128)}, u32[]{:S(2)}) copy-start(f32[16,16,128]{2,1,0:T(8,128)} %refs_5_.3) | copy-start | bytes 393220
  2.6 8.2 %copy-start = (f32[16,16,128]{2,1,0:T(8,128)S(1)}, f32[16,16,128]{2,1,0:T(8,128)}, u32[]{:S(2)}) copy-start(f32[16,16,128]{2,1,0:T(8,128)} %refs_0_.3) | copy-start | bytes 393220
  2.6 8.2 %collective-permute-start.2 = (f32[6,4,16,128]{3,2,1,0:T(8,128)}, f32[6,4,16,128]{3,2,1,0:T(8,128)S(1)}, u32[]{:S(2)}, u32[]{:S(2)}) collective-permute-start(f32[6,4,16,128]{3,2,1,0:T(8,128)} %get-tuple-element.51), channel_id=1, source_target_pairs={{0,16},{16,0},{1,17},{17,1},{2,18},{18,2},{3,19},{19,3},{4,20},{20... | collective-permute-start | bytes 589832 | tf_op jit(solution)/shard_map/ppermute | solution.py:712
  4.7 11.8 %collective-permute-start.4 = (f32[6,16,4,128]{3,2,1,0:T(4,128)}, f32[6,16,4,128]{3,2,1,0:T(4,128)S(1)}, u32[]{:S(2)}, u32[]{:S(2)}) collective-permute-start(f32[6,16,4,128]{3,2,1,0:T(4,128)} %get-tuple-element.65), channel_id=1, source_target_pairs={{0,12},{4,8},{8,4},{12,0},{1,13},{5,9},{9,5},{13,1},{2,14},{6,10},... | collective-permute-start | bytes 589832 | tf_op jit(solution)/shard_map/ppermute | solution.py:712
  6.8 9.7 %collective-permute-start.5 = (f32[6,16,4,128]{3,2,1,0:T(4,128)}, f32[6,16,4,128]{3,2,1,0:T(4,128)S(1)}, u32[]{:S(2)}, u32[]{:S(2)}) collective-permute-start(f32[6,16,4,128]{3,2,1,0:T(4,128)} %get-tuple-element.66), channel_id=1, source_target_pairs={{0,4},{4,0},{8,12},{12,8},{1,5},{5,1},{9,13},{13,9},{2,6},{6,2},{1... | collective-permute-start | bytes 589832 | tf_op jit(solution)/shard_map/ppermute | solution.py:712
  6.8 3.6 %collective-permute-start = (f32[8,16,128]{2,1,0:T(8,128)}, f32[8,16,128]{2,1,0:T(8,128)S(1)}, u32[]{:S(2)}, u32[]{:S(2)}) collective-permute-start(f32[8,16,128]{2,1,0:T(8,128)} %get-tuple-element.48), channel_id=1, source_target_pairs={{0,1},{1,0},{2,3},{3,2},{4,5},{5,4},{6,7},{7,6},{8,9},{9,8},{10,11... | collective-permute-start | bytes 196616 | tf_op jit(solution)/shard_map/ppermute | solution.py:712
  8.1 2.3 %collective-permute-start.1 = (f32[8,16,128]{2,1,0:T(8,128)}, f32[8,16,128]{2,1,0:T(8,128)S(1)}, u32[]{:S(2)}, u32[]{:S(2)}) collective-permute-start(f32[8,16,128]{2,1,0:T(8,128)} %get-tuple-element.49), channel_id=1, source_target_pairs={{0,4},{1,2},{2,1},{3,7},{4,0},{5,6},{6,5},{7,3},{8,12},{9,10},{10,... | collective-permute-start | bytes 196616 | tf_op jit(solution)/shard_map/ppermute | solution.py:723
  10.5 2.8 %collective-permute-start.3 = (f32[4,16,128]{2,1,0:T(8,128)S(1)}, f32[4,16,128]{2,1,0:T(8,128)S(1)}, u32[]{:S(2)}, u32[]{:S(2)}) collective-permute-start(f32[4,16,128]{2,1,0:T(8,128)S(1)} %get-tuple-element.64), channel_id=1, source_target_pairs={{0,16},{16,0},{1,17},{17,1},{2,18},{18,2},{3,19},{19,3},{4,20},{20... | collective-permute-start | bytes 98312 | tf_op jit(solution)/shard_map/ppermute | solution.py:712
  13.4 4.7 %collective-permute-start.6 = (f32[37,4,128]{2,1,0:T(4,128)S(1)}, f32[37,4,128]{2,1,0:T(4,128)S(1)}, u32[]{:S(2)}, u32[]{:S(2)}) collective-permute-start(f32[37,4,128]{2,1,0:T(4,128)S(1)} %get-tuple-element.68), channel_id=1, source_target_pairs={{0,16},{4,8},{8,4},{12,28},{16,0},{20,24},{24,20},{28,12},{1,17},{... | collective-permute-start | bytes 227336 | tf_op jit(solution)/shard_map/ppermute | solution.py:723
  16.1 2.1 %collective-permute-start.7 = (f32[37,4,128]{2,1,0:T(4,128)S(1)}, f32[37,4,128]{2,1,0:T(4,128)S(1)}, u32[]{:S(2)}, u32[]{:S(2)}) collective-permute-start(f32[37,4,128]{2,1,0:T(4,128)S(1)} %get-tuple-element.69), channel_id=1, source_target_pairs={{0,4},{4,0},{8,12},{12,8},{1,5},{5,1},{9,13},{13,9},{2,6},{6,2},{1... | collective-permute-start | bytes 227336 | tf_op jit(solution)/shard_map/ppermute | solution.py:712
  20.5 8.4 %collective-permute-start.8 = (f32[5,4,8,128]{3,2,1,0:T(8,128)S(1)}, f32[5,4,8,128]{3,2,1,0:T(8,128)S(1)}, u32[]{:S(2)}, u32[]{:S(2)}) collective-permute-start(f32[5,4,8,128]{3,2,1,0:T(8,128)S(1)} %get-tuple-element.72), channel_id=1, source_target_pairs={{0,16},{16,0},{1,17},{17,1},{2,18},{18,2},{3,19},{19,3},{4,20},{20... | collective-permute-start | bytes 245768 | tf_op jit(solution)/shard_map/ppermute | solution.py:712
  21.0 7.9 %collective-permute-start.9 = (f32[5,8,4,128]{3,2,1,0:T(4,128)S(1)}, f32[5,8,4,128]{3,2,1,0:T(4,128)S(1)}, u32[]{:S(2)}, u32[]{:S(2)}) collective-permute-start(f32[5,8,4,128]{3,2,1,0:T(4,128)S(1)} %get-tuple-element.73), channel_id=1, source_target_pairs={{0,12},{4,8},{8,4},{12,0},{1,13},{5,9},{9,5},{13,1},{2,14},{6,10},... | collective-permute-start | bytes 245768 | tf_op jit(solution)/shard_map/ppermute | solution.py:712
  22.4 6.5 %collective-permute-start.10 = (f32[5,8,4,128]{3,2,1,0:T(4,128)S(1)}, f32[5,8,4,128]{3,2,1,0:T(4,128)S(1)}, u32[]{:S(2)}, u32[]{:S(2)}) collective-permute-start(f32[5,8,4,128]{3,2,1,0:T(4,128)S(1)} %get-tuple-element.74), channel_id=1, source_target_pairs={{0,4},{4,0},{8,12},{12,8},{1,5},{5,1},{9,13},{13,9},{2,6},{6,2},{1... | collective-permute-start | bytes 245768 | tf_op jit(solution)/shard_map/ppermute | solution.py:712
  23.3 3.8 %collective-permute-start.11 = (f32[15,4,128]{2,1,0:T(4,128)S(1)}, f32[15,4,128]{2,1,0:T(4,128)S(1)}, u32[]{:S(2)}, u32[]{:S(2)}) collective-permute-start(f32[15,4,128]{2,1,0:T(4,128)S(1)} %get-tuple-element.75), channel_id=1, source_target_pairs={{0,20},{4,16},{8,28},{12,24},{16,4},{20,0},{24,12},{28,8},{1,21},{... | collective-permute-start | bytes 92168 | tf_op jit(solution)/shard_map/ppermute | solution.py:737
  24.4 4.5 %collective-permute-start.12 = (f32[15,4,128]{2,1,0:T(4,128)S(1)}, f32[15,4,128]{2,1,0:T(4,128)S(1)}, u32[]{:S(2)}, u32[]{:S(2)}) collective-permute-start(f32[15,4,128]{2,1,0:T(4,128)S(1)} %get-tuple-element.76), channel_id=1, source_target_pairs={{0,16},{4,24},{8,20},{12,28},{16,0},{20,8},{24,4},{28,12},{1,17},{... | collective-permute-start | bytes 92168 | tf_op jit(solution)/shard_map/ppermute | solution.py:737

commit v20 on v19

--- a/solution.py
+++ b/solution.py
@@ -479,9 +479,10 @@
     for a, values in enumerate([field1] + whole):
         level1[a] = values
     mine = slice(NEAR, NEAR + bx1)
+    near = slice(NEAR - 1, NEAR + bx1 + 1)
     inner = weight1[mine]
     diag1 = RELAX / jnp.where(inner > 0.0, inner, 1.0)
-    remain = rhs1[mine] - diag1 * field1[mine] + pull(field1, faces1)[mine]
+    remain = rhs1[mine] - diag1 * field1[mine] + pull(field1[near], [face[near] for face in faces1])[1:-1]
     left[...] = remain
     packed = level2_rows(left, (False,) * 3, 0.125, bx1 // 2, by1 // 2, LANES // 4)
     blocks = LANES // (LANES // 4)
@@ -806,7 +807,7 @@
     fine_arrays = tuple(fine_arrays) + tuple(laid[2:4]) + tuple(laid[6:])
 
     near_x = tuple(swaps("gx", sends_x, "gy"))
-    near_y = tuple(swaps("gy", (one_y, two_y))[::-1])
+    near_y = tuple(swaps("gy", (one_y, two_y), "gz")[::-1])
     near_xy = tuple(diagonal_swaps(sends_xy))
     copies, level1 = run(
         functools.partial(near_kernel, counts, devices),

time: 50.4 us -> 50.5 us (level)
  blocking collectives: 16.9 us -> 14.6 us
  waiting for transfers between devices: 7.74 us -> 9.14 us
  starting transfers between devices: 15.3 us -> 16.2 us
    all_to_all x1, blocking collectives: 16.9 us -> 14.6 us  [local(): gathered = lax.all_to_all(copies, axes, 0, 0, tiled=True)]
    ppermute x2, starting transfers between devices: 2.81 us -> 1.1 us  [diagonal_swaps(): got.append(lax.ppermute(block, ('gx', 'gy'), pairs))]
    ppermute x2 -> x3, starting transfers between devices: 3.48 us -> 4.89 us  [swaps(): got.append(lax.ppermute(block, tuple(sorted((axis, other))), pairs))]
    ppermute x2, waiting for transfers between devices: 2.81 us -> 4.21 us  [diagonal_swaps(): got.append(lax.ppermute(block, ('gx', 'gy'), pairs))]
    ppermute x9 -> x8, starting transfers between devices: 8.97 us -> 10.3 us  [swaps(): got.append(lax.ppermute(block, axis, list(enumerate(partner))))]
    ppermute x9 -> x8, waiting for transfers between devices: 3.3 us -> 3.3 us  [swaps(): got.append(lax.ppermute(block, axis, list(enumerate(partner))))]
    ppermute x2 -> x3, waiting for transfers between devices: 1.63 us -> 1.64 us  [swaps(): got.append(lax.ppermute(block, tuple(sorted((axis, other))), pairs))]
where the time goes in v20:
time: 50.5 us; the launch traced here: 50.3 us
  starting transfers between devices  16.2 us (32%)
  blocking collectives  14.6 us (29%)
  Pallas kernels  10.2 us (20%)
  waiting for transfers between devices  9.14 us (18%)
    all_to_all x1, blocking collectives, local(): gathered = lax.all_to_all(copies, axes, 0, 0, tiled=True)  14.6 us
    ppermute x8, starting transfers between devices, swaps(): got.append(lax.ppermute(block, axis, list(enumerate(partner))))  10.3 us
    pallas_call x7, Pallas kernels, run(): pl.pallas_call(kernel, out_shape=tuple((jax.ShapeDtypeStruct(shape, F32)...  10.2 us
    ppermute x3, starting transfers between devices, swaps(): got.append(lax.ppermute(block, tuple(sorted((axis, other))), pairs))  4.89 us
    ppermute x2, waiting for transfers between devices, diagonal_swaps(): got.append(lax.ppermute(block, ('gx', 'gy'), pairs))  4.21 us
    ppermute x8, waiting for transfers between devices, swaps(): got.append(lax.ppermute(block, axis, list(enumerate(partner))))  3.3 us
    ppermute x3, waiting for transfers between devices, swaps(): got.append(lax.ppermute(block, tuple(sorted((axis, other))), pairs))  1.64 us
    ppermute x2, starting transfers between devices, diagonal_swaps(): got.append(lax.ppermute(block, ('gx', 'gy'), pairs))  1.1 us
  transfers between devices with their start and end apart: 13, of which 5 were waited for; matrix products, arithmetic and copies ran while one was open for 0% of the time, Pallas kernels for 2%

profile of v20, /device:TPU:1, one launch (start us, length us, event | category | flops | bytes accessed | tf_op | source)
XLA Modules:
  0.0 50.3 jit_solution(1764818846371894585)
XLA Ops:
  0.0 2.6 %shard_map.64 = (f32[6,4,16,128]{3,2,1,0:T(8,128)}, f32[6,16,4,128]{3,2,1,0:T(4,128)}, f32[6,16,4,128]{3,2,1,0:T(4,128)}, f32[8,16,128]{2,1,0:T(8,128)}, f32[8,16,128]{2,1,0:T(8,128)}) custom-call(s32[1]{0:T(128)} %bitcast.where_ref, f32[16,16,128]{2,1,0:T(8,128)} %refs_0_.3, f32[16,16,128]{2,1,0:T(8,128)} %refs_1_.3, f32[16,16,128]{2,1,0:T(8,128)} %refs_2_.3, ...), custom_call_target="tpu_custom_call" | custom-call | bytes 3600000 | tf_op jit(solution)/shard_map/pallas_call | solution.py:684
  2.6 2.0 %collective-permute-start.2 = (f32[6,4,16,128]{3,2,1,0:T(8,128)}, f32[6,4,16,128]{3,2,1,0:T(8,128)S(1)}, u32[]{:S(2)}, u32[]{:S(2)}) collective-permute-start(f32[6,4,16,128]{3,2,1,0:T(8,128)} %get-tuple-element.51), channel_id=1, source_target_pairs={{0,16},{16,0},{1,17},{17,1},{2,18},{18,2},{3,19},{19,3},{4,20},{20... | collective-permute-start | bytes 589832 | tf_op jit(solution)/shard_map/ppermute | solution.py:713
  4.7 2.1 %collective-permute-start.4 = (f32[6,16,4,128]{3,2,1,0:T(4,128)}, f32[6,16,4,128]{3,2,1,0:T(4,128)S(1)}, u32[]{:S(2)}, u32[]{:S(2)}) collective-permute-start(f32[6,16,4,128]{3,2,1,0:T(4,128)} %get-tuple-element.65), channel_id=1, source_target_pairs={{0,12},{4,8},{8,4},{12,0},{1,13},{5,9},{9,5},{13,1},{2,14},{6,10},... | collective-permute-start | bytes 589832 | tf_op jit(solution)/shard_map/ppermute | solution.py:713
  6.8 0.0 collective-permute-start.5
  6.8 1.3 %collective-permute-start = (f32[8,16,128]{2,1,0:T(8,128)}, f32[8,16,128]{2,1,0:T(8,128)S(1)}, u32[]{:S(2)}, u32[]{:S(2)}) collective-permute-start(f32[8,16,128]{2,1,0:T(8,128)} %get-tuple-element.48), channel_id=1, source_target_pairs={{0,1},{1,0},{2,3},{3,2},{4,5},{5,4},{6,7},{7,6},{8,9},{9,8},{10,11... | collective-permute-start | bytes 196616 | tf_op jit(solution)/shard_map/ppermute | solution.py:713
  8.1 0.8 %collective-permute-start.1 = (f32[8,16,128]{2,1,0:T(8,128)}, f32[8,16,128]{2,1,0:T(8,128)S(1)}, u32[]{:S(2)}, u32[]{:S(2)}) collective-permute-start(f32[8,16,128]{2,1,0:T(8,128)} %get-tuple-element.49), channel_id=1, source_target_pairs={{0,4},{1,2},{2,1},{3,7},{4,0},{5,6},{6,5},{7,3},{8,12},{9,10},{10,... | collective-permute-start | bytes 196616 | tf_op jit(solution)/shard_map/ppermute | solution.py:724
  8.8 1.5 %collective-permute-done.one_ref = f32[8,16,128]{2,1,0:T(8,128)S(1)} collective-permute-done((f32[8,16,128]{2,1,0:T(8,128)}, f32[8,16,128]{2,1,0:T(8,128)S(1)}, u32[]{:S(2)}, u32[]{:S(2)}) %collective-permute-start) | collective-permute-done | bytes 65568 | tf_op jit(solution)/shard_map/ppermute | solution.py:713
  10.4 0.0 collective-permute-done.1.two_ref
  10.4 0.1 shard_map.65
  10.5 0.3 collective-permute-start.3
  10.8 0.0 collective-permute-done.2.refs_7_.refs_0_
  10.9 0.7 %shard_map.66 = (f32[24,24,128]{2,1,0:T(8,128)S(1)}, f32[24,24,128]{2,1,0:T(8,128)S(1)}, f32[24,24,128]{2,1,0:T(8,128)S(1)}, f32[24,24,128]{2,1,0:T(8,128)S(1)},...) custom-call(s32[1]{0:T(128)} %bitcast.where_ref, ...), custom_call_target="tpu_custom_call" | custom-call | bytes 7200000 | tf_op jit(solution)/shard_map/pallas_call | solution.py:684
  11.6 1.7 %collective-permute-done.3.refs_1_.refs_12_ = f32[4,16,128]{2,1,0:T(8,128)S(1)} collective-permute-done((f32[4,16,128]{2,1,0:T(8,128)S(1)}, f32[4,16,128]{2,1,0:T(8,128)S(1)}, u32[]{:S(2)}, u32[]{:S(2)}) %collective-permute-start.3) | collective-permute-done | bytes 32800 | tf_op jit(solution)/shard_map/ppermute | solution.py:713
  13.3 0.1 shard_map.67
  13.4 2.7 %collective-permute-start.6 = (f32[37,4,128]{2,1,0:T(4,128)S(1)}, f32[37,4,128]{2,1,0:T(4,128)S(1)}, u32[]{:S(2)}, u32[]{:S(2)}) collective-permute-start(f32[37,4,128]{2,1,0:T(4,128)S(1)} %get-tuple-element.68), channel_id=1, source_target_pairs={{0,16},{4,8},{8,4},{12,28},{16,0},{20,24},{24,20},{28,12},{1,17},{... | collective-permute-start | bytes 227336 | tf_op jit(solution)/shard_map/ppermute | solution.py:724
  16.1 0.4 collective-permute-start.7
  16.5 0.0 collective-permute-done.4.refs_13_
  16.5 0.0 collective-permute-done.5.refs_14_
  16.5 1.6 %collective-permute-done.6.refs_15_ = f32[37,4,128]{2,1,0:T(4,128)S(1)} collective-permute-done((f32[37,4,128]{2,1,0:T(4,128)S(1)}, f32[37,4,128]{2,1,0:T(4,128)S(1)}, u32[]{:S(2)}, u32[]{:S(2)}) %collective-permute-start.6) | collective-permute-done | bytes 75808 | tf_op jit(solution)/shard_map/ppermute | solution.py:724
  18.1 2.3 %shard_map.68 = (f32[24,24,128]{2,1,0:T(8,128)S(1)}, f32[24,24,128]{2,1,0:T(8,128)S(1)}, f32[24,24,128]{2,1,0:T(8,128)S(1)}, f32[24,24,128]{2,1,0:T(8,128)S(1)},...) custom-call(s32[1]{0:T(128)} %bitcast.where_ref, ...), custom_call_target="tpu_custom_call", output_to_operand_aliasing={{0}: (2, {}), {1}: (3, {}), {2}: (4, {}), {3}: (5, {}), {4}... | custom-call | bytes 14400000 | tf_op jit(solution)/shard_map/pallas_call | solution.py:684
  20.5 0.6 %collective-permute-start.8 = (f32[5,4,8,128]{3,2,1,0:T(8,128)S(1)}, f32[5,4,8,128]{3,2,1,0:T(8,128)S(1)}, u32[]{:S(2)}, u32[]{:S(2)}) collective-permute-start(f32[5,4,8,128]{3,2,1,0:T(8,128)S(1)} %get-tuple-element.72), channel_id=1, source_target_pairs={{0,16},{16,0},{1,17},{17,1},{2,18},{18,2},{3,19},{19,3},{4,20},{20... | collective-permute-start | bytes 245768 | tf_op jit(solution)/shard_map/ppermute | solution.py:713
  21.0 1.4 %collective-permute-start.9 = (f32[5,8,4,128]{3,2,1,0:T(4,128)S(1)}, f32[5,8,4,128]{3,2,1,0:T(4,128)S(1)}, u32[]{:S(2)}, u32[]{:S(2)}) collective-permute-start(f32[5,8,4,128]{3,2,1,0:T(4,128)S(1)} %get-tuple-element.73), channel_id=1, source_target_pairs={{0,1},{4,8},{8,4},{12,13},{1,0},{5,9},{9,5},{13,12},{2,3},{6,10},{... | collective-permute-start | bytes 245768 | tf_op jit(solution)/shard_map/ppermute | solution.py:724
  22.4 3.5 %collective-permute-start.10 = (f32[5,8,4,128]{3,2,1,0:T(4,128)S(1)}, f32[5,8,4,128]{3,2,1,0:T(4,128)S(1)}, u32[]{:S(2)}, u32[]{:S(2)}) collective-permute-start(f32[5,8,4,128]{3,2,1,0:T(4,128)S(1)} %get-tuple-element.74), channel_id=1, source_target_pairs={{0,4},{4,0},{8,12},{12,8},{1,5},{5,1},{9,13},{13,9},{2,6},{6,2},{1... | collective-permute-start | bytes 245768 | tf_op jit(solution)/shard_map/ppermute | solution.py:713
  26.0 1.1 %collective-permute-start.11 = (f32[15,4,128]{2,1,0:T(4,128)S(1)}, f32[15,4,128]{2,1,0:T(4,128)S(1)}, u32[]{:S(2)}, u32[]{:S(2)}) collective-permute-start(f32[15,4,128]{2,1,0:T(4,128)S(1)} %get-tuple-element.75), channel_id=1, source_target_pairs={{0,20},{4,16},{8,28},{12,24},{16,4},{20,0},{24,12},{28,8},{1,21},{... | collective-permute-start | bytes 92168 | tf_op jit(solution)/shard_map/ppermute | solution.py:738
  27.1 0.0 collective-permute-start.12
  27.1 2.2 %collective-permute-done.11.refs_3_ = f32[15,4,128]{2,1,0:T(4,128)S(1)} collective-permute-done((f32[15,4,128]{2,1,0:T(4,128)S(1)}, f32[15,4,128]{2,1,0:T(4,128)S(1)}, u32[]{:S(2)}, u32[]{:S(2)}) %collective-permute-start.11) | collective-permute-done | bytes 30752 | tf_op jit(solution)/shard_map/ppermute | solution.py:738
  29.3 2.0 %collective-permute-done.12.refs_4_ = f32[15,4,128]{2,1,0:T(4,128)S(1)} collective-permute-done((f32[15,4,128]{2,1,0:T(4,128)S(1)}, f32[15,4,128]{2,1,0:T(4,128)S(1)}, u32[]{:S(2)}, u32[]{:S(2)}) %collective-permute-start.12) | collective-permute-done | bytes 30752 | tf_op jit(solution)/shard_map/ppermute | solution.py:738
  31.3 0.0 collective-permute-done.9.refs_1_
  31.3 0.0 collective-permute-done.10.refs_2_
  31.3 0.5 shard_map.69
  31.8 14.6 %all_to_all.5.gathered = f32[32,5,4,128]{3,2,1,0:T(4,128)S(1)} all-to-all(f32[32,5,4,128]{3,2,1,0:T(4,128)S(1)} %get-tuple-element.77), channel_id=1, replica_groups=mesh['gx'=2,'gy'=4,'gz'=4] {'gx','gy','gz'}, dimensions={0} | all-to-all | bytes 655360 | tf_op jit(solution)/shard_map/all_to_all | solution.py:820
  46.4 4.0 %shard_map.70 = f32[16,16,128]{2,1,0:T(8,128)} custom-call(s32[1]{0:T(128)} %bitcast.where_ref, f32[32,5,4,128]{3,2,1,0:T(4,128)S(1)} %all_to_all.5.gathered, f32[6,16,16,128]{3,2,1,0:T(8,128)S(1)} %get-tuple-element.78.level1, f32[24,24,128]{2,1,0:T(8,128)S(1)} %get-tuple-element.79.refs_0_, f32[24,24,128]{2,1,0:T(8,128)S(1)} %get-tuple-element.80.refs_1_, ...), custom_call_target="tpu_custom_call" | custom-call | bytes 14400000 | tf_op jit(solution)/shard_map/pallas_call | solution.py:684
  (14 shorter events, 0.0 us)
Async XLA Ops:
  0.0 10.8 %copy-start.1 = (f32[16,16,128]{2,1,0:T(8,128)S(1)}, f32[16,16,128]{2,1,0:T(8,128)}, u32[]{:S(2)}) copy-start(f32[16,16,128]{2,1,0:T(8,128)} %refs_1_.3) | copy-start | bytes 393220
  0.0 10.8 %copy-start.2 = (f32[16,16,128]{2,1,0:T(8,128)S(1)}, f32[16,16,128]{2,1,0:T(8,128)}, u32[]{:S(2)}) copy-start(f32[16,16,128]{2,1,0:T(8,128)} %refs_2_.3) | copy-start | bytes 393220
  0.0 10.8 %copy-start.3 = (f32[16,16,128]{2,1,0:T(8,128)S(1)}, f32[16,16,128]{2,1,0:T(8,128)}, u32[]{:S(2)}) copy-start(f32[16,16,128]{2,1,0:T(8,128)} %refs_3_.3) | copy-start | bytes 393220
  0.0 10.8 %copy-start.4 = (f32[16,16,128]{2,1,0:T(8,128)S(1)}, f32[16,16,128]{2,1,0:T(8,128)}, u32[]{:S(2)}) copy-start(f32[16,16,128]{2,1,0:T(8,128)} %refs_4_.3) | copy-start | bytes 393220
  0.0 10.8 %copy-start.5 = (f32[16,16,128]{2,1,0:T(8,128)S(1)}, f32[16,16,128]{2,1,0:T(8,128)}, u32[]{:S(2)}) copy-start(f32[16,16,128]{2,1,0:T(8,128)} %refs_5_.3) | copy-start | bytes 393220
  2.6 8.2 %copy-start = (f32[16,16,128]{2,1,0:T(8,128)S(1)}, f32[16,16,128]{2,1,0:T(8,128)}, u32[]{:S(2)}) copy-start(f32[16,16,128]{2,1,0:T(8,128)} %refs_0_.3) | copy-start | bytes 393220
  2.6 8.2 %collective-permute-start.2 = (f32[6,4,16,128]{3,2,1,0:T(8,128)}, f32[6,4,16,128]{3,2,1,0:T(8,128)S(1)}, u32[]{:S(2)}, u32[]{:S(2)}) collective-permute-start(f32[6,4,16,128]{3,2,1,0:T(8,128)} %get-tuple-element.51), channel_id=1, source_target_pairs={{0,16},{16,0},{1,17},{17,1},{2,18},{18,2},{3,19},{19,3},{4,20},{20... | collective-permute-start | bytes 589832 | tf_op jit(solution)/shard_map/ppermute | solution.py:713
  4.7 11.8 %collective-permute-start.4 = (f32[6,16,4,128]{3,2,1,0:T(4,128)}, f32[6,16,4,128]{3,2,1,0:T(4,128)S(1)}, u32[]{:S(2)}, u32[]{:S(2)}) collective-permute-start(f32[6,16,4,128]{3,2,1,0:T(4,128)} %get-tuple-element.65), channel_id=1, source_target_pairs={{0,12},{4,8},{8,4},{12,0},{1,13},{5,9},{9,5},{13,1},{2,14},{6,10},... | collective-permute-start | bytes 589832 | tf_op jit(solution)/shard_map/ppermute | solution.py:713
  6.8 9.7 %collective-permute-start.5 = (f32[6,16,4,128]{3,2,1,0:T(4,128)}, f32[6,16,4,128]{3,2,1,0:T(4,128)S(1)}, u32[]{:S(2)}, u32[]{:S(2)}) collective-permute-start(f32[6,16,4,128]{3,2,1,0:T(4,128)} %get-tuple-element.66), channel_id=1, source_target_pairs={{0,4},{4,0},{8,12},{12,8},{1,5},{5,1},{9,13},{13,9},{2,6},{6,2},{1... | collective-permute-start | bytes 589832 | tf_op jit(solution)/shard_map/ppermute | solution.py:713
  6.8 3.6 %collective-permute-start = (f32[8,16,128]{2,1,0:T(8,128)}, f32[8,16,128]{2,1,0:T(8,128)S(1)}, u32[]{:S(2)}, u32[]{:S(2)}) collective-permute-start(f32[8,16,128]{2,1,0:T(8,128)} %get-tuple-element.48), channel_id=1, source_target_pairs={{0,1},{1,0},{2,3},{3,2},{4,5},{5,4},{6,7},{7,6},{8,9},{9,8},{10,11... | collective-permute-start | bytes 196616 | tf_op jit(solution)/shard_map/ppermute | solution.py:713
  8.1 2.3 %collective-permute-start.1 = (f32[8,16,128]{2,1,0:T(8,128)}, f32[8,16,128]{2,1,0:T(8,128)S(1)}, u32[]{:S(2)}, u32[]{:S(2)}) collective-permute-start(f32[8,16,128]{2,1,0:T(8,128)} %get-tuple-element.49), channel_id=1, source_target_pairs={{0,4},{1,2},{2,1},{3,7},{4,0},{5,6},{6,5},{7,3},{8,12},{9,10},{10,... | collective-permute-start | bytes 196616 | tf_op jit(solution)/shard_map/ppermute | solution.py:724
  10.5 2.8 %collective-permute-start.3 = (f32[4,16,128]{2,1,0:T(8,128)S(1)}, f32[4,16,128]{2,1,0:T(8,128)S(1)}, u32[]{:S(2)}, u32[]{:S(2)}) collective-permute-start(f32[4,16,128]{2,1,0:T(8,128)S(1)} %get-tuple-element.64), channel_id=1, source_target_pairs={{0,16},{16,0},{1,17},{17,1},{2,18},{18,2},{3,19},{19,3},{4,20},{20... | collective-permute-start | bytes 98312 | tf_op jit(solution)/shard_map/ppermute | solution.py:713
  13.4 4.7 %collective-permute-start.6 = (f32[37,4,128]{2,1,0:T(4,128)S(1)}, f32[37,4,128]{2,1,0:T(4,128)S(1)}, u32[]{:S(2)}, u32[]{:S(2)}) collective-permute-start(f32[37,4,128]{2,1,0:T(4,128)S(1)} %get-tuple-element.68), channel_id=1, source_target_pairs={{0,16},{4,8},{8,4},{12,28},{16,0},{20,24},{24,20},{28,12},{1,17},{... | collective-permute-start | bytes 227336 | tf_op jit(solution)/shard_map/ppermute | solution.py:724
  16.1 2.1 %collective-permute-start.7 = (f32[37,4,128]{2,1,0:T(4,128)S(1)}, f32[37,4,128]{2,1,0:T(4,128)S(1)}, u32[]{:S(2)}, u32[]{:S(2)}) collective-permute-start(f32[37,4,128]{2,1,0:T(4,128)S(1)} %get-tuple-element.69), channel_id=1, source_target_pairs={{0,4},{4,0},{8,12},{12,8},{1,5},{5,1},{9,13},{13,9},{2,6},{6,2},{1... | collective-permute-start | bytes 227336 | tf_op jit(solution)/shard_map/ppermute | solution.py:713
  20.5 10.8 %collective-permute-start.8 = (f32[5,4,8,128]{3,2,1,0:T(8,128)S(1)}, f32[5,4,8,128]{3,2,1,0:T(8,128)S(1)}, u32[]{:S(2)}, u32[]{:S(2)}) collective-permute-start(f32[5,4,8,128]{3,2,1,0:T(8,128)S(1)} %get-tuple-element.72), channel_id=1, source_target_pairs={{0,16},{16,0},{1,17},{17,1},{2,18},{18,2},{3,19},{19,3},{4,20},{20... | collective-permute-start | bytes 245768 | tf_op jit(solution)/shard_map/ppermute | solution.py:713
  21.0 10.3 %collective-permute-start.9 = (f32[5,8,4,128]{3,2,1,0:T(4,128)S(1)}, f32[5,8,4,128]{3,2,1,0:T(4,128)S(1)}, u32[]{:S(2)}, u32[]{:S(2)}) collective-permute-start(f32[5,8,4,128]{3,2,1,0:T(4,128)S(1)} %get-tuple-element.73), channel_id=1, source_target_pairs={{0,1},{4,8},{8,4},{12,13},{1,0},{5,9},{9,5},{13,12},{2,3},{6,10},{... | collective-permute-start | bytes 245768 | tf_op jit(solution)/shard_map/ppermute | solution.py:724
  22.4 8.9 %collective-permute-start.10 = (f32[5,8,4,128]{3,2,1,0:T(4,128)S(1)}, f32[5,8,4,128]{3,2,1,0:T(4,128)S(1)}, u32[]{:S(2)}, u32[]{:S(2)}) collective-permute-start(f32[5,8,4,128]{3,2,1,0:T(4,128)S(1)} %get-tuple-element.74), channel_id=1, source_target_pairs={{0,4},{4,0},{8,12},{12,8},{1,5},{5,1},{9,13},{13,9},{2,6},{6,2},{1... | collective-permute-start | bytes 245768 | tf_op jit(solution)/shard_map/ppermute | solution.py:713
  26.0 3.3 %collective-permute-start.11 = (f32[15,4,128]{2,1,0:T(4,128)S(1)}, f32[15,4,128]{2,1,0:T(4,128)S(1)}, u32[]{:S(2)}, u32[]{:S(2)}) collective-permute-start(f32[15,4,128]{2,1,0:T(4,128)S(1)} %get-tuple-element.75), channel_id=1, source_target_pairs={{0,20},{4,16},{8,28},{12,24},{16,4},{20,0},{24,12},{28,8},{1,21},{... | collective-permute-start | bytes 92168 | tf_op jit(solution)/shard_map/ppermute | solution.py:738
  27.1 4.2 %collective-permute-start.12 = (f32[15,4,128]{2,1,0:T(4,128)S(1)}, f32[15,4,128]{2,1,0:T(4,128)S(1)}, u32[]{:S(2)}, u32[]{:S(2)}) collective-permute-start(f32[15,4,128]{2,1,0:T(4,128)S(1)} %get-tuple-element.76), channel_id=1, source_target_pairs={{0,16},{4,24},{8,20},{12,28},{16,0},{20,8},{24,4},{28,12},{1,17},{... | collective-permute-start | bytes 92168 | tf_op jit(solution)/shard_map/ppermute | solution.py:738

commit v21 on v20

--- a/solution.py
+++ b/solution.py
@@ -807,7 +807,7 @@
     fine_arrays = tuple(fine_arrays) + tuple(laid[2:4]) + tuple(laid[6:])
 
     near_x = tuple(swaps("gx", sends_x, "gy"))
-    near_y = tuple(swaps("gy", (one_y, two_y), "gz")[::-1])
+    near_y = tuple(swaps("gy", (one_y, two_y))[::-1])
     near_xy = tuple(diagonal_swaps(sends_xy))
     copies, level1 = run(
         functools.partial(near_kernel, counts, devices),

time: 50.5 us -> 50.4 us (level)
  blocking collectives: 14.6 us -> 16.9 us
  waiting for transfers between devices: 9.14 us -> 7.74 us
  starting transfers between devices: 16.2 us -> 15.3 us
    all_to_all x1, blocking collectives: 14.6 us -> 16.9 us  [local(): gathered = lax.all_to_all(copies, axes, 0, 0, tiled=True)]
    ppermute x2, starting transfers between devices: 1.1 us -> 2.81 us  [diagonal_swaps(): got.append(lax.ppermute(block, ('gx', 'gy'), pairs))]
    ppermute x3 -> x2, starting transfers between devices: 4.89 us -> 3.48 us  [swaps(): got.append(lax.ppermute(block, tuple(sorted((axis, other))), pairs))]
    ppermute x2, waiting for transfers between devices: 4.21 us -> 2.81 us  [diagonal_swaps(): got.append(lax.ppermute(block, ('gx', 'gy'), pairs))]
    ppermute x8 -> x9, starting transfers between devices: 10.3 us -> 8.97 us  [swaps(): got.append(lax.ppermute(block, axis, list(enumerate(partner))))]
    ppermute x8 -> x9, waiting for transfers between devices: 3.3 us -> 3.3 us  [swaps(): got.append(lax.ppermute(block, axis, list(enumerate(partner))))]
    ppermute x3 -> x2, waiting for transfers between devices: 1.64 us -> 1.63 us  [swaps(): got.append(lax.ppermute(block, tuple(sorted((axis, other))), pairs))]
where the time goes in v21:
time: 50.4 us; the launch traced here: 50.3 us
  blocking collectives  16.9 us (34%)
  starting transfers between devices  15.3 us (30%)
  Pallas kernels  10.2 us (20%)
  waiting for transfers between devices  7.74 us (15%)
    all_to_all x1, blocking collectives, local(): gathered = lax.all_to_all(copies, axes, 0, 0, tiled=True)  16.9 us
    pallas_call x7, Pallas kernels, run(): pl.pallas_call(kernel, out_shape=tuple((jax.ShapeDtypeStruct(shape, F32)...  10.2 us
    ppermute x9, starting transfers between devices, swaps(): got.append(lax.ppermute(block, axis, list(enumerate(partner))))  8.97 us
    ppermute x2, starting transfers between devices, swaps(): got.append(lax.ppermute(block, tuple(sorted((axis, other))), pairs))  3.48 us
    ppermute x9, waiting for transfers between devices, swaps(): got.append(lax.ppermute(block, axis, list(enumerate(partner))))  3.3 us
    ppermute x2, starting transfers between devices, diagonal_swaps(): got.append(lax.ppermute(block, ('gx', 'gy'), pairs))  2.81 us
    ppermute x2, waiting for transfers between devices, diagonal_swaps(): got.append(lax.ppermute(block, ('gx', 'gy'), pairs))  2.81 us
    ppermute x2, waiting for transfers between devices, swaps(): got.append(lax.ppermute(block, tuple(sorted((axis, other))), pairs))  1.63 us
  transfers between devices with their start and end apart: 13, of which 5 were waited for; matrix products, arithmetic and copies ran while one was open for 0% of the time, Pallas kernels for 2%

profile of v21, /device:TPU:1, one launch (start us, length us, event | category | flops | bytes accessed | tf_op | source)
XLA Modules:
  0.0 50.3 jit_solution(4531213283204069105)
XLA Ops:
  0.0 2.6 %shard_map.64 = (f32[6,4,16,128]{3,2,1,0:T(8,128)}, f32[6,16,4,128]{3,2,1,0:T(4,128)}, f32[6,16,4,128]{3,2,1,0:T(4,128)}, f32[8,16,128]{2,1,0:T(8,128)}, f32[8,16,128]{2,1,0:T(8,128)}) custom-call(s32[1]{0:T(128)} %bitcast.where_ref, f32[16,16,128]{2,1,0:T(8,128)} %refs_0_.3, f32[16,16,128]{2,1,0:T(8,128)} %refs_1_.3, f32[16,16,128]{2,1,0:T(8,128)} %refs_2_.3, ...), custom_call_target="tpu_custom_call" | custom-call | bytes 3600000 | tf_op jit(solution)/shard_map/pallas_call | solution.py:684
  2.6 2.0 %collective-permute-start.2 = (f32[6,4,16,128]{3,2,1,0:T(8,128)}, f32[6,4,16,128]{3,2,1,0:T(8,128)S(1)}, u32[]{:S(2)}, u32[]{:S(2)}) collective-permute-start(f32[6,4,16,128]{3,2,1,0:T(8,128)} %get-tuple-element.51), channel_id=1, source_target_pairs={{0,16},{16,0},{1,17},{17,1},{2,18},{18,2},{3,19},{19,3},{4,20},{20... | collective-permute-start | bytes 589832 | tf_op jit(solution)/shard_map/ppermute | solution.py:713
  4.7 2.1 %collective-permute-start.4 = (f32[6,16,4,128]{3,2,1,0:T(4,128)}, f32[6,16,4,128]{3,2,1,0:T(4,128)S(1)}, u32[]{:S(2)}, u32[]{:S(2)}) collective-permute-start(f32[6,16,4,128]{3,2,1,0:T(4,128)} %get-tuple-element.65), channel_id=1, source_target_pairs={{0,12},{4,8},{8,4},{12,0},{1,13},{5,9},{9,5},{13,1},{2,14},{6,10},... | collective-permute-start | bytes 589832 | tf_op jit(solution)/shard_map/ppermute | solution.py:713
  6.8 0.0 collective-permute-start.5
  6.8 1.3 %collective-permute-start = (f32[8,16,128]{2,1,0:T(8,128)}, f32[8,16,128]{2,1,0:T(8,128)S(1)}, u32[]{:S(2)}, u32[]{:S(2)}) collective-permute-start(f32[8,16,128]{2,1,0:T(8,128)} %get-tuple-element.48), channel_id=1, source_target_pairs={{0,1},{1,0},{2,3},{3,2},{4,5},{5,4},{6,7},{7,6},{8,9},{9,8},{10,11... | collective-permute-start | bytes 196616 | tf_op jit(solution)/shard_map/ppermute | solution.py:713
  8.1 0.8 %collective-permute-start.1 = (f32[8,16,128]{2,1,0:T(8,128)}, f32[8,16,128]{2,1,0:T(8,128)S(1)}, u32[]{:S(2)}, u32[]{:S(2)}) collective-permute-start(f32[8,16,128]{2,1,0:T(8,128)} %get-tuple-element.49), channel_id=1, source_target_pairs={{0,4},{1,2},{2,1},{3,7},{4,0},{5,6},{6,5},{7,3},{8,12},{9,10},{10,... | collective-permute-start | bytes 196616 | tf_op jit(solution)/shard_map/ppermute | solution.py:724
  8.8 1.5 %collective-permute-done.one_ref = f32[8,16,128]{2,1,0:T(8,128)S(1)} collective-permute-done((f32[8,16,128]{2,1,0:T(8,128)}, f32[8,16,128]{2,1,0:T(8,128)S(1)}, u32[]{:S(2)}, u32[]{:S(2)}) %collective-permute-start) | collective-permute-done | bytes 65568 | tf_op jit(solution)/shard_map/ppermute | solution.py:713
  10.4 0.0 collective-permute-done.1.two_ref
  10.4 0.1 shard_map.65
  10.5 0.3 collective-permute-start.3
  10.8 0.0 collective-permute-done.2.refs_7_.refs_0_
  10.9 0.7 %shard_map.66 = (f32[24,24,128]{2,1,0:T(8,128)S(1)}, f32[24,24,128]{2,1,0:T(8,128)S(1)}, f32[24,24,128]{2,1,0:T(8,128)S(1)}, f32[24,24,128]{2,1,0:T(8,128)S(1)},...) custom-call(s32[1]{0:T(128)} %bitcast.where_ref, ...), custom_call_target="tpu_custom_call" | custom-call | bytes 7200000 | tf_op jit(solution)/shard_map/pallas_call | solution.py:684
  11.6 1.7 %collective-permute-done.3.refs_1_.refs_12_ = f32[4,16,128]{2,1,0:T(8,128)S(1)} collective-permute-done((f32[4,16,128]{2,1,0:T(8,128)S(1)}, f32[4,16,128]{2,1,0:T(8,128)S(1)}, u32[]{:S(2)}, u32[]{:S(2)}) %collective-permute-start.3) | collective-permute-done | bytes 32800 | tf_op jit(solution)/shard_map/ppermute | solution.py:713
  13.3 0.1 shard_map.67
  13.4 2.7 %collective-permute-start.6 = (f32[37,4,128]{2,1,0:T(4,128)S(1)}, f32[37,4,128]{2,1,0:T(4,128)S(1)}, u32[]{:S(2)}, u32[]{:S(2)}) collective-permute-start(f32[37,4,128]{2,1,0:T(4,128)S(1)} %get-tuple-element.68), channel_id=1, source_target_pairs={{0,16},{4,8},{8,4},{12,28},{16,0},{20,24},{24,20},{28,12},{1,17},{... | collective-permute-start | bytes 227336 | tf_op jit(solution)/shard_map/ppermute | solution.py:724
  16.1 0.4 collective-permute-start.7
  16.5 0.0 collective-permute-done.4.refs_13_
  16.5 1.6 %collective-permute-done.6.refs_15_ = f32[37,4,128]{2,1,0:T(4,128)S(1)} collective-permute-done((f32[37,4,128]{2,1,0:T(4,128)S(1)}, f32[37,4,128]{2,1,0:T(4,128)S(1)}, u32[]{:S(2)}, u32[]{:S(2)}) %collective-permute-start.6) | collective-permute-done | bytes 75808 | tf_op jit(solution)/shard_map/ppermute | solution.py:724
  18.1 2.3 %shard_map.68 = (f32[24,24,128]{2,1,0:T(8,128)S(1)}, f32[24,24,128]{2,1,0:T(8,128)S(1)}, f32[24,24,128]{2,1,0:T(8,128)S(1)}, f32[24,24,128]{2,1,0:T(8,128)S(1)},...) custom-call(s32[1]{0:T(128)} %bitcast.where_ref, ...), custom_call_target="tpu_custom_call", output_to_operand_aliasing={{0}: (2, {}), {1}: (3, {}), {2}: (4, {}), {3}: (5, {}), {4}... | custom-call | bytes 14400000 | tf_op jit(solution)/shard_map/pallas_call | solution.py:684
  20.5 0.6 %collective-permute-start.8 = (f32[5,4,8,128]{3,2,1,0:T(8,128)S(1)}, f32[5,4,8,128]{3,2,1,0:T(8,128)S(1)}, u32[]{:S(2)}, u32[]{:S(2)}) collective-permute-start(f32[5,4,8,128]{3,2,1,0:T(8,128)S(1)} %get-tuple-element.72), channel_id=1, source_target_pairs={{0,16},{16,0},{1,17},{17,1},{2,18},{18,2},{3,19},{19,3},{4,20},{20... | collective-permute-start | bytes 245768 | tf_op jit(solution)/shard_map/ppermute | solution.py:713
  21.0 1.4 %collective-permute-start.9 = (f32[5,8,4,128]{3,2,1,0:T(4,128)S(1)}, f32[5,8,4,128]{3,2,1,0:T(4,128)S(1)}, u32[]{:S(2)}, u32[]{:S(2)}) collective-permute-start(f32[5,8,4,128]{3,2,1,0:T(4,128)S(1)} %get-tuple-element.73), channel_id=1, source_target_pairs={{0,12},{4,8},{8,4},{12,0},{1,13},{5,9},{9,5},{13,1},{2,14},{6,10},... | collective-permute-start | bytes 245768 | tf_op jit(solution)/shard_map/ppermute | solution.py:713
  22.4 0.8 %collective-permute-start.10 = (f32[5,8,4,128]{3,2,1,0:T(4,128)S(1)}, f32[5,8,4,128]{3,2,1,0:T(4,128)S(1)}, u32[]{:S(2)}, u32[]{:S(2)}) collective-permute-start(f32[5,8,4,128]{3,2,1,0:T(4,128)S(1)} %get-tuple-element.74), channel_id=1, source_target_pairs={{0,4},{4,0},{8,12},{12,8},{1,5},{5,1},{9,13},{13,9},{2,6},{6,2},{1... | collective-permute-start | bytes 245768 | tf_op jit(solution)/shard_map/ppermute | solution.py:713
  23.3 1.1 %collective-permute-start.11 = (f32[15,4,128]{2,1,0:T(4,128)S(1)}, f32[15,4,128]{2,1,0:T(4,128)S(1)}, u32[]{:S(2)}, u32[]{:S(2)}) collective-permute-start(f32[15,4,128]{2,1,0:T(4,128)S(1)} %get-tuple-element.75), channel_id=1, source_target_pairs={{0,20},{4,16},{8,28},{12,24},{16,4},{20,0},{24,12},{28,8},{1,21},{... | collective-permute-start | bytes 92168 | tf_op jit(solution)/shard_map/ppermute | solution.py:738
  24.4 1.7 %collective-permute-start.12 = (f32[15,4,128]{2,1,0:T(4,128)S(1)}, f32[15,4,128]{2,1,0:T(4,128)S(1)}, u32[]{:S(2)}, u32[]{:S(2)}) collective-permute-start(f32[15,4,128]{2,1,0:T(4,128)S(1)} %get-tuple-element.76), channel_id=1, source_target_pairs={{0,16},{4,24},{8,20},{12,28},{16,0},{20,8},{24,4},{28,12},{1,17},{... | collective-permute-start | bytes 92168 | tf_op jit(solution)/shard_map/ppermute | solution.py:738
  26.1 1.0 %collective-permute-done.11.refs_3_ = f32[15,4,128]{2,1,0:T(4,128)S(1)} collective-permute-done((f32[15,4,128]{2,1,0:T(4,128)S(1)}, f32[15,4,128]{2,1,0:T(4,128)S(1)}, u32[]{:S(2)}, u32[]{:S(2)}) %collective-permute-start.11) | collective-permute-done | bytes 30752 | tf_op jit(solution)/shard_map/ppermute | solution.py:738
  27.1 1.8 %collective-permute-done.12.refs_4_ = f32[15,4,128]{2,1,0:T(4,128)S(1)} collective-permute-done((f32[15,4,128]{2,1,0:T(4,128)S(1)}, f32[15,4,128]{2,1,0:T(4,128)S(1)}, u32[]{:S(2)}, u32[]{:S(2)}) %collective-permute-start.12) | collective-permute-done | bytes 30752 | tf_op jit(solution)/shard_map/ppermute | solution.py:738
  28.9 0.0 collective-permute-done.8.refs_0_
  28.9 0.0 collective-permute-done.9.refs_1_
  28.9 0.0 collective-permute-done.10.refs_2_
  28.9 0.5 shard_map.69
  29.4 16.9 %all_to_all.5.gathered = f32[32,5,4,128]{3,2,1,0:T(4,128)S(1)} all-to-all(f32[32,5,4,128]{3,2,1,0:T(4,128)S(1)} %get-tuple-element.77), channel_id=1, replica_groups=mesh['gx'=2,'gy'=4,'gz'=4] {'gx','gy','gz'}, dimensions={0} | all-to-all | bytes 655360 | tf_op jit(solution)/shard_map/all_to_all | solution.py:820
  46.3 4.0 %shard_map.70 = f32[16,16,128]{2,1,0:T(8,128)} custom-call(s32[1]{0:T(128)} %bitcast.where_ref, f32[32,5,4,128]{3,2,1,0:T(4,128)S(1)} %all_to_all.5.gathered, f32[6,16,16,128]{3,2,1,0:T(8,128)S(1)} %get-tuple-element.78.level1, f32[24,24,128]{2,1,0:T(8,128)S(1)} %get-tuple-element.79.refs_0_, f32[24,24,128]{2,1,0:T(8,128)S(1)} %get-tuple-element.80.refs_1_, ...), custom_call_target="tpu_custom_call" | custom-call | bytes 14400000 | tf_op jit(solution)/shard_map/pallas_call | solution.py:684
  (14 shorter events, 0.0 us)
Async XLA Ops:
  0.0 10.8 %copy-start.1 = (f32[16,16,128]{2,1,0:T(8,128)S(1)}, f32[16,16,128]{2,1,0:T(8,128)}, u32[]{:S(2)}) copy-start(f32[16,16,128]{2,1,0:T(8,128)} %refs_1_.3) | copy-start | bytes 393220
  0.0 10.8 %copy-start.2 = (f32[16,16,128]{2,1,0:T(8,128)S(1)}, f32[16,16,128]{2,1,0:T(8,128)}, u32[]{:S(2)}) copy-start(f32[16,16,128]{2,1,0:T(8,128)} %refs_2_.3) | copy-start | bytes 393220
  0.0 10.8 %copy-start.3 = (f32[16,16,128]{2,1,0:T(8,128)S(1)}, f32[16,16,128]{2,1,0:T(8,128)}, u32[]{:S(2)}) copy-start(f32[16,16,128]{2,1,0:T(8,128)} %refs_3_.3) | copy-start | bytes 393220
  0.0 10.8 %copy-start.4 = (f32[16,16,128]{2,1,0:T(8,128)S(1)}, f32[16,16,128]{2,1,0:T(8,128)}, u32[]{:S(2)}) copy-start(f32[16,16,128]{2,1,0:T(8,128)} %refs_4_.3) | copy-start | bytes 393220
  0.0 10.8 %copy-start.5 = (f32[16,16,128]{2,1,0:T(8,128)S(1)}, f32[16,16,128]{2,1,0:T(8,128)}, u32[]{:S(2)}) copy-start(f32[16,16,128]{2,1,0:T(8,128)} %refs_5_.3) | copy-start | bytes 393220
  2.6 8.2 %copy-start = (f32[16,16,128]{2,1,0:T(8,128)S(1)}, f32[16,16,128]{2,1,0:T(8,128)}, u32[]{:S(2)}) copy-start(f32[16,16,128]{2,1,0:T(8,128)} %refs_0_.3) | copy-start | bytes 393220
  2.6 8.2 %collective-permute-start.2 = (f32[6,4,16,128]{3,2,1,0:T(8,128)}, f32[6,4,16,128]{3,2,1,0:T(8,128)S(1)}, u32[]{:S(2)}, u32[]{:S(2)}) collective-permute-start(f32[6,4,16,128]{3,2,1,0:T(8,128)} %get-tuple-element.51), channel_id=1, source_target_pairs={{0,16},{16,0},{1,17},{17,1},{2,18},{18,2},{3,19},{19,3},{4,20},{20... | collective-permute-start | bytes 589832 | tf_op jit(solution)/shard_map/ppermute | solution.py:713
  4.7 11.8 %collective-permute-start.4 = (f32[6,16,4,128]{3,2,1,0:T(4,128)}, f32[6,16,4,128]{3,2,1,0:T(4,128)S(1)}, u32[]{:S(2)}, u32[]{:S(2)}) collective-permute-start(f32[6,16,4,128]{3,2,1,0:T(4,128)} %get-tuple-element.65), channel_id=1, source_target_pairs={{0,12},{4,8},{8,4},{12,0},{1,13},{5,9},{9,5},{13,1},{2,14},{6,10},... | collective-permute-start | bytes 589832 | tf_op jit(solution)/shard_map/ppermute | solution.py:713
  6.8 9.7 %collective-permute-start.5 = (f32[6,16,4,128]{3,2,1,0:T(4,128)}, f32[6,16,4,128]{3,2,1,0:T(4,128)S(1)}, u32[]{:S(2)}, u32[]{:S(2)}) collective-permute-start(f32[6,16,4,128]{3,2,1,0:T(4,128)} %get-tuple-element.66), channel_id=1, source_target_pairs={{0,4},{4,0},{8,12},{12,8},{1,5},{5,1},{9,13},{13,9},{2,6},{6,2},{1... | collective-permute-start | bytes 589832 | tf_op jit(solution)/shard_map/ppermute | solution.py:713
  6.8 3.6 %collective-permute-start = (f32[8,16,128]{2,1,0:T(8,128)}, f32[8,16,128]{2,1,0:T(8,128)S(1)}, u32[]{:S(2)}, u32[]{:S(2)}) collective-permute-start(f32[8,16,128]{2,1,0:T(8,128)} %get-tuple-element.48), channel_id=1, source_target_pairs={{0,1},{1,0},{2,3},{3,2},{4,5},{5,4},{6,7},{7,6},{8,9},{9,8},{10,11... | collective-permute-start | bytes 196616 | tf_op jit(solution)/shard_map/ppermute | solution.py:713
  8.1 2.3 %collective-permute-start.1 = (f32[8,16,128]{2,1,0:T(8,128)}, f32[8,16,128]{2,1,0:T(8,128)S(1)}, u32[]{:S(2)}, u32[]{:S(2)}) collective-permute-start(f32[8,16,128]{2,1,0:T(8,128)} %get-tuple-element.49), channel_id=1, source_target_pairs={{0,4},{1,2},{2,1},{3,7},{4,0},{5,6},{6,5},{7,3},{8,12},{9,10},{10,... | collective-permute-start | bytes 196616 | tf_op jit(solution)/shard_map/ppermute | solution.py:724
  10.5 2.8 %collective-permute-start.3 = (f32[4,16,128]{2,1,0:T(8,128)S(1)}, f32[4,16,128]{2,1,0:T(8,128)S(1)}, u32[]{:S(2)}, u32[]{:S(2)}) collective-permute-start(f32[4,16,128]{2,1,0:T(8,128)S(1)} %get-tuple-element.64), channel_id=1, source_target_pairs={{0,16},{16,0},{1,17},{17,1},{2,18},{18,2},{3,19},{19,3},{4,20},{20... | collective-permute-start | bytes 98312 | tf_op jit(solution)/shard_map/ppermute | solution.py:713
  13.4 4.7 %collective-permute-start.6 = (f32[37,4,128]{2,1,0:T(4,128)S(1)}, f32[37,4,128]{2,1,0:T(4,128)S(1)}, u32[]{:S(2)}, u32[]{:S(2)}) collective-permute-start(f32[37,4,128]{2,1,0:T(4,128)S(1)} %get-tuple-element.68), channel_id=1, source_target_pairs={{0,16},{4,8},{8,4},{12,28},{16,0},{20,24},{24,20},{28,12},{1,17},{... | collective-permute-start | bytes 227336 | tf_op jit(solution)/shard_map/ppermute | solution.py:724
  16.1 2.1 %collective-permute-start.7 = (f32[37,4,128]{2,1,0:T(4,128)S(1)}, f32[37,4,128]{2,1,0:T(4,128)S(1)}, u32[]{:S(2)}, u32[]{:S(2)}) collective-permute-start(f32[37,4,128]{2,1,0:T(4,128)S(1)} %get-tuple-element.69), channel_id=1, source_target_pairs={{0,4},{4,0},{8,12},{12,8},{1,5},{5,1},{9,13},{13,9},{2,6},{6,2},{1... | collective-permute-start | bytes 227336 | tf_op jit(solution)/shard_map/ppermute | solution.py:713
  20.5 8.4 %collective-permute-start.8 = (f32[5,4,8,128]{3,2,1,0:T(8,128)S(1)}, f32[5,4,8,128]{3,2,1,0:T(8,128)S(1)}, u32[]{:S(2)}, u32[]{:S(2)}) collective-permute-start(f32[5,4,8,128]{3,2,1,0:T(8,128)S(1)} %get-tuple-element.72), channel_id=1, source_target_pairs={{0,16},{16,0},{1,17},{17,1},{2,18},{18,2},{3,19},{19,3},{4,20},{20... | collective-permute-start | bytes 245768 | tf_op jit(solution)/shard_map/ppermute | solution.py:713
  21.0 7.9 %collective-permute-start.9 = (f32[5,8,4,128]{3,2,1,0:T(4,128)S(1)}, f32[5,8,4,128]{3,2,1,0:T(4,128)S(1)}, u32[]{:S(2)}, u32[]{:S(2)}) collective-permute-start(f32[5,8,4,128]{3,2,1,0:T(4,128)S(1)} %get-tuple-element.73), channel_id=1, source_target_pairs={{0,12},{4,8},{8,4},{12,0},{1,13},{5,9},{9,5},{13,1},{2,14},{6,10},... | collective-permute-start | bytes 245768 | tf_op jit(solution)/shard_map/ppermute | solution.py:713
  22.4 6.5 %collective-permute-start.10 = (f32[5,8,4,128]{3,2,1,0:T(4,128)S(1)}, f32[5,8,4,128]{3,2,1,0:T(4,128)S(1)}, u32[]{:S(2)}, u32[]{:S(2)}) collective-permute-start(f32[5,8,4,128]{3,2,1,0:T(4,128)S(1)} %get-tuple-element.74), channel_id=1, source_target_pairs={{0,4},{4,0},{8,12},{12,8},{1,5},{5,1},{9,13},{13,9},{2,6},{6,2},{1... | collective-permute-start | bytes 245768 | tf_op jit(solution)/shard_map/ppermute | solution.py:713
  23.3 3.8 %collective-permute-start.11 = (f32[15,4,128]{2,1,0:T(4,128)S(1)}, f32[15,4,128]{2,1,0:T(4,128)S(1)}, u32[]{:S(2)}, u32[]{:S(2)}) collective-permute-start(f32[15,4,128]{2,1,0:T(4,128)S(1)} %get-tuple-element.75), channel_id=1, source_target_pairs={{0,20},{4,16},{8,28},{12,24},{16,4},{20,0},{24,12},{28,8},{1,21},{... | collective-permute-start | bytes 92168 | tf_op jit(solution)/shard_map/ppermute | solution.py:738
  24.4 4.5 %collective-permute-start.12 = (f32[15,4,128]{2,1,0:T(4,128)S(1)}, f32[15,4,128]{2,1,0:T(4,128)S(1)}, u32[]{:S(2)}, u32[]{:S(2)}) collective-permute-start(f32[15,4,128]{2,1,0:T(4,128)S(1)} %get-tuple-element.76), channel_id=1, source_target_pairs={{0,16},{4,24},{8,20},{12,28},{16,0},{20,8},{24,4},{28,12},{1,17},{... | collective-permute-start | bytes 92168 | tf_op jit(solution)/shard_map/ppermute | solution.py:738
